TPU v7x, 32 devices: a whole 2x2x4 slice. The times are simulated.
32 devices in a mesh: rows: 8 (over y, x, core), aux: 4 (over z).
Axes of the slice: x: 2, y: 2, z: 4, core: 2. Of those that a mesh axis runs over, the one named last changes fastest.
Arguments:
- pair_green_block: bfloat16 [65536, 2048], P('rows', 'aux'), may hold values from -6 to 6
- cholesky_factors: bfloat16 [65536, 512], P('rows', 'aux'), may hold values from -0.09375 to 0.09375
- green_one: float32 [256, 256], replicated, may hold values from -0.375 to 0.375
- screening: float32 [512], replicated, may hold values from 0.25 to 4
Outputs:
- section_slope: float32 [65536, 2048], P('rows', 'aux')
- collision: float32 [65536], P(('rows', 'aux'))
All inputs are finite; a program needn't handle non-finite values.
Results may differ from a plain program's by a relative error of at most 0.0029.
Values may be sent and summed in bfloat16 or wider, within the bound.
No kernel may reach another device: no remote copies, remote signals or barrier semaphores. Data moves between devices by JAX's collectives and lax.ppermute only.
A program may use at most 128 MiB of HBM per device.

v0:
```python
import jax
import jax.numpy as jnp
from jax import lax
from jax.sharding import PartitionSpec as P

NORB = 256
NAUX = 512


def dress_aux(projected, first_aux, green_one, screening):
    vec_count = projected.shape[0]
    block_pair_columns = projected.shape[1]
    shaped = projected.reshape(vec_count, block_pair_columns // NORB, NORB)
    dressed = jnp.einsum("qkm,ml->qkl", shaped, green_one, precision=lax.Precision.HIGHEST)
    weights = lax.dynamic_slice_in_dim(screening, first_aux, vec_count, 0)
    return (
        (dressed * weights[:, None, None])
        .reshape(vec_count, block_pair_columns)
        .astype(jnp.bfloat16)
    )


def local(pair_green_block, cholesky_factors, green_one, screening):
    highest = lax.Precision.HIGHEST
    block_pair_columns = pair_green_block.shape[1]
    orb_count = block_pair_columns // NORB
    chol_basis = lax.all_gather(cholesky_factors, "aux", axis=1, tiled=True)
    partial_projection = lax.dot_general(
        chol_basis, pair_green_block, (((0,), (0,)), ((), ())), preferred_element_type=jnp.float32
    )
    share_rows = NAUX // lax.axis_size("rows")
    auxiliary_portions = lax.psum_scatter(
        partial_projection, "rows", scatter_dimension=0, tiled=True
    )
    first_aux = lax.axis_index("rows") * share_rows
    dressed_portion = dress_aux(auxiliary_portions, first_aux, green_one, screening)
    dressed = lax.all_gather(dressed_portion, "rows", axis=0, tiled=True)
    section_slope = jnp.dot(chol_basis, dressed, preferred_element_type=jnp.float32)
    first_orb = lax.axis_index("aux") * orb_count
    green_function_columns = lax.dynamic_slice_in_dim(green_one, first_orb, orb_count, 1)
    trace_weights = green_function_columns.T.reshape(block_pair_columns)
    partial_collision = jnp.dot(
        section_slope, trace_weights, precision=highest, preferred_element_type=jnp.float32
    )
    collision = lax.psum_scatter(partial_collision, "aux", scatter_dimension=0, tiled=True)
    return (section_slope, collision)


def solution(mesh):
    placed = (P("rows", "aux"), P("rows", "aux"), P(), P())
    return jax.shard_map(
        local,
        mesh=mesh,
        in_specs=placed,
        out_specs=(P("rows", "aux"), P(("rows", "aux"))),
        check_vma=False,
    )
```

profile of v0, /device:TPU:0, one launch (start us, length us, event | category | flops | bytes accessed | tf_op | source)
XLA Modules:
  0.0 285.7 jit_solution(8495158315079013783)
XLA Ops:
  7.2 0.0 copy-start
  7.2 0.0 all-gather.2.cloned.1.call-start
  7.2 0.7 all-gather.2.cloned.1.call-update
  7.9 0.0 copy-start.1
  7.9 0.0 reduce-scatter.2.cloned.1.call-start
  8.0 153.5 %all-gather.2.cloned.1.call-done = bf16[8192,512]{1,0:T(8,128)(2,1)} async-done(((bf16[8192,128]{1,0:T(8,128)(2,1)}), bf16[8192,512]{1,0:T(8,128)(2,1)}) %all-gather.2.cloned.1.call-update) | async-done | bytes 8388624 | tf_op jit(solution)/shard_map/all_gather | solution.py:27
  161.4 11.2 %fusion.5 = f32[512,512]{1,0:T(8,128)} fusion(bf16[8192,512]{1,0:T(8,128)(2,1)} %all-gather.2.cloned.1.call-done, bf16[8192,512]{1,0:T(8,128)(2,1)} %param.4), kind=kOutput, calls=%fused_computation.8 | convolution fusion | flops 4294967296 | bytes 17825792 | tf_op jit(solution)/shard_map/dot_general | solution.py:28
  172.7 0.0 reduce-scatter.2.cloned.1.call-update
  172.7 0.0 copy-done
  172.7 0.1 dynamic-slice_bitcast_fusion
  172.8 0.1 copy.14
  172.9 0.8 dynamic_slice.6
  173.7 0.0 copy-done.1
  173.7 0.6 dynamic-slice
  174.9 32.1 %reduce-scatter.2.cloned.1.call-done = f32[64,512]{1,0:T(8,128)} async-done(((f32[512,512]{1,0:T(8,128)}), f32[64,512]{1,0:T(8,128)}) %reduce-scatter.2.cloned.1.call-update) | async-done | bytes 131088 | tf_op jit(solution)/shard_map/reduce_scatter | solution.py:32
  207.1 1.2 fusion.1
  208.3 9.8 %all_gather.7 = bf16[512,512]{1,0:T(8,128)(2,1)S(1)} all-gather(bf16[64,512]{1,0:T(8,128)(2,1)S(1)} %bitcast.26), channel_id=1, replica_groups=mesh['rows'=8,'aux'=4] {'rows'}, dimensions={0}, use_global_device_ids=true | all-gather | bytes 589824 | tf_op jit(solution)/shard_map/all_gather | solution.py:37
  218.1 11.5 %convolution_bitcast_fusion = f32[8192,512]{0,1:T(8,128)} fusion(bf16[512,512]{1,0:T(8,128)(2,1)S(1)} %all_gather.7, bf16[8192,512]{1,0:T(8,128)(2,1)} %all-gather.2.cloned.1.call-done), kind=kOutput, calls=%fused_computation | convolution fusion | flops 4294967296 | bytes 25690112 | tf_op jit(solution)/shard_map/dot_general | solution.py:38
  229.6 17.4 %copy.15 = f32[8192,512]{1,0:T(8,128)} copy(f32[8192,512]{0,1:T(8,128)} %convolution_bitcast_fusion) | data formatting | bytes 33554432
  247.0 12.2 %fusion.6 = f32[1,8192]{1,0:T(1,128)S(1)} fusion(f32[8192,512]{0,1:T(8,128)} %convolution_bitcast_fusion, f32[512,1]{0,1:T(1,128)S(1)} %bitcast.29), kind=kOutput, calls=%fused_computation.9 | convolution fusion | flops 50331648 | bytes 16812032 | tf_op jit(solution)/shard_map/dot_general | solution.py:42
  259.2 19.0 %all-reduce = f32[8192]{0:T(1024)S(1)} all-reduce(f32[8192]{0:T(1024)S(1)} %bitcast.27), channel_id=3, replica_groups=mesh['rows'=8,'aux'=4] {'aux'}, use_global_device_ids=true, to_apply=%region_1.0.clone | all-reduce | flops 8192 | bytes 65536
  278.2 0.6 dynamic-slice.1
  (2 shorter events, 0.0 us)
Async XLA Ops:
  7.2 165.6 %copy-start = (f32[256,256]{1,0:T(8,128)S(1)}, f32[256,256]{1,0:T(8,128)}, u32[]{:S(2)}) copy-start(f32[256,256]{1,0:T(8,128)} %param.6) | copy-start | bytes 786436
  7.2 154.3 %all-gather.2.cloned.1.call-start = ((), (), s32[]{:S(2)}) async-start(), calls=%async_computation.1 | async-start | bytes 10485760 | tf_op jit(solution)/shard_map/all_gather | solution.py:27
  7.9 165.8 %copy-start.1 = (u32[32]{0:T(128)S(1)}, u32[32]{0:T(128)}, u32[]{:S(2)}) copy-start(u32[32]{0:T(128)} %constant.21) | copy-start | bytes 388
  7.9 199.1 %reduce-scatter.2.cloned.1.call-start = ((), (), s32[]{:S(2)}) async-start(), calls=%async_computation.2 | async-start | bytes 1179648 | tf_op jit(solution)/shard_map/reduce_scatter | solution.py:32
Sparse Core Ops, SparseCore 0:
  9.6 151.8 all-gather.1
  172.8 34.1 reduce-scatter.1
where the time goes:
time: 286 us
  waiting for transfers between devices  186 us (65%)
  matrix products  36.2 us (13%)
  blocking collectives  28.8 us (10%)
  local copies, waits for them, and re-layouts  19.6 us (7%)
  between operations  14.8 us (5%)
    all_gather x1, waiting for transfers between devices, local(): chol_basis = lax.all_gather(cholesky_factors, 'aux', axis=1, tiled=True)  153 us
    reduce_scatter x1, waiting for transfers between devices, local(): lax.psum_scatter(partial_projection, 'rows', scatter_dimension=0, tiled=T...  32.1 us
    unnamed x1, blocking collectives  19 us
    unnamed x8, local copies, waits for them, and re-layouts  18.6 us
    dot_general x1, matrix products, local(): jnp.dot(section_slope, trace_weights, precision=highest, preferred_elemen...  12.2 us
    dot_general x1, matrix products, local(): jnp.dot(chol_basis, dressed, preferred_element_type=jnp.float32)  11.5 us
    dot_general x1, matrix products, local(): lax.dot_general(chol_basis, pair_green_block, (((0,), (0,)), ((), ())), p...  11.2 us
    all_gather x1, blocking collectives, local(): dressed = lax.all_gather(dressed_portion, 'rows', axis=0, tiled=True)  9.79 us
  transfers between devices with their start and end apart: 2, of which 2 were waited for; matrix products, arithmetic and copies ran while one was open for 1% of the time, Pallas kernels for 0%

commit v1 on v0

v1 whole, which is shorter than its diff:
```python
import functools

import jax
import jax.numpy as jnp
from jax import lax
from jax.experimental import pallas as pl
from jax.experimental.pallas import tpu as pltpu
from jax.sharding import PartitionSpec as P

HIGHEST = lax.Precision.HIGHEST
PIECES = 2


def ring_next(block, axis):
    count = lax.axis_size(axis)
    return lax.ppermute(block, axis, [(i, (i + 1) % count) for i in range(count)])


def sum_over(block, axis, bits):
    count = lax.axis_size(axis)
    for bit in bits:
        block = block + lax.ppermute(block, axis, [(i, i ^ bit) for i in range(count)])
    return block


def sum_over_rows(block):
    count = lax.axis_size("rows")
    if count & (count - 1):
        return lax.psum(block, "rows")
    bits = [1 << b for b in range(count.bit_length() - 1)]
    block = sum_over(block, "rows", bits[:1])
    rest = bits[1:]
    half = block.shape[0] // 2
    return jnp.concatenate(
        [sum_over(block[:half], "rows", rest), sum_over(block[half:], "rows", rest[::-1])], axis=0
    )


def project(piece, green_rows):
    return lax.dot_general(
        piece, green_rows, (((0,), (0,)), ((), ())), preferred_element_type=jnp.float32
    )


def slope_body(shards, pieces, blocks, *refs):
    dressed_ref, out_ref = refs[shards * pieces], refs[shards * pieces + 1]
    here = pl.program_id(0) // blocks
    for i in range(pieces):

        @pl.when(here == i)
        def _():
            basis = jnp.concatenate([refs[s * pieces + i][...] for s in range(shards)], axis=1)
            out_ref[...] = jnp.dot(basis, dressed_ref[...], preferred_element_type=jnp.float32)


def slope(steps, dressed):
    pieces = len(steps[0])
    length, vectors = steps[0][0].shape
    depth, columns = dressed.shape
    block = min(length, 1024)
    blocks = length // block
    factor_specs = [
        pl.BlockSpec((block, vectors), lambda g, i=i: (jnp.clip(g - i * blocks, 0, blocks - 1), 0))
        for _ in steps
        for i in range(pieces)
    ]
    rows = pieces * length
    return pl.pallas_call(
        functools.partial(slope_body, len(steps), pieces, blocks),
        grid=(pieces * blocks,),
        out_shape=jax.ShapeDtypeStruct((rows, columns), jnp.float32),
        in_specs=factor_specs + [pl.BlockSpec((depth, columns), lambda g: (0, 0))],
        out_specs=pl.BlockSpec((block, columns), lambda g: (g, 0)),
        compiler_params=pltpu.CompilerParams(vmem_limit_bytes=48 * 1024 * 1024),
        cost_estimate=pl.CostEstimate(
            flops=2 * rows * depth * columns,
            bytes_accessed=rows * depth * 2 + rows * columns * 4,
            transcendentals=0,
        ),
    )(*[piece for step in steps for piece in step], dressed)


def local(pair_green_block, cholesky_factors, green_one, screening):
    rows, columns = pair_green_block.shape
    vectors = cholesky_factors.shape[1]
    norb = green_one.shape[0]
    orb_count = columns // norb
    aux_size = lax.axis_size("aux")
    me = lax.axis_index("aux")
    owners = [lax.rem(me - step + aux_size, aux_size) for step in range(aux_size)]

    length = rows // PIECES
    pieces = [
        lax.slice_in_dim(cholesky_factors, i * length, (i + 1) * length, axis=0)
        for i in range(PIECES)
    ]
    steps = [pieces]
    for _ in range(1, aux_size):
        steps.append([ring_next(piece, "aux") for piece in steps[-1]])

    first_orb = me * orb_count
    trace_weights = lax.dynamic_slice_in_dim(green_one, first_orb, orb_count, 1).T.reshape(columns)

    dressed, traced = [], []
    for step, own_pieces in enumerate(steps):
        projection = sum(
            project(piece, pair_green_block[i * length : (i + 1) * length])
            for i, piece in enumerate(own_pieces)
        )
        projection = sum_over_rows(projection)
        weights = lax.dynamic_slice_in_dim(screening, owners[step] * vectors, vectors, 0)
        mixed = jnp.concatenate(
            [
                jnp.dot(projection[:, k * norb : (k + 1) * norb], green_one, precision=HIGHEST)
                for k in range(orb_count)
            ],
            axis=1,
        )
        dressed.append((mixed * weights[:, None]).astype(jnp.bfloat16))
        traced.append(jnp.sum(dressed[-1].astype(jnp.float32) * trace_weights[None, :], axis=1))

    section_slope = slope(steps, jnp.concatenate(dressed, axis=0))

    trace = jnp.zeros((aux_size, vectors), jnp.float32)
    for step in range(aux_size):
        trace = lax.dynamic_update_slice_in_dim(trace, traced[step][None], owners[step], 0)
    total = trace
    for shift in range(1, aux_size):
        total = total + lax.ppermute(
            trace, "aux", [(i, (i + shift) % aux_size) for i in range(aux_size)]
        )
    share = rows // aux_size
    collision = jnp.zeros((share,), jnp.float32)
    for step in range(aux_size):
        mine = lax.select_n(
            me * share >= length,
            *[lax.dynamic_slice_in_dim(piece, lax.rem(me * share, length), share, 0) for piece in steps[step]]
        ).astype(jnp.float32)
        vec = lax.dynamic_slice_in_dim(total, owners[step], 1, 0)[0]
        collision = collision + jnp.dot(mine, vec, precision=HIGHEST)
    return section_slope, collision


def solution(mesh):
    placed = (P("rows", "aux"), P("rows", "aux"), P(), P())
    return jax.shard_map(
        local,
        mesh=mesh,
        in_specs=placed,
        out_specs=(P("rows", "aux"), P(("rows", "aux"))),
        check_vma=False,
    )
```

time: 286 us -> 200 us (0.70)
  waiting for transfers between devices: 186 us -> 115 us
  starting transfers between devices: 0.08 us -> 30.6 us
  blocking collectives: 28.8 us -> 0 us
  local copies, waits for them, and re-layouts: 19.6 us -> 5.8 us
  between operations: 14.8 us -> 1.09 us
  Pallas kernels: 0 us -> 11.5 us
  matrix products: 36.2 us -> 27.3 us
  other arithmetic: 0 us -> 8.19 us
    all_gather x1 -> x0, waiting for transfers between devices: 153 us -> none  [local(): chol_basis = lax.all_gather(cholesky_factors, 'aux', axis=1, tiled=True)]
    ppermute x0 -> x29, waiting for transfers between devices: none -> 115 us  [the longest x6 97.4 us: ring_next(): lax.ppermute(block, axis, [(i, (i + 1) % count) for i in range(count)])]
    reduce_scatter x1 -> x0, waiting for transfers between devices: 32.1 us -> none  [local(): lax.psum_scatter(partial_projection, 'rows', scatter_dimension=0, tiled=T...]
    ppermute x0 -> x29, starting transfers between devices: none -> 30.6 us  [the longest x20 22.8 us: sum_over(): lax.ppermute(block, axis, [(i, i ^ bit) for i in range(count)])]
    unnamed x1 -> x0, blocking collectives: 19 us -> none
    unnamed x8 -> x23, local copies, waits for them, and re-layouts: 18.6 us -> 1.28 us
    pallas_call x0 -> x1, Pallas kernels: none -> 11.5 us  [slope(): pl.pallas_call(functools.partial(slope_body, len(steps), pieces, blocks),...]
    all_gather x1 -> x0, blocking collectives: 9.79 us -> none  [local(): dressed = lax.all_gather(dressed_portion, 'rows', axis=0, tiled=True)]
  transfers between devices with their start and end apart: 2 -> 29, of which waited for: 2 -> 16; matrix products, arithmetic and copies ran while one was open for 1% -> 15% of each run, Pallas kernels for 0% -> 6%
where the time goes in v1:
time: 200 us; the launch traced here: 199 us
  waiting for transfers between devices  115 us (58%)
  starting transfers between devices  30.6 us (15%)
  matrix products  27.3 us (14%)
  Pallas kernels  11.5 us (6%)
  other arithmetic  8.19 us (4%)
  local copies, waits for them, and re-layouts  5.8 us (3%)
    ppermute x6, waiting for transfers between devices, ring_next(): lax.ppermute(block, axis, [(i, (i + 1) % count) for i in range(count)])  97.4 us
    ppermute x20, starting transfers between devices, sum_over(): lax.ppermute(block, axis, [(i, i ^ bit) for i in range(count)])  22.8 us
    dot_general x8, matrix products, project(): lax.dot_general(piece, green_rows, (((0,), (0,)), ((), ())), preferred_el...  20.9 us
    ppermute x20, waiting for transfers between devices, sum_over(): lax.ppermute(block, axis, [(i, i ^ bit) for i in range(count)])  17.3 us
    pallas_call x1, Pallas kernels, slope(): pl.pallas_call(functools.partial(slope_body, len(steps), pieces, blocks),...  11.5 us
    ppermute x6, starting transfers between devices, ring_next(): lax.ppermute(block, axis, [(i, (i + 1) % count) for i in range(count)])  5.78 us
    add x16, other arithmetic, sum_over(): block + lax.ppermute(block, axis, [(i, i ^ bit) for i in range(count)])  5.04 us
    dot_general x4, matrix products, local(): collision = collision + jnp.dot(mine, vec, precision=HIGHEST)  4.19 us
  transfers between devices with their start and end apart: 29, of which 16 were waited for; matrix products, arithmetic and copies ran while one was open for 15% of the time, Pallas kernels for 6%

profile of v1, /device:TPU:0, one launch (start us, length us, event | category | flops | bytes accessed | tf_op | source)
XLA Modules:
  0.0 199.2 jit_solution(11934521733222973036)
XLA Ops:
  0.7 1.8 fusion.98
  2.5 3.1 %collective-permute-start = (bf16[4096,128]{1,0:T(8,128)(2,1)S(1)}, bf16[4096,128]{1,0:T(8,128)(2,1)S(1)}, u32[]{:S(2)}, u32[]{:S(2)}) collective-permute-start(bf16[4096,128]{1,0:T(8,128)(2,1)S(1)} %get-tuple-element.11.refs_0_), channel_id=1, source_target_pairs={{0,1},{1,2},{2,3},{3,0},{4,5},{5,6},{6,7},{7,4},{8,9},{9,10},{10,1... | collective-permute-start | bytes 3145736 | tf_op jit(solution)/shard_map/ppermute | solution.py:16
  5.6 1.6 collective-permute-start.1
  7.1 3.3 %fusion.6 = f32[128,512]{1,0:T(8,128)S(1)} fusion(bf16[8192,512]{1,0:T(8,128)(2,1)} %param.4, bf16[8192,128]{1,0:T(8,128)(2,1)} %param.5), kind=kOutput, calls=%fused_computation.6 | convolution fusion | flops 536870912 | bytes 5505024 | tf_op jit(solution)/shard_map/dot_general | solution.py:40
  10.4 2.7 %fusion.16 = f32[128,512]{1,0:T(8,128)} fusion(f32[128,512]{1,0:T(8,128)S(1)} %fusion.6, bf16[8192,512]{1,0:T(8,128)(2,1)S(1)} %copy-done.3, bf16[8192,128]{1,0:T(8,128)(2,1)} %param.5), kind=kOutput, calls=%fused_computation.16 | convolution fusion | flops 536936448 | bytes 5767168 | tf_op jit(solution)/shard_map/dot_general | solution.py:40
  13.1 1.9 collective-permute-done.6
  15.0 1.1 add.153
  16.1 1.6 collective-permute-start.7
  17.6 1.5 collective-permute-start.9
  19.1 34.2 %collective-permute-done.1.refs_3_ = bf16[4096,128]{1,0:T(8,128)(2,1)} collective-permute-done((bf16[4096,128]{1,0:T(8,128)(2,1)S(1)}, bf16[4096,128]{1,0:T(8,128)(2,1)}, u32[]{:S(2)}, u32[]{:S(2)}) %collective-permute-start.1) | collective-permute-done | bytes 1048608 | tf_op jit(solution)/shard_map/ppermute | solution.py:16
  53.3 3.2 %fusion.4 = f32[128,512]{1,0:T(8,128)S(1)} fusion(bf16[4096,128]{1,0:T(8,128)(2,1)} %collective-permute-done.1.refs_3_, bf16[8192,512]{1,0:T(8,128)(2,1)} %param.4), kind=kOutput, calls=%fused_computation.4 | convolution fusion | flops 536870912 | bytes 5505024 | tf_op jit(solution)/shard_map/dot_general | solution.py:40
  56.6 3.6 %fusion.19 = f32[128,512]{1,0:T(8,128)} fusion(f32[128,512]{1,0:T(8,128)S(1)} %fusion.4, bf16[4096,128]{1,0:T(8,128)(2,1)S(1)} %collective-permute-done.refs_2_, bf16[8192,512]{1,0:T(8,128)(2,1)} %param.4), kind=kOutput, calls=%fused_computation.17 | convolution fusion | flops 536936448 | bytes 5767168 | tf_op jit(solution)/shard_map/dot_general | solution.py:40
  61.0 1.5 collective-permute-start.10
  62.5 1.5 collective-permute-start.8
  65.8 1.3 collective-permute-done.10
  67.2 1.0 add.157
  69.1 1.1 collective-permute-start.2
  70.2 1.1 add.161
  71.3 1.6 collective-permute-start.12
  72.8 1.5 collective-permute-start.14
  74.6 1.7 collective-permute-done.12
  76.3 1.5 collective-permute-done.14
  78.4 1.5 collective-permute-start.13
  80.0 8.4 %collective-permute-done.3.refs_5_ = bf16[4096,128]{1,0:T(8,128)(2,1)} collective-permute-done((bf16[4096,128]{1,0:T(8,128)(2,1)}, bf16[4096,128]{1,0:T(8,128)(2,1)}, u32[]{:S(2)}, u32[]{:S(2)}) %collective-permute-start.3) | collective-permute-done | bytes 1048608 | tf_op jit(solution)/shard_map/ppermute | solution.py:16
  88.3 3.2 %fusion.2 = f32[128,512]{1,0:T(8,128)S(1)} fusion(bf16[4096,128]{1,0:T(8,128)(2,1)} %collective-permute-done.3.refs_5_, bf16[8192,512]{1,0:T(8,128)(2,1)} %param.4), kind=kOutput, calls=%fused_computation.2 | convolution fusion | flops 536870912 | bytes 5505024 | tf_op jit(solution)/shard_map/dot_general | solution.py:40
  91.6 19.1 %collective-permute-done.2.refs_4_ = bf16[4096,128]{1,0:T(8,128)(2,1)S(1)} collective-permute-done((bf16[4096,128]{1,0:T(8,128)(2,1)S(1)}, bf16[4096,128]{1,0:T(8,128)(2,1)S(1)}, u32[]{:S(2)}, u32[]{:S(2)}) %collective-permute-start.2) | collective-permute-done | bytes 1048608 | tf_op jit(solution)/shard_map/ppermute | solution.py:16
  110.7 3.3 %fusion.22 = f32[128,512]{1,0:T(8,128)S(1)} fusion(f32[128,512]{1,0:T(8,128)S(1)} %fusion.2, bf16[4096,128]{1,0:T(8,128)(2,1)S(1)} %collective-permute-done.2.refs_4_, bf16[8192,512]{1,0:T(8,128)(2,1)} %param.4), kind=kOutput, calls=%fused_computation.18 | convolution fusion | flops 536936448 | bytes 5767168 | tf_op jit(solution)/shard_map/dot_general | solution.py:40
  115.7 1.6 collective-permute-start.17
  117.2 1.5 collective-permute-start.19
  118.8 14.4 %collective-permute-done.5.refs_7_ = bf16[4096,128]{1,0:T(8,128)(2,1)S(1)} collective-permute-done((bf16[4096,128]{1,0:T(8,128)(2,1)}, bf16[4096,128]{1,0:T(8,128)(2,1)S(1)}, u32[]{:S(2)}, u32[]{:S(2)}) %collective-permute-start.5) | collective-permute-done | bytes 1048608 | tf_op jit(solution)/shard_map/ppermute | solution.py:16
  133.9 21.3 %collective-permute-done.4.refs_6_ = bf16[4096,128]{1,0:T(8,128)(2,1)S(1)} collective-permute-done((bf16[4096,128]{1,0:T(8,128)(2,1)S(1)}, bf16[4096,128]{1,0:T(8,128)(2,1)S(1)}, u32[]{:S(2)}, u32[]{:S(2)}) %collective-permute-start.4) | collective-permute-done | bytes 1048608 | tf_op jit(solution)/shard_map/ppermute | solution.py:16
  156.2 1.6 collective-permute-start.20
  157.7 1.5 collective-permute-start.18
  159.5 2.6 %collective-permute-done.20 = f32[64,512]{1,0:T(8,128)S(1)} collective-permute-done((f32[64,512]{1,0:T(8,128)S(1)}, f32[64,512]{1,0:T(8,128)S(1)}, u32[]{:S(2)}, u32[]{:S(2)}) %collective-permute-start.20) | collective-permute-done | bytes 131104 | tf_op jit(solution)/shard_map/ppermute | solution.py:22
  162.1 1.2 collective-permute-done.18
  164.0 1.5 collective-permute-start.24
  165.8 2.6 %collective-permute-done.22 = f32[64,512]{1,0:T(8,128)S(1)} collective-permute-done((f32[64,512]{1,0:T(8,128)S(1)}, f32[64,512]{1,0:T(8,128)S(1)}, u32[]{:S(2)}, u32[]{:S(2)}) %collective-permute-start.22) | collective-permute-done | bytes 131104 | tf_op jit(solution)/shard_map/ppermute | solution.py:22
  169.0 1.6 collective-permute-start.25
  170.6 1.5 collective-permute-start.23
  172.4 1.7 collective-permute-done.25
  174.1 1.5 collective-permute-done.23
  176.2 1.5 multiply_reduce_fusion
  178.5 1.9 collective-permute-start.26
  180.5 1.1 pad_maximum_fusion.refs_8_
  181.6 1.2 copy-done.2
  182.8 11.5 %shard_map.59 = f32[8192,512]{1,0:T(8,128)} custom-call(bf16[4096,128]{1,0:T(8,128)(2,1)S(1)} %get-tuple-element.11.refs_0_, bf16[4096,128]{1,0:T(8,128)(2,1)S(1)} %get-tuple-element.10.refs_1_, bf16[4096,128]{1,0:T(8,128)(2,1)S(1)} %collective-permute-done.refs_2_, bf16[4096,128]{1,0:T(8,128)(2,1)} %collective-permute-done.1.refs_3_, ...), custom_call_target="tpu_custom_call" | custom-call | flops 4294967296 | bytes 25165824 | tf_op jit(solution)/shard_map/pallas_call | solution.py:68
  195.4 1.6 fusion.32
  197.0 1.6 fusion.36
  (88 shorter events, 13.0 us)
Async XLA Ops:
  0.6 63.3 %copy-start = (f32[256,256]{1,0:T(8,128)S(1)}, f32[256,256]{1,0:T(8,128)}, u32[]{:S(2)}) copy-start(f32[256,256]{1,0:T(8,128)} %param.6) | copy-start | bytes 786436
  0.6 9.8 %copy-start.3 = (bf16[8192,512]{1,0:T(8,128)(2,1)S(1)}, bf16[8192,512]{1,0:T(8,128)(2,1)}, u32[]{:S(2)}) copy-start(bf16[8192,512]{1,0:T(8,128)(2,1)} %param.4) | copy-start | bytes 25165828
  2.5 54.1 %collective-permute-start = (bf16[4096,128]{1,0:T(8,128)(2,1)S(1)}, bf16[4096,128]{1,0:T(8,128)(2,1)S(1)}, u32[]{:S(2)}, u32[]{:S(2)}) collective-permute-start(bf16[4096,128]{1,0:T(8,128)(2,1)S(1)} %get-tuple-element.11.refs_0_), channel_id=1, source_target_pairs={{0,1},{1,2},{2,3},{3,0},{4,5},{5,6},{6,7},{7,4},{8,9},{9,10},{10,1... | collective-permute-start | bytes 3145736 | tf_op jit(solution)/shard_map/ppermute | solution.py:16
  5.6 47.8 %collective-permute-start.1 = (bf16[4096,128]{1,0:T(8,128)(2,1)S(1)}, bf16[4096,128]{1,0:T(8,128)(2,1)}, u32[]{:S(2)}, u32[]{:S(2)}) collective-permute-start(bf16[4096,128]{1,0:T(8,128)(2,1)S(1)} %get-tuple-element.10.refs_1_), channel_id=1, source_target_pairs={{0,1},{1,2},{2,3},{3,0},{4,5},{5,6},{6,7},{7,4},{8,9},{9,10},{10,1... | collective-permute-start | bytes 3145736 | tf_op jit(solution)/shard_map/ppermute | solution.py:16
  13.1 1.9 collective-permute-start.6
  16.1 44.2 %collective-permute-start.7 = (f32[64,512]{1,0:T(8,128)S(1)}, f32[64,512]{1,0:T(8,128)S(1)}, u32[]{:S(2)}, u32[]{:S(2)}) collective-permute-start(f32[64,512]{1,0:T(8,128)S(1)} %get-tuple-element.26), channel_id=1, source_target_pairs={{0,8},{4,12},{8,0},{12,4},{16,24},{20,28},{24,16},{28,20},{1,9},{5... | collective-permute-start | bytes 393224 | tf_op jit(solution)/shard_map/ppermute | solution.py:22
  17.6 42.6 %collective-permute-start.9 = (f32[64,512]{1,0:T(8,128)S(1)}, f32[64,512]{1,0:T(8,128)S(1)}, u32[]{:S(2)}, u32[]{:S(2)}) collective-permute-start(f32[64,512]{1,0:T(8,128)S(1)} %get-tuple-element.27), channel_id=1, source_target_pairs={{0,16},{4,20},{8,24},{12,28},{16,0},{20,4},{24,8},{28,12},{1,17},{... | collective-permute-start | bytes 393224 | tf_op jit(solution)/shard_map/ppermute | solution.py:22
  56.6 9.2 %copy-start.8 = (f32[512]{0:T(512)S(1)}, f32[512]{0:T(512)}, u32[]{:S(2)}) copy-start(f32[512]{0:T(512)} %param.7) | copy-start | bytes 6148
  60.2 9.9 %collective-permute-start.11 = (f32[128,512]{1,0:T(8,128)}, f32[128,512]{1,0:T(8,128)}, u32[]{:S(2)}, u32[]{:S(2)}) collective-permute-start(f32[128,512]{1,0:T(8,128)} %fusion.19), channel_id=1, source_target_pairs={{0,4},{4,0},{8,12},{12,8},{16,20},{20,16},{24,28},{28,24},{1,5},{5... | collective-permute-start | bytes 786440 | tf_op jit(solution)/shard_map/ppermute | solution.py:22
  60.3 28.1 %collective-permute-start.3 = (bf16[4096,128]{1,0:T(8,128)(2,1)}, bf16[4096,128]{1,0:T(8,128)(2,1)}, u32[]{:S(2)}, u32[]{:S(2)}) collective-permute-start(bf16[4096,128]{1,0:T(8,128)(2,1)} %collective-permute-done.1.refs_3_), channel_id=1, source_target_pairs={{0,1},{1,2},{2,3},{3,0},{4,5},{5,6},{6,7},{7,4},{8,9},{9,10},{10,1... | collective-permute-start | bytes 3145736 | tf_op jit(solution)/shard_map/ppermute | solution.py:16
  61.0 6.2 %collective-permute-start.10 = (f32[64,512]{1,0:T(8,128)}, f32[64,512]{1,0:T(8,128)}, u32[]{:S(2)}, u32[]{:S(2)}) collective-permute-start(f32[64,512]{1,0:T(8,128)} %get-tuple-element.25), channel_id=1, source_target_pairs={{0,8},{4,12},{8,0},{12,4},{16,24},{20,28},{24,16},{28,20},{1,9},{5... | collective-permute-start | bytes 393224 | tf_op jit(solution)/shard_map/ppermute | solution.py:22
  62.5 5.7 %collective-permute-start.8 = (f32[64,512]{1,0:T(8,128)S(1)}, f32[64,512]{1,0:T(8,128)}, u32[]{:S(2)}, u32[]{:S(2)}) collective-permute-start(f32[64,512]{1,0:T(8,128)S(1)} %get-tuple-element.24), channel_id=1, source_target_pairs={{0,16},{4,20},{8,24},{12,28},{16,0},{20,4},{24,8},{28,12},{1,17},{... | collective-permute-start | bytes 393224 | tf_op jit(solution)/shard_map/ppermute | solution.py:22
  69.1 41.6 %collective-permute-start.2 = (bf16[4096,128]{1,0:T(8,128)(2,1)S(1)}, bf16[4096,128]{1,0:T(8,128)(2,1)S(1)}, u32[]{:S(2)}, u32[]{:S(2)}) collective-permute-start(bf16[4096,128]{1,0:T(8,128)(2,1)S(1)} %collective-permute-done.refs_2_), channel_id=1, source_target_pairs={{0,1},{1,2},{2,3},{3,0},{4,5},{5,6},{6,7},{7,4},{8,9},{9,10},{10,1... | collective-permute-start | bytes 3145736 | tf_op jit(solution)/shard_map/ppermute | solution.py:16
  71.3 5.0 %collective-permute-start.12 = (f32[64,512]{1,0:T(8,128)S(1)}, f32[64,512]{1,0:T(8,128)S(1)}, u32[]{:S(2)}, u32[]{:S(2)}) collective-permute-start(f32[64,512]{1,0:T(8,128)S(1)} %get-tuple-element.22), channel_id=1, source_target_pairs={{0,8},{4,12},{8,0},{12,4},{16,24},{20,28},{24,16},{28,20},{1,9},{5... | collective-permute-start | bytes 393224 | tf_op jit(solution)/shard_map/ppermute | solution.py:22
  72.8 5.0 %collective-permute-start.14 = (f32[64,512]{1,0:T(8,128)S(1)}, f32[64,512]{1,0:T(8,128)S(1)}, u32[]{:S(2)}, u32[]{:S(2)}) collective-permute-start(f32[64,512]{1,0:T(8,128)S(1)} %get-tuple-element.23), channel_id=1, source_target_pairs={{0,16},{4,20},{8,24},{12,28},{16,0},{20,4},{24,8},{28,12},{1,17},{... | collective-permute-start | bytes 393224 | tf_op jit(solution)/shard_map/ppermute | solution.py:22
  77.8 55.4 %slice-start = ((s8[8388608]{0:T(1024)(128)(4,1)}), s8[4194304]{0:T(1024)(128)(4,1)S(1)}, s32[]{:S(2)}) async-start(s8[8388608]{0:T(1024)(128)(4,1)} %bitcast.42), calls=%async_computation | async-start | bytes 8388608
  77.8 36.6 %collective-permute-start.15 = (f32[64,512]{1,0:T(8,128)S(1)}, f32[64,512]{1,0:T(8,128)S(1)}, u32[]{:S(2)}, u32[]{:S(2)}) collective-permute-start(f32[64,512]{1,0:T(8,128)S(1)} %get-tuple-element.21), channel_id=1, source_target_pairs={{0,8},{4,12},{8,0},{12,4},{16,24},{20,28},{24,16},{28,20},{1,9},{5... | collective-permute-start | bytes 393224 | tf_op jit(solution)/shard_map/ppermute | solution.py:22
  78.4 36.0 %collective-permute-start.13 = (f32[64,512]{1,0:T(8,128)S(1)}, f32[64,512]{1,0:T(8,128)S(1)}, u32[]{:S(2)}, u32[]{:S(2)}) collective-permute-start(f32[64,512]{1,0:T(8,128)S(1)} %get-tuple-element.20), channel_id=1, source_target_pairs={{0,16},{4,20},{8,24},{12,28},{16,0},{20,4},{24,8},{28,12},{1,17},{... | collective-permute-start | bytes 393224 | tf_op jit(solution)/shard_map/ppermute | solution.py:22
  88.3 44.8 %collective-permute-start.5 = (bf16[4096,128]{1,0:T(8,128)(2,1)}, bf16[4096,128]{1,0:T(8,128)(2,1)S(1)}, u32[]{:S(2)}, u32[]{:S(2)}) collective-permute-start(bf16[4096,128]{1,0:T(8,128)(2,1)} %collective-permute-done.3.refs_5_), channel_id=1, source_target_pairs={{0,1},{1,2},{2,3},{3,0},{4,5},{5,6},{6,7},{7,4},{8,9},{9,10},{10,1... | collective-permute-start | bytes 3145736 | tf_op jit(solution)/shard_map/ppermute | solution.py:16
  91.6 41.6 %slice-start.1 = ((s8[8388608]{0:T(1024)(128)(4,1)}), s8[4194304]{0:T(1024)(128)(4,1)S(1)}, s32[]{:S(2)}) async-start(s8[8388608]{0:T(1024)(128)(4,1)} %bitcast.42), calls=%async_computation.1 | async-start | bytes 8388608
  110.7 5.0 %copy-start.1 = (bf16[4096,128]{1,0:T(8,128)(2,1)}, bf16[4096,128]{1,0:T(8,128)(2,1)S(1)}, u32[]{:S(2)}) copy-start(bf16[4096,128]{1,0:T(8,128)(2,1)S(1)} %collective-permute-done.2.refs_4_) | copy-start | bytes 3145732
  114.0 1.6 collective-permute-start.16
  114.1 41.2 %collective-permute-start.4 = (bf16[4096,128]{1,0:T(8,128)(2,1)S(1)}, bf16[4096,128]{1,0:T(8,128)(2,1)S(1)}, u32[]{:S(2)}, u32[]{:S(2)}) collective-permute-start(bf16[4096,128]{1,0:T(8,128)(2,1)S(1)} %collective-permute-done.2.refs_4_), channel_id=1, source_target_pairs={{0,1},{1,2},{2,3},{3,0},{4,5},{5,6},{6,7},{7,4},{8,9},{9,10},{10,1... | collective-permute-start | bytes 3145736 | tf_op jit(solution)/shard_map/ppermute | solution.py:16
  115.7 40.4 %collective-permute-start.17 = (f32[64,512]{1,0:T(8,128)S(1)}, f32[64,512]{1,0:T(8,128)S(1)}, u32[]{:S(2)}, u32[]{:S(2)}) collective-permute-start(f32[64,512]{1,0:T(8,128)S(1)} %get-tuple-element.18), channel_id=1, source_target_pairs={{0,8},{4,12},{8,0},{12,4},{16,24},{20,28},{24,16},{28,20},{1,9},{5... | collective-permute-start | bytes 393224 | tf_op jit(solution)/shard_map/ppermute | solution.py:22
  117.2 38.9 %collective-permute-start.19 = (f32[64,512]{1,0:T(8,128)S(1)}, f32[64,512]{1,0:T(8,128)S(1)}, u32[]{:S(2)}, u32[]{:S(2)}) collective-permute-start(f32[64,512]{1,0:T(8,128)S(1)} %get-tuple-element.19), channel_id=1, source_target_pairs={{0,16},{4,20},{8,24},{12,28},{16,0},{20,4},{24,8},{28,12},{1,17},{... | collective-permute-start | bytes 393224 | tf_op jit(solution)/shard_map/ppermute | solution.py:22
  133.2 22.8 %copy-start.6 = (bf16[4096,128]{1,0:T(8,128)(2,1)}, bf16[4096,128]{1,0:T(8,128)(2,1)S(1)}, u32[]{:S(2)}) copy-start(bf16[4096,128]{1,0:T(8,128)(2,1)S(1)} %collective-permute-done.5.refs_7_) | copy-start | bytes 3145732
  155.2 8.1 %copy-start.4 = (bf16[4096,128]{1,0:T(8,128)(2,1)}, bf16[4096,128]{1,0:T(8,128)(2,1)S(1)}, u32[]{:S(2)}) copy-start(bf16[4096,128]{1,0:T(8,128)(2,1)S(1)} %collective-permute-done.4.refs_6_) | copy-start | bytes 3145732
  156.0 7.3 %collective-permute-start.21 = (f32[128,512]{1,0:T(8,128)S(1)}, f32[128,512]{1,0:T(8,128)S(1)}, u32[]{:S(2)}, u32[]{:S(2)}) collective-permute-start(f32[128,512]{1,0:T(8,128)S(1)} %fusion.25), channel_id=1, source_target_pairs={{0,4},{4,0},{8,12},{12,8},{16,20},{20,16},{24,28},{28,24},{1,5},{5... | collective-permute-start | bytes 786440 | tf_op jit(solution)/shard_map/ppermute | solution.py:22
  156.2 5.9 %collective-permute-start.20 = (f32[64,512]{1,0:T(8,128)S(1)}, f32[64,512]{1,0:T(8,128)S(1)}, u32[]{:S(2)}, u32[]{:S(2)}) collective-permute-start(f32[64,512]{1,0:T(8,128)S(1)} %get-tuple-element.17), channel_id=1, source_target_pairs={{0,8},{4,12},{8,0},{12,4},{16,24},{20,28},{24,16},{28,20},{1,9},{5... | collective-permute-start | bytes 393224 | tf_op jit(solution)/shard_map/ppermute | solution.py:22
  157.7 5.6 %collective-permute-start.18 = (f32[64,512]{1,0:T(8,128)S(1)}, f32[64,512]{1,0:T(8,128)S(1)}, u32[]{:S(2)}, u32[]{:S(2)}) collective-permute-start(f32[64,512]{1,0:T(8,128)S(1)} %get-tuple-element.16), channel_id=1, source_target_pairs={{0,16},{4,20},{8,24},{12,28},{16,0},{20,4},{24,8},{28,12},{1,17},{... | collective-permute-start | bytes 393224 | tf_op jit(solution)/shard_map/ppermute | solution.py:22
  163.4 5.0 %collective-permute-start.22 = (f32[64,512]{1,0:T(8,128)S(1)}, f32[64,512]{1,0:T(8,128)S(1)}, u32[]{:S(2)}, u32[]{:S(2)}) collective-permute-start(f32[64,512]{1,0:T(8,128)S(1)} %get-tuple-element.14), channel_id=1, source_target_pairs={{0,8},{4,12},{8,0},{12,4},{16,24},{20,28},{24,16},{28,20},{1,9},{5... | collective-permute-start | bytes 393224 | tf_op jit(solution)/shard_map/ppermute | solution.py:22
  164.0 5.0 %collective-permute-start.24 = (f32[64,512]{1,0:T(8,128)S(1)}, f32[64,512]{1,0:T(8,128)S(1)}, u32[]{:S(2)}, u32[]{:S(2)}) collective-permute-start(f32[64,512]{1,0:T(8,128)S(1)} %get-tuple-element.15), channel_id=1, source_target_pairs={{0,16},{4,20},{8,24},{12,28},{16,0},{20,4},{24,8},{28,12},{1,17},{... | collective-permute-start | bytes 393224 | tf_op jit(solution)/shard_map/ppermute | solution.py:22
  169.0 5.0 %collective-permute-start.25 = (f32[64,512]{1,0:T(8,128)S(1)}, f32[64,512]{1,0:T(8,128)S(1)}, u32[]{:S(2)}, u32[]{:S(2)}) collective-permute-start(f32[64,512]{1,0:T(8,128)S(1)} %get-tuple-element.13), channel_id=1, source_target_pairs={{0,8},{4,12},{8,0},{12,4},{16,24},{20,28},{24,16},{28,20},{1,9},{5... | collective-permute-start | bytes 393224 | tf_op jit(solution)/shard_map/ppermute | solution.py:22
  170.6 5.0 %collective-permute-start.23 = (f32[64,512]{1,0:T(8,128)S(1)}, f32[64,512]{1,0:T(8,128)S(1)}, u32[]{:S(2)}, u32[]{:S(2)}) collective-permute-start(f32[64,512]{1,0:T(8,128)S(1)} %get-tuple-element.12), channel_id=1, source_target_pairs={{0,16},{4,20},{8,24},{12,28},{16,0},{20,4},{24,8},{28,12},{1,17},{... | collective-permute-start | bytes 393224 | tf_op jit(solution)/shard_map/ppermute | solution.py:22
  178.4 15.9 %collective-permute-start.28 = (f32[4,128]{1,0:T(4,128)S(1)}, f32[4,128]{1,0:T(4,128)S(1)}, u32[]{:S(2)}, u32[]{:S(2)}) collective-permute-start(f32[4,128]{1,0:T(4,128)S(1)} %dynamic_update_slice.15), channel_id=1, source_target_pairs={{0,3},{1,0},{2,1},{3,2},{4,7},{5,4},{6,5},{7,6},{8,11},{9,8},{10,9... | collective-permute-start | bytes 6152 | tf_op jit(solution)/shard_map/ppermute | solution.py:129
  178.5 15.9 %collective-permute-start.27 = (f32[4,128]{1,0:T(4,128)S(1)}, f32[4,128]{1,0:T(4,128)S(1)}, u32[]{:S(2)}, u32[]{:S(2)}) collective-permute-start(f32[4,128]{1,0:T(4,128)S(1)} %dynamic_update_slice.15), channel_id=1, source_target_pairs={{0,2},{1,3},{2,0},{3,1},{4,6},{5,7},{6,4},{7,5},{8,10},{9,11},{10,... | collective-permute-start | bytes 6152 | tf_op jit(solution)/shard_map/ppermute | solution.py:129
  178.5 15.8 %collective-permute-start.26 = (f32[4,128]{1,0:T(4,128)S(1)}, f32[4,128]{1,0:T(4,128)S(1)}, u32[]{:S(2)}, u32[]{:S(2)}) collective-permute-start(f32[4,128]{1,0:T(4,128)S(1)} %dynamic_update_slice.15), channel_id=1, source_target_pairs={{0,1},{1,2},{2,3},{3,0},{4,5},{5,6},{6,7},{7,4},{8,9},{9,10},{10,1... | collective-permute-start | bytes 6152 | tf_op jit(solution)/shard_map/ppermute | solution.py:129
  181.5 1.2 copy-start.2
  182.8 12.1 %copy-start.5 = (bf16[4096,128]{1,0:T(8,128)(2,1)S(1)}, bf16[4096,128]{1,0:T(8,128)(2,1)}, u32[]{:S(2)}) copy-start(bf16[4096,128]{1,0:T(8,128)(2,1)} %copy-done.4) | copy-start | bytes 3145732
  182.8 12.1 %copy-start.7 = (bf16[4096,128]{1,0:T(8,128)(2,1)S(1)}, bf16[4096,128]{1,0:T(8,128)(2,1)}, u32[]{:S(2)}) copy-start(bf16[4096,128]{1,0:T(8,128)(2,1)} %copy-done.6) | copy-start | bytes 3145732

commit v2 on v1

v2 whole, which is shorter than its diff:
```python
import functools

import jax
import jax.numpy as jnp
from jax import lax
from jax.experimental import pallas as pl
from jax.experimental.pallas import tpu as pltpu
from jax.sharding import PartitionSpec as P

HIGHEST = lax.Precision.HIGHEST
PIECES = 2
MIB = 1024 * 1024
FREE = pl.CostEstimate(flops=0, bytes_accessed=0, transcendentals=0)
ANYWHERE = pl.BlockSpec(memory_space=pl.ANY)


def shifted(block, axis, shift):
    count = lax.axis_size(axis)
    return lax.ppermute(block, axis, [(i, (i + shift) % count) for i in range(count)])


def exchanged(block, axis, bit):
    count = lax.axis_size(axis)
    return lax.ppermute(block, axis, [(i, i ^ bit) for i in range(count)])


def project_body(blocks, halved, *refs):
    piece_ref, green_ref, acc_ref = refs[:3]
    total_ref = refs[-1]
    at = pl.program_id(0)

    @pl.when(at == 0)
    def _():
        total_ref[...] = acc_ref[...]

    total_ref[...] += lax.dot_general(
        piece_ref[...], green_ref[...], (((0,), (0,)), ((), ())), preferred_element_type=jnp.float32
    )

    @pl.when(at == blocks - 1)
    def _():
        if halved:
            keep_ref, send_ref = refs[-3:-1]
            half = keep_ref.shape[0]
            upper = lax.rem(lax.axis_index("rows"), 2)
            keep_ref[...] = total_ref[pl.ds(upper * half, half), :]
            send_ref[...] = total_ref[pl.ds((1 - upper) * half, half), :]
        else:
            refs[-2][...] = total_ref[...]


def project(piece, green, first, so_far, halved, after):
    length, vectors = piece.shape
    columns = green.shape[1]
    block = min(length, 1024)
    blocks = length // block
    start = first // block
    whole = pl.BlockSpec((vectors, columns), lambda i: (0, 0))
    part = pl.BlockSpec((vectors // 2, columns), lambda i: (0, 0))
    return pl.pallas_call(
        functools.partial(project_body, blocks, halved),
        grid=(blocks,),
        out_shape=[jax.ShapeDtypeStruct((vectors // 2, columns), jnp.float32)] * 2
        if halved
        else jax.ShapeDtypeStruct((vectors, columns), jnp.float32),
        in_specs=[
            pl.BlockSpec((block, vectors), lambda i: (i, 0)),
            pl.BlockSpec((block, columns), lambda i: (i + start, 0)),
            whole,
        ]
        + [ANYWHERE] * len(after),
        out_specs=[part] * 2 if halved else whole,
        scratch_shapes=[pltpu.VMEM((vectors, columns), jnp.float32)],
        compiler_params=pltpu.CompilerParams(vmem_limit_bytes=12 * MIB),
        cost_estimate=FREE,
    )(piece, green, so_far, *after)


def dress_body(step, mine_ref, other_ref, weights_ref, green_ref, dressed_ref):
    half = mine_ref.shape[0]
    norb = green_ref.shape[0]
    aux_size = lax.axis_size("aux")
    owner = lax.rem(lax.axis_index("aux") - step + aux_size, aux_size)
    upper = lax.rem(lax.axis_index("rows"), 2)
    weights = weights_ref[pl.ds((owner * 2 + upper) * half, half), :]
    total = mine_ref[...] + other_ref[...]
    green = green_ref[...]
    for first in range(0, total.shape[1], norb):
        mixed = jnp.dot(
            total[:, first : first + norb],
            green,
            precision=HIGHEST,
            preferred_element_type=jnp.float32,
        )
        dressed_ref[:, first : first + norb] = (mixed * weights).astype(jnp.bfloat16)


def dress(step, mine, other, weights, green_one):
    return pl.pallas_call(
        functools.partial(dress_body, step),
        out_shape=jax.ShapeDtypeStruct(mine.shape, jnp.bfloat16),
        cost_estimate=FREE,
    )(mine, other, weights, green_one)


def join_body(mine_ref, other_ref, trace_ref, dressed_ref, traced_ref):
    half = mine_ref.shape[0]
    upper = lax.rem(lax.axis_index("rows"), 2)
    dressed_ref[pl.ds(pl.multiple_of(upper * half, half), half), :] = mine_ref[...]
    dressed_ref[pl.ds(pl.multiple_of((1 - upper) * half, half), half), :] = other_ref[...]
    traced_ref[...] = lax.dot_general(
        trace_ref[...],
        dressed_ref[...].astype(jnp.float32),
        (((1,), (1,)), ((), ())),
        precision=HIGHEST,
        preferred_element_type=jnp.float32,
    )


def join(mine, other, trace_weights):
    half, columns = mine.shape
    return pl.pallas_call(
        join_body,
        out_shape=[
            jax.ShapeDtypeStruct((2 * half, columns), jnp.bfloat16),
            jax.ShapeDtypeStruct((1, 2 * half), jnp.float32),
        ],
        cost_estimate=FREE,
    )(mine, other, trace_weights)


def sum_and_dress(step, keep, send, weights, green_one, trace_weights):
    count = lax.axis_size("rows")
    total, other = keep, exchanged(send, "rows", 1)
    bit = 2
    while bit < count:
        total = total + other
        other = exchanged(total, "rows", bit)
        bit *= 2
    mine = dress(step, total, other, weights, green_one)
    return join(mine, exchanged(mine, "rows", 1), trace_weights)


def slope_body(shards, pieces, blocks, *refs):
    dressed_refs, out_ref = refs[shards * pieces : -1], refs[-1]
    here = pl.program_id(0) // blocks
    dressed = jnp.concatenate([ref[...] for ref in dressed_refs], axis=0)
    for i in range(pieces):

        @pl.when(here == i)
        def _():
            basis = jnp.concatenate([refs[s * pieces + i][...] for s in range(shards)], axis=1)
            out_ref[...] = jnp.dot(basis, dressed, preferred_element_type=jnp.float32)


def slope(steps, dressed):
    pieces = len(steps[0])
    length, vectors = steps[0][0].shape
    columns = dressed[0].shape[1]
    depth = len(steps) * vectors
    block = min(length, 512)
    blocks = length // block
    factor_specs = [
        pl.BlockSpec((block, vectors), lambda g, i=i: (jnp.clip(g - i * blocks, 0, blocks - 1), 0))
        for _ in steps
        for i in range(pieces)
    ]
    rows = pieces * length
    return pl.pallas_call(
        functools.partial(slope_body, len(steps), pieces, blocks),
        grid=(pieces * blocks,),
        out_shape=jax.ShapeDtypeStruct((rows, columns), jnp.float32),
        in_specs=factor_specs + [pl.BlockSpec((vectors, columns), lambda g: (0, 0))] * len(steps),
        out_specs=pl.BlockSpec((block, columns), lambda g: (g, 0)),
        compiler_params=pltpu.CompilerParams(vmem_limit_bytes=16 * MIB),
        cost_estimate=pl.CostEstimate(
            flops=2 * rows * depth * columns,
            bytes_accessed=rows * depth * 2 + rows * columns * 4,
            transcendentals=0,
        ),
    )(*[piece for step in steps for piece in step], *dressed)


def collide_body(shards, pieces, per_piece, me_ref, *refs):
    trace_refs, out_ref = refs[shards * pieces : -1], refs[-1]
    trace = trace_refs[0][...]
    for shift in range(1, shards):
        came = trace_refs[shift][...]
        trace = trace + jnp.concatenate([came[shards - shift :], came[: shards - shift]], axis=0)
    here = me_ref[0] // per_piece
    for i in range(pieces):

        @pl.when(here == i)
        def _():
            total = jnp.zeros(out_ref.shape, jnp.float32)
            for s in range(shards):
                row = trace[s : s + 1]
                high = row.astype(jnp.bfloat16)
                rest = row - high.astype(jnp.float32)
                middle = rest.astype(jnp.bfloat16)
                low = (rest - middle.astype(jnp.float32)).astype(jnp.bfloat16)
                for part in (low, middle, high):
                    total += lax.dot_general(
                        part,
                        refs[s * pieces + i][...],
                        (((1,), (1,)), ((), ())),
                        preferred_element_type=jnp.float32,
                    )
            out_ref[...] = total


def collide(steps, traces):
    shards, pieces = len(steps), len(steps[0])
    length, vectors = steps[0][0].shape
    per_piece = shards // pieces
    share = length // per_piece
    return pl.pallas_call(
        functools.partial(collide_body, shards, pieces, per_piece),
        grid_spec=pltpu.PrefetchScalarGridSpec(
            num_scalar_prefetch=1,
            grid=(1,),
            in_specs=[
                pl.BlockSpec(
                    (share, vectors),
                    lambda g, me, i=i: (jnp.clip(me[0] - i * per_piece, 0, per_piece - 1), 0),
                )
                for _ in steps
                for i in range(pieces)
            ]
            + [pl.BlockSpec((shards, vectors), lambda g, me: (0, 0))] * shards,
            out_specs=pl.BlockSpec((1, share), lambda g, me: (0, 0)),
        ),
        out_shape=jax.ShapeDtypeStruct((1, share), jnp.float32),
        compiler_params=pltpu.CompilerParams(vmem_limit_bytes=16 * MIB),
        cost_estimate=FREE,
    )(
        lax.axis_index("aux").astype(jnp.int32)[None],
        *[piece for step in steps for piece in step],
        *traces,
    )[0]


def local(pair_green_block, cholesky_factors, green_one, screening):
    rows, columns = pair_green_block.shape
    vectors = cholesky_factors.shape[1]
    norb = green_one.shape[0]
    orb_count = columns // norb
    aux_size = lax.axis_size("aux")
    me = lax.axis_index("aux")
    length = rows // PIECES

    trace_weights = lax.dynamic_slice_in_dim(
        green_one, me * orb_count, orb_count, 1
    ).T.reshape(1, columns)
    weights = screening[:, None]
    zeros = jnp.zeros((vectors, columns), jnp.float32)

    steps, dressed, traced = [], [], []
    for step in range(aux_size):
        if step == 0:
            pieces = [
                lax.slice_in_dim(cholesky_factors, i * length, (i + 1) * length, axis=0)
                for i in range(PIECES)
            ]
        else:
            pieces = [shifted(piece, "aux", 1) for piece in steps[-1]]
        steps.append(pieces)
        so_far = zeros
        for i, piece in enumerate(pieces):
            so_far = project(
                piece, pair_green_block, i * length, so_far, i == PIECES - 1,
                dressed[-1:] + traced[-1:],
            )
        both, trace = sum_and_dress(step, *so_far, weights, green_one, trace_weights)
        dressed.append(both)
        traced.append(trace)

    trace = jnp.concatenate(traced, axis=0)
    traces = [trace] + [shifted(trace, "aux", shift) for shift in range(1, aux_size)]
    section_slope = slope(steps, dressed)
    return section_slope, collide(steps, traces)


def solution(mesh):
    placed = (P("rows", "aux"), P("rows", "aux"), P(), P())
    return jax.shard_map(
        local,
        mesh=mesh,
        in_specs=placed,
        out_specs=(P("rows", "aux"), P(("rows", "aux"))),
        check_vma=False,
    )
```

time: 200 us -> 220 us (1.10)
  Pallas kernels: 11.5 us -> 53.2 us
  matrix products: 27.3 us -> 0 us
  local copies, waits for them, and re-layouts: 5.8 us -> 28.8 us
  other arithmetic: 8.19 us -> 0.78 us
  waiting for transfers between devices: 115 us -> 109 us
  starting transfers between devices: 30.6 us -> 25.7 us
    pallas_call x0 -> x17, Pallas kernels: none -> 37.4 us  [the longest x8 17.7 us: project(): pl.pallas_call(functools.partial(project_body, blocks, halved), grid=(blo...]
    dot_general x20 -> x0, matrix products: 27.3 us -> none  [the longest x8 20.9 us: project(): lax.dot_general(piece, green_rows, (((0,), (0,)), ((), ())), preferred_el...]
    unnamed x23 -> x57, local copies, waits for them, and re-layouts: 1.28 us -> 25.2 us
    add x18 -> x8, other arithmetic: 5.67 us -> 0.16 us  [sum_and_dress(): total = total + other]
    ppermute x29 -> x25, waiting for transfers between devices: 115 us -> 109 us  [the longest x9 74.4 us: shifted(): lax.ppermute(block, axis, [(i, (i + shift) % count) for i in range(count)])]
    ppermute x29 -> x25, starting transfers between devices: 30.6 us -> 25.7 us  [the longest x16 15.4 us: exchanged(): return lax.ppermute(block, axis, [(i, i ^ bit) for i in range(count)])]
    pallas_call x1, Pallas kernels: 11.5 us -> 15.8 us  [slope(): pl.pallas_call(functools.partial(slope_body, len(steps), pieces, blocks),...]
  transfers between devices with their start and end apart: 29 -> 25, of which waited for: 16 -> 18; matrix products, arithmetic and copies ran while one was open for 15% -> 1% of each run, Pallas kernels for 6% -> 19%
where the time goes in v2:
time: 220 us; the launch traced here: 219 us
  waiting for transfers between devices  109 us (50%)
  Pallas kernels  53.2 us (24%)
  local copies, waits for them, and re-layouts  28.8 us (13%)
  starting transfers between devices  25.7 us (12%)
    ppermute x9, waiting for transfers between devices, shifted(): lax.ppermute(block, axis, [(i, (i + shift) % count) for i in range(count)])  74.4 us
    ppermute x16, waiting for transfers between devices, exchanged(): return lax.ppermute(block, axis, [(i, i ^ bit) for i in range(count)])  34.9 us
    unnamed x57, local copies, waits for them, and re-layouts  25.2 us
    pallas_call x8, Pallas kernels, project(): pl.pallas_call(functools.partial(project_body, blocks, halved), grid=(blo...  17.7 us
    pallas_call x1, Pallas kernels, slope(): pl.pallas_call(functools.partial(slope_body, len(steps), pieces, blocks),...  15.8 us
    ppermute x16, starting transfers between devices, exchanged(): return lax.ppermute(block, axis, [(i, i ^ bit) for i in range(count)])  15.4 us
    ppermute x9, starting transfers between devices, shifted(): lax.ppermute(block, axis, [(i, (i + shift) % count) for i in range(count)])  10.3 us
    pallas_call x4, Pallas kernels, dress(): pl.pallas_call(functools.partial(dress_body, step), out_shape=jax.ShapeDt...  8.79 us
  transfers between devices with their start and end apart: 25, of which 18 were waited for; matrix products, arithmetic and copies ran while one was open for 1% of the time, Pallas kernels for 19%

profile of v2, /device:TPU:0, one launch (start us, length us, event | category | flops | bytes accessed | tf_op | source)
XLA Modules:
  0.0 218.6 jit_solution(2083834382166424367)
XLA Ops:
  0.6 1.7 fusion
  2.3 3.1 %collective-permute-start = (bf16[4096,128]{1,0:T(8,128)(2,1)S(1)}, bf16[4096,128]{1,0:T(8,128)(2,1)S(1)}, u32[]{:S(2)}, u32[]{:S(2)}) collective-permute-start(bf16[4096,128]{1,0:T(8,128)(2,1)S(1)} %get-tuple-element.35.refs_0_), channel_id=1, source_target_pairs={{0,1},{1,2},{2,3},{3,0},{4,5},{5,6},{6,7},{7,4},{8,9},{9,10},{10,1... | collective-permute-start | bytes 3145736 | tf_op jit(solution)/shard_map/ppermute | solution.py:19
  5.4 1.6 collective-permute-start.1
  7.0 24.4 %collective-permute-done.refs_0_.refs_2_ = bf16[4096,128]{1,0:T(8,128)(2,1)S(1)} collective-permute-done((bf16[4096,128]{1,0:T(8,128)(2,1)S(1)}, bf16[4096,128]{1,0:T(8,128)(2,1)S(1)}, u32[]{:S(2)}, u32[]{:S(2)}) %collective-permute-start) | collective-permute-done | bytes 1048608 | tf_op jit(solution)/shard_map/ppermute | solution.py:19
  31.4 22.4 %collective-permute-done.1.refs_0_.refs_3_ = bf16[4096,128]{1,0:T(8,128)(2,1)S(1)} collective-permute-done((bf16[4096,128]{1,0:T(8,128)(2,1)S(1)}, bf16[4096,128]{1,0:T(8,128)(2,1)S(1)}, u32[]{:S(2)}, u32[]{:S(2)}) %collective-permute-start.1) | collective-permute-done | bytes 1048608 | tf_op jit(solution)/shard_map/ppermute | solution.py:19
  53.9 3.7 %copy-done = bf16[8192,512]{1,0:T(8,128)(2,1)S(1)} copy-done((bf16[8192,512]{1,0:T(8,128)(2,1)S(1)}, bf16[8192,512]{1,0:T(8,128)(2,1)}, u32[]{:S(2)}) %copy-start) | copy-done | bytes 8388632
  59.0 2.0 copy-done.1
  61.0 1.4 shard_map.60
  63.9 1.8 collective-permute-start.7
  65.7 3.8 %collective-permute-done.7 = f32[64,512]{1,0:T(8,128)S(1)} collective-permute-done((f32[64,512]{1,0:T(8,128)S(1)}, f32[64,512]{1,0:T(8,128)S(1)}, u32[]{:S(2)}, u32[]{:S(2)}) %collective-permute-start.7) | collective-permute-done | bytes 131104 | tf_op jit(solution)/shard_map/ppermute | solution.py:24
  69.5 1.8 collective-permute-start.8
  71.4 5.1 %collective-permute-done.2.refs_0_.refs_4_ = bf16[4096,128]{1,0:T(8,128)(2,1)} collective-permute-done((bf16[4096,128]{1,0:T(8,128)(2,1)S(1)}, bf16[4096,128]{1,0:T(8,128)(2,1)}, u32[]{:S(2)}, u32[]{:S(2)}) %collective-permute-start.2) | collective-permute-done | bytes 1048608 | tf_op jit(solution)/shard_map/ppermute | solution.py:19
  76.5 22.4 %collective-permute-done.3.refs_0_.refs_5_ = bf16[4096,128]{1,0:T(8,128)(2,1)} collective-permute-done((bf16[4096,128]{1,0:T(8,128)(2,1)S(1)}, bf16[4096,128]{1,0:T(8,128)(2,1)}, u32[]{:S(2)}, u32[]{:S(2)}) %collective-permute-start.3) | collective-permute-done | bytes 1048608 | tf_op jit(solution)/shard_map/ppermute | solution.py:19
  99.8 2.2 %shard_map.61.mine_ref = bf16[64,512]{1,0:T(8,128)(2,1)} custom-call(f32[64,512]{1,0:T(8,128)} %copy-done.21, f32[64,512]{1,0:T(8,128)} %collective-permute-done.8.other_ref, f32[512,1]{1,0:T(8,128)} %copy.7.weights_ref, f32[256,256]{1,0:T(8,128)} %green_ref.7), custom_call_target="tpu_custom_call" | custom-call | tf_op jit(solution)/shard_map/pallas_call | solution.py:99
  103.7 1.8 shard_map.62
  105.5 3.4 %copy-done.2 = bf16[8192,512]{1,0:T(8,128)(2,1)S(1)} copy-done((bf16[8192,512]{1,0:T(8,128)(2,1)S(1)}, bf16[8192,512]{1,0:T(8,128)(2,1)}, u32[]{:S(2)}) %copy-start.2) | copy-done | bytes 8388632
  111.9 1.4 shard_map.64
  114.9 1.8 collective-permute-start.11
  116.7 4.0 %collective-permute-done.11 = f32[64,512]{1,0:T(8,128)S(1)} collective-permute-done((f32[64,512]{1,0:T(8,128)S(1)}, f32[64,512]{1,0:T(8,128)S(1)}, u32[]{:S(2)}, u32[]{:S(2)}) %collective-permute-start.11) | collective-permute-done | bytes 131104 | tf_op jit(solution)/shard_map/ppermute | solution.py:24
  120.7 1.8 collective-permute-start.12
  122.6 3.4 %collective-permute-done.12.other_ref = f32[64,512]{1,0:T(8,128)} collective-permute-done((f32[64,512]{1,0:T(8,128)S(1)}, f32[64,512]{1,0:T(8,128)}, u32[]{:S(2)}, u32[]{:S(2)}) %collective-permute-start.12) | collective-permute-done | bytes 131104 | tf_op jit(solution)/shard_map/ppermute | solution.py:24
  126.0 2.2 %shard_map.65.mine_ref = bf16[64,512]{1,0:T(8,128)(2,1)} custom-call(f32[64,512]{1,0:T(8,128)} %copy-done.23, f32[64,512]{1,0:T(8,128)} %collective-permute-done.12.other_ref, f32[512,1]{1,0:T(8,128)} %copy.7.weights_ref, f32[256,256]{1,0:T(8,128)} %green_ref.7), custom_call_target="tpu_custom_call" | custom-call | tf_op jit(solution)/shard_map/pallas_call | solution.py:99
  128.2 1.5 collective-permute-done.13.other_ref
  130.3 1.8 shard_map.66
  132.0 3.4 %copy-done.3 = bf16[8192,512]{1,0:T(8,128)(2,1)S(1)} copy-done((bf16[8192,512]{1,0:T(8,128)(2,1)S(1)}, bf16[8192,512]{1,0:T(8,128)(2,1)}, u32[]{:S(2)}) %copy-start.3) | copy-done | bytes 8388632
  137.0 3.0 %shard_map.67.refs_2_ = f32[128,512]{1,0:T(8,128)S(1)} custom-call(bf16[4096,128]{1,0:T(8,128)(2,1)} %collective-permute-done.2.refs_0_.refs_4_, bf16[8192,512]{1,0:T(8,128)(2,1)S(1)} %copy-done.3, f32[128,512]{1,0:T(8,128)S(1)} %broadcast_in_dim.9.refs_2_, bf16[128,512]{1,0:T(8,128)(2,1)S(1)} %copy-done.10, f32[1,128]{1,0:T(1,128)S(1)} %copy-done.17), custom_call_target="tpu_custom_call" | custom-call | tf_op jit(solution)/shard_map/pallas_call | solution.py:60
  140.0 3.0 %shard_map.68 = (f32[64,512]{1,0:T(8,128)S(1)}, f32[64,512]{1,0:T(8,128)S(1)}) custom-call(bf16[4096,128]{1,0:T(8,128)(2,1)} %collective-permute-done.3.refs_0_.refs_5_, bf16[8192,512]{1,0:T(8,128)(2,1)S(1)} %copy-done.3, f32[128,512]{1,0:T(8,128)S(1)} %shard_map.67.refs_2_, bf16[128,512]{1,0:T(8,128)(2,1)S(1)} %copy-done.10, f32[1,128]{1,0:T(1,128)S(1)} %copy-done.17), custom_call_target="tpu_custom_call" | custom-call | tf_op jit(solution)/shard_map/pallas_call | solution.py:60
  144.4 1.8 collective-permute-start.15
  146.2 3.9 %collective-permute-done.15 = f32[64,512]{1,0:T(8,128)S(1)} collective-permute-done((f32[64,512]{1,0:T(8,128)S(1)}, f32[64,512]{1,0:T(8,128)S(1)}, u32[]{:S(2)}, u32[]{:S(2)}) %collective-permute-start.15) | collective-permute-done | bytes 131104 | tf_op jit(solution)/shard_map/ppermute | solution.py:24
  150.1 1.8 collective-permute-start.16
  151.9 3.3 %collective-permute-done.16.other_ref = f32[64,512]{1,0:T(8,128)} collective-permute-done((f32[64,512]{1,0:T(8,128)S(1)}, f32[64,512]{1,0:T(8,128)}, u32[]{:S(2)}, u32[]{:S(2)}) %collective-permute-start.16) | collective-permute-done | bytes 131104 | tf_op jit(solution)/shard_map/ppermute | solution.py:24
  155.2 2.2 %shard_map.69.mine_ref = bf16[64,512]{1,0:T(8,128)(2,1)} custom-call(f32[64,512]{1,0:T(8,128)} %copy-done.24, f32[64,512]{1,0:T(8,128)} %collective-permute-done.16.other_ref, f32[512,1]{1,0:T(8,128)} %copy.7.weights_ref, f32[256,256]{1,0:T(8,128)} %green_ref.7), custom_call_target="tpu_custom_call" | custom-call | tf_op jit(solution)/shard_map/pallas_call | solution.py:99
  157.4 1.5 collective-permute-done.17.other_ref
  159.5 1.7 shard_map.70
  161.2 3.4 %copy-done.4 = bf16[8192,512]{1,0:T(8,128)(2,1)S(1)} copy-done((bf16[8192,512]{1,0:T(8,128)(2,1)S(1)}, bf16[8192,512]{1,0:T(8,128)(2,1)}, u32[]{:S(2)}) %copy-start.4) | copy-done | bytes 8388632
  166.1 3.0 %shard_map.71.refs_2_ = f32[128,512]{1,0:T(8,128)S(1)} custom-call(bf16[4096,128]{1,0:T(8,128)(2,1)} %collective-permute-done.4.refs_0_.refs_6_, bf16[8192,512]{1,0:T(8,128)(2,1)S(1)} %copy-done.4, f32[128,512]{1,0:T(8,128)S(1)} %broadcast_in_dim.9.refs_2_, bf16[128,512]{1,0:T(8,128)(2,1)S(1)} %copy-done.12, f32[1,128]{1,0:T(1,128)S(1)} %copy-done.19), custom_call_target="tpu_custom_call" | custom-call | tf_op jit(solution)/shard_map/pallas_call | solution.py:60
  169.2 3.1 %shard_map.72 = (f32[64,512]{1,0:T(8,128)S(1)}, f32[64,512]{1,0:T(8,128)S(1)}) custom-call(bf16[4096,128]{1,0:T(8,128)(2,1)} %collective-permute-done.5.refs_0_.refs_7_, bf16[8192,512]{1,0:T(8,128)(2,1)S(1)} %copy-done.4, f32[128,512]{1,0:T(8,128)S(1)} %shard_map.71.refs_2_, bf16[128,512]{1,0:T(8,128)(2,1)S(1)} %copy-done.12, f32[1,128]{1,0:T(1,128)S(1)} %copy-done.20), custom_call_target="tpu_custom_call" | custom-call | tf_op jit(solution)/shard_map/pallas_call | solution.py:60
  173.7 1.8 collective-permute-start.19
  175.5 3.8 %collective-permute-done.19 = f32[64,512]{1,0:T(8,128)S(1)} collective-permute-done((f32[64,512]{1,0:T(8,128)S(1)}, f32[64,512]{1,0:T(8,128)S(1)}, u32[]{:S(2)}, u32[]{:S(2)}) %collective-permute-start.19) | collective-permute-done | bytes 131104 | tf_op jit(solution)/shard_map/ppermute | solution.py:24
  180.0 1.7 collective-permute-start.20
  181.8 3.3 %collective-permute-done.20.other_ref = f32[64,512]{1,0:T(8,128)} collective-permute-done((f32[64,512]{1,0:T(8,128)S(1)}, f32[64,512]{1,0:T(8,128)}, u32[]{:S(2)}, u32[]{:S(2)}) %collective-permute-start.20) | collective-permute-done | bytes 131104 | tf_op jit(solution)/shard_map/ppermute | solution.py:24
  185.1 2.2 %shard_map.73.mine_ref = bf16[64,512]{1,0:T(8,128)(2,1)} custom-call(f32[64,512]{1,0:T(8,128)} %copy-done.22, f32[64,512]{1,0:T(8,128)} %collective-permute-done.20.other_ref, f32[512,1]{1,0:T(8,128)} %copy.7.weights_ref, f32[256,256]{1,0:T(8,128)} %green_ref.7), custom_call_target="tpu_custom_call" | custom-call | tf_op jit(solution)/shard_map/pallas_call | solution.py:99
  187.3 1.6 collective-permute-done.21.other_ref
  188.9 1.7 shard_map.74
  191.2 1.6 collective-permute-start.22
  192.8 2.8 %collective-permute-start.23 = (f32[4,128]{1,0:T(4,128)S(1)}, f32[4,128]{1,0:T(4,128)S(1)}, u32[]{:S(2)}, u32[]{:S(2)}) collective-permute-start(f32[4,128]{1,0:T(4,128)S(1)} %pad_maximum_fusion.refs_8_), channel_id=1, source_target_pairs={{0,2},{1,3},{2,0},{3,1},{4,6},{5,7},{6,4},{7,5},{8,10},{9,11},{10,... | collective-permute-start | bytes 6152 | tf_op jit(solution)/shard_map/ppermute | solution.py:19
  198.9 15.8 %shard_map.75 = f32[8192,512]{1,0:T(8,128)} custom-call(bf16[4096,128]{1,0:T(8,128)(2,1)S(1)} %get-tuple-element.35.refs_0_, bf16[4096,128]{1,0:T(8,128)(2,1)S(1)} %get-tuple-element.34.refs_0_.refs_1_, bf16[4096,128]{1,0:T(8,128)(2,1)S(1)} %collective-permute-done.refs_0_.refs_2_, bf16[4096,128]{1,0:T(8,128)(2,1)S(1)} %copy-done.7, ...), custom_call_target="tpu_custom_call" | custom-call | flops 4294967296 | bytes 25165824 | tf_op jit(solution)/shard_map/pallas_call | solution.py:169
  214.8 3.9 %shard_map.76 = f32[1,2048]{1,0:T(1,128)} custom-call(s32[1]{0:T(128)} %bitcast.2.me_ref, bf16[4096,128]{1,0:T(8,128)(2,1)S(1)} %get-tuple-element.35.refs_0_, bf16[4096,128]{1,0:T(8,128)(2,1)S(1)} %get-tuple-element.34.refs_0_.refs_1_, bf16[4096,128]{1,0:T(8,128)(2,1)S(1)} %collective-permute-done.refs_0_.refs_2_, bf16[4096,128]{1,0:T(8,128)(2,1)S(1)} %copy-done.7, ...), custom_call_target="tpu_custom_call" | custom-call | tf_op jit(solution)/shard_map/pallas_call | solution.py:217
  (91 shorter events, 21.9 us)
Async XLA Ops:
  2.3 29.1 %collective-permute-start = (bf16[4096,128]{1,0:T(8,128)(2,1)S(1)}, bf16[4096,128]{1,0:T(8,128)(2,1)S(1)}, u32[]{:S(2)}, u32[]{:S(2)}) collective-permute-start(bf16[4096,128]{1,0:T(8,128)(2,1)S(1)} %get-tuple-element.35.refs_0_), channel_id=1, source_target_pairs={{0,1},{1,2},{2,3},{3,0},{4,5},{5,6},{6,7},{7,4},{8,9},{9,10},{10,1... | collective-permute-start | bytes 3145736 | tf_op jit(solution)/shard_map/ppermute | solution.py:19
  5.4 48.5 %collective-permute-start.1 = (bf16[4096,128]{1,0:T(8,128)(2,1)S(1)}, bf16[4096,128]{1,0:T(8,128)(2,1)S(1)}, u32[]{:S(2)}, u32[]{:S(2)}) collective-permute-start(bf16[4096,128]{1,0:T(8,128)(2,1)S(1)} %get-tuple-element.34.refs_0_.refs_1_), channel_id=1, source_target_pairs={{0,1},{1,2},{2,3},{3,0},{4,5},{5,6},{6,7},{7,4},{8,9},{9,10},{10,1... | collective-permute-start | bytes 3145736 | tf_op jit(solution)/shard_map/ppermute | solution.py:19
  31.4 45.0 %collective-permute-start.2 = (bf16[4096,128]{1,0:T(8,128)(2,1)S(1)}, bf16[4096,128]{1,0:T(8,128)(2,1)}, u32[]{:S(2)}, u32[]{:S(2)}) collective-permute-start(bf16[4096,128]{1,0:T(8,128)(2,1)S(1)} %collective-permute-done.refs_0_.refs_2_), channel_id=1, source_target_pairs={{0,1},{1,2},{2,3},{3,0},{4,5},{5,6},{6,7},{7,4},{8,9},{9,10},{10,1... | collective-permute-start | bytes 3145736 | tf_op jit(solution)/shard_map/ppermute | solution.py:19
  53.9 8.6 %copy-start.5 = (bf16[4096,128]{1,0:T(8,128)(2,1)}, bf16[4096,128]{1,0:T(8,128)(2,1)S(1)}, u32[]{:S(2)}) copy-start(bf16[4096,128]{1,0:T(8,128)(2,1)S(1)} %collective-permute-done.1.refs_0_.refs_3_) | copy-start | bytes 3145732
  53.9 45.0 %collective-permute-start.3 = (bf16[4096,128]{1,0:T(8,128)(2,1)S(1)}, bf16[4096,128]{1,0:T(8,128)(2,1)}, u32[]{:S(2)}, u32[]{:S(2)}) collective-permute-start(bf16[4096,128]{1,0:T(8,128)(2,1)S(1)} %collective-permute-done.1.refs_0_.refs_3_), channel_id=1, source_target_pairs={{0,1},{1,2},{2,3},{3,0},{4,5},{5,6},{6,7},{7,4},{8,9},{9,10},{10,1... | collective-permute-start | bytes 3145736 | tf_op jit(solution)/shard_map/ppermute | solution.py:19
  53.9 3.7 %copy-start = (bf16[8192,512]{1,0:T(8,128)(2,1)S(1)}, bf16[8192,512]{1,0:T(8,128)(2,1)}, u32[]{:S(2)}) copy-start(bf16[8192,512]{1,0:T(8,128)(2,1)} %refs_1_.15) | copy-start | bytes 25165828
  57.6 3.4 %copy-start.1 = (bf16[8192,512]{1,0:T(8,128)(2,1)S(1)}, bf16[8192,512]{1,0:T(8,128)(2,1)}, u32[]{:S(2)}) copy-start(bf16[8192,512]{1,0:T(8,128)(2,1)} %refs_1_.15) | copy-start | bytes 25165828
  57.7 41.3 %copy-start.27 = (f32[512]{0:T(512)S(1)}, f32[512]{0:T(512)}, u32[]{:S(2)}) copy-start(f32[512]{0:T(512)} %param.7) | copy-start | bytes 6148
  62.5 1.4 collective-permute-start.6
  63.9 5.6 %collective-permute-start.7 = (f32[64,512]{1,0:T(8,128)S(1)}, f32[64,512]{1,0:T(8,128)S(1)}, u32[]{:S(2)}, u32[]{:S(2)}) collective-permute-start(f32[64,512]{1,0:T(8,128)S(1)} %add.27), channel_id=1, source_target_pairs={{0,8},{4,12},{8,0},{12,4},{16,24},{20,28},{24,16},{28,20},{1,9},{5... | collective-permute-start | bytes 393224 | tf_op jit(solution)/shard_map/ppermute | solution.py:24
  69.5 30.3 %copy-start.21 = (f32[64,512]{1,0:T(8,128)}, f32[64,512]{1,0:T(8,128)S(1)}, u32[]{:S(2)}) copy-start(f32[64,512]{1,0:T(8,128)S(1)} %add.28.mine_ref) | copy-start | bytes 393220
  69.5 30.3 %collective-permute-start.8 = (f32[64,512]{1,0:T(8,128)S(1)}, f32[64,512]{1,0:T(8,128)}, u32[]{:S(2)}, u32[]{:S(2)}) collective-permute-start(f32[64,512]{1,0:T(8,128)S(1)} %add.28.mine_ref), channel_id=1, source_target_pairs={{0,16},{4,20},{8,24},{12,28},{16,0},{20,4},{24,8},{28,12},{1,17},{... | collective-permute-start | bytes 393224 | tf_op jit(solution)/shard_map/ppermute | solution.py:24
  76.4 84.8 %collective-permute-start.4 = (bf16[4096,128]{1,0:T(8,128)(2,1)}, bf16[4096,128]{1,0:T(8,128)(2,1)}, u32[]{:S(2)}, u32[]{:S(2)}) collective-permute-start(bf16[4096,128]{1,0:T(8,128)(2,1)} %collective-permute-done.2.refs_0_.refs_4_), channel_id=1, source_target_pairs={{0,1},{1,2},{2,3},{3,0},{4,5},{5,6},{6,7},{7,4},{8,9},{9,10},{10,1... | collective-permute-start | bytes 3145736 | tf_op jit(solution)/shard_map/ppermute | solution.py:19
  98.9 70.3 %collective-permute-start.5 = (bf16[4096,128]{1,0:T(8,128)(2,1)}, bf16[4096,128]{1,0:T(8,128)(2,1)}, u32[]{:S(2)}, u32[]{:S(2)}) collective-permute-start(bf16[4096,128]{1,0:T(8,128)(2,1)} %collective-permute-done.3.refs_0_.refs_5_), channel_id=1, source_target_pairs={{0,1},{1,2},{2,3},{3,0},{4,5},{5,6},{6,7},{7,4},{8,9},{9,10},{10,1... | collective-permute-start | bytes 3145736 | tf_op jit(solution)/shard_map/ppermute | solution.py:19
  102.0 1.7 collective-permute-start.9
  105.5 6.4 %copy-start.16 = (f32[1,128]{1,0:T(1,128)S(1)}, f32[1,128]{1,0:T(1,128)}, u32[]{:S(2)}) copy-start(f32[1,128]{1,0:T(1,128)} %get-tuple-element.21.refs_4_) | copy-start | bytes 1540
  105.5 3.4 %copy-start.2 = (bf16[8192,512]{1,0:T(8,128)(2,1)S(1)}, bf16[8192,512]{1,0:T(8,128)(2,1)}, u32[]{:S(2)}) copy-start(bf16[8192,512]{1,0:T(8,128)(2,1)} %refs_1_.15) | copy-start | bytes 25165828
  108.9 0.9 copy-start.8
  109.8 0.7 copy-start.15
  110.5 1.4 copy-start.6
  113.3 1.6 collective-permute-start.10
  114.9 5.8 %collective-permute-start.11 = (f32[64,512]{1,0:T(8,128)S(1)}, f32[64,512]{1,0:T(8,128)S(1)}, u32[]{:S(2)}, u32[]{:S(2)}) collective-permute-start(f32[64,512]{1,0:T(8,128)S(1)} %add.30), channel_id=1, source_target_pairs={{0,8},{4,12},{8,0},{12,4},{16,24},{20,28},{24,16},{28,20},{1,9},{5... | collective-permute-start | bytes 393224 | tf_op jit(solution)/shard_map/ppermute | solution.py:24
  120.7 5.2 %copy-start.23 = (f32[64,512]{1,0:T(8,128)}, f32[64,512]{1,0:T(8,128)S(1)}, u32[]{:S(2)}) copy-start(f32[64,512]{1,0:T(8,128)S(1)} %add.31.mine_ref) | copy-start | bytes 393220
  120.7 5.2 %collective-permute-start.12 = (f32[64,512]{1,0:T(8,128)S(1)}, f32[64,512]{1,0:T(8,128)}, u32[]{:S(2)}, u32[]{:S(2)}) collective-permute-start(f32[64,512]{1,0:T(8,128)S(1)} %add.31.mine_ref), channel_id=1, source_target_pairs={{0,16},{4,20},{8,24},{12,28},{16,0},{20,4},{24,8},{28,12},{1,17},{... | collective-permute-start | bytes 393224 | tf_op jit(solution)/shard_map/ppermute | solution.py:24
  128.2 1.5 collective-permute-start.13
  132.0 3.4 %copy-start.3 = (bf16[8192,512]{1,0:T(8,128)(2,1)S(1)}, bf16[8192,512]{1,0:T(8,128)(2,1)}, u32[]{:S(2)}) copy-start(bf16[8192,512]{1,0:T(8,128)(2,1)} %refs_1_.15) | copy-start | bytes 25165828
  135.4 0.9 copy-start.10
  143.0 1.4 collective-permute-start.14
  144.4 5.6 %collective-permute-start.15 = (f32[64,512]{1,0:T(8,128)S(1)}, f32[64,512]{1,0:T(8,128)S(1)}, u32[]{:S(2)}, u32[]{:S(2)}) collective-permute-start(f32[64,512]{1,0:T(8,128)S(1)} %add.32), channel_id=1, source_target_pairs={{0,8},{4,12},{8,0},{12,4},{16,24},{20,28},{24,16},{28,20},{1,9},{5... | collective-permute-start | bytes 393224 | tf_op jit(solution)/shard_map/ppermute | solution.py:24
  150.1 5.2 %copy-start.24 = (f32[64,512]{1,0:T(8,128)}, f32[64,512]{1,0:T(8,128)S(1)}, u32[]{:S(2)}) copy-start(f32[64,512]{1,0:T(8,128)S(1)} %add.33.mine_ref) | copy-start | bytes 393220
  150.1 5.1 %collective-permute-start.16 = (f32[64,512]{1,0:T(8,128)S(1)}, f32[64,512]{1,0:T(8,128)}, u32[]{:S(2)}, u32[]{:S(2)}) collective-permute-start(f32[64,512]{1,0:T(8,128)S(1)} %add.33.mine_ref), channel_id=1, source_target_pairs={{0,16},{4,20},{8,24},{12,28},{16,0},{20,4},{24,8},{28,12},{1,17},{... | collective-permute-start | bytes 393224 | tf_op jit(solution)/shard_map/ppermute | solution.py:24
  157.4 1.5 collective-permute-start.17
  161.2 8.0 %copy-start.20 = (f32[1,128]{1,0:T(1,128)S(1)}, f32[1,128]{1,0:T(1,128)}, u32[]{:S(2)}) copy-start(f32[1,128]{1,0:T(1,128)} %get-tuple-element.29.refs_4_) | copy-start | bytes 1540
  161.2 3.4 %copy-start.4 = (bf16[8192,512]{1,0:T(8,128)(2,1)S(1)}, bf16[8192,512]{1,0:T(8,128)(2,1)}, u32[]{:S(2)}) copy-start(bf16[8192,512]{1,0:T(8,128)(2,1)} %refs_1_.15) | copy-start | bytes 25165828
  164.6 0.9 copy-start.12
  166.1 24.5 %copy-start.18 = (f32[1,128]{1,0:T(1,128)S(1)}, f32[1,128]{1,0:T(1,128)}, u32[]{:S(2)}) copy-start(f32[1,128]{1,0:T(1,128)} %get-tuple-element.25.refs_4_) | copy-start | bytes 1540
  166.1 30.6 %copy-start.9 = (bf16[128,512]{1,0:T(8,128)(2,1)S(1)}, bf16[128,512]{1,0:T(8,128)(2,1)}, u32[]{:S(2)}) copy-start(bf16[128,512]{1,0:T(8,128)(2,1)} %get-tuple-element.20.refs_3_.refs_8_) | copy-start | bytes 393220
  169.2 27.6 %copy-start.11 = (bf16[128,512]{1,0:T(8,128)(2,1)S(1)}, bf16[128,512]{1,0:T(8,128)(2,1)}, u32[]{:S(2)}) copy-start(bf16[128,512]{1,0:T(8,128)(2,1)} %get-tuple-element.24.refs_3_.refs_9_) | copy-start | bytes 393220
  169.2 27.6 %copy-start.13 = (bf16[128,512]{1,0:T(8,128)(2,1)S(1)}, bf16[128,512]{1,0:T(8,128)(2,1)}, u32[]{:S(2)}) copy-start(bf16[128,512]{1,0:T(8,128)(2,1)} %get-tuple-element.28.refs_3_.refs_10_) | copy-start | bytes 393220
  172.3 1.4 collective-permute-start.18
  173.7 5.6 %collective-permute-start.19 = (f32[64,512]{1,0:T(8,128)S(1)}, f32[64,512]{1,0:T(8,128)S(1)}, u32[]{:S(2)}, u32[]{:S(2)}) collective-permute-start(f32[64,512]{1,0:T(8,128)S(1)} %add.34), channel_id=1, source_target_pairs={{0,8},{4,12},{8,0},{12,4},{16,24},{20,28},{24,16},{28,20},{1,9},{5... | collective-permute-start | bytes 393224 | tf_op jit(solution)/shard_map/ppermute | solution.py:24
  180.0 5.1 %collective-permute-start.20 = (f32[64,512]{1,0:T(8,128)S(1)}, f32[64,512]{1,0:T(8,128)}, u32[]{:S(2)}, u32[]{:S(2)}) collective-permute-start(f32[64,512]{1,0:T(8,128)S(1)} %add.35.mine_ref), channel_id=1, source_target_pairs={{0,16},{4,20},{8,24},{12,28},{16,0},{20,4},{24,8},{28,12},{1,17},{... | collective-permute-start | bytes 393224 | tf_op jit(solution)/shard_map/ppermute | solution.py:24
  187.3 1.6 collective-permute-start.21
  191.2 23.5 %collective-permute-start.22 = (f32[4,128]{1,0:T(4,128)S(1)}, f32[4,128]{1,0:T(4,128)S(1)}, u32[]{:S(2)}, u32[]{:S(2)}) collective-permute-start(f32[4,128]{1,0:T(4,128)S(1)} %pad_maximum_fusion.refs_8_), channel_id=1, source_target_pairs={{0,1},{1,2},{2,3},{3,0},{4,5},{5,6},{6,7},{7,4},{8,9},{9,10},{10,1... | collective-permute-start | bytes 6152 | tf_op jit(solution)/shard_map/ppermute | solution.py:19
  192.8 21.9 %collective-permute-start.23 = (f32[4,128]{1,0:T(4,128)S(1)}, f32[4,128]{1,0:T(4,128)S(1)}, u32[]{:S(2)}, u32[]{:S(2)}) collective-permute-start(f32[4,128]{1,0:T(4,128)S(1)} %pad_maximum_fusion.refs_8_), channel_id=1, source_target_pairs={{0,2},{1,3},{2,0},{3,1},{4,6},{5,7},{6,4},{7,5},{8,10},{9,11},{10,... | collective-permute-start | bytes 6152 | tf_op jit(solution)/shard_map/ppermute | solution.py:19
  195.6 19.1 %collective-permute-start.24 = (f32[4,128]{1,0:T(4,128)S(1)}, f32[4,128]{1,0:T(4,128)S(1)}, u32[]{:S(2)}, u32[]{:S(2)}) collective-permute-start(f32[4,128]{1,0:T(4,128)S(1)} %pad_maximum_fusion.refs_8_), channel_id=1, source_target_pairs={{0,3},{1,0},{2,1},{3,2},{4,7},{5,4},{6,5},{7,6},{8,11},{9,8},{10,9... | collective-permute-start | bytes 6152 | tf_op jit(solution)/shard_map/ppermute | solution.py:19
  196.8 1.2 copy-start.7
  198.0 0.9 copy-start.14
  (5 other events, 3.2 us)

commit v3 on v0

v3 whole, which is shorter than its diff:
```python
import functools

import jax
import jax.numpy as jnp
from jax import lax
from jax.experimental import pallas as pl
from jax.experimental.pallas import tpu as pltpu
from jax.sharding import PartitionSpec as P

HIGHEST = lax.Precision.HIGHEST
PIECES = 2
MIB = 1024 * 1024
FREE = pl.CostEstimate(flops=0, bytes_accessed=0, transcendentals=0)
ANYWHERE = pl.BlockSpec(memory_space=pl.ANY)


def shifted(block, axis, shift):
    count = lax.axis_size(axis)
    return lax.ppermute(block, axis, [(i, (i + shift) % count) for i in range(count)])


def exchanged(block, axis, bit):
    count = lax.axis_size(axis)
    return lax.ppermute(block, axis, [(i, i ^ bit) for i in range(count)])


def gate_body(*refs):
    del refs


def gate(block, *after):
    return pl.pallas_call(
        gate_body,
        out_shape=jax.ShapeDtypeStruct(block.shape, block.dtype),
        in_specs=[ANYWHERE] * (1 + len(after)),
        out_specs=ANYWHERE,
        input_output_aliases={0: 0},
        cost_estimate=FREE,
    )(block, *after)


def project_body(first, block, piece_ref, green_ref, acc_ref, total_ref):
    total_ref[...] = acc_ref[...]

    def step(piece, green):
        total_ref[...] += lax.dot_general(
            piece[...], green[...], (((0,), (0,)), ((), ())), preferred_element_type=jnp.float32
        )

    length, vectors = piece_ref.shape
    columns = green_ref.shape[1]
    pltpu.emit_pipeline(
        step,
        grid=(length // block,),
        in_specs=[
            pl.BlockSpec((block, vectors), lambda i: (i, 0)),
            pl.BlockSpec((block, columns), lambda i: (i + first // block, 0)),
        ],
    )(piece_ref, green_ref)


def project(piece, green, first, so_far):
    length, vectors = piece.shape
    columns = green.shape[1]
    in_vmem = pl.BlockSpec(memory_space=pltpu.VMEM)
    return pl.pallas_call(
        functools.partial(project_body, first, min(length, 1024)),
        out_shape=jax.ShapeDtypeStruct((vectors, columns), jnp.float32),
        in_specs=[ANYWHERE, pl.BlockSpec(memory_space=pltpu.HBM), in_vmem],
        out_specs=in_vmem,
        compiler_params=pltpu.CompilerParams(vmem_limit_bytes=12 * MIB),
        cost_estimate=FREE,
    )(piece, green, so_far)


def project_plain(piece, green_rows):
    return lax.dot_general(
        piece, green_rows, (((0,), (0,)), ((), ())), preferred_element_type=jnp.float32
    )


def dress(projection, weights, green_one, trace_weights):
    norb = green_one.shape[0]
    mixed = jnp.concatenate(
        [
            jnp.dot(projection[:, first : first + norb], green_one, precision=HIGHEST)
            for first in range(0, projection.shape[1], norb)
        ],
        axis=1,
    )
    rounded = lax.reduce_precision(mixed * weights[:, None], 8, 7)
    traced = lax.dot_general(
        trace_weights, rounded, (((1,), (1,)), ((), ())), precision=HIGHEST
    )
    return rounded.astype(jnp.bfloat16), traced


def dress_kernel_body(step, mine_ref, other_ref, weights_ref, green_ref, dressed_ref):
    half = mine_ref.shape[0]
    norb = green_ref.shape[0]
    aux_size = lax.axis_size("aux")
    owner = lax.rem(lax.axis_index("aux") - step + aux_size, aux_size)
    upper = lax.rem(lax.axis_index("rows"), 2)
    weights = weights_ref[pl.ds((owner * 2 + upper) * half, half), :]
    total = mine_ref[...] + other_ref[...]
    green = green_ref[...]
    for first in range(0, total.shape[1], norb):
        mixed = jnp.dot(
            total[:, first : first + norb],
            green,
            precision=HIGHEST,
            preferred_element_type=jnp.float32,
        )
        dressed_ref[:, first : first + norb] = (mixed * weights).astype(jnp.bfloat16)


def dress_kernel(step, mine, other, weights, green_one):
    return pl.pallas_call(
        functools.partial(dress_kernel_body, step),
        out_shape=jax.ShapeDtypeStruct(mine.shape, jnp.bfloat16),
        cost_estimate=FREE,
    )(mine, other, weights, green_one)


def join_kernel_body(mine_ref, other_ref, trace_ref, dressed_ref, traced_ref):
    half = mine_ref.shape[0]
    upper = lax.rem(lax.axis_index("rows"), 2)
    dressed_ref[pl.ds(pl.multiple_of(upper * half, half), half), :] = mine_ref[...]
    dressed_ref[pl.ds(pl.multiple_of((1 - upper) * half, half), half), :] = other_ref[...]
    row = trace_ref[...]
    high = row.astype(jnp.bfloat16).astype(jnp.float32)
    middle = (row - high).astype(jnp.bfloat16).astype(jnp.float32)
    parts = jnp.concatenate(
        [row - high - middle, middle, high, jnp.zeros((5, row.shape[1]), jnp.float32)], axis=0
    )
    traced = lax.dot_general(
        parts.astype(jnp.bfloat16),
        dressed_ref[...],
        (((1,), (1,)), ((), ())),
        preferred_element_type=jnp.float32,
    )
    traced_ref[...] = jnp.sum(traced, axis=0, keepdims=True)


def join_kernel(mine, other, trace_weights):
    half, columns = mine.shape
    return pl.pallas_call(
        join_kernel_body,
        out_shape=[
            jax.ShapeDtypeStruct((2 * half, columns), jnp.bfloat16),
            jax.ShapeDtypeStruct((1, 2 * half), jnp.float32),
        ],
        cost_estimate=FREE,
    )(mine, other, trace_weights)


def sum_and_dress(step, projection, weights, green_one, trace_weights):
    count, aux_size = lax.axis_size("rows"), lax.axis_size("aux")
    half = projection.shape[0] // 2
    upper = lax.rem(lax.axis_index("rows"), 2) == 1
    low, high = projection[:half], projection[half:]
    total = jnp.where(upper, high, low)
    other = exchanged(jnp.where(upper, low, high), "rows", 1)
    bit = 2
    while bit < count:
        total = total + other
        other = exchanged(total, "rows", bit)
        bit *= 2
    if step < aux_size - 1:
        mine = dress_kernel(step, total, other, weights[:, None], green_one)
        return join_kernel(mine, exchanged(mine, "rows", 1), trace_weights)
    owner = lax.rem(lax.axis_index("aux") - step + aux_size, aux_size)
    first = (2 * owner + lax.rem(lax.axis_index("rows"), 2)) * half
    mine, mine_traced = dress(
        total + other,
        lax.dynamic_slice_in_dim(weights, first, half, 0),
        green_one,
        trace_weights,
    )
    other = exchanged(mine, "rows", 1)
    other_traced = exchanged(mine_traced, "rows", 1)
    dressed = jnp.concatenate(
        [jnp.where(upper, other, mine), jnp.where(upper, mine, other)], axis=0
    )
    traced = jnp.concatenate(
        [jnp.where(upper, other_traced, mine_traced), jnp.where(upper, mine_traced, other_traced)],
        axis=1,
    )
    return dressed, traced


def slope_body(shards, pieces, blocks, share_blocks, me_ref, *refs):
    factor_refs = refs[: shards * pieces]
    dressed_refs = refs[shards * pieces : shards * pieces + shards]
    trace_refs = refs[shards * pieces + shards : -3]
    slope_ref, collision_ref, trace_ref = refs[-3:]
    at = pl.program_id(0)

    @pl.when(at == 0)
    def _():
        trace = trace_refs[0][...]
        for shift in range(1, shards):
            came = trace_refs[shift][...]
            trace = trace + jnp.concatenate(
                [came[shards - shift :], came[: shards - shift]], axis=0
            )
        row = jnp.concatenate([trace[s : s + 1] for s in range(shards)], axis=1)
        high = row.astype(jnp.bfloat16).astype(jnp.float32)
        middle = (row - high).astype(jnp.bfloat16).astype(jnp.float32)
        low = row - high - middle
        trace_ref[...] = jnp.concatenate(
            [low, middle, high, jnp.zeros((5, row.shape[1]), jnp.float32)], axis=0
        ).astype(jnp.bfloat16)

    dressed = jnp.concatenate([ref[...] for ref in dressed_refs], axis=0)
    first = me_ref[0] * share_blocks
    for i in range(pieces):

        @pl.when(at // blocks == i)
        def _():
            basis = jnp.concatenate(
                [factor_refs[s * pieces + i][...] for s in range(shards)], axis=1
            )
            slope_ref[...] = jnp.dot(basis, dressed, preferred_element_type=jnp.float32)

            @pl.when((at >= first) & (at < first + share_blocks))
            def _():
                parts = lax.dot_general(
                    trace_ref[...],
                    basis,
                    (((1,), (1,)), ((), ())),
                    preferred_element_type=jnp.float32,
                )
                collision_ref[pl.ds(at - first, 1), :] = jnp.sum(parts, axis=0, keepdims=True)


def slope(steps, dressed, traces):
    shards, pieces = len(steps), len(steps[0])
    length, vectors = steps[0][0].shape
    columns = dressed[0].shape[1]
    depth = shards * vectors
    rows = pieces * length
    share = rows // shards
    block = min(length, share, 1024)
    blocks = length // block
    factor_specs = [
        pl.BlockSpec(
            (block, vectors), lambda g, me, i=i: (jnp.clip(g - i * blocks, 0, blocks - 1), 0)
        )
        for _ in steps
        for i in range(pieces)
    ]
    whole = lambda g, me: (0, 0)
    slopes, collision = pl.pallas_call(
        functools.partial(slope_body, shards, pieces, blocks, share // block),
        grid_spec=pltpu.PrefetchScalarGridSpec(
            num_scalar_prefetch=1,
            grid=(pieces * blocks,),
            in_specs=factor_specs
            + [pl.BlockSpec((vectors, columns), whole)] * shards
            + [pl.BlockSpec((shards, vectors), whole)] * shards,
            out_specs=[
                pl.BlockSpec((block, columns), lambda g, me: (g, 0)),
                pl.BlockSpec((share // block, block), whole),
            ],
            scratch_shapes=[pltpu.VMEM((8, depth), jnp.bfloat16)],
        ),
        out_shape=[
            jax.ShapeDtypeStruct((rows, columns), jnp.float32),
            jax.ShapeDtypeStruct((share // block, block), jnp.float32),
        ],
        compiler_params=pltpu.CompilerParams(vmem_limit_bytes=20 * MIB),
        cost_estimate=pl.CostEstimate(
            flops=2 * rows * depth * columns,
            bytes_accessed=rows * depth * 2 + rows * columns * 4,
            transcendentals=0,
        ),
    )(
        lax.axis_index("aux").astype(jnp.int32)[None],
        *[piece for step in steps for piece in step],
        *dressed,
        *traces,
    )
    return slopes, collision.reshape(share)


def local(pair_green_block, cholesky_factors, green_one, screening):
    rows, columns = pair_green_block.shape
    vectors = cholesky_factors.shape[1]
    norb = green_one.shape[0]
    orb_count = columns // norb
    aux_size = lax.axis_size("aux")
    me = lax.axis_index("aux")
    length = rows // PIECES

    trace_weights = lax.dynamic_slice_in_dim(
        green_one, me * orb_count, orb_count, 1
    ).T.reshape(1, columns)
    steps, dressed, traced = [], [], []
    for step in range(aux_size):
        total = jnp.zeros((vectors, columns), jnp.float32)
        pieces = []
        for i in range(PIECES):
            green = (pair_green_block, i * length)
            if step == 0:
                piece = lax.slice_in_dim(cholesky_factors, i * length, (i + 1) * length, axis=0)
            elif i == 0:
                piece = gate(shifted(steps[-1][i], "aux", 1), dressed[-1], traced[-1])
            else:
                piece = gate(shifted(steps[-1][i], "aux", 1), total)
            pieces.append(piece)
            if step < aux_size - 1:
                total = project(piece, pair_green_block, i * length, total)
            else:
                total = total + project_plain(
                    piece, pair_green_block[i * length : (i + 1) * length]
                )
        steps.append(pieces)
        both, trace = sum_and_dress(step, total, screening, green_one, trace_weights)
        dressed.append(both)
        traced.append(trace)

    trace = jnp.concatenate(traced, axis=0)
    traces = [trace] + [shifted(trace, "aux", shift) for shift in range(1, aux_size)]
    return slope(steps, dressed, traces)


def solution(mesh):
    placed = (P("rows", "aux"), P("rows", "aux"), P(), P())
    return jax.shard_map(
        local,
        mesh=mesh,
        in_specs=placed,
        out_specs=(P("rows", "aux"), P(("rows", "aux"))),
        check_vma=False,
    )
```

time: 286 us -> 188 us (0.66)
  waiting for transfers between devices: 186 us -> 74.8 us
  Pallas kernels: 0 us -> 37.7 us
  blocking collectives: 28.8 us -> 0 us
  matrix products: 36.2 us -> 10 us
  starting transfers between devices: 0.08 us -> 25.1 us
  local copies, waits for them, and re-layouts: 19.6 us -> 35.6 us
  between operations: 14.8 us -> 1.03 us
    all_gather x1 -> x0, waiting for transfers between devices: 153 us -> none  [local(): chol_basis = lax.all_gather(cholesky_factors, 'aux', axis=1, tiled=True)]
    ppermute x0 -> x26, waiting for transfers between devices: none -> 74.8 us  [the longest x9 37.6 us: shifted(): lax.ppermute(block, axis, [(i, (i + shift) % count) for i in range(count)])]
    pallas_call x0 -> x19, Pallas kernels: none -> 37.7 us  [the longest x6 14.4 us: project(): pl.pallas_call(functools.partial(project_body, first, min(length, 1024)),...]
    reduce_scatter x1 -> x0, waiting for transfers between devices: 32.1 us -> none  [local(): lax.psum_scatter(partial_projection, 'rows', scatter_dimension=0, tiled=T...]
    dot_general x4 -> x5, matrix products: 36.2 us -> 10 us  [the longest x2 7.36 us: project_plain(): lax.dot_general(piece, green_rows, (((0,), (0,)), ((), ())), preferred_el...]
    ppermute x0 -> x26, starting transfers between devices: none -> 25.1 us  [the longest x17 14.3 us: exchanged(): return lax.ppermute(block, axis, [(i, i ^ bit) for i in range(count)])]
    unnamed x1 -> x0, blocking collectives: 19 us -> none
    unnamed x8 -> x68, local copies, waits for them, and re-layouts: 18.6 us -> 31.9 us
  transfers between devices with their start and end apart: 2 -> 26, of which waited for: 2 -> 21; matrix products, arithmetic and copies ran while one was open for 1% -> 4% of each run, Pallas kernels for 0% -> 14%
where the time goes in v3:
time: 188 us; the launch traced here: 187 us
  waiting for transfers between devices  74.8 us (40%)
  Pallas kernels  37.7 us (20%)
  local copies, waits for them, and re-layouts  35.6 us (19%)
  starting transfers between devices  25.1 us (13%)
  matrix products  10 us (5%)
  other arithmetic  2.82 us (2%)
    ppermute x9, waiting for transfers between devices, shifted(): lax.ppermute(block, axis, [(i, (i + shift) % count) for i in range(count)])  37.6 us
    ppermute x17, waiting for transfers between devices, exchanged(): return lax.ppermute(block, axis, [(i, i ^ bit) for i in range(count)])  37.2 us
    unnamed x68, local copies, waits for them, and re-layouts  31.9 us
    pallas_call x6, Pallas kernels, project(): pl.pallas_call(functools.partial(project_body, first, min(length, 1024)),...  14.4 us
    ppermute x17, starting transfers between devices, exchanged(): return lax.ppermute(block, axis, [(i, i ^ bit) for i in range(count)])  14.3 us
    pallas_call x1, Pallas kernels, slope(): pl.pallas_call(functools.partial(slope_body, shards, pieces, blocks, shar...  11.8 us
    ppermute x9, starting transfers between devices, shifted(): lax.ppermute(block, axis, [(i, (i + shift) % count) for i in range(count)])  10.7 us
    dot_general x2, matrix products, project_plain(): lax.dot_general(piece, green_rows, (((0,), (0,)), ((), ())), preferred_el...  7.36 us
  transfers between devices with their start and end apart: 26, of which 21 were waited for; matrix products, arithmetic and copies ran while one was open for 4% of the time, Pallas kernels for 14%

profile of v3, /device:TPU:0, one launch (start us, length us, event | category | flops | bytes accessed | tf_op | source)
XLA Modules:
  0.0 187.0 jit_solution(17353656947644219102)
XLA Ops:
  0.6 1.7 fusion.17
  2.3 3.1 %collective-permute-start = (bf16[4096,128]{1,0:T(8,128)(2,1)S(1)}, bf16[4096,128]{1,0:T(8,128)(2,1)S(1)}, u32[]{:S(2)}, u32[]{:S(2)}) collective-permute-start(bf16[4096,128]{1,0:T(8,128)(2,1)S(1)} %get-tuple-element.19.piece_ref.refs_0_), channel_id=1, source_target_pairs={{0,1},{1,2},{2,3},{3,0},{4,5},{5,6},{6,7},{7,4},{8,9},{9,10},{10,1... | collective-permute-start | bytes 3145736 | tf_op jit(solution)/shard_map/ppermute | solution.py:19
  5.4 1.6 collective-permute-start.5
  7.0 3.4 %copy-done = bf16[8192,512]{1,0:T(8,128)(2,1)S(1)} copy-done((bf16[8192,512]{1,0:T(8,128)(2,1)S(1)}, bf16[8192,512]{1,0:T(8,128)(2,1)}, u32[]{:S(2)}) %copy-start) | copy-done | bytes 8388632
  10.4 2.0 %shard_map.59.acc_ref = f32[128,512]{1,0:T(8,128)S(1)} custom-call(bf16[4096,128]{1,0:T(8,128)(2,1)S(1)} %get-tuple-element.19.piece_ref.refs_0_, bf16[8192,512]{1,0:T(8,128)(2,1)S(1)} %copy-done, f32[128,512]{1,0:T(8,128)S(1)} %broadcast_1_acc_ref.2.acc_ref), custom_call_target="tpu_custom_call" | custom-call | tf_op jit(solution)/shard_map/pallas_call | solution.py:66
  12.4 2.1 %shard_map.60 = f32[128,512]{1,0:T(8,128)S(1)} custom-call(bf16[4096,128]{1,0:T(8,128)(2,1)S(1)} %get-tuple-element.18.piece_ref.refs_1_, bf16[8192,512]{1,0:T(8,128)(2,1)S(1)} %copy-done, f32[128,512]{1,0:T(8,128)S(1)} %shard_map.59.acc_ref), custom_call_target="tpu_custom_call" | custom-call | tf_op jit(solution)/shard_map/pallas_call | solution.py:66
  16.0 1.6 collective-permute-start.2
  17.6 4.0 %collective-permute-done.2 = f32[64,512]{1,0:T(8,128)S(1)} collective-permute-done((f32[64,512]{1,0:T(8,128)S(1)}, f32[64,512]{1,0:T(8,128)S(1)}, u32[]{:S(2)}, u32[]{:S(2)}) %collective-permute-start.2) | collective-permute-done | bytes 131104 | tf_op jit(solution)/shard_map/ppermute | solution.py:24
  21.6 1.6 collective-permute-start.3
  24.1 2.7 %collective-permute-done.3.other_ref = f32[64,512]{1,0:T(8,128)} collective-permute-done((f32[64,512]{1,0:T(8,128)S(1)}, f32[64,512]{1,0:T(8,128)}, u32[]{:S(2)}, u32[]{:S(2)}) %collective-permute-start.3) | collective-permute-done | bytes 131104 | tf_op jit(solution)/shard_map/ppermute | solution.py:24
  26.8 2.2 %shard_map.61.mine_ref = bf16[64,512]{1,0:T(8,128)(2,1)} custom-call(f32[64,512]{1,0:T(8,128)} %copy-done.22, f32[64,512]{1,0:T(8,128)} %collective-permute-done.3.other_ref, f32[512,1]{1,0:T(8,128)} %copy.13.weights_ref, f32[256,256]{1,0:T(8,128)} %green_ref.17), custom_call_target="tpu_custom_call" | custom-call | tf_op jit(solution)/shard_map/pallas_call | solution.py:118
  30.7 1.6 shard_map.62
  33.3 1.6 collective-permute-start.6
  34.8 3.4 %copy-done.1 = bf16[8192,512]{1,0:T(8,128)(2,1)S(1)} copy-done((bf16[8192,512]{1,0:T(8,128)(2,1)S(1)}, bf16[8192,512]{1,0:T(8,128)(2,1)}, u32[]{:S(2)}) %copy-start.1) | copy-done | bytes 8388632
  39.5 2.1 %shard_map.64.refs_1_.acc_ref = f32[128,512]{1,0:T(8,128)S(1)} custom-call(bf16[4096,128]{1,0:T(8,128)(2,1)S(1)} %copy-done.6, bf16[8192,512]{1,0:T(8,128)(2,1)S(1)} %copy-done.1, f32[128,512]{1,0:T(8,128)S(1)} %broadcast_1_acc_ref.2.acc_ref), custom_call_target="tpu_custom_call" | custom-call | tf_op jit(solution)/shard_map/pallas_call | solution.py:66
  42.2 11.8 %collective-permute-done.5.refs_0_ = bf16[4096,128]{1,0:T(8,128)(2,1)} collective-permute-done((bf16[4096,128]{1,0:T(8,128)(2,1)S(1)}, bf16[4096,128]{1,0:T(8,128)(2,1)}, u32[]{:S(2)}, u32[]{:S(2)}) %collective-permute-start.5) | collective-permute-done | bytes 1048608 | tf_op jit(solution)/shard_map/ppermute | solution.py:19
  54.0 3.4 %copy-done.2 = bf16[8192,512]{1,0:T(8,128)(2,1)S(1)} copy-done((bf16[8192,512]{1,0:T(8,128)(2,1)S(1)}, bf16[8192,512]{1,0:T(8,128)(2,1)}, u32[]{:S(2)}) %copy-start.2) | copy-done | bytes 8388632
  58.3 3.1 %shard_map.66 = f32[128,512]{1,0:T(8,128)S(1)} custom-call(bf16[4096,128]{1,0:T(8,128)(2,1)} %shard_map.65.piece_ref.refs_3_, bf16[8192,512]{1,0:T(8,128)(2,1)S(1)} %copy-done.2, f32[128,512]{1,0:T(8,128)S(1)} %copy-done.16), custom_call_target="tpu_custom_call" | custom-call | tf_op jit(solution)/shard_map/pallas_call | solution.py:66
  63.0 1.8 collective-permute-start.8
  64.8 3.8 %collective-permute-done.8 = f32[64,512]{1,0:T(8,128)S(1)} collective-permute-done((f32[64,512]{1,0:T(8,128)S(1)}, f32[64,512]{1,0:T(8,128)S(1)}, u32[]{:S(2)}, u32[]{:S(2)}) %collective-permute-start.8) | collective-permute-done | bytes 131104 | tf_op jit(solution)/shard_map/ppermute | solution.py:24
  68.6 1.8 collective-permute-start.9
  70.4 3.2 %collective-permute-done.9.other_ref = f32[64,512]{1,0:T(8,128)S(1)} collective-permute-done((f32[64,512]{1,0:T(8,128)S(1)}, f32[64,512]{1,0:T(8,128)S(1)}, u32[]{:S(2)}, u32[]{:S(2)}) %collective-permute-start.9) | collective-permute-done | bytes 131104 | tf_op jit(solution)/shard_map/ppermute | solution.py:24
  74.3 2.2 %shard_map.67.mine_ref = bf16[64,512]{1,0:T(8,128)(2,1)} custom-call(f32[64,512]{1,0:T(8,128)} %copy-done.24, f32[64,512]{1,0:T(8,128)} %copy-done.26, f32[512,1]{1,0:T(8,128)} %copy.13.weights_ref, f32[256,256]{1,0:T(8,128)} %green_ref.17), custom_call_target="tpu_custom_call" | custom-call | tf_op jit(solution)/shard_map/pallas_call | solution.py:118
  76.5 1.5 collective-permute-done.10.other_ref
  78.6 1.6 shard_map.68
  81.2 1.6 collective-permute-start.12
  82.8 3.4 %copy-done.3 = bf16[8192,512]{1,0:T(8,128)(2,1)S(1)} copy-done((bf16[8192,512]{1,0:T(8,128)(2,1)S(1)}, bf16[8192,512]{1,0:T(8,128)(2,1)}, u32[]{:S(2)}) %copy-start.3) | copy-done | bytes 8388632
  87.4 2.0 %shard_map.70.refs_1_.acc_ref = f32[128,512]{1,0:T(8,128)S(1)} custom-call(bf16[4096,128]{1,0:T(8,128)(2,1)S(1)} %copy-done.9, bf16[8192,512]{1,0:T(8,128)(2,1)S(1)} %copy-done.3, f32[128,512]{1,0:T(8,128)S(1)} %broadcast_1_acc_ref.2.acc_ref), custom_call_target="tpu_custom_call" | custom-call | tf_op jit(solution)/shard_map/pallas_call | solution.py:66
  90.2 8.7 %collective-permute-done.11.refs_0_ = bf16[4096,128]{1,0:T(8,128)(2,1)} collective-permute-done((bf16[4096,128]{1,0:T(8,128)(2,1)}, bf16[4096,128]{1,0:T(8,128)(2,1)}, u32[]{:S(2)}, u32[]{:S(2)}) %collective-permute-start.11) | collective-permute-done | bytes 1048608 | tf_op jit(solution)/shard_map/ppermute | solution.py:19
  98.9 3.4 %copy-done.4 = bf16[8192,512]{1,0:T(8,128)(2,1)S(1)} copy-done((bf16[8192,512]{1,0:T(8,128)(2,1)S(1)}, bf16[8192,512]{1,0:T(8,128)(2,1)}, u32[]{:S(2)}) %copy-start.4) | copy-done | bytes 8388632
  103.3 3.1 %shard_map.72 = f32[128,512]{1,0:T(8,128)S(1)} custom-call(bf16[4096,128]{1,0:T(8,128)(2,1)} %shard_map.71.piece_ref.refs_5_, bf16[8192,512]{1,0:T(8,128)(2,1)S(1)} %copy-done.4, f32[128,512]{1,0:T(8,128)S(1)} %copy-done.14), custom_call_target="tpu_custom_call" | custom-call | tf_op jit(solution)/shard_map/pallas_call | solution.py:66
  107.8 1.8 collective-permute-start.14
  109.6 3.8 %collective-permute-done.14 = f32[64,512]{1,0:T(8,128)S(1)} collective-permute-done((f32[64,512]{1,0:T(8,128)S(1)}, f32[64,512]{1,0:T(8,128)S(1)}, u32[]{:S(2)}, u32[]{:S(2)}) %collective-permute-start.14) | collective-permute-done | bytes 131104 | tf_op jit(solution)/shard_map/ppermute | solution.py:24
  113.5 1.8 collective-permute-start.15
  115.3 3.2 %collective-permute-done.15.other_ref = f32[64,512]{1,0:T(8,128)S(1)} collective-permute-done((f32[64,512]{1,0:T(8,128)S(1)}, f32[64,512]{1,0:T(8,128)S(1)}, u32[]{:S(2)}, u32[]{:S(2)}) %collective-permute-start.15) | collective-permute-done | bytes 131104 | tf_op jit(solution)/shard_map/ppermute | solution.py:24
  119.2 2.2 %shard_map.73.mine_ref = bf16[64,512]{1,0:T(8,128)(2,1)} custom-call(f32[64,512]{1,0:T(8,128)} %copy-done.23, f32[64,512]{1,0:T(8,128)} %copy-done.25, f32[512,1]{1,0:T(8,128)} %copy.13.weights_ref, f32[256,256]{1,0:T(8,128)} %green_ref.17), custom_call_target="tpu_custom_call" | custom-call | tf_op jit(solution)/shard_map/pallas_call | solution.py:118
  121.4 1.5 collective-permute-done.16.other_ref
  123.5 1.6 shard_map.74
  126.2 4.1 %fusion.2.refs_1_ = f32[128,512]{1,0:T(8,128)} fusion(bf16[4096,128]{1,0:T(8,128)(2,1)} %shard_map.75.refs_6_, bf16[8192,512]{1,0:T(8,128)(2,1)} %green_ref.16), kind=kOutput, calls=%fused_computation.2 | convolution fusion | flops 536870912 | bytes 5505024 | tf_op jit(solution)/shard_map/dot_general | solution.py:77
  130.3 12.8 %collective-permute-done.17.refs_0_ = bf16[4096,128]{1,0:T(8,128)(2,1)} collective-permute-done((bf16[4096,128]{1,0:T(8,128)(2,1)}, bf16[4096,128]{1,0:T(8,128)(2,1)}, u32[]{:S(2)}, u32[]{:S(2)}) %collective-permute-start.17) | collective-permute-done | bytes 1048608 | tf_op jit(solution)/shard_map/ppermute | solution.py:19
  143.0 3.3 %fusion.4 = f32[128,512]{1,0:T(8,128)S(1)} fusion(f32[128,512]{1,0:T(8,128)} %fusion.2.refs_1_, bf16[4096,128]{1,0:T(8,128)(2,1)} %shard_map.76.refs_7_, bf16[8192,512]{1,0:T(8,128)(2,1)} %green_ref.16), kind=kOutput, calls=%fused_computation.4 | convolution fusion | flops 536936448 | bytes 5767168 | tf_op jit(solution)/shard_map/dot_general | solution.py:77
  147.8 1.6 collective-permute-start.19
  149.3 4.1 %collective-permute-done.19 = f32[64,512]{1,0:T(8,128)S(1)} collective-permute-done((f32[64,512]{1,0:T(8,128)S(1)}, f32[64,512]{1,0:T(8,128)S(1)}, u32[]{:S(2)}, u32[]{:S(2)}) %collective-permute-start.19) | collective-permute-done | bytes 131104 | tf_op jit(solution)/shard_map/ppermute | solution.py:24
  154.1 1.5 collective-permute-start.20
  155.7 3.7 %collective-permute-done.20 = f32[64,512]{1,0:T(8,128)} collective-permute-done((f32[64,512]{1,0:T(8,128)}, f32[64,512]{1,0:T(8,128)}, u32[]{:S(2)}, u32[]{:S(2)}) %collective-permute-start.20) | collective-permute-done | bytes 131104 | tf_op jit(solution)/shard_map/ppermute | solution.py:24
  165.0 1.7 collective-permute-start.25
  168.6 2.6 %collective-permute-done.24.refs_14_ = f32[4,128]{1,0:T(4,128)S(1)} collective-permute-done((f32[4,128]{1,0:T(4,128)S(1)}, f32[4,128]{1,0:T(4,128)S(1)}, u32[]{:S(2)}, u32[]{:S(2)}) %collective-permute-start.24) | collective-permute-done | bytes 2080 | tf_op jit(solution)/shard_map/ppermute | solution.py:19
  174.6 11.8 %shard_map.77 = (f32[8192,512]{1,0:T(8,128)}, f32[2,1024]{1,0:T(2,128)S(1)}) custom-call(s32[1]{0:T(128)} %bitcast.me_ref, bf16[4096,128]{1,0:T(8,128)(2,1)S(1)} %copy-done.12, bf16[4096,128]{1,0:T(8,128)(2,1)S(1)} %get-tuple-element.18.piece_ref.refs_1_, bf16[4096,128]{1,0:T(8,128)(2,1)S(1)} %copy-done.7, bf16[4096,128]{1,0:T(8,128)(2,1)} %shard_map.65.piece_ref.refs_3_, ...), custom_call_target="tpu_custom_call" | custom-call | flops 4294967296 | bytes 25165824 | tf_op jit(solution)/shard_map/pallas_call | solution.py:254
  (120 shorter events, 32.0 us)
Async XLA Ops:
  2.3 12.2 %copy-start.11 = (bf16[4096,128]{1,0:T(8,128)(2,1)}, bf16[4096,128]{1,0:T(8,128)(2,1)S(1)}, u32[]{:S(2)}) copy-start(bf16[4096,128]{1,0:T(8,128)(2,1)S(1)} %get-tuple-element.19.piece_ref.refs_0_) | copy-start | bytes 3145732
  2.3 30.0 %collective-permute-start = (bf16[4096,128]{1,0:T(8,128)(2,1)S(1)}, bf16[4096,128]{1,0:T(8,128)(2,1)S(1)}, u32[]{:S(2)}, u32[]{:S(2)}) collective-permute-start(bf16[4096,128]{1,0:T(8,128)(2,1)S(1)} %get-tuple-element.19.piece_ref.refs_0_), channel_id=1, source_target_pairs={{0,1},{1,2},{2,3},{3,0},{4,5},{5,6},{6,7},{7,4},{8,9},{9,10},{10,1... | collective-permute-start | bytes 3145736 | tf_op jit(solution)/shard_map/ppermute | solution.py:19
  5.4 48.6 %collective-permute-start.5 = (bf16[4096,128]{1,0:T(8,128)(2,1)S(1)}, bf16[4096,128]{1,0:T(8,128)(2,1)}, u32[]{:S(2)}, u32[]{:S(2)}) collective-permute-start(bf16[4096,128]{1,0:T(8,128)(2,1)S(1)} %get-tuple-element.18.piece_ref.refs_1_), channel_id=1, source_target_pairs={{0,1},{1,2},{2,3},{3,0},{4,5},{5,6},{6,7},{7,4},{8,9},{9,10},{10,1... | collective-permute-start | bytes 3145736 | tf_op jit(solution)/shard_map/ppermute | solution.py:19
  7.0 3.4 %copy-start = (bf16[8192,512]{1,0:T(8,128)(2,1)S(1)}, bf16[8192,512]{1,0:T(8,128)(2,1)}, u32[]{:S(2)}) copy-start(bf16[8192,512]{1,0:T(8,128)(2,1)} %green_ref.16) | copy-start | bytes 25165828
  10.4 12.9 %copy-start.30 = (f32[512]{0:T(512)S(1)}, f32[512]{0:T(512)}, u32[]{:S(2)}) copy-start(f32[512]{0:T(512)} %param.7) | copy-start | bytes 6148
  14.5 1.4 collective-permute-start.1
  16.0 5.6 %collective-permute-start.2 = (f32[64,512]{1,0:T(8,128)S(1)}, f32[64,512]{1,0:T(8,128)S(1)}, u32[]{:S(2)}, u32[]{:S(2)}) collective-permute-start(f32[64,512]{1,0:T(8,128)S(1)} %select_add_fusion.3), channel_id=1, source_target_pairs={{0,8},{4,12},{8,0},{12,4},{16,24},{20,28},{24,16},{28,20},{1,9},{5... | collective-permute-start | bytes 393224 | tf_op jit(solution)/shard_map/ppermute | solution.py:24
  21.6 5.2 %copy-start.22 = (f32[64,512]{1,0:T(8,128)}, f32[64,512]{1,0:T(8,128)S(1)}, u32[]{:S(2)}) copy-start(f32[64,512]{1,0:T(8,128)S(1)} %add.46.mine_ref) | copy-start | bytes 393220
  21.6 5.1 %collective-permute-start.3 = (f32[64,512]{1,0:T(8,128)S(1)}, f32[64,512]{1,0:T(8,128)}, u32[]{:S(2)}, u32[]{:S(2)}) collective-permute-start(f32[64,512]{1,0:T(8,128)S(1)} %add.46.mine_ref), channel_id=1, source_target_pairs={{0,16},{4,20},{8,24},{12,28},{16,0},{20,4},{24,8},{28,12},{1,17},{... | collective-permute-start | bytes 393224 | tf_op jit(solution)/shard_map/ppermute | solution.py:24
  29.0 1.7 collective-permute-start.4
  33.3 47.0 %collective-permute-start.6 = (bf16[4096,128]{1,0:T(8,128)(2,1)}, bf16[4096,128]{1,0:T(8,128)(2,1)S(1)}, u32[]{:S(2)}, u32[]{:S(2)}) collective-permute-start(bf16[4096,128]{1,0:T(8,128)(2,1)} %shard_map.63.piece_ref.refs_2_), channel_id=1, source_target_pairs={{0,1},{1,2},{2,3},{3,0},{4,5},{5,6},{6,7},{7,4},{8,9},{9,10},{10,1... | collective-permute-start | bytes 3145736 | tf_op jit(solution)/shard_map/ppermute | solution.py:19
  34.8 3.4 %copy-start.1 = (bf16[8192,512]{1,0:T(8,128)(2,1)S(1)}, bf16[8192,512]{1,0:T(8,128)(2,1)}, u32[]{:S(2)}) copy-start(bf16[8192,512]{1,0:T(8,128)(2,1)} %green_ref.16) | copy-start | bytes 25165828
  38.2 1.2 copy-start.6
  54.0 3.4 %copy-start.2 = (bf16[8192,512]{1,0:T(8,128)(2,1)S(1)}, bf16[8192,512]{1,0:T(8,128)(2,1)}, u32[]{:S(2)}) copy-start(bf16[8192,512]{1,0:T(8,128)(2,1)} %green_ref.16) | copy-start | bytes 25165828
  61.4 37.5 %collective-permute-start.11 = (bf16[4096,128]{1,0:T(8,128)(2,1)}, bf16[4096,128]{1,0:T(8,128)(2,1)}, u32[]{:S(2)}, u32[]{:S(2)}) collective-permute-start(bf16[4096,128]{1,0:T(8,128)(2,1)} %shard_map.65.piece_ref.refs_3_), channel_id=1, source_target_pairs={{0,1},{1,2},{2,3},{3,0},{4,5},{5,6},{6,7},{7,4},{8,9},{9,10},{10,1... | collective-permute-start | bytes 3145736 | tf_op jit(solution)/shard_map/ppermute | solution.py:19
  61.5 1.4 collective-permute-start.7
  63.0 5.6 %collective-permute-start.8 = (f32[64,512]{1,0:T(8,128)S(1)}, f32[64,512]{1,0:T(8,128)S(1)}, u32[]{:S(2)}, u32[]{:S(2)}) collective-permute-start(f32[64,512]{1,0:T(8,128)S(1)} %select_add_fusion.2), channel_id=1, source_target_pairs={{0,8},{4,12},{8,0},{12,4},{16,24},{20,28},{24,16},{28,20},{1,9},{5... | collective-permute-start | bytes 393224 | tf_op jit(solution)/shard_map/ppermute | solution.py:24
  68.6 5.0 %copy-start.24 = (f32[64,512]{1,0:T(8,128)}, f32[64,512]{1,0:T(8,128)S(1)}, u32[]{:S(2)}) copy-start(f32[64,512]{1,0:T(8,128)S(1)} %add.49.mine_ref) | copy-start | bytes 393220
  68.6 5.0 %collective-permute-start.9 = (f32[64,512]{1,0:T(8,128)S(1)}, f32[64,512]{1,0:T(8,128)S(1)}, u32[]{:S(2)}, u32[]{:S(2)}) collective-permute-start(f32[64,512]{1,0:T(8,128)S(1)} %add.49.mine_ref), channel_id=1, source_target_pairs={{0,16},{4,20},{8,24},{12,28},{16,0},{20,4},{24,8},{28,12},{1,17},{... | collective-permute-start | bytes 393224 | tf_op jit(solution)/shard_map/ppermute | solution.py:24
  76.5 1.5 collective-permute-start.10
  81.2 43.9 %collective-permute-start.12 = (bf16[4096,128]{1,0:T(8,128)(2,1)}, bf16[4096,128]{1,0:T(8,128)(2,1)S(1)}, u32[]{:S(2)}, u32[]{:S(2)}) collective-permute-start(bf16[4096,128]{1,0:T(8,128)(2,1)} %shard_map.69.piece_ref.refs_4_), channel_id=1, source_target_pairs={{0,1},{1,2},{2,3},{3,0},{4,5},{5,6},{6,7},{7,4},{8,9},{9,10},{10,1... | collective-permute-start | bytes 3145736 | tf_op jit(solution)/shard_map/ppermute | solution.py:19
  82.8 3.4 %copy-start.3 = (bf16[8192,512]{1,0:T(8,128)(2,1)S(1)}, bf16[8192,512]{1,0:T(8,128)(2,1)}, u32[]{:S(2)}) copy-start(bf16[8192,512]{1,0:T(8,128)(2,1)} %green_ref.16) | copy-start | bytes 25165828
  86.2 1.2 copy-start.9
  98.9 3.4 %copy-start.4 = (bf16[8192,512]{1,0:T(8,128)(2,1)S(1)}, bf16[8192,512]{1,0:T(8,128)(2,1)}, u32[]{:S(2)}) copy-start(bf16[8192,512]{1,0:T(8,128)(2,1)} %green_ref.16) | copy-start | bytes 25165828
  106.4 1.4 collective-permute-start.13
  106.5 36.6 %collective-permute-start.17 = (bf16[4096,128]{1,0:T(8,128)(2,1)}, bf16[4096,128]{1,0:T(8,128)(2,1)}, u32[]{:S(2)}, u32[]{:S(2)}) collective-permute-start(bf16[4096,128]{1,0:T(8,128)(2,1)} %shard_map.71.piece_ref.refs_5_), channel_id=1, source_target_pairs={{0,1},{1,2},{2,3},{3,0},{4,5},{5,6},{6,7},{7,4},{8,9},{9,10},{10,1... | collective-permute-start | bytes 3145736 | tf_op jit(solution)/shard_map/ppermute | solution.py:19
  107.8 5.6 %collective-permute-start.14 = (f32[64,512]{1,0:T(8,128)S(1)}, f32[64,512]{1,0:T(8,128)S(1)}, u32[]{:S(2)}, u32[]{:S(2)}) collective-permute-start(f32[64,512]{1,0:T(8,128)S(1)} %select_add_fusion.1), channel_id=1, source_target_pairs={{0,8},{4,12},{8,0},{12,4},{16,24},{20,28},{24,16},{28,20},{1,9},{5... | collective-permute-start | bytes 393224 | tf_op jit(solution)/shard_map/ppermute | solution.py:24
  113.5 5.0 %copy-start.23 = (f32[64,512]{1,0:T(8,128)}, f32[64,512]{1,0:T(8,128)S(1)}, u32[]{:S(2)}) copy-start(f32[64,512]{1,0:T(8,128)S(1)} %add.51.mine_ref) | copy-start | bytes 393220
  113.5 5.0 %collective-permute-start.15 = (f32[64,512]{1,0:T(8,128)S(1)}, f32[64,512]{1,0:T(8,128)S(1)}, u32[]{:S(2)}, u32[]{:S(2)}) collective-permute-start(f32[64,512]{1,0:T(8,128)S(1)} %add.51.mine_ref), channel_id=1, source_target_pairs={{0,16},{4,20},{8,24},{12,28},{16,0},{20,4},{24,8},{28,12},{1,17},{... | collective-permute-start | bytes 393224 | tf_op jit(solution)/shard_map/ppermute | solution.py:24
  121.4 1.5 collective-permute-start.16
  126.1 36.7 %copy-start.29 = (f32[1,1,2,256]{3,1,2,0:T(1,128)S(1)}, f32[1,1,2,256]{3,1,2,0:T(1,128)}, u32[]{:S(2)}) copy-start(f32[1,1,2,256]{3,1,2,0:T(1,128)} %copy.18) | copy-start | bytes 6148
  126.1 38.1 %copy-start.31 = (f32[1,128]{1,0:T(1,128)S(1)}, f32[1,128]{1,0:T(1,128)}, u32[]{:S(2)}) copy-start(f32[1,128]{1,0:T(1,128)} %get-tuple-element.11.refs_2_) | copy-start | bytes 1540
  126.1 38.1 %copy-start.32 = (f32[1,128]{1,0:T(1,128)S(1)}, f32[1,128]{1,0:T(1,128)}, u32[]{:S(2)}) copy-start(f32[1,128]{1,0:T(1,128)} %get-tuple-element.13.refs_2_) | copy-start | bytes 1540
  126.1 46.0 %copy-start.7 = (bf16[4096,128]{1,0:T(8,128)(2,1)S(1)}, bf16[4096,128]{1,0:T(8,128)(2,1)}, u32[]{:S(2)}) copy-start(bf16[4096,128]{1,0:T(8,128)(2,1)} %shard_map.63.piece_ref.refs_2_) | copy-start | bytes 3145732
  126.1 46.0 %copy-start.10 = (bf16[4096,128]{1,0:T(8,128)(2,1)S(1)}, bf16[4096,128]{1,0:T(8,128)(2,1)}, u32[]{:S(2)}) copy-start(bf16[4096,128]{1,0:T(8,128)(2,1)} %shard_map.69.piece_ref.refs_4_) | copy-start | bytes 3145732
  126.1 46.0 %copy-start.19 = (bf16[128,512]{1,0:T(8,128)(2,1)S(1)}, bf16[128,512]{1,0:T(8,128)(2,1)}, u32[]{:S(2)}) copy-start(bf16[128,512]{1,0:T(8,128)(2,1)} %get-tuple-element.10.refs_1_.refs_8_) | copy-start | bytes 393220
  126.1 46.0 %copy-start.20 = (bf16[128,512]{1,0:T(8,128)(2,1)S(1)}, bf16[128,512]{1,0:T(8,128)(2,1)}, u32[]{:S(2)}) copy-start(bf16[128,512]{1,0:T(8,128)(2,1)} %get-tuple-element.12.refs_1_.refs_9_) | copy-start | bytes 393220
  126.2 46.0 %copy-start.21 = (bf16[128,512]{1,0:T(8,128)(2,1)S(1)}, bf16[128,512]{1,0:T(8,128)(2,1)}, u32[]{:S(2)}) copy-start(bf16[128,512]{1,0:T(8,128)(2,1)} %get-tuple-element.14.refs_1_.refs_10_) | copy-start | bytes 393220
  146.3 1.4 collective-permute-start.18
  147.8 5.6 %collective-permute-start.19 = (f32[64,512]{1,0:T(8,128)S(1)}, f32[64,512]{1,0:T(8,128)S(1)}, u32[]{:S(2)}, u32[]{:S(2)}) collective-permute-start(f32[64,512]{1,0:T(8,128)S(1)} %select_add_fusion), channel_id=1, source_target_pairs={{0,8},{4,12},{8,0},{12,4},{16,24},{20,28},{24,16},{28,20},{1,9},{5... | collective-permute-start | bytes 393224 | tf_op jit(solution)/shard_map/ppermute | solution.py:24
  154.1 5.3 %collective-permute-start.20 = (f32[64,512]{1,0:T(8,128)}, f32[64,512]{1,0:T(8,128)}, u32[]{:S(2)}, u32[]{:S(2)}) collective-permute-start(f32[64,512]{1,0:T(8,128)} %add.54), channel_id=1, source_target_pairs={{0,16},{4,20},{8,24},{12,28},{16,0},{20,4},{24,8},{28,12},{1,17},{... | collective-permute-start | bytes 393224 | tf_op jit(solution)/shard_map/ppermute | solution.py:24
  163.0 1.2 collective-permute-start.22
  163.2 4.6 %collective-permute-start.21 = (bf16[64,512]{1,0:T(8,128)(2,1)S(1)}, bf16[64,512]{1,0:T(8,128)(2,1)S(1)}, u32[]{:S(2)}, u32[]{:S(2)}) collective-permute-start(bf16[64,512]{1,0:T(8,128)(2,1)S(1)} %fusion.10), channel_id=1, source_target_pairs={{0,4},{4,0},{8,12},{12,8},{16,20},{20,16},{24,28},{28,24},{1,5},{5... | collective-permute-start | bytes 196616 | tf_op jit(solution)/shard_map/ppermute | solution.py:24
  165.0 3.6 %collective-permute-start.25 = (f32[4,128]{1,0:T(4,128)S(1)}, f32[4,128]{1,0:T(4,128)S(1)}, u32[]{:S(2)}, u32[]{:S(2)}) collective-permute-start(f32[4,128]{1,0:T(4,128)S(1)} %maximum_maximum_fusion.refs_12_), channel_id=1, source_target_pairs={{0,3},{1,0},{2,1},{3,2},{4,7},{5,4},{6,5},{7,6},{8,11},{9,8},{10,9... | collective-permute-start | bytes 6152 | tf_op jit(solution)/shard_map/ppermute | solution.py:19
  166.7 4.5 %collective-permute-start.24 = (f32[4,128]{1,0:T(4,128)S(1)}, f32[4,128]{1,0:T(4,128)S(1)}, u32[]{:S(2)}, u32[]{:S(2)}) collective-permute-start(f32[4,128]{1,0:T(4,128)S(1)} %maximum_maximum_fusion.refs_12_), channel_id=1, source_target_pairs={{0,2},{1,3},{2,0},{3,1},{4,6},{5,7},{6,4},{7,5},{8,10},{9,11},{10,... | collective-permute-start | bytes 6152 | tf_op jit(solution)/shard_map/ppermute | solution.py:19
  166.7 5.4 %collective-permute-start.23 = (f32[4,128]{1,0:T(4,128)S(1)}, f32[4,128]{1,0:T(4,128)S(1)}, u32[]{:S(2)}, u32[]{:S(2)}) collective-permute-start(f32[4,128]{1,0:T(4,128)S(1)} %maximum_maximum_fusion.refs_12_), channel_id=1, source_target_pairs={{0,1},{1,2},{2,3},{3,0},{4,5},{5,6},{6,7},{7,4},{8,9},{9,10},{10,1... | collective-permute-start | bytes 6152 | tf_op jit(solution)/shard_map/ppermute | solution.py:19
  172.1 1.2 copy-start.12
  173.4 1.2 copy-start.18
  (11 other events, 8.9 us)

commit v4 on v3

--- a/solution.py
+++ b/solution.py
@@ -12,6 +12,18 @@
 MIB = 1024 * 1024
 FREE = pl.CostEstimate(flops=0, bytes_accessed=0, transcendentals=0)
 ANYWHERE = pl.BlockSpec(memory_space=pl.ANY)
+IN_VMEM = pl.BlockSpec(memory_space=pltpu.VMEM)
+
+
+vmem_shape = pltpu.VMEM
+
+
+def in_vmem(block):
+    return pltpu.with_memory_space_constraint(block, pltpu.VMEM)
+
+
+def in_hbm(block):
+    return pltpu.with_memory_space_constraint(block, pltpu.HBM)
 
 
 def shifted(block, axis, shift):
@@ -35,42 +47,60 @@
         in_specs=[ANYWHERE] * (1 + len(after)),
         out_specs=ANYWHERE,
         input_output_aliases={0: 0},
-        cost_estimate=FREE,
-    )(block, *after)
+        compiler_params=pltpu.CompilerParams(vmem_limit_bytes=2 * MIB),
+        cost_estimate=FREE,
+    )(in_vmem(block), *after)
+
+
+def load_body(count, *refs):
+    arrays, copies, semaphores = refs[:count], refs[count : 2 * count], refs[-1]
+    moves = [
+        pltpu.make_async_copy(array, copy, semaphores.at[i])
+        for i, (array, copy) in enumerate(zip(arrays, copies))
+    ]
+    for move in moves:
+        move.start()
+    for move in moves:
+        move.wait()
+
+
+def load(*arrays):
+    return pl.pallas_call(
+        functools.partial(load_body, len(arrays)),
+        out_shape=[vmem_shape(array.shape, array.dtype) for array in arrays],
+        in_specs=[pl.BlockSpec(memory_space=pltpu.HBM)] * len(arrays),
+        out_specs=[IN_VMEM] * len(arrays),
+        scratch_shapes=[pltpu.SemaphoreType.DMA((len(arrays),))],
+        compiler_params=pltpu.CompilerParams(vmem_limit_bytes=2 * MIB),
+        cost_estimate=FREE,
+    )(*[in_hbm(array) for array in arrays])
 
 
 def project_body(first, block, piece_ref, green_ref, acc_ref, total_ref):
     total_ref[...] = acc_ref[...]
 
-    def step(piece, green):
+    @pl.loop(0, piece_ref.shape[0] // block)
+    def _(i):
+        at = pl.multiple_of(i * block, block)
         total_ref[...] += lax.dot_general(
-            piece[...], green[...], (((0,), (0,)), ((), ())), preferred_element_type=jnp.float32
+            piece_ref[pl.ds(at, block), :],
+            green_ref[pl.ds(first + at, block), :],
+            (((0,), (0,)), ((), ())),
+            preferred_element_type=jnp.float32,
         )
-
-    length, vectors = piece_ref.shape
-    columns = green_ref.shape[1]
-    pltpu.emit_pipeline(
-        step,
-        grid=(length // block,),
-        in_specs=[
-            pl.BlockSpec((block, vectors), lambda i: (i, 0)),
-            pl.BlockSpec((block, columns), lambda i: (i + first // block, 0)),
-        ],
-    )(piece_ref, green_ref)
 
 
 def project(piece, green, first, so_far):
     length, vectors = piece.shape
     columns = green.shape[1]
-    in_vmem = pl.BlockSpec(memory_space=pltpu.VMEM)
     return pl.pallas_call(
         functools.partial(project_body, first, min(length, 1024)),
         out_shape=jax.ShapeDtypeStruct((vectors, columns), jnp.float32),
-        in_specs=[ANYWHERE, pl.BlockSpec(memory_space=pltpu.HBM), in_vmem],
-        out_specs=in_vmem,
-        compiler_params=pltpu.CompilerParams(vmem_limit_bytes=12 * MIB),
-        cost_estimate=FREE,
-    )(piece, green, so_far)
+        in_specs=[IN_VMEM] * 3,
+        out_specs=IN_VMEM,
+        compiler_params=pltpu.CompilerParams(vmem_limit_bytes=6 * MIB),
+        cost_estimate=FREE,
+    )(in_vmem(piece), green, so_far)
 
 
 def project_plain(piece, green_rows):
@@ -118,6 +148,7 @@
     return pl.pallas_call(
         functools.partial(dress_kernel_body, step),
         out_shape=jax.ShapeDtypeStruct(mine.shape, jnp.bfloat16),
+        compiler_params=pltpu.CompilerParams(vmem_limit_bytes=6 * MIB),
         cost_estimate=FREE,
     )(mine, other, weights, green_one)
 
@@ -150,6 +181,7 @@
             jax.ShapeDtypeStruct((2 * half, columns), jnp.bfloat16),
             jax.ShapeDtypeStruct((1, 2 * half), jnp.float32),
         ],
+        compiler_params=pltpu.CompilerParams(vmem_limit_bytes=6 * MIB),
         cost_estimate=FREE,
     )(mine, other, trace_weights)
 
@@ -189,12 +221,13 @@
     return dressed, traced
 
 
-def slope_body(shards, pieces, blocks, share_blocks, me_ref, *refs):
+def slope_body(shards, pieces, block, share_blocks, me_ref, *refs):
     factor_refs = refs[: shards * pieces]
     dressed_refs = refs[shards * pieces : shards * pieces + shards]
     trace_refs = refs[shards * pieces + shards : -3]
     slope_ref, collision_ref, trace_ref = refs[-3:]
     at = pl.program_id(0)
+    blocks = factor_refs[0].shape[0] // block
 
     @pl.when(at == 0)
     def _():
@@ -218,8 +251,9 @@
 
         @pl.when(at // blocks == i)
         def _():
+            here = pl.ds(pl.multiple_of((at - i * blocks) * block, block), block)
             basis = jnp.concatenate(
-                [factor_refs[s * pieces + i][...] for s in range(shards)], axis=1
+                [factor_refs[s * pieces + i][here, :] for s in range(shards)], axis=1
             )
             slope_ref[...] = jnp.dot(basis, dressed, preferred_element_type=jnp.float32)
 
@@ -231,7 +265,12 @@
                     (((1,), (1,)), ((), ())),
                     preferred_element_type=jnp.float32,
                 )
-                collision_ref[pl.ds(at - first, 1), :] = jnp.sum(parts, axis=0, keepdims=True)
+                there = (
+                    slice(None)
+                    if share_blocks == 1
+                    else pl.ds(pl.multiple_of((at - first) * block, block), block)
+                )
+                collision_ref[:, there] = jnp.sum(parts, axis=0, keepdims=True)
 
 
 def slope(steps, dressed, traces):
@@ -242,34 +281,26 @@
     rows = pieces * length
     share = rows // shards
     block = min(length, share, 1024)
-    blocks = length // block
-    factor_specs = [
-        pl.BlockSpec(
-            (block, vectors), lambda g, me, i=i: (jnp.clip(g - i * blocks, 0, blocks - 1), 0)
-        )
-        for _ in steps
-        for i in range(pieces)
-    ]
     whole = lambda g, me: (0, 0)
     slopes, collision = pl.pallas_call(
-        functools.partial(slope_body, shards, pieces, blocks, share // block),
+        functools.partial(slope_body, shards, pieces, block, share // block),
         grid_spec=pltpu.PrefetchScalarGridSpec(
             num_scalar_prefetch=1,
-            grid=(pieces * blocks,),
-            in_specs=factor_specs
+            grid=(rows // block,),
+            in_specs=[IN_VMEM] * (shards * pieces)
             + [pl.BlockSpec((vectors, columns), whole)] * shards
             + [pl.BlockSpec((shards, vectors), whole)] * shards,
             out_specs=[
                 pl.BlockSpec((block, columns), lambda g, me: (g, 0)),
-                pl.BlockSpec((share // block, block), whole),
+                pl.BlockSpec((1, share), whole),
             ],
             scratch_shapes=[pltpu.VMEM((8, depth), jnp.bfloat16)],
         ),
         out_shape=[
             jax.ShapeDtypeStruct((rows, columns), jnp.float32),
-            jax.ShapeDtypeStruct((share // block, block), jnp.float32),
+            jax.ShapeDtypeStruct((1, share), jnp.float32),
         ],
-        compiler_params=pltpu.CompilerParams(vmem_limit_bytes=20 * MIB),
+        compiler_params=pltpu.CompilerParams(vmem_limit_bytes=16 * MIB),
         cost_estimate=pl.CostEstimate(
             flops=2 * rows * depth * columns,
             bytes_accessed=rows * depth * 2 + rows * columns * 4,
@@ -277,7 +308,7 @@
         ),
     )(
         lax.axis_index("aux").astype(jnp.int32)[None],
-        *[piece for step in steps for piece in step],
+        *[in_vmem(piece) for step in steps for piece in step],
         *dressed,
         *traces,
     )
@@ -293,6 +324,7 @@
     me = lax.axis_index("aux")
     length = rows // PIECES
 
+    green, green_one = load(pair_green_block, green_one)
     trace_weights = lax.dynamic_slice_in_dim(
         green_one, me * orb_count, orb_count, 1
     ).T.reshape(1, columns)
@@ -301,20 +333,18 @@
         total = jnp.zeros((vectors, columns), jnp.float32)
         pieces = []
         for i in range(PIECES):
-            green = (pair_green_block, i * length)
+            first = i * length
             if step == 0:
-                piece = lax.slice_in_dim(cholesky_factors, i * length, (i + 1) * length, axis=0)
+                piece = lax.slice_in_dim(cholesky_factors, first, first + length, axis=0)
             elif i == 0:
                 piece = gate(shifted(steps[-1][i], "aux", 1), dressed[-1], traced[-1])
             else:
                 piece = gate(shifted(steps[-1][i], "aux", 1), total)
             pieces.append(piece)
             if step < aux_size - 1:
-                total = project(piece, pair_green_block, i * length, total)
+                total = project(piece, green, first, total)
             else:
-                total = total + project_plain(
-                    piece, pair_green_block[i * length : (i + 1) * length]
-                )
+                total = total + project_plain(piece, green[first : first + length])
         steps.append(pieces)
         both, trace = sum_and_dress(step, total, screening, green_one, trace_weights)
         dressed.append(both)

time: 188 us -> 185 us (0.984)
  waiting for transfers between devices: 74.8 us -> 116 us
  local copies, waits for them, and re-layouts: 35.6 us -> 13.6 us
  Pallas kernels: 37.7 us -> 28.1 us
  matrix products: 10 us -> 2.22 us
  starting transfers between devices: 25.1 us -> 22.1 us
    ppermute x9, waiting for transfers between devices: 37.6 us -> 78 us  [shifted(): lax.ppermute(block, axis, [(i, (i + shift) % count) for i in range(count)])]
    unnamed x68 -> x35, local copies, waits for them, and re-layouts: 31.9 us -> 9.79 us
    dot_general x2, matrix products: 7.36 us -> 1.48 us  [project_plain(): lax.dot_general(piece, green_rows, (((0,), (0,)), ((), ())), preferred_el...]
    pallas_call x3, Pallas kernels: 6.61 us -> 1.26 us  [dress_kernel(): pl.pallas_call(functools.partial(dress_kernel_body, step), out_shape=jax....]
    pallas_call x3, Pallas kernels: 4.89 us -> 0.47 us  [join_kernel(): pl.pallas_call(join_kernel_body, out_shape=[jax.ShapeDtypeStruct((2 * hal...]
    ppermute x9, starting transfers between devices: 10.7 us -> 7.61 us  [shifted(): lax.ppermute(block, axis, [(i, (i + shift) % count) for i in range(count)])]
    pallas_call x1 -> x2, Pallas kernels: 11.8 us -> 14.7 us  [the longest x1 11.3 us: slope(): pl.pallas_call(functools.partial(slope_body, shards, pieces, block, share...]
    pallas_call x6, Pallas kernels: 14.4 us -> 11.6 us  [project(): pl.pallas_call(functools.partial(project_body, first, min(length, 1024)),...]
  transfers between devices with their start and end apart: 26 -> 26, of which waited for: 21 -> 25; matrix products, arithmetic and copies ran while one was open for 4% -> 1% of each run, Pallas kernels for 14% -> 9%
where the time goes in v4:
time: 185 us
  waiting for transfers between devices  116 us (63%)
  Pallas kernels  28.1 us (15%)
  starting transfers between devices  22.1 us (12%)
  local copies, waits for them, and re-layouts  13.6 us (7%)
  matrix products  2.22 us (1%)
  other arithmetic  2.13 us (1%)
    ppermute x9, waiting for transfers between devices, shifted(): lax.ppermute(block, axis, [(i, (i + shift) % count) for i in range(count)])  78 us
    ppermute x17, waiting for transfers between devices, exchanged(): return lax.ppermute(block, axis, [(i, i ^ bit) for i in range(count)])  37.7 us
    ppermute x17, starting transfers between devices, exchanged(): return lax.ppermute(block, axis, [(i, i ^ bit) for i in range(count)])  14.5 us
    pallas_call x6, Pallas kernels, project(): pl.pallas_call(functools.partial(project_body, first, min(length, 1024)),...  11.6 us
    pallas_call x1, Pallas kernels, slope(): pl.pallas_call(functools.partial(slope_body, shards, pieces, block, share...  11.3 us
    unnamed x35, local copies, waits for them, and re-layouts  9.79 us
    ppermute x9, starting transfers between devices, shifted(): lax.ppermute(block, axis, [(i, (i + shift) % count) for i in range(count)])  7.61 us
  transfers between devices with their start and end apart: 26, of which 25 were waited for; matrix products, arithmetic and copies ran while one was open for 1% of the time, Pallas kernels for 9%

profile of v4, /device:TPU:0, one launch (start us, length us, event | category | flops | bytes accessed | tf_op | source)
XLA Modules:
  0.0 184.8 jit_solution(522669923037412)
XLA Ops:
  0.6 2.7 %fusion.17 = (bf16[4096,128]{1,0:T(8,128)(2,1)}, bf16[4096,128]{1,0:T(8,128)(2,1)S(1)}) fusion(bf16[8192,128]{1,0:T(8,128)(2,1)} %param.5), kind=kLoop, calls=%fused_computation.30 | loop fusion | bytes 4194304 | tf_op jit(solution)/shard_map/slice | solution.py:338
  3.3 3.0 %collective-permute-start = (bf16[4096,128]{1,0:T(8,128)(2,1)S(1)}, bf16[4096,128]{1,0:T(8,128)(2,1)S(1)}, u32[]{:S(2)}, u32[]{:S(2)}) collective-permute-start(bf16[4096,128]{1,0:T(8,128)(2,1)S(1)} %get-tuple-element.23.piece_ref.refs_0_), channel_id=1, source_target_pairs={{0,1},{1,2},{2,3},{3,0},{4,5},{5,6},{6,7},{7,4},{8,9},{9,10},{10,1... | collective-permute-start | bytes 3145736 | tf_op jit(solution)/shard_map/ppermute | solution.py:31
  6.3 1.6 collective-permute-start.5
  7.9 3.4 %shard_map.59 = (bf16[8192,512]{1,0:T(8,128)(2,1)S(1)}, f32[256,256]{1,0:T(8,128)S(1)}) custom-call(bf16[8192,512]{1,0:T(8,128)(2,1)} %refs_0_.1, f32[256,256]{1,0:T(8,128)} %refs_1_.1), custom_call_target="tpu_custom_call" | custom-call | tf_op jit(solution)/shard_map/pallas_call | solution.py:68
  11.4 1.4 shard_map.60.acc_ref
  12.8 3.4 %shard_map.61 = f32[128,512]{1,0:T(8,128)S(1)} custom-call(bf16[4096,128]{1,0:T(8,128)(2,1)} %get-tuple-element.22.piece_ref.refs_1_, bf16[8192,512]{1,0:T(8,128)(2,1)S(1)} %get-tuple-element.12.green_ref, f32[128,512]{1,0:T(8,128)S(1)} %shard_map.60.acc_ref), custom_call_target="tpu_custom_call" | custom-call | tf_op jit(solution)/shard_map/pallas_call | solution.py:96
  16.3 1.3 collective-permute-done.1
  17.7 1.6 collective-permute-start.2
  19.2 4.1 %collective-permute-done.2 = f32[64,512]{1,0:T(8,128)S(1)} collective-permute-done((f32[64,512]{1,0:T(8,128)S(1)}, f32[64,512]{1,0:T(8,128)S(1)}, u32[]{:S(2)}, u32[]{:S(2)}) %collective-permute-start.2) | collective-permute-done | bytes 131104 | tf_op jit(solution)/shard_map/ppermute | solution.py:36
  23.3 1.6 collective-permute-start.3
  25.1 3.3 %collective-permute-done.3.other_ref = f32[64,512]{1,0:T(8,128)S(1)} collective-permute-done((f32[64,512]{1,0:T(8,128)S(1)}, f32[64,512]{1,0:T(8,128)S(1)}, u32[]{:S(2)}, u32[]{:S(2)}) %collective-permute-start.3) | collective-permute-done | bytes 131104 | tf_op jit(solution)/shard_map/ppermute | solution.py:36
  29.0 1.0 collective-permute-done.4.other_ref
  30.2 2.1 %collective-permute-done.refs_0_ = bf16[4096,128]{1,0:T(8,128)(2,1)S(1)} collective-permute-done((bf16[4096,128]{1,0:T(8,128)(2,1)S(1)}, bf16[4096,128]{1,0:T(8,128)(2,1)S(1)}, u32[]{:S(2)}, u32[]{:S(2)}) %collective-permute-start) | collective-permute-done | bytes 1048608 | tf_op jit(solution)/shard_map/ppermute | solution.py:31
  32.4 3.4 %copy-done.1 = bf16[8192,512]{1,0:T(8,128)(2,1)S(1)} copy-done((bf16[8192,512]{1,0:T(8,128)(2,1)S(1)}, bf16[8192,512]{1,0:T(8,128)(2,1)}, u32[]{:S(2)}) %copy-start.1) | copy-done | bytes 8388632
  35.8 1.4 shard_map.65.refs_1_.acc_ref
  37.2 17.7 %collective-permute-done.5.refs_0_ = bf16[4096,128]{1,0:T(8,128)(2,1)} collective-permute-done((bf16[4096,128]{1,0:T(8,128)(2,1)}, bf16[4096,128]{1,0:T(8,128)(2,1)}, u32[]{:S(2)}, u32[]{:S(2)}) %collective-permute-start.5) | collective-permute-done | bytes 1048608 | tf_op jit(solution)/shard_map/ppermute | solution.py:31
  54.9 2.8 %shard_map.67 = f32[128,512]{1,0:T(8,128)S(1)} custom-call(bf16[4096,128]{1,0:T(8,128)(2,1)} %shard_map.66.piece_ref.refs_3_, bf16[8192,512]{1,0:T(8,128)(2,1)S(1)} %copy-done.1, f32[128,512]{1,0:T(8,128)S(1)} %shard_map.65.refs_1_.acc_ref), custom_call_target="tpu_custom_call" | custom-call | tf_op jit(solution)/shard_map/pallas_call | solution.py:96
  57.9 1.3 collective-permute-done.7
  59.2 1.8 collective-permute-start.8
  61.0 3.8 %collective-permute-done.8 = f32[64,512]{1,0:T(8,128)S(1)} collective-permute-done((f32[64,512]{1,0:T(8,128)S(1)}, f32[64,512]{1,0:T(8,128)S(1)}, u32[]{:S(2)}, u32[]{:S(2)}) %collective-permute-start.8) | collective-permute-done | bytes 131104 | tf_op jit(solution)/shard_map/ppermute | solution.py:36
  64.9 1.8 collective-permute-start.9
  66.7 3.2 %collective-permute-done.9.other_ref = f32[64,512]{1,0:T(8,128)S(1)} collective-permute-done((f32[64,512]{1,0:T(8,128)S(1)}, f32[64,512]{1,0:T(8,128)S(1)}, u32[]{:S(2)}, u32[]{:S(2)}) %collective-permute-start.9) | collective-permute-done | bytes 131104 | tf_op jit(solution)/shard_map/ppermute | solution.py:36
  70.4 1.2 collective-permute-done.10.other_ref
  71.8 5.5 %collective-permute-done.6.refs_0_ = bf16[4096,128]{1,0:T(8,128)(2,1)S(1)} collective-permute-done((bf16[4096,128]{1,0:T(8,128)(2,1)S(1)}, bf16[4096,128]{1,0:T(8,128)(2,1)S(1)}, u32[]{:S(2)}, u32[]{:S(2)}) %collective-permute-start.6) | collective-permute-done | bytes 1048608 | tf_op jit(solution)/shard_map/ppermute | solution.py:31
  77.3 1.3 shard_map.71.refs_1_.acc_ref
  78.7 21.1 %collective-permute-done.11.refs_0_ = bf16[4096,128]{1,0:T(8,128)(2,1)S(1)} collective-permute-done((bf16[4096,128]{1,0:T(8,128)(2,1)}, bf16[4096,128]{1,0:T(8,128)(2,1)S(1)}, u32[]{:S(2)}, u32[]{:S(2)}) %collective-permute-start.11) | collective-permute-done | bytes 1048608 | tf_op jit(solution)/shard_map/ppermute | solution.py:31
  99.8 1.3 shard_map.73
  101.3 1.2 collective-permute-done.13
  102.6 1.8 collective-permute-start.14
  104.4 3.8 %collective-permute-done.14 = f32[64,512]{1,0:T(8,128)S(1)} collective-permute-done((f32[64,512]{1,0:T(8,128)S(1)}, f32[64,512]{1,0:T(8,128)S(1)}, u32[]{:S(2)}, u32[]{:S(2)}) %collective-permute-start.14) | collective-permute-done | bytes 131104 | tf_op jit(solution)/shard_map/ppermute | solution.py:36
  108.2 1.8 collective-permute-start.15
  110.0 3.2 %collective-permute-done.15.other_ref = f32[64,512]{1,0:T(8,128)S(1)} collective-permute-done((f32[64,512]{1,0:T(8,128)S(1)}, f32[64,512]{1,0:T(8,128)S(1)}, u32[]{:S(2)}, u32[]{:S(2)}) %collective-permute-start.15) | collective-permute-done | bytes 131104 | tf_op jit(solution)/shard_map/ppermute | solution.py:36
  113.7 1.2 collective-permute-done.16.other_ref
  115.1 7.1 %collective-permute-done.12.refs_0_ = bf16[4096,128]{1,0:T(8,128)(2,1)S(1)} collective-permute-done((bf16[4096,128]{1,0:T(8,128)(2,1)S(1)}, bf16[4096,128]{1,0:T(8,128)(2,1)S(1)}, u32[]{:S(2)}, u32[]{:S(2)}) %collective-permute-start.12) | collective-permute-done | bytes 1048608 | tf_op jit(solution)/shard_map/ppermute | solution.py:31
  123.6 20.2 %collective-permute-done.17.refs_0_ = bf16[4096,128]{1,0:T(8,128)(2,1)S(1)} collective-permute-done((bf16[4096,128]{1,0:T(8,128)(2,1)S(1)}, bf16[4096,128]{1,0:T(8,128)(2,1)S(1)}, u32[]{:S(2)}, u32[]{:S(2)}) %collective-permute-start.17) | collective-permute-done | bytes 1048608 | tf_op jit(solution)/shard_map/ppermute | solution.py:31
  145.0 1.3 collective-permute-done.18
  146.3 1.6 collective-permute-start.19
  147.9 4.1 %collective-permute-done.19 = f32[64,512]{1,0:T(8,128)S(1)} collective-permute-done((f32[64,512]{1,0:T(8,128)S(1)}, f32[64,512]{1,0:T(8,128)S(1)}, u32[]{:S(2)}, u32[]{:S(2)}) %collective-permute-start.19) | collective-permute-done | bytes 131104 | tf_op jit(solution)/shard_map/ppermute | solution.py:36
  152.6 1.5 collective-permute-start.20
  154.9 3.0 %collective-permute-done.20 = f32[64,512]{1,0:T(8,128)} collective-permute-done((f32[64,512]{1,0:T(8,128)}, f32[64,512]{1,0:T(8,128)}, u32[]{:S(2)}, u32[]{:S(2)}) %collective-permute-start.20) | collective-permute-done | bytes 131104 | tf_op jit(solution)/shard_map/ppermute | solution.py:36
  157.9 1.0 add.55
  160.9 1.7 collective-permute-start.25
  162.6 1.0 collective-permute-start.23
  164.5 2.6 %collective-permute-done.24.refs_14_ = f32[4,128]{1,0:T(4,128)S(1)} collective-permute-done((f32[4,128]{1,0:T(4,128)S(1)}, f32[4,128]{1,0:T(4,128)S(1)}, u32[]{:S(2)}, u32[]{:S(2)}) %collective-permute-start.24) | collective-permute-done | bytes 2080 | tf_op jit(solution)/shard_map/ppermute | solution.py:31
  168.0 1.2 copy-done.5
  169.3 1.2 copy-done.7
  170.5 1.2 copy-done.9
  173.5 11.3 %shard_map.78 = (f32[8192,512]{1,0:T(8,128)}, f32[1,2048]{1,0:T(1,128)}) custom-call(s32[1]{0:T(128)} %bitcast.me_ref, bf16[4096,128]{1,0:T(8,128)(2,1)S(1)} %copy-done.5, bf16[4096,128]{1,0:T(8,128)(2,1)} %get-tuple-element.22.piece_ref.refs_1_, bf16[4096,128]{1,0:T(8,128)(2,1)S(1)} %shard_map.64.piece_ref.refs_2_, ...), custom_call_target="tpu_custom_call" | custom-call | flops 4294967296 | bytes 25165824 | tf_op jit(solution)/shard_map/pallas_call | solution.py:285
  (89 shorter events, 12.4 us)
Async XLA Ops:
  3.3 9.5 %copy-start.4 = (bf16[4096,128]{1,0:T(8,128)(2,1)}, bf16[4096,128]{1,0:T(8,128)(2,1)S(1)}, u32[]{:S(2)}) copy-start(bf16[4096,128]{1,0:T(8,128)(2,1)S(1)} %get-tuple-element.23.piece_ref.refs_0_) | copy-start | bytes 3145732
  3.3 29.0 %collective-permute-start = (bf16[4096,128]{1,0:T(8,128)(2,1)S(1)}, bf16[4096,128]{1,0:T(8,128)(2,1)S(1)}, u32[]{:S(2)}, u32[]{:S(2)}) collective-permute-start(bf16[4096,128]{1,0:T(8,128)(2,1)S(1)} %get-tuple-element.23.piece_ref.refs_0_), channel_id=1, source_target_pairs={{0,1},{1,2},{2,3},{3,0},{4,5},{5,6},{6,7},{7,4},{8,9},{9,10},{10,1... | collective-permute-start | bytes 3145736 | tf_op jit(solution)/shard_map/ppermute | solution.py:31
  6.3 48.6 %collective-permute-start.5 = (bf16[4096,128]{1,0:T(8,128)(2,1)}, bf16[4096,128]{1,0:T(8,128)(2,1)}, u32[]{:S(2)}, u32[]{:S(2)}) collective-permute-start(bf16[4096,128]{1,0:T(8,128)(2,1)} %get-tuple-element.22.piece_ref.refs_1_), channel_id=1, source_target_pairs={{0,1},{1,2},{2,3},{3,0},{4,5},{5,6},{6,7},{7,4},{8,9},{9,10},{10,1... | collective-permute-start | bytes 3145736 | tf_op jit(solution)/shard_map/ppermute | solution.py:31
  11.3 4.9 %copy-start = (bf16[8192,512]{1,0:T(8,128)(2,1)}, bf16[8192,512]{1,0:T(8,128)(2,1)S(1)}, u32[]{:S(2)}) copy-start(bf16[8192,512]{1,0:T(8,128)(2,1)S(1)} %get-tuple-element.12.green_ref) | copy-start | bytes 25165828
  11.4 13.5 %copy-start.14 = (f32[512]{0:T(512)S(1)}, f32[512]{0:T(512)}, u32[]{:S(2)}) copy-start(f32[512]{0:T(512)} %param.7) | copy-start | bytes 6148
  16.2 1.4 collective-permute-start.1
  17.7 5.6 %collective-permute-start.2 = (f32[64,512]{1,0:T(8,128)S(1)}, f32[64,512]{1,0:T(8,128)S(1)}, u32[]{:S(2)}, u32[]{:S(2)}) collective-permute-start(f32[64,512]{1,0:T(8,128)S(1)} %select_add_fusion.3), channel_id=1, source_target_pairs={{0,8},{4,12},{8,0},{12,4},{16,24},{20,28},{24,16},{28,20},{1,9},{5... | collective-permute-start | bytes 393224 | tf_op jit(solution)/shard_map/ppermute | solution.py:36
  23.3 5.0 %collective-permute-start.3 = (f32[64,512]{1,0:T(8,128)S(1)}, f32[64,512]{1,0:T(8,128)S(1)}, u32[]{:S(2)}, u32[]{:S(2)}) collective-permute-start(f32[64,512]{1,0:T(8,128)S(1)} %add.46.mine_ref), channel_id=1, source_target_pairs={{0,16},{4,20},{8,24},{12,28},{16,0},{20,4},{24,8},{28,12},{1,17},{... | collective-permute-start | bytes 393224 | tf_op jit(solution)/shard_map/ppermute | solution.py:36
  28.8 1.3 collective-permute-start.4
  32.3 44.9 %collective-permute-start.6 = (bf16[4096,128]{1,0:T(8,128)(2,1)S(1)}, bf16[4096,128]{1,0:T(8,128)(2,1)S(1)}, u32[]{:S(2)}, u32[]{:S(2)}) collective-permute-start(bf16[4096,128]{1,0:T(8,128)(2,1)S(1)} %shard_map.64.piece_ref.refs_2_), channel_id=1, source_target_pairs={{0,1},{1,2},{2,3},{3,0},{4,5},{5,6},{6,7},{7,4},{8,9},{9,10},{10,1... | collective-permute-start | bytes 3145736 | tf_op jit(solution)/shard_map/ppermute | solution.py:31
  32.4 3.4 %copy-start.1 = (bf16[8192,512]{1,0:T(8,128)(2,1)S(1)}, bf16[8192,512]{1,0:T(8,128)(2,1)}, u32[]{:S(2)}) copy-start(bf16[8192,512]{1,0:T(8,128)(2,1)} %copy-done) | copy-start | bytes 25165828
  37.2 40.2 %slice-start = ((s8[8388608]{0:T(1024)(128)(4,1)}), s8[4194304]{0:T(1024)(128)(4,1)S(1)}, s32[]{:S(2)}) async-start(s8[8388608]{0:T(1024)(128)(4,1)} %bitcast.18), calls=%async_computation | async-start | bytes 8388608
  54.9 22.4 %slice-start.1 = ((s8[8388608]{0:T(1024)(128)(4,1)}), s8[4194304]{0:T(1024)(128)(4,1)S(1)}, s32[]{:S(2)}) async-start(s8[8388608]{0:T(1024)(128)(4,1)} %bitcast.18), calls=%async_computation.1 | async-start | bytes 8388608
  57.7 42.1 %collective-permute-start.11 = (bf16[4096,128]{1,0:T(8,128)(2,1)}, bf16[4096,128]{1,0:T(8,128)(2,1)S(1)}, u32[]{:S(2)}, u32[]{:S(2)}) collective-permute-start(bf16[4096,128]{1,0:T(8,128)(2,1)} %shard_map.66.piece_ref.refs_3_), channel_id=1, source_target_pairs={{0,1},{1,2},{2,3},{3,0},{4,5},{5,6},{6,7},{7,4},{8,9},{9,10},{10,1... | collective-permute-start | bytes 3145736 | tf_op jit(solution)/shard_map/ppermute | solution.py:31
  57.8 1.4 collective-permute-start.7
  59.2 5.6 %collective-permute-start.8 = (f32[64,512]{1,0:T(8,128)S(1)}, f32[64,512]{1,0:T(8,128)S(1)}, u32[]{:S(2)}, u32[]{:S(2)}) collective-permute-start(f32[64,512]{1,0:T(8,128)S(1)} %select_add_fusion.2), channel_id=1, source_target_pairs={{0,8},{4,12},{8,0},{12,4},{16,24},{20,28},{24,16},{28,20},{1,9},{5... | collective-permute-start | bytes 393224 | tf_op jit(solution)/shard_map/ppermute | solution.py:36
  64.9 5.0 %collective-permute-start.9 = (f32[64,512]{1,0:T(8,128)S(1)}, f32[64,512]{1,0:T(8,128)S(1)}, u32[]{:S(2)}, u32[]{:S(2)}) collective-permute-start(f32[64,512]{1,0:T(8,128)S(1)} %add.49.mine_ref), channel_id=1, source_target_pairs={{0,16},{4,20},{8,24},{12,28},{16,0},{20,4},{24,8},{28,12},{1,17},{... | collective-permute-start | bytes 393224 | tf_op jit(solution)/shard_map/ppermute | solution.py:36
  70.3 1.3 collective-permute-start.10
  71.8 27.9 %copy-start.10 = (bf16[128,512]{1,0:T(8,128)(2,1)}, bf16[128,512]{1,0:T(8,128)(2,1)S(1)}, u32[]{:S(2)}) copy-start(bf16[128,512]{1,0:T(8,128)(2,1)S(1)} %get-tuple-element.16.refs_1_.refs_9_) | copy-start | bytes 393220
  77.3 44.9 %collective-permute-start.12 = (bf16[4096,128]{1,0:T(8,128)(2,1)S(1)}, bf16[4096,128]{1,0:T(8,128)(2,1)S(1)}, u32[]{:S(2)}, u32[]{:S(2)}) collective-permute-start(bf16[4096,128]{1,0:T(8,128)(2,1)S(1)} %shard_map.70.piece_ref.refs_4_), channel_id=1, source_target_pairs={{0,1},{1,2},{2,3},{3,0},{4,5},{5,6},{6,7},{7,4},{8,9},{9,10},{10,1... | collective-permute-start | bytes 3145736 | tf_op jit(solution)/shard_map/ppermute | solution.py:31
  99.8 23.9 %copy-start.2 = (bf16[4096,128]{1,0:T(8,128)(2,1)}, bf16[4096,128]{1,0:T(8,128)(2,1)S(1)}, u32[]{:S(2)}) copy-start(bf16[4096,128]{1,0:T(8,128)(2,1)S(1)} %shard_map.72.piece_ref.refs_5_) | copy-start | bytes 3145732
  101.1 1.4 collective-permute-start.13
  101.2 42.7 %collective-permute-start.17 = (bf16[4096,128]{1,0:T(8,128)(2,1)S(1)}, bf16[4096,128]{1,0:T(8,128)(2,1)S(1)}, u32[]{:S(2)}, u32[]{:S(2)}) collective-permute-start(bf16[4096,128]{1,0:T(8,128)(2,1)S(1)} %shard_map.72.piece_ref.refs_5_), channel_id=1, source_target_pairs={{0,1},{1,2},{2,3},{3,0},{4,5},{5,6},{6,7},{7,4},{8,9},{9,10},{10,1... | collective-permute-start | bytes 3145736 | tf_op jit(solution)/shard_map/ppermute | solution.py:31
  102.6 5.6 %collective-permute-start.14 = (f32[64,512]{1,0:T(8,128)S(1)}, f32[64,512]{1,0:T(8,128)S(1)}, u32[]{:S(2)}, u32[]{:S(2)}) collective-permute-start(f32[64,512]{1,0:T(8,128)S(1)} %select_add_fusion.1), channel_id=1, source_target_pairs={{0,8},{4,12},{8,0},{12,4},{16,24},{20,28},{24,16},{28,20},{1,9},{5... | collective-permute-start | bytes 393224 | tf_op jit(solution)/shard_map/ppermute | solution.py:36
  108.2 5.0 %collective-permute-start.15 = (f32[64,512]{1,0:T(8,128)S(1)}, f32[64,512]{1,0:T(8,128)S(1)}, u32[]{:S(2)}, u32[]{:S(2)}) collective-permute-start(f32[64,512]{1,0:T(8,128)S(1)} %add.51.mine_ref), channel_id=1, source_target_pairs={{0,16},{4,20},{8,24},{12,28},{16,0},{20,4},{24,8},{28,12},{1,17},{... | collective-permute-start | bytes 393224 | tf_op jit(solution)/shard_map/ppermute | solution.py:36
  113.7 1.3 collective-permute-start.16
  122.2 0.7 copy-start.12
  122.9 22.0 %copy-start.8 = (bf16[4096,128]{1,0:T(8,128)(2,1)}, bf16[4096,128]{1,0:T(8,128)(2,1)S(1)}, u32[]{:S(2)}) copy-start(bf16[4096,128]{1,0:T(8,128)(2,1)S(1)} %shard_map.76.refs_6_) | copy-start | bytes 3145732
  143.9 24.2 %copy-start.3 = (bf16[4096,128]{1,0:T(8,128)(2,1)S(1)}, bf16[4096,128]{1,0:T(8,128)(2,1)}, u32[]{:S(2)}) copy-start(bf16[4096,128]{1,0:T(8,128)(2,1)} %copy-done.2) | copy-start | bytes 3145732
  143.9 1.0 copy-start.6
  144.9 1.4 collective-permute-start.18
  146.3 5.6 %collective-permute-start.19 = (f32[64,512]{1,0:T(8,128)S(1)}, f32[64,512]{1,0:T(8,128)S(1)}, u32[]{:S(2)}, u32[]{:S(2)}) collective-permute-start(f32[64,512]{1,0:T(8,128)S(1)} %select_add_fusion), channel_id=1, source_target_pairs={{0,8},{4,12},{8,0},{12,4},{16,24},{20,28},{24,16},{28,20},{1,9},{5... | collective-permute-start | bytes 393224 | tf_op jit(solution)/shard_map/ppermute | solution.py:36
  152.6 5.3 %collective-permute-start.20 = (f32[64,512]{1,0:T(8,128)}, f32[64,512]{1,0:T(8,128)}, u32[]{:S(2)}, u32[]{:S(2)}) collective-permute-start(f32[64,512]{1,0:T(8,128)} %add.54), channel_id=1, source_target_pairs={{0,16},{4,20},{8,24},{12,28},{16,0},{20,4},{24,8},{28,12},{1,17},{... | collective-permute-start | bytes 393224 | tf_op jit(solution)/shard_map/ppermute | solution.py:36
  159.6 1.2 collective-permute-start.22
  159.8 3.9 %collective-permute-start.21 = (bf16[64,512]{1,0:T(8,128)(2,1)S(1)}, bf16[64,512]{1,0:T(8,128)(2,1)S(1)}, u32[]{:S(2)}, u32[]{:S(2)}) collective-permute-start(bf16[64,512]{1,0:T(8,128)(2,1)S(1)} %fusion.10), channel_id=1, source_target_pairs={{0,4},{4,0},{8,12},{12,8},{16,20},{20,16},{24,28},{28,24},{1,5},{5... | collective-permute-start | bytes 196616 | tf_op jit(solution)/shard_map/ppermute | solution.py:36
  160.9 3.6 %collective-permute-start.25 = (f32[4,128]{1,0:T(4,128)S(1)}, f32[4,128]{1,0:T(4,128)S(1)}, u32[]{:S(2)}, u32[]{:S(2)}) collective-permute-start(f32[4,128]{1,0:T(4,128)S(1)} %maximum_maximum_fusion.refs_12_), channel_id=1, source_target_pairs={{0,3},{1,0},{2,1},{3,2},{4,7},{5,4},{6,5},{7,6},{8,11},{9,8},{10,9... | collective-permute-start | bytes 6152 | tf_op jit(solution)/shard_map/ppermute | solution.py:31
  162.6 4.5 %collective-permute-start.24 = (f32[4,128]{1,0:T(4,128)S(1)}, f32[4,128]{1,0:T(4,128)S(1)}, u32[]{:S(2)}, u32[]{:S(2)}) collective-permute-start(f32[4,128]{1,0:T(4,128)S(1)} %maximum_maximum_fusion.refs_12_), channel_id=1, source_target_pairs={{0,2},{1,3},{2,0},{3,1},{4,6},{5,7},{6,4},{7,5},{8,10},{9,11},{10,... | collective-permute-start | bytes 6152 | tf_op jit(solution)/shard_map/ppermute | solution.py:31
  162.6 5.4 %collective-permute-start.23 = (f32[4,128]{1,0:T(4,128)S(1)}, f32[4,128]{1,0:T(4,128)S(1)}, u32[]{:S(2)}, u32[]{:S(2)}) collective-permute-start(f32[4,128]{1,0:T(4,128)S(1)} %maximum_maximum_fusion.refs_12_), channel_id=1, source_target_pairs={{0,1},{1,2},{2,3},{3,0},{4,5},{5,6},{6,7},{7,4},{8,9},{9,10},{10,1... | collective-permute-start | bytes 6152 | tf_op jit(solution)/shard_map/ppermute | solution.py:31
  168.0 1.2 copy-start.5
  169.3 1.2 copy-start.7
  170.5 1.2 copy-start.9
  171.7 0.9 copy-start.11
  172.6 0.9 copy-start.13

commit v5 on v4

--- a/solution.py
+++ b/solution.py
@@ -40,7 +40,7 @@
     del refs
 
 
-def gate(block, *after):
+def gate(block, place, *after):
     return pl.pallas_call(
         gate_body,
         out_shape=jax.ShapeDtypeStruct(block.shape, block.dtype),
@@ -49,7 +49,7 @@
         input_output_aliases={0: 0},
         compiler_params=pltpu.CompilerParams(vmem_limit_bytes=2 * MIB),
         cost_estimate=FREE,
-    )(in_vmem(block), *after)
+    )(place(block), *after)
 
 
 def load_body(count, *refs):
@@ -100,7 +100,7 @@
         out_specs=IN_VMEM,
         compiler_params=pltpu.CompilerParams(vmem_limit_bytes=6 * MIB),
         cost_estimate=FREE,
-    )(in_vmem(piece), green, so_far)
+    )(piece, green, so_far)
 
 
 def project_plain(piece, green_rows):
@@ -109,23 +109,20 @@
     )
 
 
-def dress(projection, weights, green_one, trace_weights):
-    norb = green_one.shape[0]
-    mixed = jnp.concatenate(
-        [
-            jnp.dot(projection[:, first : first + norb], green_one, precision=HIGHEST)
-            for first in range(0, projection.shape[1], norb)
-        ],
-        axis=1,
-    )
-    rounded = lax.reduce_precision(mixed * weights[:, None], 8, 7)
-    traced = lax.dot_general(
-        trace_weights, rounded, (((1,), (1,)), ((), ())), precision=HIGHEST
-    )
-    return rounded.astype(jnp.bfloat16), traced
-
-
-def dress_kernel_body(step, mine_ref, other_ref, weights_ref, green_ref, dressed_ref):
+def add_body(left_ref, right_ref, sum_ref):
+    sum_ref[...] = left_ref[...] + right_ref[...]
+
+
+def add(left, right):
+    return pl.pallas_call(
+        add_body,
+        out_shape=jax.ShapeDtypeStruct(left.shape, left.dtype),
+        compiler_params=pltpu.CompilerParams(vmem_limit_bytes=4 * MIB),
+        cost_estimate=FREE,
+    )(in_vmem(left), in_vmem(right))
+
+
+def dress_body(step, mine_ref, other_ref, weights_ref, green_ref, dressed_ref):
     half = mine_ref.shape[0]
     norb = green_ref.shape[0]
     aux_size = lax.axis_size("aux")
@@ -144,16 +141,16 @@
         dressed_ref[:, first : first + norb] = (mixed * weights).astype(jnp.bfloat16)
 
 
-def dress_kernel(step, mine, other, weights, green_one):
-    return pl.pallas_call(
-        functools.partial(dress_kernel_body, step),
+def dress(step, mine, other, weights, green_one):
+    return pl.pallas_call(
+        functools.partial(dress_body, step),
         out_shape=jax.ShapeDtypeStruct(mine.shape, jnp.bfloat16),
         compiler_params=pltpu.CompilerParams(vmem_limit_bytes=6 * MIB),
         cost_estimate=FREE,
-    )(mine, other, weights, green_one)
-
-
-def join_kernel_body(mine_ref, other_ref, trace_ref, dressed_ref, traced_ref):
+    )(in_vmem(mine), in_vmem(other), weights, in_vmem(green_one))
+
+
+def join_body(mine_ref, other_ref, trace_ref, dressed_ref, traced_ref):
     half = mine_ref.shape[0]
     upper = lax.rem(lax.axis_index("rows"), 2)
     dressed_ref[pl.ds(pl.multiple_of(upper * half, half), half), :] = mine_ref[...]
@@ -173,21 +170,21 @@
     traced_ref[...] = jnp.sum(traced, axis=0, keepdims=True)
 
 
-def join_kernel(mine, other, trace_weights):
+def join(mine, other, trace_weights):
     half, columns = mine.shape
     return pl.pallas_call(
-        join_kernel_body,
+        join_body,
         out_shape=[
             jax.ShapeDtypeStruct((2 * half, columns), jnp.bfloat16),
             jax.ShapeDtypeStruct((1, 2 * half), jnp.float32),
         ],
         compiler_params=pltpu.CompilerParams(vmem_limit_bytes=6 * MIB),
         cost_estimate=FREE,
-    )(mine, other, trace_weights)
+    )(in_vmem(mine), in_vmem(other), trace_weights)
 
 
 def sum_and_dress(step, projection, weights, green_one, trace_weights):
-    count, aux_size = lax.axis_size("rows"), lax.axis_size("aux")
+    count = lax.axis_size("rows")
     half = projection.shape[0] // 2
     upper = lax.rem(lax.axis_index("rows"), 2) == 1
     low, high = projection[:half], projection[half:]
@@ -195,39 +192,37 @@
     other = exchanged(jnp.where(upper, low, high), "rows", 1)
     bit = 2
     while bit < count:
-        total = total + other
+        total = add(total, other)
         other = exchanged(total, "rows", bit)
         bit *= 2
-    if step < aux_size - 1:
-        mine = dress_kernel(step, total, other, weights[:, None], green_one)
-        return join_kernel(mine, exchanged(mine, "rows", 1), trace_weights)
-    owner = lax.rem(lax.axis_index("aux") - step + aux_size, aux_size)
-    first = (2 * owner + lax.rem(lax.axis_index("rows"), 2)) * half
-    mine, mine_traced = dress(
-        total + other,
-        lax.dynamic_slice_in_dim(weights, first, half, 0),
-        green_one,
-        trace_weights,
-    )
-    other = exchanged(mine, "rows", 1)
-    other_traced = exchanged(mine_traced, "rows", 1)
-    dressed = jnp.concatenate(
-        [jnp.where(upper, other, mine), jnp.where(upper, mine, other)], axis=0
-    )
-    traced = jnp.concatenate(
-        [jnp.where(upper, other_traced, mine_traced), jnp.where(upper, mine_traced, other_traced)],
-        axis=1,
-    )
-    return dressed, traced
-
-
-def slope_body(shards, pieces, block, share_blocks, me_ref, *refs):
-    factor_refs = refs[: shards * pieces]
-    dressed_refs = refs[shards * pieces : shards * pieces + shards]
-    trace_refs = refs[shards * pieces + shards : -3]
-    slope_ref, collision_ref, trace_ref = refs[-3:]
+    mine = dress(step, total, other, weights, green_one)
+    return join(mine, exchanged(mine, "rows", 1), trace_weights)
+
+
+SLOTS = 3
+PARTS = 4
+
+
+def slope_body(shards, pieces, steps, share_blocks, me_ref, *refs):
+    count = 1 + (shards - 1) * pieces
+    factor_refs = refs[:count]
+    dressed_refs = refs[count : count + shards]
+    trace_refs = refs[count + shards : count + 2 * shards]
+    slope_ref, collision_ref, trace_ref, dressed_ref, held_ref, semaphores = refs[count + 2 * shards :]
     at = pl.program_id(0)
-    blocks = factor_refs[0].shape[0] // block
+    block = held_ref.shape[1]
+    part = block // PARTS
+
+    def copies(step):
+        slot = lax.rem(step, SLOTS)
+        return [
+            pltpu.make_async_copy(
+                held_ref.at[slot, pl.ds(i * part, part), :],
+                slope_ref.at[pl.ds(pl.multiple_of(step * block, block) + i * part, part), :],
+                semaphores.at[slot, i],
+            )
+            for i in range(PARTS)
+        ]
 
     @pl.when(at == 0)
     def _():
@@ -244,18 +239,27 @@
         trace_ref[...] = jnp.concatenate(
             [low, middle, high, jnp.zeros((5, row.shape[1]), jnp.float32)], axis=0
         ).astype(jnp.bfloat16)
-
-    dressed = jnp.concatenate([ref[...] for ref in dressed_refs], axis=0)
+        dressed_ref[...] = jnp.concatenate([ref[...] for ref in dressed_refs], axis=0)
+
+    @pl.when(at >= SLOTS)
+    def _():
+        for copy in copies(at - SLOTS):
+            copy.wait()
+
     first = me_ref[0] * share_blocks
+    slot = lax.rem(at, SLOTS)
     for i in range(pieces):
 
-        @pl.when(at // blocks == i)
+        @pl.when(at // (steps // pieces) == i)
         def _():
-            here = pl.ds(pl.multiple_of((at - i * blocks) * block, block), block)
             basis = jnp.concatenate(
-                [factor_refs[s * pieces + i][here, :] for s in range(shards)], axis=1
+                [factor_refs[0][...]]
+                + [factor_refs[1 + s * pieces + i][...] for s in range(shards - 1)],
+                axis=1,
             )
-            slope_ref[...] = jnp.dot(basis, dressed, preferred_element_type=jnp.float32)
+            held_ref[slot] = jnp.dot(
+                basis, dressed_ref[...], preferred_element_type=jnp.float32
+            )
 
             @pl.when((at >= first) & (at < first + share_blocks))
             def _():
@@ -272,35 +276,56 @@
                 )
                 collision_ref[:, there] = jnp.sum(parts, axis=0, keepdims=True)
 
-
-def slope(steps, dressed, traces):
-    shards, pieces = len(steps), len(steps[0])
-    length, vectors = steps[0][0].shape
+    for copy in copies(at):
+        copy.start()
+
+    @pl.when(at == steps - 1)
+    def _():
+        for back in range(min(SLOTS, steps) - 1, -1, -1):
+            for copy in copies(at - back):
+                copy.wait()
+
+
+def slope(own, steps, dressed, traces):
+    shards, pieces = len(dressed), len(steps[0])
+    rows, vectors = own.shape
     columns = dressed[0].shape[1]
     depth = shards * vectors
-    rows = pieces * length
     share = rows // shards
-    block = min(length, share, 1024)
+    block = min(rows // pieces, share, 1024)
+    blocks = rows // pieces // block
     whole = lambda g, me: (0, 0)
+    factor_specs = [pl.BlockSpec((block, vectors), lambda g, me: (g, 0))] + [
+        pl.BlockSpec(
+            (block, vectors), lambda g, me, i=i: (jnp.clip(g - i * blocks, 0, blocks - 1), 0)
+        )
+        for _ in steps
+        for i in range(pieces)
+    ]
     slopes, collision = pl.pallas_call(
-        functools.partial(slope_body, shards, pieces, block, share // block),
+        functools.partial(slope_body, shards, pieces, rows // block, share // block),
         grid_spec=pltpu.PrefetchScalarGridSpec(
             num_scalar_prefetch=1,
             grid=(rows // block,),
-            in_specs=[IN_VMEM] * (shards * pieces)
+            in_specs=factor_specs
             + [pl.BlockSpec((vectors, columns), whole)] * shards
             + [pl.BlockSpec((shards, vectors), whole)] * shards,
             out_specs=[
-                pl.BlockSpec((block, columns), lambda g, me: (g, 0)),
+                pl.BlockSpec(memory_space=pl.ANY),
                 pl.BlockSpec((1, share), whole),
             ],
-            scratch_shapes=[pltpu.VMEM((8, depth), jnp.bfloat16)],
+            scratch_shapes=[
+                pltpu.VMEM((8, depth), jnp.bfloat16),
+                pltpu.VMEM((depth, columns), jnp.bfloat16),
+                pltpu.VMEM((SLOTS, block, columns), jnp.float32),
+                pltpu.SemaphoreType.DMA((SLOTS, PARTS)),
+            ],
         ),
         out_shape=[
             jax.ShapeDtypeStruct((rows, columns), jnp.float32),
             jax.ShapeDtypeStruct((1, share), jnp.float32),
         ],
-        compiler_params=pltpu.CompilerParams(vmem_limit_bytes=16 * MIB),
+        compiler_params=pltpu.CompilerParams(vmem_limit_bytes=24 * MIB),
         cost_estimate=pl.CostEstimate(
             flops=2 * rows * depth * columns,
             bytes_accessed=rows * depth * 2 + rows * columns * 4,
@@ -308,8 +333,11 @@
         ),
     )(
         lax.axis_index("aux").astype(jnp.int32)[None],
-        *[in_vmem(piece) for step in steps for piece in step],
-        *dressed,
+        in_hbm(own),
+        *[in_hbm(piece) for step in steps[:-1] for piece in step],
+        *[in_vmem(piece) for piece in steps[-1]],
+        *[in_hbm(both) for both in dressed[:-1]],
+        in_vmem(dressed[-1]),
         *traces,
     )
     return slopes, collision.reshape(share)
@@ -328,31 +356,41 @@
     trace_weights = lax.dynamic_slice_in_dim(
         green_one, me * orb_count, orb_count, 1
     ).T.reshape(1, columns)
-    steps, dressed, traced = [], [], []
-    for step in range(aux_size):
-        total = jnp.zeros((vectors, columns), jnp.float32)
-        pieces = []
+    weights = screening[:, None]
+    zeros = jnp.zeros((vectors, columns), jnp.float32)
+
+    dressed, traced = [], []
+
+    def finish(step, total):
+        both, trace = sum_and_dress(step, total, weights, green_one, trace_weights)
+        dressed.append(both)
+        traced.append(trace)
+
+    held = [
+        lax.slice_in_dim(cholesky_factors, i * length, (i + 1) * length, axis=0)
+        for i in range(PIECES)
+    ]
+    finish(0, project(cholesky_factors, green, 0, zeros))
+    steps = []
+    for step in range(1, aux_size):
+        total, pieces = zeros, []
         for i in range(PIECES):
+            after = (dressed[-1], traced[-1]) if i == 0 else (total,)
+            place = in_hbm if step < aux_size - 1 else in_vmem
+            piece = gate(shifted(held[i], "aux", 1), place, *after)
+            pieces.append(piece)
             first = i * length
-            if step == 0:
-                piece = lax.slice_in_dim(cholesky_factors, first, first + length, axis=0)
-            elif i == 0:
-                piece = gate(shifted(steps[-1][i], "aux", 1), dressed[-1], traced[-1])
-            else:
-                piece = gate(shifted(steps[-1][i], "aux", 1), total)
-            pieces.append(piece)
             if step < aux_size - 1:
                 total = project(piece, green, first, total)
             else:
                 total = total + project_plain(piece, green[first : first + length])
+        held = pieces
         steps.append(pieces)
-        both, trace = sum_and_dress(step, total, screening, green_one, trace_weights)
-        dressed.append(both)
-        traced.append(trace)
+        finish(step, total)
 
     trace = jnp.concatenate(traced, axis=0)
     traces = [trace] + [shifted(trace, "aux", shift) for shift in range(1, aux_size)]
-    return slope(steps, dressed, traces)
+    return slope(cholesky_factors, steps, dressed, traces)
 
 
 def solution(mesh):

time: 185 us -> 180 us (0.973)
  waiting for transfers between devices: 116 us -> 111 us
  Pallas kernels: 28.1 us -> 30.9 us
  other arithmetic: 2.13 us -> 0.11 us
    ppermute x9, waiting for transfers between devices: 78 us -> 71.8 us  [shifted(): lax.ppermute(block, axis, [(i, (i + shift) % count) for i in range(count)])]
    pallas_call x7 -> x17, Pallas kernels: 13.1 us -> 15.6 us  [the longest x1 13.2 us: slope(): pl.pallas_call(functools.partial(slope_body, shards, pieces, rows // bloc...]
    ppermute x17 -> x16, waiting for transfers between devices: 37.7 us -> 39.1 us  [exchanged(): return lax.ppermute(block, axis, [(i, i ^ bit) for i in range(count)])]
    ppermute x17 -> x16, starting transfers between devices: 14.5 us -> 14 us  [exchanged(): return lax.ppermute(block, axis, [(i, i ^ bit) for i in range(count)])]
    pallas_call x6 -> x5, Pallas kernels: 11.6 us -> 11.9 us  [project(): pl.pallas_call(functools.partial(project_body, first, min(length, 1024)),...]
    unnamed x35 -> x23, local copies, waits for them, and re-layouts: 9.79 us -> 9.69 us
  transfers between devices with their start and end apart: 26 -> 25, of which waited for: 25 -> 25; matrix products, arithmetic and copies ran while one was open for 1% -> 1% of each run, Pallas kernels for 9% -> 10%
where the time goes in v5:
time: 180 us
  waiting for transfers between devices  111 us (62%)
  Pallas kernels  30.9 us (17%)
  starting transfers between devices  22.2 us (12%)
  local copies, waits for them, and re-layouts  13.2 us (7%)
    ppermute x9, waiting for transfers between devices, shifted(): lax.ppermute(block, axis, [(i, (i + shift) % count) for i in range(count)])  71.8 us
    ppermute x16, waiting for transfers between devices, exchanged(): return lax.ppermute(block, axis, [(i, i ^ bit) for i in range(count)])  39.1 us
    ppermute x16, starting transfers between devices, exchanged(): return lax.ppermute(block, axis, [(i, i ^ bit) for i in range(count)])  14 us
    pallas_call x1, Pallas kernels, slope(): pl.pallas_call(functools.partial(slope_body, shards, pieces, rows // bloc...  13.2 us
    pallas_call x5, Pallas kernels, project(): pl.pallas_call(functools.partial(project_body, first, min(length, 1024)),...  11.9 us
    unnamed x23, local copies, waits for them, and re-layouts  9.69 us
    ppermute x9, starting transfers between devices, shifted(): lax.ppermute(block, axis, [(i, (i + shift) % count) for i in range(count)])  8.19 us
  transfers between devices with their start and end apart: 25, of which 25 were waited for; matrix products, arithmetic and copies ran while one was open for 1% of the time, Pallas kernels for 10%

profile of v5, /device:TPU:0, one launch (start us, length us, event | category | flops | bytes accessed | tf_op | source)
XLA Modules:
  0.0 179.7 jit_solution(7940280300031252955)
XLA Ops:
  0.6 3.1 %fusion.7 = (bf16[4096,128]{1,0:T(8,128)(2,1)}, bf16[4096,128]{1,0:T(8,128)(2,1)}) fusion(bf16[8192,128]{1,0:T(8,128)(2,1)} %refs_0_.3), kind=kLoop, calls=%fused_computation.15 | loop fusion | bytes 4194304 | tf_op jit(solution)/shard_map/slice | solution.py:370
  3.8 3.0 %collective-permute-start = (bf16[4096,128]{1,0:T(8,128)(2,1)}, bf16[4096,128]{1,0:T(8,128)(2,1)}, u32[]{:S(2)}, u32[]{:S(2)}) collective-permute-start(bf16[4096,128]{1,0:T(8,128)(2,1)} %get-tuple-element.27), channel_id=1, source_target_pairs={{0,1},{1,2},{2,3},{3,0},{4,5},{5,6},{6,7},{7,4},{8,9},{9,10},{10,1... | collective-permute-start | bytes 3145736 | tf_op jit(solution)/shard_map/ppermute | solution.py:31
  6.8 1.6 collective-permute-start.5
  8.4 3.4 %shard_map.59 = (bf16[8192,512]{1,0:T(8,128)(2,1)S(1)}, f32[256,256]{1,0:T(8,128)S(1)}) custom-call(bf16[8192,512]{1,0:T(8,128)(2,1)} %refs_0_.2, f32[256,256]{1,0:T(8,128)} %refs_1_.1), custom_call_target="tpu_custom_call" | custom-call | tf_op jit(solution)/shard_map/pallas_call | solution.py:68
  11.8 2.8 %shard_map.60 = f32[128,512]{1,0:T(8,128)S(1)} custom-call(bf16[8192,128]{1,0:T(8,128)(2,1)S(1)} %copy-done.2, bf16[8192,512]{1,0:T(8,128)(2,1)S(1)} %get-tuple-element.14.green_ref, f32[128,512]{1,0:T(8,128)S(1)} %broadcast_in_dim.10.acc_ref), custom_call_target="tpu_custom_call" | custom-call | tf_op jit(solution)/shard_map/pallas_call | solution.py:96
  14.6 3.4 %copy-done = bf16[8192,512]{1,0:T(8,128)(2,1)} copy-done((bf16[8192,512]{1,0:T(8,128)(2,1)}, bf16[8192,512]{1,0:T(8,128)(2,1)S(1)}, u32[]{:S(2)}) %copy-start) | copy-done | bytes 8388632
  18.1 1.3 collective-permute-done.1.right_ref
  19.5 1.6 collective-permute-start.2
  21.0 4.1 %collective-permute-done.2.right_ref = f32[64,512]{1,0:T(8,128)S(1)} collective-permute-done((f32[64,512]{1,0:T(8,128)S(1)}, f32[64,512]{1,0:T(8,128)S(1)}, u32[]{:S(2)}, u32[]{:S(2)}) %collective-permute-start.2) | collective-permute-done | bytes 131104 | tf_op jit(solution)/shard_map/ppermute | solution.py:36
  25.1 1.6 collective-permute-start.3
  26.8 3.3 %collective-permute-done.3.other_ref = f32[64,512]{1,0:T(8,128)S(1)} collective-permute-done((f32[64,512]{1,0:T(8,128)S(1)}, f32[64,512]{1,0:T(8,128)S(1)}, u32[]{:S(2)}, u32[]{:S(2)}) %collective-permute-start.3) | collective-permute-done | bytes 131104 | tf_op jit(solution)/shard_map/ppermute | solution.py:36
  30.8 1.0 collective-permute-done.4.other_ref
  32.0 1.1 collective-permute-done.refs_0_
  33.7 3.4 %copy-done.1 = bf16[8192,512]{1,0:T(8,128)(2,1)S(1)} copy-done((bf16[8192,512]{1,0:T(8,128)(2,1)S(1)}, bf16[8192,512]{1,0:T(8,128)(2,1)}, u32[]{:S(2)}) %copy-start.1) | copy-done | bytes 8388632
  37.1 2.6 %shard_map.66.refs_1_.acc_ref = f32[128,512]{1,0:T(8,128)S(1)} custom-call(bf16[4096,128]{1,0:T(8,128)(2,1)} %shard_map.65.piece_ref.refs_1_, bf16[8192,512]{1,0:T(8,128)(2,1)S(1)} %copy-done.1, f32[128,512]{1,0:T(8,128)S(1)} %broadcast_in_dim.10.acc_ref), custom_call_target="tpu_custom_call" | custom-call | tf_op jit(solution)/shard_map/pallas_call | solution.py:96
  39.6 15.9 %collective-permute-done.5.refs_0_ = bf16[4096,128]{1,0:T(8,128)(2,1)} collective-permute-done((bf16[4096,128]{1,0:T(8,128)(2,1)}, bf16[4096,128]{1,0:T(8,128)(2,1)}, u32[]{:S(2)}, u32[]{:S(2)}) %collective-permute-start.5) | collective-permute-done | bytes 1048608 | tf_op jit(solution)/shard_map/ppermute | solution.py:31
  55.6 2.7 %shard_map.68 = f32[128,512]{1,0:T(8,128)S(1)} custom-call(bf16[4096,128]{1,0:T(8,128)(2,1)} %shard_map.67.piece_ref.refs_2_, bf16[8192,512]{1,0:T(8,128)(2,1)S(1)} %copy-done.1, f32[128,512]{1,0:T(8,128)S(1)} %shard_map.66.refs_1_.acc_ref), custom_call_target="tpu_custom_call" | custom-call | tf_op jit(solution)/shard_map/pallas_call | solution.py:96
  58.5 1.3 collective-permute-done.7.right_ref
  59.9 1.8 collective-permute-start.8
  61.6 3.8 %collective-permute-done.8.right_ref = f32[64,512]{1,0:T(8,128)S(1)} collective-permute-done((f32[64,512]{1,0:T(8,128)S(1)}, f32[64,512]{1,0:T(8,128)S(1)}, u32[]{:S(2)}, u32[]{:S(2)}) %collective-permute-start.8) | collective-permute-done | bytes 131104 | tf_op jit(solution)/shard_map/ppermute | solution.py:36
  65.5 1.8 %collective-permute-start.9 = (f32[64,512]{1,0:T(8,128)S(1)}, f32[64,512]{1,0:T(8,128)S(1)}, u32[]{:S(2)}, u32[]{:S(2)}) collective-permute-start(f32[64,512]{1,0:T(8,128)S(1)} %shard_map.70.mine_ref), channel_id=1, source_target_pairs={{0,16},{4,20},{8,24},{12,28},{16,0},{20,4},{24,8},{28,12},{1,17},{... | collective-permute-start | bytes 393224 | tf_op jit(solution)/shard_map/ppermute | solution.py:36
  67.3 3.2 %collective-permute-done.9.other_ref = f32[64,512]{1,0:T(8,128)S(1)} collective-permute-done((f32[64,512]{1,0:T(8,128)S(1)}, f32[64,512]{1,0:T(8,128)S(1)}, u32[]{:S(2)}, u32[]{:S(2)}) %collective-permute-start.9) | collective-permute-done | bytes 131104 | tf_op jit(solution)/shard_map/ppermute | solution.py:36
  71.0 1.2 collective-permute-done.10.other_ref
  72.4 5.5 %collective-permute-done.6.refs_0_ = bf16[4096,128]{1,0:T(8,128)(2,1)S(1)} collective-permute-done((bf16[4096,128]{1,0:T(8,128)(2,1)}, bf16[4096,128]{1,0:T(8,128)(2,1)S(1)}, u32[]{:S(2)}, u32[]{:S(2)}) %collective-permute-start.6) | collective-permute-done | bytes 1048608 | tf_op jit(solution)/shard_map/ppermute | solution.py:31
  78.0 1.0 copy-done.3
  79.6 1.3 copy-done.4
  80.9 1.3 shard_map.74.refs_1_.acc_ref
  82.2 18.3 %collective-permute-done.11.refs_0_ = bf16[4096,128]{1,0:T(8,128)(2,1)} collective-permute-done((bf16[4096,128]{1,0:T(8,128)(2,1)}, bf16[4096,128]{1,0:T(8,128)(2,1)}, u32[]{:S(2)}, u32[]{:S(2)}) %collective-permute-start.11) | collective-permute-done | bytes 1048608 | tf_op jit(solution)/shard_map/ppermute | solution.py:31
  100.5 2.5 %shard_map.76 = f32[128,512]{1,0:T(8,128)S(1)} custom-call(bf16[4096,128]{1,0:T(8,128)(2,1)} %shard_map.75.piece_ref.refs_4_, bf16[8192,512]{1,0:T(8,128)(2,1)S(1)} %bitcast.11, f32[128,512]{1,0:T(8,128)S(1)} %shard_map.74.refs_1_.acc_ref), custom_call_target="tpu_custom_call" | custom-call | tf_op jit(solution)/shard_map/pallas_call | solution.py:96
  103.3 1.3 collective-permute-done.13.right_ref
  104.6 1.8 collective-permute-start.14
  106.4 3.8 %collective-permute-done.14.right_ref = f32[64,512]{1,0:T(8,128)S(1)} collective-permute-done((f32[64,512]{1,0:T(8,128)S(1)}, f32[64,512]{1,0:T(8,128)S(1)}, u32[]{:S(2)}, u32[]{:S(2)}) %collective-permute-start.14) | collective-permute-done | bytes 131104 | tf_op jit(solution)/shard_map/ppermute | solution.py:36
  110.3 1.8 %collective-permute-start.15 = (f32[64,512]{1,0:T(8,128)S(1)}, f32[64,512]{1,0:T(8,128)S(1)}, u32[]{:S(2)}, u32[]{:S(2)}) collective-permute-start(f32[64,512]{1,0:T(8,128)S(1)} %shard_map.78.mine_ref), channel_id=1, source_target_pairs={{0,16},{4,20},{8,24},{12,28},{16,0},{20,4},{24,8},{28,12},{1,17},{... | collective-permute-start | bytes 393224 | tf_op jit(solution)/shard_map/ppermute | solution.py:36
  112.1 3.2 %collective-permute-done.15.other_ref = f32[64,512]{1,0:T(8,128)S(1)} collective-permute-done((f32[64,512]{1,0:T(8,128)S(1)}, f32[64,512]{1,0:T(8,128)S(1)}, u32[]{:S(2)}, u32[]{:S(2)}) %collective-permute-start.15) | collective-permute-done | bytes 131104 | tf_op jit(solution)/shard_map/ppermute | solution.py:36
  115.8 1.2 collective-permute-done.16.other_ref
  117.2 5.7 %collective-permute-done.12.refs_0_ = bf16[4096,128]{1,0:T(8,128)(2,1)S(1)} collective-permute-done((bf16[4096,128]{1,0:T(8,128)(2,1)}, bf16[4096,128]{1,0:T(8,128)(2,1)S(1)}, u32[]{:S(2)}, u32[]{:S(2)}) %collective-permute-start.12) | collective-permute-done | bytes 1048608 | tf_op jit(solution)/shard_map/ppermute | solution.py:31
  123.6 20.9 %collective-permute-done.17.refs_0_ = bf16[4096,128]{1,0:T(8,128)(2,1)S(1)} collective-permute-done((bf16[4096,128]{1,0:T(8,128)(2,1)}, bf16[4096,128]{1,0:T(8,128)(2,1)S(1)}, u32[]{:S(2)}, u32[]{:S(2)}) %collective-permute-start.17) | collective-permute-done | bytes 1048608 | tf_op jit(solution)/shard_map/ppermute | solution.py:31
  145.4 1.3 collective-permute-done.18.right_ref
  146.8 1.6 collective-permute-start.19
  148.3 4.1 %collective-permute-done.19.right_ref = f32[64,512]{1,0:T(8,128)S(1)} collective-permute-done((f32[64,512]{1,0:T(8,128)S(1)}, f32[64,512]{1,0:T(8,128)S(1)}, u32[]{:S(2)}, u32[]{:S(2)}) %collective-permute-start.19) | collective-permute-done | bytes 131104 | tf_op jit(solution)/shard_map/ppermute | solution.py:36
  152.4 1.6 collective-permute-start.20
  154.0 3.4 %collective-permute-done.20.other_ref = f32[64,512]{1,0:T(8,128)S(1)} collective-permute-done((f32[64,512]{1,0:T(8,128)S(1)}, f32[64,512]{1,0:T(8,128)S(1)}, u32[]{:S(2)}, u32[]{:S(2)}) %collective-permute-start.20) | collective-permute-done | bytes 131104 | tf_op jit(solution)/shard_map/ppermute | solution.py:36
  157.9 1.2 collective-permute-done.21.other_ref
  159.4 1.8 collective-permute-start.24
  161.2 1.0 collective-permute-start.22
  163.0 2.6 %collective-permute-done.23.refs_13_ = f32[4,128]{1,0:T(4,128)S(1)} collective-permute-done((f32[4,128]{1,0:T(4,128)S(1)}, f32[4,128]{1,0:T(4,128)S(1)}, u32[]{:S(2)}, u32[]{:S(2)}) %collective-permute-start.23) | collective-permute-done | bytes 2080 | tf_op jit(solution)/shard_map/ppermute | solution.py:31
  165.6 0.9 collective-permute-done.22.refs_12_
  166.5 13.2 %shard_map.87 = (f32[8192,512]{1,0:T(8,128)}, f32[1,2048]{1,0:T(1,128)}) custom-call(s32[1]{0:T(128)} %bitcast.me_ref, bf16[8192,128]{1,0:T(8,128)(2,1)} %refs_0_.3, bf16[4096,128]{1,0:T(8,128)(2,1)} %shard_map.65.piece_ref.refs_1_, bf16[4096,128]{1,0:T(8,128)(2,1)} %shard_map.67.piece_ref.refs_2_, bf16[4096,128]{1,0:T(8,128)(2,1)} %shard_map.73.piece_ref.refs_3_, ...), custom_call_target="tpu_custom_call" | custom-call | flops 4294967296 | bytes 25165824 | tf_op jit(solution)/shard_map/pallas_call | solution.py:305
  (67 shorter events, 7.2 us)
Async XLA Ops:
  0.6 11.2 %copy-start.2 = (bf16[8192,128]{1,0:T(8,128)(2,1)S(1)}, bf16[8192,128]{1,0:T(8,128)(2,1)}, u32[]{:S(2)}) copy-start(bf16[8192,128]{1,0:T(8,128)(2,1)} %refs_0_.3) | copy-start | bytes 6291460
  3.8 29.3 %collective-permute-start = (bf16[4096,128]{1,0:T(8,128)(2,1)}, bf16[4096,128]{1,0:T(8,128)(2,1)}, u32[]{:S(2)}, u32[]{:S(2)}) collective-permute-start(bf16[4096,128]{1,0:T(8,128)(2,1)} %get-tuple-element.27), channel_id=1, source_target_pairs={{0,1},{1,2},{2,3},{3,0},{4,5},{5,6},{6,7},{7,4},{8,9},{9,10},{10,1... | collective-permute-start | bytes 3145736 | tf_op jit(solution)/shard_map/ppermute | solution.py:31
  6.8 48.8 %collective-permute-start.5 = (bf16[4096,128]{1,0:T(8,128)(2,1)}, bf16[4096,128]{1,0:T(8,128)(2,1)}, u32[]{:S(2)}, u32[]{:S(2)}) collective-permute-start(bf16[4096,128]{1,0:T(8,128)(2,1)} %get-tuple-element.26), channel_id=1, source_target_pairs={{0,1},{1,2},{2,3},{3,0},{4,5},{5,6},{6,7},{7,4},{8,9},{9,10},{10,1... | collective-permute-start | bytes 3145736 | tf_op jit(solution)/shard_map/ppermute | solution.py:31
  11.8 14.9 %copy-start.8 = (f32[512]{0:T(512)S(1)}, f32[512]{0:T(512)}, u32[]{:S(2)}) copy-start(f32[512]{0:T(512)} %param.7) | copy-start | bytes 6148
  14.6 3.4 %copy-start = (bf16[8192,512]{1,0:T(8,128)(2,1)}, bf16[8192,512]{1,0:T(8,128)(2,1)S(1)}, u32[]{:S(2)}) copy-start(bf16[8192,512]{1,0:T(8,128)(2,1)S(1)} %get-tuple-element.14.green_ref) | copy-start | bytes 25165828
  18.0 1.4 collective-permute-start.1
  19.5 5.6 %collective-permute-start.2 = (f32[64,512]{1,0:T(8,128)S(1)}, f32[64,512]{1,0:T(8,128)S(1)}, u32[]{:S(2)}, u32[]{:S(2)}) collective-permute-start(f32[64,512]{1,0:T(8,128)S(1)} %shard_map.61.left_ref), channel_id=1, source_target_pairs={{0,8},{4,12},{8,0},{12,4},{16,24},{20,28},{24,16},{28,20},{1,9},{5... | collective-permute-start | bytes 393224 | tf_op jit(solution)/shard_map/ppermute | solution.py:36
  25.1 5.0 %collective-permute-start.3 = (f32[64,512]{1,0:T(8,128)S(1)}, f32[64,512]{1,0:T(8,128)S(1)}, u32[]{:S(2)}, u32[]{:S(2)}) collective-permute-start(f32[64,512]{1,0:T(8,128)S(1)} %shard_map.62.mine_ref), channel_id=1, source_target_pairs={{0,16},{4,20},{8,24},{12,28},{16,0},{20,4},{24,8},{28,12},{1,17},{... | collective-permute-start | bytes 393224 | tf_op jit(solution)/shard_map/ppermute | solution.py:36
  30.6 1.3 collective-permute-start.4
  32.0 26.3 %copy-start.5 = (bf16[128,512]{1,0:T(8,128)(2,1)}, bf16[128,512]{1,0:T(8,128)(2,1)S(1)}, u32[]{:S(2)}) copy-start(bf16[128,512]{1,0:T(8,128)(2,1)S(1)} %get-tuple-element.16.refs_1_.refs_7_) | copy-start | bytes 393220
  33.1 44.8 %collective-permute-start.6 = (bf16[4096,128]{1,0:T(8,128)(2,1)}, bf16[4096,128]{1,0:T(8,128)(2,1)S(1)}, u32[]{:S(2)}, u32[]{:S(2)}) collective-permute-start(bf16[4096,128]{1,0:T(8,128)(2,1)} %shard_map.65.piece_ref.refs_1_), channel_id=1, source_target_pairs={{0,1},{1,2},{2,3},{3,0},{4,5},{5,6},{6,7},{7,4},{8,9},{9,10},{10,1... | collective-permute-start | bytes 3145736 | tf_op jit(solution)/shard_map/ppermute | solution.py:31
  33.7 3.4 %copy-start.1 = (bf16[8192,512]{1,0:T(8,128)(2,1)S(1)}, bf16[8192,512]{1,0:T(8,128)(2,1)}, u32[]{:S(2)}) copy-start(bf16[8192,512]{1,0:T(8,128)(2,1)} %copy-done) | copy-start | bytes 25165828
  39.6 40.0 %slice-start = ((s8[8388608]{0:T(1024)(128)(4,1)}), s8[4194304]{0:T(1024)(128)(4,1)S(1)}, s32[]{:S(2)}) async-start(s8[8388608]{0:T(1024)(128)(4,1)} %bitcast.10), calls=%async_computation | async-start | bytes 8388608
  55.6 24.0 %slice-start.1 = ((s8[8388608]{0:T(1024)(128)(4,1)}), s8[4194304]{0:T(1024)(128)(4,1)S(1)}, s32[]{:S(2)}) async-start(s8[8388608]{0:T(1024)(128)(4,1)} %bitcast.10), calls=%async_computation.1 | async-start | bytes 8388608
  58.3 42.2 %collective-permute-start.11 = (bf16[4096,128]{1,0:T(8,128)(2,1)}, bf16[4096,128]{1,0:T(8,128)(2,1)}, u32[]{:S(2)}, u32[]{:S(2)}) collective-permute-start(bf16[4096,128]{1,0:T(8,128)(2,1)} %shard_map.67.piece_ref.refs_2_), channel_id=1, source_target_pairs={{0,1},{1,2},{2,3},{3,0},{4,5},{5,6},{6,7},{7,4},{8,9},{9,10},{10,1... | collective-permute-start | bytes 3145736 | tf_op jit(solution)/shard_map/ppermute | solution.py:31
  58.4 1.4 collective-permute-start.7
  59.9 5.6 %collective-permute-start.8 = (f32[64,512]{1,0:T(8,128)S(1)}, f32[64,512]{1,0:T(8,128)S(1)}, u32[]{:S(2)}, u32[]{:S(2)}) collective-permute-start(f32[64,512]{1,0:T(8,128)S(1)} %shard_map.69.left_ref), channel_id=1, source_target_pairs={{0,8},{4,12},{8,0},{12,4},{16,24},{20,28},{24,16},{28,20},{1,9},{5... | collective-permute-start | bytes 393224 | tf_op jit(solution)/shard_map/ppermute | solution.py:36
  65.5 5.0 %collective-permute-start.9 = (f32[64,512]{1,0:T(8,128)S(1)}, f32[64,512]{1,0:T(8,128)S(1)}, u32[]{:S(2)}, u32[]{:S(2)}) collective-permute-start(f32[64,512]{1,0:T(8,128)S(1)} %shard_map.70.mine_ref), channel_id=1, source_target_pairs={{0,16},{4,20},{8,24},{12,28},{16,0},{20,4},{24,8},{28,12},{1,17},{... | collective-permute-start | bytes 393224 | tf_op jit(solution)/shard_map/ppermute | solution.py:36
  70.9 1.3 collective-permute-start.10
  78.0 1.0 copy-start.3
  78.9 0.7 copy-start.6
  79.6 43.3 %collective-permute-start.12 = (bf16[4096,128]{1,0:T(8,128)(2,1)}, bf16[4096,128]{1,0:T(8,128)(2,1)S(1)}, u32[]{:S(2)}, u32[]{:S(2)}) collective-permute-start(bf16[4096,128]{1,0:T(8,128)(2,1)} %shard_map.73.piece_ref.refs_3_), channel_id=1, source_target_pairs={{0,1},{1,2},{2,3},{3,0},{4,5},{5,6},{6,7},{7,4},{8,9},{9,10},{10,1... | collective-permute-start | bytes 3145736 | tf_op jit(solution)/shard_map/ppermute | solution.py:31
  79.6 1.3 copy-start.4
  103.1 41.4 %collective-permute-start.17 = (bf16[4096,128]{1,0:T(8,128)(2,1)}, bf16[4096,128]{1,0:T(8,128)(2,1)S(1)}, u32[]{:S(2)}, u32[]{:S(2)}) collective-permute-start(bf16[4096,128]{1,0:T(8,128)(2,1)} %shard_map.75.piece_ref.refs_4_), channel_id=1, source_target_pairs={{0,1},{1,2},{2,3},{3,0},{4,5},{5,6},{6,7},{7,4},{8,9},{9,10},{10,1... | collective-permute-start | bytes 3145736 | tf_op jit(solution)/shard_map/ppermute | solution.py:31
  103.2 1.4 collective-permute-start.13
  104.6 5.6 %collective-permute-start.14 = (f32[64,512]{1,0:T(8,128)S(1)}, f32[64,512]{1,0:T(8,128)S(1)}, u32[]{:S(2)}, u32[]{:S(2)}) collective-permute-start(f32[64,512]{1,0:T(8,128)S(1)} %shard_map.77.left_ref), channel_id=1, source_target_pairs={{0,8},{4,12},{8,0},{12,4},{16,24},{20,28},{24,16},{28,20},{1,9},{5... | collective-permute-start | bytes 393224 | tf_op jit(solution)/shard_map/ppermute | solution.py:36
  110.3 5.0 %collective-permute-start.15 = (f32[64,512]{1,0:T(8,128)S(1)}, f32[64,512]{1,0:T(8,128)S(1)}, u32[]{:S(2)}, u32[]{:S(2)}) collective-permute-start(f32[64,512]{1,0:T(8,128)S(1)} %shard_map.78.mine_ref), channel_id=1, source_target_pairs={{0,16},{4,20},{8,24},{12,28},{16,0},{20,4},{24,8},{28,12},{1,17},{... | collective-permute-start | bytes 393224 | tf_op jit(solution)/shard_map/ppermute | solution.py:36
  115.7 1.3 collective-permute-start.16
  117.2 29.6 %copy-start.7 = (bf16[128,512]{1,0:T(8,128)(2,1)}, bf16[128,512]{1,0:T(8,128)(2,1)S(1)}, u32[]{:S(2)}) copy-start(bf16[128,512]{1,0:T(8,128)(2,1)S(1)} %get-tuple-element.20.refs_1_.refs_9_) | copy-start | bytes 393220
  145.3 1.4 collective-permute-start.18
  146.8 5.6 %collective-permute-start.19 = (f32[64,512]{1,0:T(8,128)S(1)}, f32[64,512]{1,0:T(8,128)S(1)}, u32[]{:S(2)}, u32[]{:S(2)}) collective-permute-start(f32[64,512]{1,0:T(8,128)S(1)} %shard_map.83.left_ref), channel_id=1, source_target_pairs={{0,8},{4,12},{8,0},{12,4},{16,24},{20,28},{24,16},{28,20},{1,9},{5... | collective-permute-start | bytes 393224 | tf_op jit(solution)/shard_map/ppermute | solution.py:36
  152.4 5.0 %collective-permute-start.20 = (f32[64,512]{1,0:T(8,128)S(1)}, f32[64,512]{1,0:T(8,128)S(1)}, u32[]{:S(2)}, u32[]{:S(2)}) collective-permute-start(f32[64,512]{1,0:T(8,128)S(1)} %shard_map.84.mine_ref), channel_id=1, source_target_pairs={{0,16},{4,20},{8,24},{12,28},{16,0},{20,4},{24,8},{28,12},{1,17},{... | collective-permute-start | bytes 393224 | tf_op jit(solution)/shard_map/ppermute | solution.py:36
  157.8 1.3 collective-permute-start.21
  159.4 3.6 %collective-permute-start.24 = (f32[4,128]{1,0:T(4,128)S(1)}, f32[4,128]{1,0:T(4,128)S(1)}, u32[]{:S(2)}, u32[]{:S(2)}) collective-permute-start(f32[4,128]{1,0:T(4,128)S(1)} %pad_maximum_fusion.refs_11_), channel_id=1, source_target_pairs={{0,3},{1,0},{2,1},{3,2},{4,7},{5,4},{6,5},{7,6},{8,11},{9,8},{10,9... | collective-permute-start | bytes 6152 | tf_op jit(solution)/shard_map/ppermute | solution.py:31
  161.2 4.5 %collective-permute-start.23 = (f32[4,128]{1,0:T(4,128)S(1)}, f32[4,128]{1,0:T(4,128)S(1)}, u32[]{:S(2)}, u32[]{:S(2)}) collective-permute-start(f32[4,128]{1,0:T(4,128)S(1)} %pad_maximum_fusion.refs_11_), channel_id=1, source_target_pairs={{0,2},{1,3},{2,0},{3,1},{4,6},{5,7},{6,4},{7,5},{8,10},{9,11},{10,... | collective-permute-start | bytes 6152 | tf_op jit(solution)/shard_map/ppermute | solution.py:31
  161.2 5.4 %collective-permute-start.22 = (f32[4,128]{1,0:T(4,128)S(1)}, f32[4,128]{1,0:T(4,128)S(1)}, u32[]{:S(2)}, u32[]{:S(2)}) collective-permute-start(f32[4,128]{1,0:T(4,128)S(1)} %pad_maximum_fusion.refs_11_), channel_id=1, source_target_pairs={{0,1},{1,2},{2,3},{3,0},{4,5},{5,6},{6,7},{7,4},{8,9},{9,10},{10,1... | collective-permute-start | bytes 6152 | tf_op jit(solution)/shard_map/ppermute | solution.py:31

commit v6 on v5

--- a/solution.py
+++ b/solution.py
@@ -76,6 +76,26 @@
     )(*[in_hbm(array) for array in arrays])
 
 
+def cut_body(first, array_ref, piece_ref, semaphore):
+    move = pltpu.make_async_copy(
+        array_ref.at[pl.ds(first, piece_ref.shape[0]), :], piece_ref, semaphore
+    )
+    move.start()
+    move.wait()
+
+
+def cut(array, first, length):
+    return pl.pallas_call(
+        functools.partial(cut_body, first),
+        out_shape=vmem_shape((length,) + array.shape[1:], array.dtype),
+        in_specs=[pl.BlockSpec(memory_space=pltpu.HBM)],
+        out_specs=IN_VMEM,
+        scratch_shapes=[pltpu.SemaphoreType.DMA],
+        compiler_params=pltpu.CompilerParams(vmem_limit_bytes=2 * MIB),
+        cost_estimate=FREE,
+    )(in_hbm(array))
+
+
 def project_body(first, block, piece_ref, green_ref, acc_ref, total_ref):
     total_ref[...] = acc_ref[...]
 
@@ -109,27 +129,34 @@
     )
 
 
-def add_body(left_ref, right_ref, sum_ref):
-    sum_ref[...] = left_ref[...] + right_ref[...]
-
-
-def add(left, right):
+def add_up(arrays):
+    while len(arrays) > 1:
+        arrays = [arrays[i] + arrays[i + 1] for i in range(0, len(arrays), 2)]
+    return arrays[0]
+
+
+def add_body(*refs):
+    refs[-1][...] = add_up([ref[...] for ref in refs[:-1]])
+
+
+def add(*arrays):
     return pl.pallas_call(
         add_body,
-        out_shape=jax.ShapeDtypeStruct(left.shape, left.dtype),
+        out_shape=jax.ShapeDtypeStruct(arrays[0].shape, arrays[0].dtype),
         compiler_params=pltpu.CompilerParams(vmem_limit_bytes=4 * MIB),
         cost_estimate=FREE,
-    )(in_vmem(left), in_vmem(right))
-
-
-def dress_body(step, mine_ref, other_ref, weights_ref, green_ref, dressed_ref):
-    half = mine_ref.shape[0]
+    )(*[in_vmem(array) for array in arrays])
+
+
+def dress_body(step, *refs):
+    summand_refs, (weights_ref, green_ref, dressed_ref) = refs[:-3], refs[-3:]
+    half = dressed_ref.shape[0]
     norb = green_ref.shape[0]
     aux_size = lax.axis_size("aux")
     owner = lax.rem(lax.axis_index("aux") - step + aux_size, aux_size)
     upper = lax.rem(lax.axis_index("rows"), 2)
     weights = weights_ref[pl.ds((owner * 2 + upper) * half, half), :]
-    total = mine_ref[...] + other_ref[...]
+    total = add_up([ref[...] for ref in summand_refs])
     green = green_ref[...]
     for first in range(0, total.shape[1], norb):
         mixed = jnp.dot(
@@ -141,13 +168,13 @@
         dressed_ref[:, first : first + norb] = (mixed * weights).astype(jnp.bfloat16)
 
 
-def dress(step, mine, other, weights, green_one):
+def dress(step, summands, weights, green_one):
     return pl.pallas_call(
         functools.partial(dress_body, step),
-        out_shape=jax.ShapeDtypeStruct(mine.shape, jnp.bfloat16),
+        out_shape=jax.ShapeDtypeStruct(summands[0].shape, jnp.bfloat16),
         compiler_params=pltpu.CompilerParams(vmem_limit_bytes=6 * MIB),
         cost_estimate=FREE,
-    )(in_vmem(mine), in_vmem(other), weights, in_vmem(green_one))
+    )(*[in_vmem(summand) for summand in summands], weights, in_vmem(green_one))
 
 
 def join_body(mine_ref, other_ref, trace_ref, dressed_ref, traced_ref):
@@ -188,102 +215,106 @@
     half = projection.shape[0] // 2
     upper = lax.rem(lax.axis_index("rows"), 2) == 1
     low, high = projection[:half], projection[half:]
-    total = jnp.where(upper, high, low)
-    other = exchanged(jnp.where(upper, low, high), "rows", 1)
-    bit = 2
-    while bit < count:
-        total = add(total, other)
-        other = exchanged(total, "rows", bit)
-        bit *= 2
-    mine = dress(step, total, other, weights, green_one)
+    summands = [
+        jnp.where(upper, high, low),
+        exchanged(jnp.where(upper, low, high), "rows", 1),
+    ]
+    bits = [1 << b for b in range(1, count.bit_length() - 1)]
+    while bits:
+        total = add(*summands)
+        partners = [bits[0]] if len(bits) == 1 else [bits[0], bits[1], bits[0] ^ bits[1]]
+        summands = [total] + [exchanged(total, "rows", partner) for partner in partners]
+        bits = bits[2:]
+    mine = dress(step, summands, weights, green_one)
     return join(mine, exchanged(mine, "rows", 1), trace_weights)
 
 
 SLOTS = 3
-PARTS = 4
-
-
-def slope_body(shards, pieces, steps, share_blocks, me_ref, *refs):
-    count = 1 + (shards - 1) * pieces
-    factor_refs = refs[:count]
-    dressed_refs = refs[count : count + shards]
-    trace_refs = refs[count + shards : count + 2 * shards]
-    slope_ref, collision_ref, trace_ref, dressed_ref, held_ref, semaphores = refs[count + 2 * shards :]
-    at = pl.program_id(0)
+PARTS = 2
+
+
+def slope_body(pieces, me_ref, *refs):
+    slope_ref, collision_ref, factors_ref, dressed_ref, held_ref, came, gone = refs[-7:]
+    shards = factors_ref.shape[0] + 1
+    early = 1 + (shards - 2) * pieces
+    early_refs, last_refs = refs[:early], refs[early : early + pieces]
+    dressed_refs = refs[early + pieces : early + pieces + shards]
+    trace_refs = refs[early + pieces + shards : early + pieces + 2 * shards]
+    rows = factors_ref.shape[1]
     block = held_ref.shape[1]
+    steps, length = rows // block, rows // pieces
+    share_blocks = rows // shards // block
     part = block // PARTS
 
-    def copies(step):
-        slot = lax.rem(step, SLOTS)
+    def arrivals(at):
+        first = at * block
+        sources = [early_refs[0].at[pl.ds(first, block), :]] + [
+            early_refs[1 + s * pieces + first // length].at[pl.ds(first % length, block), :]
+            for s in range(shards - 2)
+        ]
         return [
             pltpu.make_async_copy(
-                held_ref.at[slot, pl.ds(i * part, part), :],
-                slope_ref.at[pl.ds(pl.multiple_of(step * block, block) + i * part, part), :],
-                semaphores.at[slot, i],
+                source, factors_ref.at[s, pl.ds(first, block), :], came.at[at, s]
+            )
+            for s, source in enumerate(sources)
+        ]
+
+    def departures(at):
+        return [
+            pltpu.make_async_copy(
+                held_ref.at[at % SLOTS, pl.ds(i * part, part), :],
+                slope_ref.at[pl.ds(at * block + i * part, part), :],
+                gone.at[at % SLOTS, i],
             )
             for i in range(PARTS)
         ]
 
-    @pl.when(at == 0)
-    def _():
-        trace = trace_refs[0][...]
-        for shift in range(1, shards):
-            came = trace_refs[shift][...]
-            trace = trace + jnp.concatenate(
-                [came[shards - shift :], came[: shards - shift]], axis=0
+    for at in range(steps):
+        for copy in arrivals(at):
+            copy.start()
+
+    trace = trace_refs[0][...]
+    for shift in range(1, shards):
+        other = trace_refs[shift][...]
+        trace = trace + jnp.concatenate([other[shards - shift :], other[: shards - shift]], axis=0)
+    row = jnp.concatenate([trace[s : s + 1] for s in range(shards)], axis=1)
+    high = row.astype(jnp.bfloat16).astype(jnp.float32)
+    middle = (row - high).astype(jnp.bfloat16).astype(jnp.float32)
+    low = row - high - middle
+    thirds = jnp.concatenate(
+        [low, middle, high, jnp.zeros((5, row.shape[1]), jnp.float32)], axis=0
+    ).astype(jnp.bfloat16)
+    dressed_ref[...] = jnp.concatenate([ref[...] for ref in dressed_refs], axis=0)
+
+    for at in range(steps):
+        for copy in arrivals(at):
+            copy.wait()
+        if at >= SLOTS:
+            for copy in departures(at - SLOTS):
+                copy.wait()
+        first = at * block
+        basis = jnp.concatenate(
+            [factors_ref[s, pl.ds(first, block), :] for s in range(shards - 1)]
+            + [last_refs[first // length][pl.ds(first % length, block), :]],
+            axis=1,
+        )
+        held_ref[at % SLOTS] = jnp.dot(
+            basis, dressed_ref[...], preferred_element_type=jnp.float32
+        )
+        for copy in departures(at):
+            copy.start()
+
+        @pl.when(me_ref[0] == at // share_blocks)
+        def _():
+            parts = lax.dot_general(
+                thirds, basis, (((1,), (1,)), ((), ())), preferred_element_type=jnp.float32
             )
-        row = jnp.concatenate([trace[s : s + 1] for s in range(shards)], axis=1)
-        high = row.astype(jnp.bfloat16).astype(jnp.float32)
-        middle = (row - high).astype(jnp.bfloat16).astype(jnp.float32)
-        low = row - high - middle
-        trace_ref[...] = jnp.concatenate(
-            [low, middle, high, jnp.zeros((5, row.shape[1]), jnp.float32)], axis=0
-        ).astype(jnp.bfloat16)
-        dressed_ref[...] = jnp.concatenate([ref[...] for ref in dressed_refs], axis=0)
-
-    @pl.when(at >= SLOTS)
-    def _():
-        for copy in copies(at - SLOTS):
+            there = pl.ds(at % share_blocks * block, block)
+            collision_ref[:, there] = jnp.sum(parts, axis=0, keepdims=True)
+
+    for at in range(max(steps - SLOTS, 0), steps):
+        for copy in departures(at):
             copy.wait()
-
-    first = me_ref[0] * share_blocks
-    slot = lax.rem(at, SLOTS)
-    for i in range(pieces):
-
-        @pl.when(at // (steps // pieces) == i)
-        def _():
-            basis = jnp.concatenate(
-                [factor_refs[0][...]]
-                + [factor_refs[1 + s * pieces + i][...] for s in range(shards - 1)],
-                axis=1,
-            )
-            held_ref[slot] = jnp.dot(
-                basis, dressed_ref[...], preferred_element_type=jnp.float32
-            )
-
-            @pl.when((at >= first) & (at < first + share_blocks))
-            def _():
-                parts = lax.dot_general(
-                    trace_ref[...],
-                    basis,
-                    (((1,), (1,)), ((), ())),
-                    preferred_element_type=jnp.float32,
-                )
-                there = (
-                    slice(None)
-                    if share_blocks == 1
-                    else pl.ds(pl.multiple_of((at - first) * block, block), block)
-                )
-                collision_ref[:, there] = jnp.sum(parts, axis=0, keepdims=True)
-
-    for copy in copies(at):
-        copy.start()
-
-    @pl.when(at == steps - 1)
-    def _():
-        for back in range(min(SLOTS, steps) - 1, -1, -1):
-            for copy in copies(at - back):
-                copy.wait()
 
 
 def slope(own, steps, dressed, traces):
@@ -293,39 +324,27 @@
     depth = shards * vectors
     share = rows // shards
     block = min(rows // pieces, share, 1024)
-    blocks = rows // pieces // block
-    whole = lambda g, me: (0, 0)
-    factor_specs = [pl.BlockSpec((block, vectors), lambda g, me: (g, 0))] + [
-        pl.BlockSpec(
-            (block, vectors), lambda g, me, i=i: (jnp.clip(g - i * blocks, 0, blocks - 1), 0)
-        )
-        for _ in steps
-        for i in range(pieces)
-    ]
+    far = pl.BlockSpec(memory_space=pltpu.HBM)
+    early = [own] + [piece for step in steps[:-1] for piece in step]
+    near = [*steps[-1], *dressed, *traces]
     slopes, collision = pl.pallas_call(
-        functools.partial(slope_body, shards, pieces, rows // block, share // block),
-        grid_spec=pltpu.PrefetchScalarGridSpec(
-            num_scalar_prefetch=1,
-            grid=(rows // block,),
-            in_specs=factor_specs
-            + [pl.BlockSpec((vectors, columns), whole)] * shards
-            + [pl.BlockSpec((shards, vectors), whole)] * shards,
-            out_specs=[
-                pl.BlockSpec(memory_space=pl.ANY),
-                pl.BlockSpec((1, share), whole),
-            ],
-            scratch_shapes=[
-                pltpu.VMEM((8, depth), jnp.bfloat16),
-                pltpu.VMEM((depth, columns), jnp.bfloat16),
-                pltpu.VMEM((SLOTS, block, columns), jnp.float32),
-                pltpu.SemaphoreType.DMA((SLOTS, PARTS)),
-            ],
-        ),
+        functools.partial(slope_body, pieces),
+        in_specs=[pl.BlockSpec(memory_space=pltpu.SMEM)]
+        + [far] * len(early)
+        + [IN_VMEM] * len(near),
+        out_specs=[far, IN_VMEM],
+        scratch_shapes=[
+            pltpu.VMEM((shards - 1, rows, vectors), jnp.bfloat16),
+            pltpu.VMEM((depth, columns), jnp.bfloat16),
+            pltpu.VMEM((SLOTS, block, columns), jnp.float32),
+            pltpu.SemaphoreType.DMA((rows // block, shards - 1)),
+            pltpu.SemaphoreType.DMA((SLOTS, PARTS)),
+        ],
         out_shape=[
             jax.ShapeDtypeStruct((rows, columns), jnp.float32),
             jax.ShapeDtypeStruct((1, share), jnp.float32),
         ],
-        compiler_params=pltpu.CompilerParams(vmem_limit_bytes=24 * MIB),
+        compiler_params=pltpu.CompilerParams(vmem_limit_bytes=28 * MIB),
         cost_estimate=pl.CostEstimate(
             flops=2 * rows * depth * columns,
             bytes_accessed=rows * depth * 2 + rows * columns * 4,
@@ -333,11 +352,9 @@
         ),
     )(
         lax.axis_index("aux").astype(jnp.int32)[None],
-        in_hbm(own),
-        *[in_hbm(piece) for step in steps[:-1] for piece in step],
+        *[in_hbm(piece) for piece in early],
         *[in_vmem(piece) for piece in steps[-1]],
-        *[in_hbm(both) for both in dressed[:-1]],
-        in_vmem(dressed[-1]),
+        *[in_vmem(both) for both in dressed],
         *traces,
     )
     return slopes, collision.reshape(share)
@@ -366,10 +383,7 @@
         dressed.append(both)
         traced.append(trace)
 
-    held = [
-        lax.slice_in_dim(cholesky_factors, i * length, (i + 1) * length, axis=0)
-        for i in range(PIECES)
-    ]
+    held = [cut(cholesky_factors, i * length, length) for i in range(PIECES)]
     finish(0, project(cholesky_factors, green, 0, zeros))
     steps = []
     for step in range(1, aux_size):

time: 180 us -> 175 us (0.972)
  waiting for transfers between devices: 111 us -> 105 us
  starting transfers between devices: 22.2 us -> 24 us
    ppermute x16 -> x20, waiting for transfers between devices: 39.1 us -> 33.7 us  [exchanged(): return lax.ppermute(block, axis, [(i, i ^ bit) for i in range(count)])]
    slice x1 -> x0, local copies, waits for them, and re-layouts: 3.13 us -> none  [local(): lax.slice_in_dim(cholesky_factors, i * length, (i + 1) * length, axis=0)]
    unnamed x23 -> x21, local copies, waits for them, and re-layouts: 9.69 us -> 11.3 us
    pallas_call x9 -> x7, Pallas kernels: 13.3 us -> 14.3 us  [the longest x1 9.66 us: slope(): pl.pallas_call(functools.partial(slope_body, pieces), in_specs=[pl.BlockS...]
    ppermute x16 -> x20, starting transfers between devices: 14 us -> 14.8 us  [exchanged(): return lax.ppermute(block, axis, [(i, i ^ bit) for i in range(count)])]
  transfers between devices with their start and end apart: 25 -> 29, of which waited for: 25 -> 29; matrix products, arithmetic and copies ran while one was open for 1% -> 1% of each run, Pallas kernels for 10% -> 10%
where the time goes in v6:
time: 175 us; the launch traced here: 174 us
  waiting for transfers between devices  105 us (60%)
  Pallas kernels  30.9 us (18%)
  starting transfers between devices  24 us (14%)
  local copies, waits for them, and re-layouts  11.6 us (7%)
    ppermute x9, waiting for transfers between devices, shifted(): lax.ppermute(block, axis, [(i, (i + shift) % count) for i in range(count)])  71.6 us
    ppermute x20, waiting for transfers between devices, exchanged(): return lax.ppermute(block, axis, [(i, i ^ bit) for i in range(count)])  33.7 us
    ppermute x20, starting transfers between devices, exchanged(): return lax.ppermute(block, axis, [(i, i ^ bit) for i in range(count)])  14.8 us
    unnamed x21, local copies, waits for them, and re-layouts  11.3 us
    pallas_call x5, Pallas kernels, project(): pl.pallas_call(functools.partial(project_body, first, min(length, 1024)),...  10.8 us
    pallas_call x1, Pallas kernels, slope(): pl.pallas_call(functools.partial(slope_body, pieces), in_specs=[pl.BlockS...  9.66 us
    ppermute x9, starting transfers between devices, shifted(): lax.ppermute(block, axis, [(i, (i + shift) % count) for i in range(count)])  9.17 us
    pallas_call x2, Pallas kernels, cut(): pl.pallas_call(functools.partial(cut_body, first), out_shape=vmem_shape((...  4.56 us
  transfers between devices with their start and end apart: 29, of which 29 were waited for; matrix products, arithmetic and copies ran while one was open for 1% of the time, Pallas kernels for 10%

profile of v6, /device:TPU:0, one launch (start us, length us, event | category | flops | bytes accessed | tf_op | source)
XLA Modules:
  0.0 174.3 jit_solution(3806357045782097563)
XLA Ops:
  0.6 2.4 %shard_map.59 = bf16[4096,128]{1,0:T(8,128)(2,1)} custom-call(bf16[8192,128]{1,0:T(8,128)(2,1)} %refs_0_.3), custom_call_target="tpu_custom_call" | custom-call | tf_op jit(solution)/shard_map/pallas_call | solution.py:88
  3.0 3.1 %collective-permute-start = (bf16[4096,128]{1,0:T(8,128)(2,1)}, bf16[4096,128]{1,0:T(8,128)(2,1)}, u32[]{:S(2)}, u32[]{:S(2)}) collective-permute-start(bf16[4096,128]{1,0:T(8,128)(2,1)} %shard_map.59), channel_id=1, source_target_pairs={{0,1},{1,2},{2,3},{3,0},{4,5},{5,6},{6,7},{7,4},{8,9},{9,10},{10,1... | collective-permute-start | bytes 3145736 | tf_op jit(solution)/shard_map/ppermute | solution.py:31
  6.1 2.2 %shard_map.66 = bf16[4096,128]{1,0:T(8,128)(2,1)} custom-call(bf16[8192,128]{1,0:T(8,128)(2,1)} %refs_0_.3), custom_call_target="tpu_custom_call" | custom-call | tf_op jit(solution)/shard_map/pallas_call | solution.py:88
  8.3 1.6 collective-permute-start.6
  9.9 3.4 %shard_map.60 = (bf16[8192,512]{1,0:T(8,128)(2,1)S(1)}, f32[256,256]{1,0:T(8,128)S(1)}) custom-call(bf16[8192,512]{1,0:T(8,128)(2,1)} %refs_0_.2, f32[256,256]{1,0:T(8,128)} %refs_1_.1), custom_call_target="tpu_custom_call" | custom-call | tf_op jit(solution)/shard_map/pallas_call | solution.py:68
  13.4 2.8 %shard_map.61 = f32[128,512]{1,0:T(8,128)S(1)} custom-call(bf16[8192,128]{1,0:T(8,128)(2,1)S(1)} %copy-done.2, bf16[8192,512]{1,0:T(8,128)(2,1)S(1)} %get-tuple-element.14.green_ref, f32[128,512]{1,0:T(8,128)S(1)} %broadcast_in_dim.10.acc_ref), custom_call_target="tpu_custom_call" | custom-call | tf_op jit(solution)/shard_map/pallas_call | solution.py:116
  16.2 3.4 %copy-done = bf16[8192,512]{1,0:T(8,128)(2,1)} copy-done((bf16[8192,512]{1,0:T(8,128)(2,1)}, bf16[8192,512]{1,0:T(8,128)(2,1)S(1)}, u32[]{:S(2)}) %copy-start) | copy-done | bytes 8388632
  19.7 1.3 collective-permute-done.1.refs_1_
  21.0 2.5 %collective-permute-start.4 = (f32[64,512]{1,0:T(8,128)S(1)}, f32[64,512]{1,0:T(8,128)S(1)}, u32[]{:S(2)}, u32[]{:S(2)}) collective-permute-start(f32[64,512]{1,0:T(8,128)S(1)} %shard_map.62.refs_0_), channel_id=1, source_target_pairs={{0,24},{4,28},{8,16},{12,20},{16,8},{20,12},{24,0},{28,4},{1,25},{... | collective-permute-start | bytes 393224 | tf_op jit(solution)/shard_map/ppermute | solution.py:36
  24.7 3.1 %collective-permute-done.4.refs_3_ = f32[64,512]{1,0:T(8,128)S(1)} collective-permute-done((f32[64,512]{1,0:T(8,128)S(1)}, f32[64,512]{1,0:T(8,128)S(1)}, u32[]{:S(2)}, u32[]{:S(2)}) %collective-permute-start.4) | collective-permute-done | bytes 131104 | tf_op jit(solution)/shard_map/ppermute | solution.py:36
  27.8 2.5 %collective-permute-done.3.refs_2_ = f32[64,512]{1,0:T(8,128)S(1)} collective-permute-done((f32[64,512]{1,0:T(8,128)S(1)}, f32[64,512]{1,0:T(8,128)S(1)}, u32[]{:S(2)}, u32[]{:S(2)}) %collective-permute-start.3) | collective-permute-done | bytes 131104 | tf_op jit(solution)/shard_map/ppermute | solution.py:36
  31.1 1.0 collective-permute-done.5.other_ref
  32.4 1.6 collective-permute-start.7
  34.0 3.4 %copy-done.1 = bf16[8192,512]{1,0:T(8,128)(2,1)S(1)} copy-done((bf16[8192,512]{1,0:T(8,128)(2,1)S(1)}, bf16[8192,512]{1,0:T(8,128)(2,1)}, u32[]{:S(2)}) %copy-start.1) | copy-done | bytes 8388632
  37.4 2.6 %shard_map.67.refs_1_.acc_ref = f32[128,512]{1,0:T(8,128)S(1)} custom-call(bf16[4096,128]{1,0:T(8,128)(2,1)} %shard_map.65.piece_ref.refs_1_, bf16[8192,512]{1,0:T(8,128)(2,1)S(1)} %copy-done.1, f32[128,512]{1,0:T(8,128)S(1)} %broadcast_in_dim.10.acc_ref), custom_call_target="tpu_custom_call" | custom-call | tf_op jit(solution)/shard_map/pallas_call | solution.py:116
  40.0 14.9 %collective-permute-done.6.refs_0_ = bf16[4096,128]{1,0:T(8,128)(2,1)} collective-permute-done((bf16[4096,128]{1,0:T(8,128)(2,1)}, bf16[4096,128]{1,0:T(8,128)(2,1)}, u32[]{:S(2)}, u32[]{:S(2)}) %collective-permute-start.6) | collective-permute-done | bytes 1048608 | tf_op jit(solution)/shard_map/ppermute | solution.py:31
  54.9 2.8 %shard_map.69 = f32[128,512]{1,0:T(8,128)S(1)} custom-call(bf16[4096,128]{1,0:T(8,128)(2,1)} %shard_map.68.piece_ref.refs_2_, bf16[8192,512]{1,0:T(8,128)(2,1)S(1)} %copy-done.1, f32[128,512]{1,0:T(8,128)S(1)} %shard_map.67.refs_1_.acc_ref), custom_call_target="tpu_custom_call" | custom-call | tf_op jit(solution)/shard_map/pallas_call | solution.py:116
  57.8 1.3 collective-permute-done.8.refs_1_
  59.2 2.7 %collective-permute-start.11 = (f32[64,512]{1,0:T(8,128)S(1)}, f32[64,512]{1,0:T(8,128)S(1)}, u32[]{:S(2)}, u32[]{:S(2)}) collective-permute-start(f32[64,512]{1,0:T(8,128)S(1)} %shard_map.70.refs_0_), channel_id=1, source_target_pairs={{0,24},{4,28},{8,16},{12,20},{16,8},{20,12},{24,0},{28,4},{1,25},{... | collective-permute-start | bytes 393224 | tf_op jit(solution)/shard_map/ppermute | solution.py:36
  62.7 3.1 %collective-permute-done.11.refs_3_ = f32[64,512]{1,0:T(8,128)S(1)} collective-permute-done((f32[64,512]{1,0:T(8,128)S(1)}, f32[64,512]{1,0:T(8,128)S(1)}, u32[]{:S(2)}, u32[]{:S(2)}) %collective-permute-start.11) | collective-permute-done | bytes 131104 | tf_op jit(solution)/shard_map/ppermute | solution.py:36
  65.8 2.7 %collective-permute-done.10.refs_2_ = f32[64,512]{1,0:T(8,128)S(1)} collective-permute-done((f32[64,512]{1,0:T(8,128)S(1)}, f32[64,512]{1,0:T(8,128)S(1)}, u32[]{:S(2)}, u32[]{:S(2)}) %collective-permute-start.10) | collective-permute-done | bytes 131104 | tf_op jit(solution)/shard_map/ppermute | solution.py:36
  69.3 1.2 collective-permute-done.12.other_ref
  70.7 6.6 %collective-permute-done.7.refs_0_ = bf16[4096,128]{1,0:T(8,128)(2,1)S(1)} collective-permute-done((bf16[4096,128]{1,0:T(8,128)(2,1)}, bf16[4096,128]{1,0:T(8,128)(2,1)S(1)}, u32[]{:S(2)}, u32[]{:S(2)}) %collective-permute-start.7) | collective-permute-done | bytes 1048608 | tf_op jit(solution)/shard_map/ppermute | solution.py:31
  77.3 1.0 copy-done.3
  78.3 1.3 copy-done.4
  79.5 1.3 shard_map.74.refs_1_.acc_ref
  80.8 18.9 %collective-permute-done.13.refs_0_ = bf16[4096,128]{1,0:T(8,128)(2,1)S(1)} collective-permute-done((bf16[4096,128]{1,0:T(8,128)(2,1)}, bf16[4096,128]{1,0:T(8,128)(2,1)S(1)}, u32[]{:S(2)}, u32[]{:S(2)}) %collective-permute-start.13) | collective-permute-done | bytes 1048608 | tf_op jit(solution)/shard_map/ppermute | solution.py:31
  99.7 1.0 copy-done.5
  100.7 1.3 copy-done.6
  102.0 1.3 shard_map.76
  103.4 1.3 collective-permute-done.15.refs_1_
  104.8 2.7 %collective-permute-start.18 = (f32[64,512]{1,0:T(8,128)S(1)}, f32[64,512]{1,0:T(8,128)S(1)}, u32[]{:S(2)}, u32[]{:S(2)}) collective-permute-start(f32[64,512]{1,0:T(8,128)S(1)} %shard_map.77.refs_0_), channel_id=1, source_target_pairs={{0,24},{4,28},{8,16},{12,20},{16,8},{20,12},{24,0},{28,4},{1,25},{... | collective-permute-start | bytes 393224 | tf_op jit(solution)/shard_map/ppermute | solution.py:36
  108.4 3.1 %collective-permute-done.18.refs_3_ = f32[64,512]{1,0:T(8,128)S(1)} collective-permute-done((f32[64,512]{1,0:T(8,128)S(1)}, f32[64,512]{1,0:T(8,128)S(1)}, u32[]{:S(2)}, u32[]{:S(2)}) %collective-permute-start.18) | collective-permute-done | bytes 131104 | tf_op jit(solution)/shard_map/ppermute | solution.py:36
  111.4 2.7 %collective-permute-done.17.refs_2_ = f32[64,512]{1,0:T(8,128)S(1)} collective-permute-done((f32[64,512]{1,0:T(8,128)S(1)}, f32[64,512]{1,0:T(8,128)S(1)}, u32[]{:S(2)}, u32[]{:S(2)}) %collective-permute-start.17) | collective-permute-done | bytes 131104 | tf_op jit(solution)/shard_map/ppermute | solution.py:36
  114.9 1.2 collective-permute-done.19.other_ref
  116.3 5.9 %collective-permute-done.14.refs_0_ = bf16[4096,128]{1,0:T(8,128)(2,1)S(1)} collective-permute-done((bf16[4096,128]{1,0:T(8,128)(2,1)}, bf16[4096,128]{1,0:T(8,128)(2,1)S(1)}, u32[]{:S(2)}, u32[]{:S(2)}) %collective-permute-start.14) | collective-permute-done | bytes 1048608 | tf_op jit(solution)/shard_map/ppermute | solution.py:31
  122.9 20.9 %collective-permute-done.20.refs_0_ = bf16[4096,128]{1,0:T(8,128)(2,1)S(1)} collective-permute-done((bf16[4096,128]{1,0:T(8,128)(2,1)}, bf16[4096,128]{1,0:T(8,128)(2,1)S(1)}, u32[]{:S(2)}, u32[]{:S(2)}) %collective-permute-start.20) | collective-permute-done | bytes 1048608 | tf_op jit(solution)/shard_map/ppermute | solution.py:31
  144.7 1.3 collective-permute-done.21.refs_1_
  146.1 2.5 %collective-permute-start.24 = (f32[64,512]{1,0:T(8,128)S(1)}, f32[64,512]{1,0:T(8,128)S(1)}, u32[]{:S(2)}, u32[]{:S(2)}) collective-permute-start(f32[64,512]{1,0:T(8,128)S(1)} %shard_map.82.refs_0_), channel_id=1, source_target_pairs={{0,24},{4,28},{8,16},{12,20},{16,8},{20,12},{24,0},{28,4},{1,25},{... | collective-permute-start | bytes 393224 | tf_op jit(solution)/shard_map/ppermute | solution.py:36
  149.7 3.2 %collective-permute-done.24.refs_3_ = f32[64,512]{1,0:T(8,128)S(1)} collective-permute-done((f32[64,512]{1,0:T(8,128)S(1)}, f32[64,512]{1,0:T(8,128)S(1)}, u32[]{:S(2)}, u32[]{:S(2)}) %collective-permute-start.24) | collective-permute-done | bytes 131104 | tf_op jit(solution)/shard_map/ppermute | solution.py:36
  152.9 2.5 %collective-permute-done.23.refs_2_ = f32[64,512]{1,0:T(8,128)S(1)} collective-permute-done((f32[64,512]{1,0:T(8,128)S(1)}, f32[64,512]{1,0:T(8,128)S(1)}, u32[]{:S(2)}, u32[]{:S(2)}) %collective-permute-start.23) | collective-permute-done | bytes 131104 | tf_op jit(solution)/shard_map/ppermute | solution.py:36
  156.0 1.2 collective-permute-done.25.other_ref
  157.4 1.8 %collective-permute-start.28 = (f32[4,128]{1,0:T(4,128)S(1)}, f32[4,128]{1,0:T(4,128)S(1)}, u32[]{:S(2)}, u32[]{:S(2)}) collective-permute-start(f32[4,128]{1,0:T(4,128)S(1)} %pad_maximum_fusion.refs_11_), channel_id=1, source_target_pairs={{0,3},{1,0},{2,1},{3,2},{4,7},{5,4},{6,5},{7,6},{8,11},{9,8},{10,9... | collective-permute-start | bytes 6152 | tf_op jit(solution)/shard_map/ppermute | solution.py:31
  159.2 1.0 collective-permute-start.26
  160.3 0.8 collective-permute-done.28.refs_14_
  161.1 2.6 %collective-permute-done.27.refs_13_ = f32[4,128]{1,0:T(4,128)S(1)} collective-permute-done((f32[4,128]{1,0:T(4,128)S(1)}, f32[4,128]{1,0:T(4,128)S(1)}, u32[]{:S(2)}, u32[]{:S(2)}) %collective-permute-start.27) | collective-permute-done | bytes 2080 | tf_op jit(solution)/shard_map/ppermute | solution.py:31
  163.7 0.9 collective-permute-done.26.refs_12_
  164.6 9.7 %shard_map.85 = (f32[8192,512]{1,0:T(8,128)}, f32[1,2048]{1,0:T(1,128)}) custom-call(s32[1]{0:T(128)} %bitcast.me_ref, bf16[8192,128]{1,0:T(8,128)(2,1)} %refs_0_.3, bf16[4096,128]{1,0:T(8,128)(2,1)} %shard_map.65.piece_ref.refs_1_, bf16[4096,128]{1,0:T(8,128)(2,1)} %shard_map.68.piece_ref.refs_2_, bf16[4096,128]{1,0:T(8,128)(2,1)} %shard_map.73.piece_ref.refs_3_, ...), custom_call_target="tpu_custom_call" | custom-call | flops 4294967296 | bytes 25165824 | tf_op jit(solution)/shard_map/pallas_call | solution.py:330
  (70 shorter events, 9.7 us)
Async XLA Ops:
  0.6 12.7 %copy-start.2 = (bf16[8192,128]{1,0:T(8,128)(2,1)S(1)}, bf16[8192,128]{1,0:T(8,128)(2,1)}, u32[]{:S(2)}) copy-start(bf16[8192,128]{1,0:T(8,128)(2,1)} %refs_0_.3) | copy-start | bytes 6291460
  3.0 29.4 %collective-permute-start = (bf16[4096,128]{1,0:T(8,128)(2,1)}, bf16[4096,128]{1,0:T(8,128)(2,1)}, u32[]{:S(2)}, u32[]{:S(2)}) collective-permute-start(bf16[4096,128]{1,0:T(8,128)(2,1)} %shard_map.59), channel_id=1, source_target_pairs={{0,1},{1,2},{2,3},{3,0},{4,5},{5,6},{6,7},{7,4},{8,9},{9,10},{10,1... | collective-permute-start | bytes 3145736 | tf_op jit(solution)/shard_map/ppermute | solution.py:31
  8.3 46.6 %collective-permute-start.6 = (bf16[4096,128]{1,0:T(8,128)(2,1)}, bf16[4096,128]{1,0:T(8,128)(2,1)}, u32[]{:S(2)}, u32[]{:S(2)}) collective-permute-start(bf16[4096,128]{1,0:T(8,128)(2,1)} %shard_map.66), channel_id=1, source_target_pairs={{0,1},{1,2},{2,3},{3,0},{4,5},{5,6},{6,7},{7,4},{8,9},{9,10},{10,1... | collective-permute-start | bytes 3145736 | tf_op jit(solution)/shard_map/ppermute | solution.py:31
  9.9 14.7 %copy-start.7 = (f32[512]{0:T(512)S(1)}, f32[512]{0:T(512)}, u32[]{:S(2)}) copy-start(f32[512]{0:T(512)} %param.7) | copy-start | bytes 6148
  16.2 3.4 %copy-start = (bf16[8192,512]{1,0:T(8,128)(2,1)}, bf16[8192,512]{1,0:T(8,128)(2,1)S(1)}, u32[]{:S(2)}) copy-start(bf16[8192,512]{1,0:T(8,128)(2,1)S(1)} %get-tuple-element.14.green_ref) | copy-start | bytes 25165828
  19.6 1.4 collective-permute-start.1
  21.0 6.8 %collective-permute-start.4 = (f32[64,512]{1,0:T(8,128)S(1)}, f32[64,512]{1,0:T(8,128)S(1)}, u32[]{:S(2)}, u32[]{:S(2)}) collective-permute-start(f32[64,512]{1,0:T(8,128)S(1)} %shard_map.62.refs_0_), channel_id=1, source_target_pairs={{0,24},{4,28},{8,16},{12,20},{16,8},{20,12},{24,0},{28,4},{1,25},{... | collective-permute-start | bytes 393224 | tf_op jit(solution)/shard_map/ppermute | solution.py:36
  23.5 6.8 %collective-permute-start.3 = (f32[64,512]{1,0:T(8,128)S(1)}, f32[64,512]{1,0:T(8,128)S(1)}, u32[]{:S(2)}, u32[]{:S(2)}) collective-permute-start(f32[64,512]{1,0:T(8,128)S(1)} %shard_map.62.refs_0_), channel_id=1, source_target_pairs={{0,16},{4,20},{8,24},{12,28},{16,0},{20,4},{24,8},{28,12},{1,17},{... | collective-permute-start | bytes 393224 | tf_op jit(solution)/shard_map/ppermute | solution.py:36
  24.0 6.4 %collective-permute-start.2 = (f32[64,512]{1,0:T(8,128)S(1)}, f32[64,512]{1,0:T(8,128)S(1)}, u32[]{:S(2)}, u32[]{:S(2)}) collective-permute-start(f32[64,512]{1,0:T(8,128)S(1)} %shard_map.62.refs_0_), channel_id=1, source_target_pairs={{0,8},{4,12},{8,0},{12,4},{16,24},{20,28},{24,16},{28,20},{1,9},{5... | collective-permute-start | bytes 393224 | tf_op jit(solution)/shard_map/ppermute | solution.py:36
  30.8 1.3 collective-permute-start.5
  32.4 44.8 %collective-permute-start.7 = (bf16[4096,128]{1,0:T(8,128)(2,1)}, bf16[4096,128]{1,0:T(8,128)(2,1)S(1)}, u32[]{:S(2)}, u32[]{:S(2)}) collective-permute-start(bf16[4096,128]{1,0:T(8,128)(2,1)} %shard_map.65.piece_ref.refs_1_), channel_id=1, source_target_pairs={{0,1},{1,2},{2,3},{3,0},{4,5},{5,6},{6,7},{7,4},{8,9},{9,10},{10,1... | collective-permute-start | bytes 3145736 | tf_op jit(solution)/shard_map/ppermute | solution.py:31
  34.0 3.4 %copy-start.1 = (bf16[8192,512]{1,0:T(8,128)(2,1)S(1)}, bf16[8192,512]{1,0:T(8,128)(2,1)}, u32[]{:S(2)}) copy-start(bf16[8192,512]{1,0:T(8,128)(2,1)} %copy-done) | copy-start | bytes 25165828
  40.0 38.3 %slice-start = ((s8[8388608]{0:T(1024)(128)(4,1)}), s8[4194304]{0:T(1024)(128)(4,1)S(1)}, s32[]{:S(2)}) async-start(s8[8388608]{0:T(1024)(128)(4,1)} %bitcast.10), calls=%async_computation | async-start | bytes 8388608
  54.9 23.4 %slice-start.1 = ((s8[8388608]{0:T(1024)(128)(4,1)}), s8[4194304]{0:T(1024)(128)(4,1)S(1)}, s32[]{:S(2)}) async-start(s8[8388608]{0:T(1024)(128)(4,1)} %bitcast.10), calls=%async_computation.1 | async-start | bytes 8388608
  54.9 44.8 %collective-permute-start.13 = (bf16[4096,128]{1,0:T(8,128)(2,1)}, bf16[4096,128]{1,0:T(8,128)(2,1)S(1)}, u32[]{:S(2)}, u32[]{:S(2)}) collective-permute-start(bf16[4096,128]{1,0:T(8,128)(2,1)} %shard_map.68.piece_ref.refs_2_), channel_id=1, source_target_pairs={{0,1},{1,2},{2,3},{3,0},{4,5},{5,6},{6,7},{7,4},{8,9},{9,10},{10,1... | collective-permute-start | bytes 3145736 | tf_op jit(solution)/shard_map/ppermute | solution.py:31
  57.7 1.4 collective-permute-start.8
  59.2 6.6 %collective-permute-start.11 = (f32[64,512]{1,0:T(8,128)S(1)}, f32[64,512]{1,0:T(8,128)S(1)}, u32[]{:S(2)}, u32[]{:S(2)}) collective-permute-start(f32[64,512]{1,0:T(8,128)S(1)} %shard_map.70.refs_0_), channel_id=1, source_target_pairs={{0,24},{4,28},{8,16},{12,20},{16,8},{20,12},{24,0},{28,4},{1,25},{... | collective-permute-start | bytes 393224 | tf_op jit(solution)/shard_map/ppermute | solution.py:36
  61.9 6.6 %collective-permute-start.10 = (f32[64,512]{1,0:T(8,128)S(1)}, f32[64,512]{1,0:T(8,128)S(1)}, u32[]{:S(2)}, u32[]{:S(2)}) collective-permute-start(f32[64,512]{1,0:T(8,128)S(1)} %shard_map.70.refs_0_), channel_id=1, source_target_pairs={{0,16},{4,20},{8,24},{12,28},{16,0},{20,4},{24,8},{28,12},{1,17},{... | collective-permute-start | bytes 393224 | tf_op jit(solution)/shard_map/ppermute | solution.py:36
  62.4 6.4 %collective-permute-start.9 = (f32[64,512]{1,0:T(8,128)S(1)}, f32[64,512]{1,0:T(8,128)S(1)}, u32[]{:S(2)}, u32[]{:S(2)}) collective-permute-start(f32[64,512]{1,0:T(8,128)S(1)} %shard_map.70.refs_0_), channel_id=1, source_target_pairs={{0,8},{4,12},{8,0},{12,4},{16,24},{20,28},{24,16},{28,20},{1,9},{5... | collective-permute-start | bytes 393224 | tf_op jit(solution)/shard_map/ppermute | solution.py:36
  69.2 1.3 collective-permute-start.12
  77.3 1.0 copy-start.3
  78.2 44.0 %collective-permute-start.14 = (bf16[4096,128]{1,0:T(8,128)(2,1)}, bf16[4096,128]{1,0:T(8,128)(2,1)S(1)}, u32[]{:S(2)}, u32[]{:S(2)}) collective-permute-start(bf16[4096,128]{1,0:T(8,128)(2,1)} %shard_map.73.piece_ref.refs_3_), channel_id=1, source_target_pairs={{0,1},{1,2},{2,3},{3,0},{4,5},{5,6},{6,7},{7,4},{8,9},{9,10},{10,1... | collective-permute-start | bytes 3145736 | tf_op jit(solution)/shard_map/ppermute | solution.py:31
  78.3 1.3 copy-start.4
  99.7 1.0 copy-start.5
  100.7 43.1 %collective-permute-start.20 = (bf16[4096,128]{1,0:T(8,128)(2,1)}, bf16[4096,128]{1,0:T(8,128)(2,1)S(1)}, u32[]{:S(2)}, u32[]{:S(2)}) collective-permute-start(bf16[4096,128]{1,0:T(8,128)(2,1)} %shard_map.75.piece_ref.refs_4_), channel_id=1, source_target_pairs={{0,1},{1,2},{2,3},{3,0},{4,5},{5,6},{6,7},{7,4},{8,9},{9,10},{10,1... | collective-permute-start | bytes 3145736 | tf_op jit(solution)/shard_map/ppermute | solution.py:31
  100.7 1.3 copy-start.6
  103.4 1.4 collective-permute-start.15
  104.8 6.6 %collective-permute-start.18 = (f32[64,512]{1,0:T(8,128)S(1)}, f32[64,512]{1,0:T(8,128)S(1)}, u32[]{:S(2)}, u32[]{:S(2)}) collective-permute-start(f32[64,512]{1,0:T(8,128)S(1)} %shard_map.77.refs_0_), channel_id=1, source_target_pairs={{0,24},{4,28},{8,16},{12,20},{16,8},{20,12},{24,0},{28,4},{1,25},{... | collective-permute-start | bytes 393224 | tf_op jit(solution)/shard_map/ppermute | solution.py:36
  107.5 6.6 %collective-permute-start.17 = (f32[64,512]{1,0:T(8,128)S(1)}, f32[64,512]{1,0:T(8,128)S(1)}, u32[]{:S(2)}, u32[]{:S(2)}) collective-permute-start(f32[64,512]{1,0:T(8,128)S(1)} %shard_map.77.refs_0_), channel_id=1, source_target_pairs={{0,16},{4,20},{8,24},{12,28},{16,0},{20,4},{24,8},{28,12},{1,17},{... | collective-permute-start | bytes 393224 | tf_op jit(solution)/shard_map/ppermute | solution.py:36
  108.0 6.4 %collective-permute-start.16 = (f32[64,512]{1,0:T(8,128)S(1)}, f32[64,512]{1,0:T(8,128)S(1)}, u32[]{:S(2)}, u32[]{:S(2)}) collective-permute-start(f32[64,512]{1,0:T(8,128)S(1)} %shard_map.77.refs_0_), channel_id=1, source_target_pairs={{0,8},{4,12},{8,0},{12,4},{16,24},{20,28},{24,16},{28,20},{1,9},{5... | collective-permute-start | bytes 393224 | tf_op jit(solution)/shard_map/ppermute | solution.py:36
  114.9 1.3 collective-permute-start.19
  144.7 1.4 collective-permute-start.21
  146.1 6.8 %collective-permute-start.24 = (f32[64,512]{1,0:T(8,128)S(1)}, f32[64,512]{1,0:T(8,128)S(1)}, u32[]{:S(2)}, u32[]{:S(2)}) collective-permute-start(f32[64,512]{1,0:T(8,128)S(1)} %shard_map.82.refs_0_), channel_id=1, source_target_pairs={{0,24},{4,28},{8,16},{12,20},{16,8},{20,12},{24,0},{28,4},{1,25},{... | collective-permute-start | bytes 393224 | tf_op jit(solution)/shard_map/ppermute | solution.py:36
  148.6 6.8 %collective-permute-start.23 = (f32[64,512]{1,0:T(8,128)S(1)}, f32[64,512]{1,0:T(8,128)S(1)}, u32[]{:S(2)}, u32[]{:S(2)}) collective-permute-start(f32[64,512]{1,0:T(8,128)S(1)} %shard_map.82.refs_0_), channel_id=1, source_target_pairs={{0,16},{4,20},{8,24},{12,28},{16,0},{20,4},{24,8},{28,12},{1,17},{... | collective-permute-start | bytes 393224 | tf_op jit(solution)/shard_map/ppermute | solution.py:36
  149.1 6.4 %collective-permute-start.22 = (f32[64,512]{1,0:T(8,128)S(1)}, f32[64,512]{1,0:T(8,128)S(1)}, u32[]{:S(2)}, u32[]{:S(2)}) collective-permute-start(f32[64,512]{1,0:T(8,128)S(1)} %shard_map.82.refs_0_), channel_id=1, source_target_pairs={{0,8},{4,12},{8,0},{12,4},{16,24},{20,28},{24,16},{28,20},{1,9},{5... | collective-permute-start | bytes 393224 | tf_op jit(solution)/shard_map/ppermute | solution.py:36
  155.9 1.3 collective-permute-start.25
  157.4 3.6 %collective-permute-start.28 = (f32[4,128]{1,0:T(4,128)S(1)}, f32[4,128]{1,0:T(4,128)S(1)}, u32[]{:S(2)}, u32[]{:S(2)}) collective-permute-start(f32[4,128]{1,0:T(4,128)S(1)} %pad_maximum_fusion.refs_11_), channel_id=1, source_target_pairs={{0,3},{1,0},{2,1},{3,2},{4,7},{5,4},{6,5},{7,6},{8,11},{9,8},{10,9... | collective-permute-start | bytes 6152 | tf_op jit(solution)/shard_map/ppermute | solution.py:31
  159.2 4.5 %collective-permute-start.27 = (f32[4,128]{1,0:T(4,128)S(1)}, f32[4,128]{1,0:T(4,128)S(1)}, u32[]{:S(2)}, u32[]{:S(2)}) collective-permute-start(f32[4,128]{1,0:T(4,128)S(1)} %pad_maximum_fusion.refs_11_), channel_id=1, source_target_pairs={{0,2},{1,3},{2,0},{3,1},{4,6},{5,7},{6,4},{7,5},{8,10},{9,11},{10,... | collective-permute-start | bytes 6152 | tf_op jit(solution)/shard_map/ppermute | solution.py:31
  159.2 5.4 %collective-permute-start.26 = (f32[4,128]{1,0:T(4,128)S(1)}, f32[4,128]{1,0:T(4,128)S(1)}, u32[]{:S(2)}, u32[]{:S(2)}) collective-permute-start(f32[4,128]{1,0:T(4,128)S(1)} %pad_maximum_fusion.refs_11_), channel_id=1, source_target_pairs={{0,1},{1,2},{2,3},{3,0},{4,5},{5,6},{6,7},{7,4},{8,9},{9,10},{10,1... | collective-permute-start | bytes 6152 | tf_op jit(solution)/shard_map/ppermute | solution.py:31

commit v7 on v6

--- a/solution.py
+++ b/solution.py
@@ -76,12 +76,21 @@
     )(*[in_hbm(array) for array in arrays])
 
 
-def cut_body(first, array_ref, piece_ref, semaphore):
-    move = pltpu.make_async_copy(
-        array_ref.at[pl.ds(first, piece_ref.shape[0]), :], piece_ref, semaphore
-    )
-    move.start()
-    move.wait()
+def cut_body(first, array_ref, piece_ref, semaphores):
+    parts = semaphores.shape[0]
+    part = piece_ref.shape[0] // parts
+    moves = [
+        pltpu.make_async_copy(
+            array_ref.at[pl.ds(first + i * part, part), :],
+            piece_ref.at[pl.ds(i * part, part), :],
+            semaphores.at[i],
+        )
+        for i in range(parts)
+    ]
+    for move in moves:
+        move.start()
+    for move in moves:
+        move.wait()
 
 
 def cut(array, first, length):
@@ -90,7 +99,7 @@
         out_shape=vmem_shape((length,) + array.shape[1:], array.dtype),
         in_specs=[pl.BlockSpec(memory_space=pltpu.HBM)],
         out_specs=IN_VMEM,
-        scratch_shapes=[pltpu.SemaphoreType.DMA],
+        scratch_shapes=[pltpu.SemaphoreType.DMA((4,))],
         compiler_params=pltpu.CompilerParams(vmem_limit_bytes=2 * MIB),
         cost_estimate=FREE,
     )(in_hbm(array))
@@ -129,23 +138,24 @@
     )
 
 
-def add_up(arrays):
-    while len(arrays) > 1:
-        arrays = [arrays[i] + arrays[i + 1] for i in range(0, len(arrays), 2)]
-    return arrays[0]
-
-
-def add_body(*refs):
-    refs[-1][...] = add_up([ref[...] for ref in refs[:-1]])
-
-
-def add(*arrays):
-    return pl.pallas_call(
-        add_body,
-        out_shape=jax.ShapeDtypeStruct(arrays[0].shape, arrays[0].dtype),
+def add_body(parts, *refs):
+    pairs = refs[:-parts]
+    sums = [pairs[i][...] + pairs[i + 1][...] for i in range(0, len(pairs), 2)]
+    total = sums[0] if len(sums) == 1 else jnp.concatenate(sums, axis=0)
+    length = total.shape[0] // parts
+    for i in range(parts):
+        refs[i - parts][...] = total[i * length : (i + 1) * length]
+
+
+def add(*pairs):
+    rows = sum(array.shape[0] for array in pairs) // 4
+    shape = jax.ShapeDtypeStruct((rows,) + pairs[0].shape[1:], pairs[0].dtype)
+    return pl.pallas_call(
+        functools.partial(add_body, 2),
+        out_shape=[shape] * 2,
         compiler_params=pltpu.CompilerParams(vmem_limit_bytes=4 * MIB),
         cost_estimate=FREE,
-    )(*[in_vmem(array) for array in arrays])
+    )(*[in_vmem(array) for array in pairs])
 
 
 def dress_body(step, *refs):
@@ -156,7 +166,13 @@
     owner = lax.rem(lax.axis_index("aux") - step + aux_size, aux_size)
     upper = lax.rem(lax.axis_index("rows"), 2)
     weights = weights_ref[pl.ds((owner * 2 + upper) * half, half), :]
-    total = add_up([ref[...] for ref in summand_refs])
+    total = jnp.concatenate(
+        [
+            summand_refs[i][...] + summand_refs[i + 1][...]
+            for i in range(0, len(summand_refs), 2)
+        ],
+        axis=0,
+    )
     green = green_ref[...]
     for first in range(0, total.shape[1], norb):
         mixed = jnp.dot(
@@ -168,13 +184,14 @@
         dressed_ref[:, first : first + norb] = (mixed * weights).astype(jnp.bfloat16)
 
 
-def dress(step, summands, weights, green_one):
+def dress(step, pairs, weights, green_one):
+    rows = sum(array.shape[0] for array in pairs) // 2
     return pl.pallas_call(
         functools.partial(dress_body, step),
-        out_shape=jax.ShapeDtypeStruct(summands[0].shape, jnp.bfloat16),
+        out_shape=jax.ShapeDtypeStruct((rows, pairs[0].shape[1]), jnp.bfloat16),
         compiler_params=pltpu.CompilerParams(vmem_limit_bytes=6 * MIB),
         cost_estimate=FREE,
-    )(*[in_vmem(summand) for summand in summands], weights, in_vmem(green_one))
+    )(*[in_vmem(array) for array in pairs], weights, in_vmem(green_one))
 
 
 def join_body(mine_ref, other_ref, trace_ref, dressed_ref, traced_ref):
@@ -215,22 +232,25 @@
     half = projection.shape[0] // 2
     upper = lax.rem(lax.axis_index("rows"), 2) == 1
     low, high = projection[:half], projection[half:]
-    summands = [
+    pairs = [
         jnp.where(upper, high, low),
         exchanged(jnp.where(upper, low, high), "rows", 1),
     ]
     bits = [1 << b for b in range(1, count.bit_length() - 1)]
-    while bits:
-        total = add(*summands)
-        partners = [bits[0]] if len(bits) == 1 else [bits[0], bits[1], bits[0] ^ bits[1]]
-        summands = [total] + [exchanged(total, "rows", partner) for partner in partners]
-        bits = bits[2:]
-    mine = dress(step, summands, weights, green_one)
+    for i, bit in enumerate(bits):
+        other_bit = bits[i ^ 1] if i ^ 1 < len(bits) else bit
+        first, second = add(*pairs)
+        pairs = [
+            first,
+            exchanged(first, "rows", bit),
+            second,
+            exchanged(second, "rows", other_bit),
+        ]
+    mine = dress(step, pairs, weights, green_one)
     return join(mine, exchanged(mine, "rows", 1), trace_weights)
 
 
-SLOTS = 3
-PARTS = 2
+SLOTS = 4
 
 
 def slope_body(pieces, me_ref, *refs):
@@ -241,43 +261,41 @@
     dressed_refs = refs[early + pieces : early + pieces + shards]
     trace_refs = refs[early + pieces + shards : early + pieces + 2 * shards]
     rows = factors_ref.shape[1]
-    block = held_ref.shape[1]
+    chunk, block = rows // came.shape[0], held_ref.shape[1]
     steps, length = rows // block, rows // pieces
     share_blocks = rows // shards // block
-    part = block // PARTS
 
     def arrivals(at):
-        first = at * block
-        sources = [early_refs[0].at[pl.ds(first, block), :]] + [
-            early_refs[1 + s * pieces + first // length].at[pl.ds(first % length, block), :]
+        first = at * chunk
+        sources = [early_refs[0].at[pl.ds(first, chunk), :]] + [
+            early_refs[1 + s * pieces + first // length].at[pl.ds(first % length, chunk), :]
             for s in range(shards - 2)
         ]
         return [
             pltpu.make_async_copy(
-                source, factors_ref.at[s, pl.ds(first, block), :], came.at[at, s]
+                source, factors_ref.at[s, pl.ds(first, chunk), :], came.at[at, s]
             )
             for s, source in enumerate(sources)
         ]
 
-    def departures(at):
-        return [
-            pltpu.make_async_copy(
-                held_ref.at[at % SLOTS, pl.ds(i * part, part), :],
-                slope_ref.at[pl.ds(at * block + i * part, part), :],
-                gone.at[at % SLOTS, i],
-            )
-            for i in range(PARTS)
-        ]
-
-    for at in range(steps):
+    def departure(at):
+        return pltpu.make_async_copy(
+            held_ref.at[at % SLOTS], slope_ref.at[pl.ds(at * block, block), :], gone.at[at % SLOTS]
+        )
+
+    for at in range(rows // chunk):
         for copy in arrivals(at):
             copy.start()
 
-    trace = trace_refs[0][...]
-    for shift in range(1, shards):
-        other = trace_refs[shift][...]
-        trace = trace + jnp.concatenate([other[shards - shift :], other[: shards - shift]], axis=0)
-    row = jnp.concatenate([trace[s : s + 1] for s in range(shards)], axis=1)
+    me = me_ref[0]
+    rows_of_trace = []
+    for s in range(shards):
+        total = trace_refs[0][s : s + 1, :]
+        for bits in range(1, shards):
+            theirs = lax.rem((me ^ bits) - me + s + shards, shards)
+            total = total + trace_refs[bits][pl.ds(theirs, 1), :]
+        rows_of_trace.append(total)
+    row = jnp.concatenate(rows_of_trace, axis=1)
     high = row.astype(jnp.bfloat16).astype(jnp.float32)
     middle = (row - high).astype(jnp.bfloat16).astype(jnp.float32)
     low = row - high - middle
@@ -287,11 +305,11 @@
     dressed_ref[...] = jnp.concatenate([ref[...] for ref in dressed_refs], axis=0)
 
     for at in range(steps):
-        for copy in arrivals(at):
-            copy.wait()
+        if at * block % chunk == 0:
+            for copy in arrivals(at * block // chunk):
+                copy.wait()
         if at >= SLOTS:
-            for copy in departures(at - SLOTS):
-                copy.wait()
+            departure(at - SLOTS).wait()
         first = at * block
         basis = jnp.concatenate(
             [factors_ref[s, pl.ds(first, block), :] for s in range(shards - 1)]
@@ -301,10 +319,9 @@
         held_ref[at % SLOTS] = jnp.dot(
             basis, dressed_ref[...], preferred_element_type=jnp.float32
         )
-        for copy in departures(at):
-            copy.start()
-
-        @pl.when(me_ref[0] == at // share_blocks)
+        departure(at).start()
+
+        @pl.when(me == at // share_blocks)
         def _():
             parts = lax.dot_general(
                 thirds, basis, (((1,), (1,)), ((), ())), preferred_element_type=jnp.float32
@@ -313,8 +330,7 @@
             collision_ref[:, there] = jnp.sum(parts, axis=0, keepdims=True)
 
     for at in range(max(steps - SLOTS, 0), steps):
-        for copy in departures(at):
-            copy.wait()
+        departure(at).wait()
 
 
 def slope(own, steps, dressed, traces):
@@ -323,7 +339,8 @@
     columns = dressed[0].shape[1]
     depth = shards * vectors
     share = rows // shards
-    block = min(rows // pieces, share, 1024)
+    chunk = min(rows // pieces, share, 1024)
+    block = min(chunk, 512)
     far = pl.BlockSpec(memory_space=pltpu.HBM)
     early = [own] + [piece for step in steps[:-1] for piece in step]
     near = [*steps[-1], *dressed, *traces]
@@ -337,8 +354,8 @@
             pltpu.VMEM((shards - 1, rows, vectors), jnp.bfloat16),
             pltpu.VMEM((depth, columns), jnp.bfloat16),
             pltpu.VMEM((SLOTS, block, columns), jnp.float32),
-            pltpu.SemaphoreType.DMA((rows // block, shards - 1)),
-            pltpu.SemaphoreType.DMA((SLOTS, PARTS)),
+            pltpu.SemaphoreType.DMA((rows // chunk, shards - 1)),
+            pltpu.SemaphoreType.DMA((SLOTS,)),
         ],
         out_shape=[
             jax.ShapeDtypeStruct((rows, columns), jnp.float32),
@@ -403,7 +420,7 @@
         finish(step, total)
 
     trace = jnp.concatenate(traced, axis=0)
-    traces = [trace] + [shifted(trace, "aux", shift) for shift in range(1, aux_size)]
+    traces = [trace] + [exchanged(trace, "aux", bits) for bits in range(1, aux_size)]
     return slope(cholesky_factors, steps, dressed, traces)
 
 

time: 175 us -> 177 us (1.011)
  starting transfers between devices: 24 us -> 32.6 us
  waiting for transfers between devices: 105 us -> 98 us
    ppermute x20 -> x27, starting transfers between devices: 14.8 us -> 26.2 us  [exchanged(): return lax.ppermute(block, axis, [(i, i ^ bit) for i in range(count)])]
    ppermute x9 -> x6, waiting for transfers between devices: 71.6 us -> 60.3 us  [shifted(): lax.ppermute(block, axis, [(i, (i + shift) % count) for i in range(count)])]
    ppermute x20 -> x27, waiting for transfers between devices: 33.7 us -> 37.7 us  [exchanged(): return lax.ppermute(block, axis, [(i, i ^ bit) for i in range(count)])]
    ppermute x9 -> x6, starting transfers between devices: 9.17 us -> 6.4 us  [shifted(): lax.ppermute(block, axis, [(i, (i + shift) % count) for i in range(count)])]
  transfers between devices with their start and end apart: 29 -> 33, of which waited for: 29 -> 31; matrix products, arithmetic and copies ran while one was open for 1% -> 1% of each run, Pallas kernels for 10% -> 10%
where the time goes in v7:
time: 177 us
  waiting for transfers between devices  98 us (55%)
  starting transfers between devices  32.6 us (18%)
  Pallas kernels  32 us (18%)
  local copies, waits for them, and re-layouts  11.6 us (7%)
    ppermute x6, waiting for transfers between devices, shifted(): lax.ppermute(block, axis, [(i, (i + shift) % count) for i in range(count)])  60.3 us
    ppermute x27, waiting for transfers between devices, exchanged(): return lax.ppermute(block, axis, [(i, i ^ bit) for i in range(count)])  37.7 us
    ppermute x27, starting transfers between devices, exchanged(): return lax.ppermute(block, axis, [(i, i ^ bit) for i in range(count)])  26.2 us
    unnamed x21, local copies, waits for them, and re-layouts  11.3 us
    pallas_call x1, Pallas kernels, slope(): pl.pallas_call(functools.partial(slope_body, pieces), in_specs=[pl.BlockS...  10.8 us
    pallas_call x5, Pallas kernels, project(): pl.pallas_call(functools.partial(project_body, first, min(length, 1024)),...  10.8 us
    ppermute x6, starting transfers between devices, shifted(): lax.ppermute(block, axis, [(i, (i + shift) % count) for i in range(count)])  6.4 us
    pallas_call x2, Pallas kernels, cut(): pl.pallas_call(functools.partial(cut_body, first), out_shape=vmem_shape((...  4.54 us
  transfers between devices with their start and end apart: 33, of which 31 were waited for; matrix products, arithmetic and copies ran while one was open for 1% of the time, Pallas kernels for 10%

profile of v7, /device:TPU:0, one launch (start us, length us, event | category | flops | bytes accessed | tf_op | source)
XLA Modules:
  0.0 176.8 jit_solution(7614944701407111357)
XLA Ops:
  0.6 2.4 %shard_map.59 = bf16[4096,128]{1,0:T(8,128)(2,1)} custom-call(bf16[8192,128]{1,0:T(8,128)(2,1)} %refs_0_.3), custom_call_target="tpu_custom_call" | custom-call | tf_op jit(solution)/shard_map/pallas_call | solution.py:97
  3.0 3.1 %collective-permute-start = (bf16[4096,128]{1,0:T(8,128)(2,1)}, bf16[4096,128]{1,0:T(8,128)(2,1)}, u32[]{:S(2)}, u32[]{:S(2)}) collective-permute-start(bf16[4096,128]{1,0:T(8,128)(2,1)} %shard_map.59), channel_id=1, source_target_pairs={{0,1},{1,2},{2,3},{3,0},{4,5},{5,6},{6,7},{7,4},{8,9},{9,10},{10,1... | collective-permute-start | bytes 3145736 | tf_op jit(solution)/shard_map/ppermute | solution.py:31
  6.1 2.2 %shard_map.67 = bf16[4096,128]{1,0:T(8,128)(2,1)} custom-call(bf16[8192,128]{1,0:T(8,128)(2,1)} %refs_0_.3), custom_call_target="tpu_custom_call" | custom-call | tf_op jit(solution)/shard_map/pallas_call | solution.py:97
  8.3 1.6 collective-permute-start.7
  9.9 3.4 %shard_map.60 = (bf16[8192,512]{1,0:T(8,128)(2,1)S(1)}, f32[256,256]{1,0:T(8,128)S(1)}) custom-call(bf16[8192,512]{1,0:T(8,128)(2,1)} %refs_0_.2, f32[256,256]{1,0:T(8,128)} %refs_1_.1), custom_call_target="tpu_custom_call" | custom-call | tf_op jit(solution)/shard_map/pallas_call | solution.py:68
  13.4 2.8 %shard_map.61 = f32[128,512]{1,0:T(8,128)S(1)} custom-call(bf16[8192,128]{1,0:T(8,128)(2,1)S(1)} %copy-done.2, bf16[8192,512]{1,0:T(8,128)(2,1)S(1)} %get-tuple-element.30.green_ref, f32[128,512]{1,0:T(8,128)S(1)} %broadcast_in_dim.10.acc_ref), custom_call_target="tpu_custom_call" | custom-call | tf_op jit(solution)/shard_map/pallas_call | solution.py:125
  16.2 3.4 %copy-done = bf16[8192,512]{1,0:T(8,128)(2,1)} copy-done((bf16[8192,512]{1,0:T(8,128)(2,1)}, bf16[8192,512]{1,0:T(8,128)(2,1)S(1)}, u32[]{:S(2)}) %copy-start) | copy-done | bytes 8388632
  19.7 1.3 collective-permute-done.1.refs_1_
  21.0 1.5 collective-permute-start.2
  22.5 1.5 collective-permute-start.3
  25.3 1.5 collective-permute-done.3.refs_3_
  26.8 1.6 collective-permute-start.4
  29.1 2.0 %collective-permute-done.4.refs_1_ = f32[32,512]{1,0:T(8,128)S(1)} collective-permute-done((f32[32,512]{1,0:T(8,128)S(1)}, f32[32,512]{1,0:T(8,128)S(1)}, u32[]{:S(2)}, u32[]{:S(2)}) %collective-permute-start.4) | collective-permute-done | bytes 65568 | tf_op jit(solution)/shard_map/ppermute | solution.py:36
  31.2 1.5 collective-permute-done.5.refs_3_
  34.6 1.6 collective-permute-start.8
  36.2 3.4 %copy-done.1 = bf16[8192,512]{1,0:T(8,128)(2,1)S(1)} copy-done((bf16[8192,512]{1,0:T(8,128)(2,1)S(1)}, bf16[8192,512]{1,0:T(8,128)(2,1)}, u32[]{:S(2)}) %copy-start.1) | copy-done | bytes 8388632
  39.6 2.6 %shard_map.68.refs_1_.acc_ref = f32[128,512]{1,0:T(8,128)S(1)} custom-call(bf16[4096,128]{1,0:T(8,128)(2,1)} %shard_map.66.piece_ref.refs_1_, bf16[8192,512]{1,0:T(8,128)(2,1)S(1)} %copy-done.1, f32[128,512]{1,0:T(8,128)S(1)} %broadcast_in_dim.10.acc_ref), custom_call_target="tpu_custom_call" | custom-call | tf_op jit(solution)/shard_map/pallas_call | solution.py:125
  42.2 12.7 %collective-permute-done.7.refs_0_ = bf16[4096,128]{1,0:T(8,128)(2,1)} collective-permute-done((bf16[4096,128]{1,0:T(8,128)(2,1)}, bf16[4096,128]{1,0:T(8,128)(2,1)}, u32[]{:S(2)}, u32[]{:S(2)}) %collective-permute-start.7) | collective-permute-done | bytes 1048608 | tf_op jit(solution)/shard_map/ppermute | solution.py:31
  54.9 2.8 %shard_map.70 = f32[128,512]{1,0:T(8,128)S(1)} custom-call(bf16[4096,128]{1,0:T(8,128)(2,1)} %shard_map.69.piece_ref.refs_2_, bf16[8192,512]{1,0:T(8,128)(2,1)S(1)} %copy-done.1, f32[128,512]{1,0:T(8,128)S(1)} %shard_map.68.refs_1_.acc_ref), custom_call_target="tpu_custom_call" | custom-call | tf_op jit(solution)/shard_map/pallas_call | solution.py:125
  57.8 1.3 collective-permute-done.9.refs_1_
  59.1 1.8 %collective-permute-start.10 = (f32[32,512]{1,0:T(8,128)S(1)}, f32[32,512]{1,0:T(8,128)S(1)}, u32[]{:S(2)}, u32[]{:S(2)}) collective-permute-start(f32[32,512]{1,0:T(8,128)S(1)} %get-tuple-element.38.refs_0_), channel_id=1, source_target_pairs={{0,8},{4,12},{8,0},{12,4},{16,24},{20,28},{24,16},{28,20},{1,9},{5... | collective-permute-start | bytes 196616 | tf_op jit(solution)/shard_map/ppermute | solution.py:36
  60.9 1.5 collective-permute-start.11
  63.5 1.7 collective-permute-done.11.refs_3_
  65.2 1.6 collective-permute-start.12
  67.3 2.2 %collective-permute-done.12.refs_1_ = f32[32,512]{1,0:T(8,128)S(1)} collective-permute-done((f32[32,512]{1,0:T(8,128)S(1)}, f32[32,512]{1,0:T(8,128)S(1)}, u32[]{:S(2)}, u32[]{:S(2)}) %collective-permute-start.12) | collective-permute-done | bytes 65568 | tf_op jit(solution)/shard_map/ppermute | solution.py:36
  69.5 1.5 collective-permute-done.13.refs_3_
  72.9 4.3 %collective-permute-done.8.refs_0_ = bf16[4096,128]{1,0:T(8,128)(2,1)S(1)} collective-permute-done((bf16[4096,128]{1,0:T(8,128)(2,1)}, bf16[4096,128]{1,0:T(8,128)(2,1)S(1)}, u32[]{:S(2)}, u32[]{:S(2)}) %collective-permute-start.8) | collective-permute-done | bytes 1048608 | tf_op jit(solution)/shard_map/ppermute | solution.py:31
  80.8 18.9 %collective-permute-done.15.refs_0_ = bf16[4096,128]{1,0:T(8,128)(2,1)S(1)} collective-permute-done((bf16[4096,128]{1,0:T(8,128)(2,1)}, bf16[4096,128]{1,0:T(8,128)(2,1)S(1)}, u32[]{:S(2)}, u32[]{:S(2)}) %collective-permute-start.15) | collective-permute-done | bytes 1048608 | tf_op jit(solution)/shard_map/ppermute | solution.py:31
  102.0 1.3 shard_map.78
  103.4 1.3 collective-permute-done.17.refs_1_
  104.8 1.8 %collective-permute-start.18 = (f32[32,512]{1,0:T(8,128)S(1)}, f32[32,512]{1,0:T(8,128)S(1)}, u32[]{:S(2)}, u32[]{:S(2)}) collective-permute-start(f32[32,512]{1,0:T(8,128)S(1)} %get-tuple-element.44.refs_0_), channel_id=1, source_target_pairs={{0,8},{4,12},{8,0},{12,4},{16,24},{20,28},{24,16},{28,20},{1,9},{5... | collective-permute-start | bytes 196616 | tf_op jit(solution)/shard_map/ppermute | solution.py:36
  106.6 1.5 collective-permute-start.19
  109.1 1.7 collective-permute-done.19.refs_3_
  110.8 1.6 collective-permute-start.20
  113.0 2.2 %collective-permute-done.20.refs_1_ = f32[32,512]{1,0:T(8,128)S(1)} collective-permute-done((f32[32,512]{1,0:T(8,128)S(1)}, f32[32,512]{1,0:T(8,128)S(1)}, u32[]{:S(2)}, u32[]{:S(2)}) %collective-permute-start.20) | collective-permute-done | bytes 65568 | tf_op jit(solution)/shard_map/ppermute | solution.py:36
  115.2 1.5 collective-permute-done.21.refs_3_
  118.6 3.6 %collective-permute-done.16.refs_0_ = bf16[4096,128]{1,0:T(8,128)(2,1)S(1)} collective-permute-done((bf16[4096,128]{1,0:T(8,128)(2,1)}, bf16[4096,128]{1,0:T(8,128)(2,1)S(1)}, u32[]{:S(2)}, u32[]{:S(2)}) %collective-permute-start.16) | collective-permute-done | bytes 1048608 | tf_op jit(solution)/shard_map/ppermute | solution.py:31
  122.9 20.9 %collective-permute-done.23.refs_0_ = bf16[4096,128]{1,0:T(8,128)(2,1)S(1)} collective-permute-done((bf16[4096,128]{1,0:T(8,128)(2,1)}, bf16[4096,128]{1,0:T(8,128)(2,1)S(1)}, u32[]{:S(2)}, u32[]{:S(2)}) %collective-permute-start.23) | collective-permute-done | bytes 1048608 | tf_op jit(solution)/shard_map/ppermute | solution.py:31
  144.7 1.3 collective-permute-done.24.refs_1_
  146.1 1.6 collective-permute-start.25
  147.6 1.5 collective-permute-start.26
  150.4 1.5 collective-permute-done.26.refs_3_
  151.9 1.6 collective-permute-start.27
  154.1 2.2 %collective-permute-done.27.refs_1_ = f32[32,512]{1,0:T(8,128)S(1)} collective-permute-done((f32[32,512]{1,0:T(8,128)S(1)}, f32[32,512]{1,0:T(8,128)S(1)}, u32[]{:S(2)}, u32[]{:S(2)}) %collective-permute-start.27) | collective-permute-done | bytes 65568 | tf_op jit(solution)/shard_map/ppermute | solution.py:36
  156.3 1.5 collective-permute-done.28.refs_3_
  159.7 1.8 %collective-permute-start.32 = (f32[4,128]{1,0:T(4,128)S(1)}, f32[4,128]{1,0:T(4,128)S(1)}, u32[]{:S(2)}, u32[]{:S(2)}) collective-permute-start(f32[4,128]{1,0:T(4,128)S(1)} %pad_maximum_fusion.refs_11_), channel_id=1, source_target_pairs={{0,3},{1,2},{2,1},{3,0},{4,7},{5,6},{6,5},{7,4},{8,11},{9,10},{10,... | collective-permute-start | bytes 6152 | tf_op jit(solution)/shard_map/ppermute | solution.py:36
  161.5 2.6 %collective-permute-start.30 = (f32[4,128]{1,0:T(4,128)S(1)}, f32[4,128]{1,0:T(4,128)S(1)}, u32[]{:S(2)}, u32[]{:S(2)}) collective-permute-start(f32[4,128]{1,0:T(4,128)S(1)} %pad_maximum_fusion.refs_11_), channel_id=1, source_target_pairs={{0,1},{1,0},{2,3},{3,2},{4,5},{5,4},{6,7},{7,6},{8,9},{9,8},{10,11... | collective-permute-start | bytes 6152 | tf_op jit(solution)/shard_map/ppermute | solution.py:36
  166.0 10.8 %shard_map.89 = (f32[8192,512]{1,0:T(8,128)}, f32[1,2048]{1,0:T(1,128)}) custom-call(s32[1]{0:T(128)} %bitcast.me_ref, bf16[8192,128]{1,0:T(8,128)(2,1)} %refs_0_.3, bf16[4096,128]{1,0:T(8,128)(2,1)} %shard_map.66.piece_ref.refs_1_, bf16[4096,128]{1,0:T(8,128)(2,1)} %shard_map.69.piece_ref.refs_2_, bf16[4096,128]{1,0:T(8,128)(2,1)} %shard_map.75.piece_ref.refs_3_, ...), custom_call_target="tpu_custom_call" | custom-call | flops 4294967296 | bytes 25165824 | tf_op jit(solution)/shard_map/pallas_call | solution.py:347
  (82 shorter events, 24.3 us)
Async XLA Ops:
  0.6 12.7 %copy-start.2 = (bf16[8192,128]{1,0:T(8,128)(2,1)S(1)}, bf16[8192,128]{1,0:T(8,128)(2,1)}, u32[]{:S(2)}) copy-start(bf16[8192,128]{1,0:T(8,128)(2,1)} %refs_0_.3) | copy-start | bytes 6291460
  3.0 31.6 %collective-permute-start = (bf16[4096,128]{1,0:T(8,128)(2,1)}, bf16[4096,128]{1,0:T(8,128)(2,1)}, u32[]{:S(2)}, u32[]{:S(2)}) collective-permute-start(bf16[4096,128]{1,0:T(8,128)(2,1)} %shard_map.59), channel_id=1, source_target_pairs={{0,1},{1,2},{2,3},{3,0},{4,5},{5,6},{6,7},{7,4},{8,9},{9,10},{10,1... | collective-permute-start | bytes 3145736 | tf_op jit(solution)/shard_map/ppermute | solution.py:31
  8.3 46.6 %collective-permute-start.7 = (bf16[4096,128]{1,0:T(8,128)(2,1)}, bf16[4096,128]{1,0:T(8,128)(2,1)}, u32[]{:S(2)}, u32[]{:S(2)}) collective-permute-start(bf16[4096,128]{1,0:T(8,128)(2,1)} %shard_map.67), channel_id=1, source_target_pairs={{0,1},{1,2},{2,3},{3,0},{4,5},{5,6},{6,7},{7,4},{8,9},{9,10},{10,1... | collective-permute-start | bytes 3145736 | tf_op jit(solution)/shard_map/ppermute | solution.py:31
  9.9 19.1 %copy-start.7 = (f32[512]{0:T(512)S(1)}, f32[512]{0:T(512)}, u32[]{:S(2)}) copy-start(f32[512]{0:T(512)} %param.7) | copy-start | bytes 6148
  16.2 3.4 %copy-start = (bf16[8192,512]{1,0:T(8,128)(2,1)}, bf16[8192,512]{1,0:T(8,128)(2,1)S(1)}, u32[]{:S(2)}) copy-start(bf16[8192,512]{1,0:T(8,128)(2,1)S(1)} %get-tuple-element.30.green_ref) | copy-start | bytes 25165828
  19.6 1.4 collective-permute-start.1
  21.0 4.3 %collective-permute-start.2 = (f32[32,512]{1,0:T(8,128)S(1)}, f32[32,512]{1,0:T(8,128)S(1)}, u32[]{:S(2)}, u32[]{:S(2)}) collective-permute-start(f32[32,512]{1,0:T(8,128)S(1)} %get-tuple-element.31.refs_0_), channel_id=1, source_target_pairs={{0,8},{4,12},{8,0},{12,4},{16,24},{20,28},{24,16},{28,20},{1,9},{5... | collective-permute-start | bytes 196616 | tf_op jit(solution)/shard_map/ppermute | solution.py:36
  22.5 4.3 %collective-permute-start.3 = (f32[32,512]{1,0:T(8,128)S(1)}, f32[32,512]{1,0:T(8,128)S(1)}, u32[]{:S(2)}, u32[]{:S(2)}) collective-permute-start(f32[32,512]{1,0:T(8,128)S(1)} %get-tuple-element.32.refs_2_), channel_id=1, source_target_pairs={{0,16},{4,20},{8,24},{12,28},{16,0},{20,4},{24,8},{28,12},{1,17},{... | collective-permute-start | bytes 196616 | tf_op jit(solution)/shard_map/ppermute | solution.py:36
  26.8 4.3 %collective-permute-start.4 = (f32[32,512]{1,0:T(8,128)S(1)}, f32[32,512]{1,0:T(8,128)S(1)}, u32[]{:S(2)}, u32[]{:S(2)}) collective-permute-start(f32[32,512]{1,0:T(8,128)S(1)} %get-tuple-element.33.refs_0_), channel_id=1, source_target_pairs={{0,16},{4,20},{8,24},{12,28},{16,0},{20,4},{24,8},{28,12},{1,17},{... | collective-permute-start | bytes 196616 | tf_op jit(solution)/shard_map/ppermute | solution.py:36
  28.4 4.3 %collective-permute-start.5 = (f32[32,512]{1,0:T(8,128)S(1)}, f32[32,512]{1,0:T(8,128)S(1)}, u32[]{:S(2)}, u32[]{:S(2)}) collective-permute-start(f32[32,512]{1,0:T(8,128)S(1)} %get-tuple-element.34.refs_2_), channel_id=1, source_target_pairs={{0,8},{4,12},{8,0},{12,4},{16,24},{20,28},{24,16},{28,20},{1,9},{5... | collective-permute-start | bytes 196616 | tf_op jit(solution)/shard_map/ppermute | solution.py:36
  33.1 1.3 collective-permute-start.6
  34.6 42.6 %collective-permute-start.8 = (bf16[4096,128]{1,0:T(8,128)(2,1)}, bf16[4096,128]{1,0:T(8,128)(2,1)S(1)}, u32[]{:S(2)}, u32[]{:S(2)}) collective-permute-start(bf16[4096,128]{1,0:T(8,128)(2,1)} %shard_map.66.piece_ref.refs_1_), channel_id=1, source_target_pairs={{0,1},{1,2},{2,3},{3,0},{4,5},{5,6},{6,7},{7,4},{8,9},{9,10},{10,1... | collective-permute-start | bytes 3145736 | tf_op jit(solution)/shard_map/ppermute | solution.py:31
  36.2 3.4 %copy-start.1 = (bf16[8192,512]{1,0:T(8,128)(2,1)S(1)}, bf16[8192,512]{1,0:T(8,128)(2,1)}, u32[]{:S(2)}) copy-start(bf16[8192,512]{1,0:T(8,128)(2,1)} %copy-done) | copy-start | bytes 25165828
  42.2 36.0 %slice-start = ((s8[8388608]{0:T(1024)(128)(4,1)}), s8[4194304]{0:T(1024)(128)(4,1)S(1)}, s32[]{:S(2)}) async-start(s8[8388608]{0:T(1024)(128)(4,1)} %bitcast.10), calls=%async_computation | async-start | bytes 8388608
  54.9 23.4 %slice-start.1 = ((s8[8388608]{0:T(1024)(128)(4,1)}), s8[4194304]{0:T(1024)(128)(4,1)S(1)}, s32[]{:S(2)}) async-start(s8[8388608]{0:T(1024)(128)(4,1)} %bitcast.10), calls=%async_computation.1 | async-start | bytes 8388608
  54.9 44.8 %collective-permute-start.15 = (bf16[4096,128]{1,0:T(8,128)(2,1)}, bf16[4096,128]{1,0:T(8,128)(2,1)S(1)}, u32[]{:S(2)}, u32[]{:S(2)}) collective-permute-start(bf16[4096,128]{1,0:T(8,128)(2,1)} %shard_map.69.piece_ref.refs_2_), channel_id=1, source_target_pairs={{0,1},{1,2},{2,3},{3,0},{4,5},{5,6},{6,7},{7,4},{8,9},{9,10},{10,1... | collective-permute-start | bytes 3145736 | tf_op jit(solution)/shard_map/ppermute | solution.py:31
  57.7 1.4 collective-permute-start.9
  59.1 4.3 %collective-permute-start.10 = (f32[32,512]{1,0:T(8,128)S(1)}, f32[32,512]{1,0:T(8,128)S(1)}, u32[]{:S(2)}, u32[]{:S(2)}) collective-permute-start(f32[32,512]{1,0:T(8,128)S(1)} %get-tuple-element.38.refs_0_), channel_id=1, source_target_pairs={{0,8},{4,12},{8,0},{12,4},{16,24},{20,28},{24,16},{28,20},{1,9},{5... | collective-permute-start | bytes 196616 | tf_op jit(solution)/shard_map/ppermute | solution.py:36
  60.9 4.3 %collective-permute-start.11 = (f32[32,512]{1,0:T(8,128)S(1)}, f32[32,512]{1,0:T(8,128)S(1)}, u32[]{:S(2)}, u32[]{:S(2)}) collective-permute-start(f32[32,512]{1,0:T(8,128)S(1)} %get-tuple-element.39.refs_2_), channel_id=1, source_target_pairs={{0,16},{4,20},{8,24},{12,28},{16,0},{20,4},{24,8},{28,12},{1,17},{... | collective-permute-start | bytes 196616 | tf_op jit(solution)/shard_map/ppermute | solution.py:36
  65.2 4.3 %collective-permute-start.12 = (f32[32,512]{1,0:T(8,128)S(1)}, f32[32,512]{1,0:T(8,128)S(1)}, u32[]{:S(2)}, u32[]{:S(2)}) collective-permute-start(f32[32,512]{1,0:T(8,128)S(1)} %get-tuple-element.40.refs_0_), channel_id=1, source_target_pairs={{0,16},{4,20},{8,24},{12,28},{16,0},{20,4},{24,8},{28,12},{1,17},{... | collective-permute-start | bytes 196616 | tf_op jit(solution)/shard_map/ppermute | solution.py:36
  66.8 4.3 %collective-permute-start.13 = (f32[32,512]{1,0:T(8,128)S(1)}, f32[32,512]{1,0:T(8,128)S(1)}, u32[]{:S(2)}, u32[]{:S(2)}) collective-permute-start(f32[32,512]{1,0:T(8,128)S(1)} %get-tuple-element.41.refs_2_), channel_id=1, source_target_pairs={{0,8},{4,12},{8,0},{12,4},{16,24},{20,28},{24,16},{28,20},{1,9},{5... | collective-permute-start | bytes 196616 | tf_op jit(solution)/shard_map/ppermute | solution.py:36
  71.5 1.3 collective-permute-start.14
  77.2 1.0 copy-start.3
  78.2 44.0 %collective-permute-start.16 = (bf16[4096,128]{1,0:T(8,128)(2,1)}, bf16[4096,128]{1,0:T(8,128)(2,1)S(1)}, u32[]{:S(2)}, u32[]{:S(2)}) collective-permute-start(bf16[4096,128]{1,0:T(8,128)(2,1)} %shard_map.75.piece_ref.refs_3_), channel_id=1, source_target_pairs={{0,1},{1,2},{2,3},{3,0},{4,5},{5,6},{6,7},{7,4},{8,9},{9,10},{10,1... | collective-permute-start | bytes 3145736 | tf_op jit(solution)/shard_map/ppermute | solution.py:31
  78.3 1.3 copy-start.4
  99.7 1.0 copy-start.5
  100.7 43.1 %collective-permute-start.23 = (bf16[4096,128]{1,0:T(8,128)(2,1)}, bf16[4096,128]{1,0:T(8,128)(2,1)S(1)}, u32[]{:S(2)}, u32[]{:S(2)}) collective-permute-start(bf16[4096,128]{1,0:T(8,128)(2,1)} %shard_map.77.piece_ref.refs_4_), channel_id=1, source_target_pairs={{0,1},{1,2},{2,3},{3,0},{4,5},{5,6},{6,7},{7,4},{8,9},{9,10},{10,1... | collective-permute-start | bytes 3145736 | tf_op jit(solution)/shard_map/ppermute | solution.py:31
  100.7 1.3 copy-start.6
  103.4 1.4 collective-permute-start.17
  104.8 4.3 %collective-permute-start.18 = (f32[32,512]{1,0:T(8,128)S(1)}, f32[32,512]{1,0:T(8,128)S(1)}, u32[]{:S(2)}, u32[]{:S(2)}) collective-permute-start(f32[32,512]{1,0:T(8,128)S(1)} %get-tuple-element.44.refs_0_), channel_id=1, source_target_pairs={{0,8},{4,12},{8,0},{12,4},{16,24},{20,28},{24,16},{28,20},{1,9},{5... | collective-permute-start | bytes 196616 | tf_op jit(solution)/shard_map/ppermute | solution.py:36
  106.6 4.3 %collective-permute-start.19 = (f32[32,512]{1,0:T(8,128)S(1)}, f32[32,512]{1,0:T(8,128)S(1)}, u32[]{:S(2)}, u32[]{:S(2)}) collective-permute-start(f32[32,512]{1,0:T(8,128)S(1)} %get-tuple-element.45.refs_2_), channel_id=1, source_target_pairs={{0,16},{4,20},{8,24},{12,28},{16,0},{20,4},{24,8},{28,12},{1,17},{... | collective-permute-start | bytes 196616 | tf_op jit(solution)/shard_map/ppermute | solution.py:36
  110.8 4.3 %collective-permute-start.20 = (f32[32,512]{1,0:T(8,128)S(1)}, f32[32,512]{1,0:T(8,128)S(1)}, u32[]{:S(2)}, u32[]{:S(2)}) collective-permute-start(f32[32,512]{1,0:T(8,128)S(1)} %get-tuple-element.46.refs_0_), channel_id=1, source_target_pairs={{0,16},{4,20},{8,24},{12,28},{16,0},{20,4},{24,8},{28,12},{1,17},{... | collective-permute-start | bytes 196616 | tf_op jit(solution)/shard_map/ppermute | solution.py:36
  112.4 4.3 %collective-permute-start.21 = (f32[32,512]{1,0:T(8,128)S(1)}, f32[32,512]{1,0:T(8,128)S(1)}, u32[]{:S(2)}, u32[]{:S(2)}) collective-permute-start(f32[32,512]{1,0:T(8,128)S(1)} %get-tuple-element.47.refs_2_), channel_id=1, source_target_pairs={{0,8},{4,12},{8,0},{12,4},{16,24},{20,28},{24,16},{28,20},{1,9},{5... | collective-permute-start | bytes 196616 | tf_op jit(solution)/shard_map/ppermute | solution.py:36
  117.1 1.3 collective-permute-start.22
  144.7 1.4 collective-permute-start.24
  146.1 4.3 %collective-permute-start.25 = (f32[32,512]{1,0:T(8,128)S(1)}, f32[32,512]{1,0:T(8,128)S(1)}, u32[]{:S(2)}, u32[]{:S(2)}) collective-permute-start(f32[32,512]{1,0:T(8,128)S(1)} %get-tuple-element.50.refs_0_), channel_id=1, source_target_pairs={{0,8},{4,12},{8,0},{12,4},{16,24},{20,28},{24,16},{28,20},{1,9},{5... | collective-permute-start | bytes 196616 | tf_op jit(solution)/shard_map/ppermute | solution.py:36
  147.6 4.3 %collective-permute-start.26 = (f32[32,512]{1,0:T(8,128)S(1)}, f32[32,512]{1,0:T(8,128)S(1)}, u32[]{:S(2)}, u32[]{:S(2)}) collective-permute-start(f32[32,512]{1,0:T(8,128)S(1)} %get-tuple-element.51.refs_2_), channel_id=1, source_target_pairs={{0,16},{4,20},{8,24},{12,28},{16,0},{20,4},{24,8},{28,12},{1,17},{... | collective-permute-start | bytes 196616 | tf_op jit(solution)/shard_map/ppermute | solution.py:36
  151.9 4.3 %collective-permute-start.27 = (f32[32,512]{1,0:T(8,128)S(1)}, f32[32,512]{1,0:T(8,128)S(1)}, u32[]{:S(2)}, u32[]{:S(2)}) collective-permute-start(f32[32,512]{1,0:T(8,128)S(1)} %get-tuple-element.52.refs_0_), channel_id=1, source_target_pairs={{0,16},{4,20},{8,24},{12,28},{16,0},{20,4},{24,8},{28,12},{1,17},{... | collective-permute-start | bytes 196616 | tf_op jit(solution)/shard_map/ppermute | solution.py:36
  153.5 4.3 %collective-permute-start.28 = (f32[32,512]{1,0:T(8,128)S(1)}, f32[32,512]{1,0:T(8,128)S(1)}, u32[]{:S(2)}, u32[]{:S(2)}) collective-permute-start(f32[32,512]{1,0:T(8,128)S(1)} %get-tuple-element.53.refs_2_), channel_id=1, source_target_pairs={{0,8},{4,12},{8,0},{12,4},{16,24},{20,28},{24,16},{28,20},{1,9},{5... | collective-permute-start | bytes 196616 | tf_op jit(solution)/shard_map/ppermute | solution.py:36
  158.2 1.3 collective-permute-start.29
  159.7 5.4 %collective-permute-start.32 = (f32[4,128]{1,0:T(4,128)S(1)}, f32[4,128]{1,0:T(4,128)S(1)}, u32[]{:S(2)}, u32[]{:S(2)}) collective-permute-start(f32[4,128]{1,0:T(4,128)S(1)} %pad_maximum_fusion.refs_11_), channel_id=1, source_target_pairs={{0,3},{1,2},{2,1},{3,0},{4,7},{5,6},{6,5},{7,4},{8,11},{9,10},{10,... | collective-permute-start | bytes 6152 | tf_op jit(solution)/shard_map/ppermute | solution.py:36
  161.5 4.5 %collective-permute-start.31 = (f32[4,128]{1,0:T(4,128)S(1)}, f32[4,128]{1,0:T(4,128)S(1)}, u32[]{:S(2)}, u32[]{:S(2)}) collective-permute-start(f32[4,128]{1,0:T(4,128)S(1)} %pad_maximum_fusion.refs_11_), channel_id=1, source_target_pairs={{0,2},{1,3},{2,0},{3,1},{4,6},{5,7},{6,4},{7,5},{8,10},{9,11},{10,... | collective-permute-start | bytes 6152 | tf_op jit(solution)/shard_map/ppermute | solution.py:36
  161.5 4.5 %collective-permute-start.30 = (f32[4,128]{1,0:T(4,128)S(1)}, f32[4,128]{1,0:T(4,128)S(1)}, u32[]{:S(2)}, u32[]{:S(2)}) collective-permute-start(f32[4,128]{1,0:T(4,128)S(1)} %pad_maximum_fusion.refs_11_), channel_id=1, source_target_pairs={{0,1},{1,0},{2,3},{3,2},{4,5},{5,4},{6,7},{7,6},{8,9},{9,8},{10,11... | collective-permute-start | bytes 6152 | tf_op jit(solution)/shard_map/ppermute | solution.py:36

commit v8 on v6

--- a/solution.py
+++ b/solution.py
@@ -233,24 +233,18 @@
 PARTS = 2
 
 
-def slope_body(pieces, me_ref, *refs):
-    slope_ref, collision_ref, factors_ref, dressed_ref, held_ref, came, gone = refs[-7:]
-    shards = factors_ref.shape[0] + 1
-    early = 1 + (shards - 2) * pieces
-    early_refs, last_refs = refs[:early], refs[early : early + pieces]
-    dressed_refs = refs[early + pieces : early + pieces + shards]
-    trace_refs = refs[early + pieces + shards : early + pieces + 2 * shards]
-    rows = factors_ref.shape[1]
-    block = held_ref.shape[1]
-    steps, length = rows // block, rows // pieces
-    share_blocks = rows // shards // block
-    part = block // PARTS
+def slope_early_body(pieces, *refs):
+    slope_ref, factors_ref, came = refs[-3:]
+    shards, rows = factors_ref.shape[:2]
+    factor_refs, dressed_refs = refs[: 1 + (shards - 1) * pieces], refs[-3 - shards : -3]
+    steps, length = came.shape[0], rows // pieces
+    block = rows // steps
 
     def arrivals(at):
         first = at * block
-        sources = [early_refs[0].at[pl.ds(first, block), :]] + [
-            early_refs[1 + s * pieces + first // length].at[pl.ds(first % length, block), :]
-            for s in range(shards - 2)
+        sources = [factor_refs[0].at[pl.ds(first, block), :]] + [
+            factor_refs[1 + s * pieces + first // length].at[pl.ds(first % length, block), :]
+            for s in range(shards - 1)
         ]
         return [
             pltpu.make_async_copy(
@@ -258,6 +252,49 @@
             )
             for s, source in enumerate(sources)
         ]
+
+    for at in range(steps):
+        for copy in arrivals(at):
+            copy.start()
+    dressed = jnp.concatenate([ref[...] for ref in dressed_refs], axis=0)
+    for at in range(steps):
+        for copy in arrivals(at):
+            copy.wait()
+        here = pl.ds(at * block, block)
+        basis = jnp.concatenate([factors_ref[s, here, :] for s in range(shards)], axis=1)
+        slope_ref[here, :] = jnp.dot(basis, dressed, preferred_element_type=jnp.float32)
+
+
+def slope_early(factors, pieces, dressed):
+    rows, vectors = factors[0].shape
+    columns = dressed[0].shape[1]
+    block = min(rows // pieces, 1024)
+    return pl.pallas_call(
+        functools.partial(slope_early_body, pieces),
+        in_specs=[pl.BlockSpec(memory_space=pltpu.HBM)] * len(factors) + [IN_VMEM] * len(dressed),
+        out_specs=IN_VMEM,
+        out_shape=vmem_shape((rows, columns), jnp.float32),
+        scratch_shapes=[
+            pltpu.VMEM((len(dressed), rows, vectors), jnp.bfloat16),
+            pltpu.SemaphoreType.DMA((rows // block, len(dressed))),
+        ],
+        compiler_params=pltpu.CompilerParams(vmem_limit_bytes=14 * MIB),
+        cost_estimate=FREE,
+    )(*[in_hbm(piece) for piece in factors], *[in_vmem(both) for both in dressed])
+
+
+def slope_body(pieces, *refs):
+    slope_ref, collision_ref, share_ref, held_ref, came, gone = refs[-6:]
+    shards = share_ref.shape[0] + 1
+    count = 1 + (shards - 2) * pieces
+    factor_refs, last_refs = refs[:count], refs[count : count + pieces]
+    early_ref, dressed_ref = refs[count + pieces : count + pieces + 2]
+    trace_refs = refs[count + pieces + 2 : -6]
+    rows, share, block = early_ref.shape[0], share_ref.shape[1], held_ref.shape[1]
+    steps, length = rows // block, rows // pieces
+    per_piece = length // share
+    part = block // PARTS
+    me = lax.axis_index("aux")
 
     def departures(at):
         return [
@@ -269,8 +306,36 @@
             for i in range(PARTS)
         ]
 
+    def arrivals(i):
+        there = pl.ds(pl.multiple_of(me * share, share), share)
+        here = pl.ds(pl.multiple_of((me - i * per_piece) * share, share), share)
+        sources = [factor_refs[0].at[there, :]] + [
+            factor_refs[1 + s * pieces + i].at[here, :] for s in range(shards - 2)
+        ]
+        return [
+            pltpu.make_async_copy(source, share_ref.at[s], came.at[s])
+            for s, source in enumerate(sources)
+        ]
+
+    for i in range(pieces):
+
+        @pl.when(me // per_piece == i)
+        def _():
+            for copy in arrivals(i):
+                copy.start()
+
+    dressed = dressed_ref[...]
     for at in range(steps):
-        for copy in arrivals(at):
+        if at >= SLOTS:
+            for copy in departures(at - SLOTS):
+                copy.wait()
+        first = at * block
+        held_ref[at % SLOTS] = early_ref[pl.ds(first, block), :] + jnp.dot(
+            last_refs[first // length][pl.ds(first % length, block), :],
+            dressed,
+            preferred_element_type=jnp.float32,
+        )
+        for copy in departures(at):
             copy.start()
 
     trace = trace_refs[0][...]
@@ -284,77 +349,58 @@
     thirds = jnp.concatenate(
         [low, middle, high, jnp.zeros((5, row.shape[1]), jnp.float32)], axis=0
     ).astype(jnp.bfloat16)
-    dressed_ref[...] = jnp.concatenate([ref[...] for ref in dressed_refs], axis=0)
-
-    for at in range(steps):
-        for copy in arrivals(at):
-            copy.wait()
-        if at >= SLOTS:
-            for copy in departures(at - SLOTS):
+    for i in range(pieces):
+
+        @pl.when(me // per_piece == i)
+        def _():
+            for copy in arrivals(i):
                 copy.wait()
-        first = at * block
-        basis = jnp.concatenate(
-            [factors_ref[s, pl.ds(first, block), :] for s in range(shards - 1)]
-            + [last_refs[first // length][pl.ds(first % length, block), :]],
-            axis=1,
-        )
-        held_ref[at % SLOTS] = jnp.dot(
-            basis, dressed_ref[...], preferred_element_type=jnp.float32
-        )
-        for copy in departures(at):
-            copy.start()
-
-        @pl.when(me_ref[0] == at // share_blocks)
-        def _():
+            here = pl.ds(pl.multiple_of((me - i * per_piece) * share, share), share)
+            basis = jnp.concatenate(
+                [share_ref[s] for s in range(shards - 1)] + [last_refs[i][here, :]], axis=1
+            )
             parts = lax.dot_general(
                 thirds, basis, (((1,), (1,)), ((), ())), preferred_element_type=jnp.float32
             )
-            there = pl.ds(at % share_blocks * block, block)
-            collision_ref[:, there] = jnp.sum(parts, axis=0, keepdims=True)
+            collision_ref[...] = jnp.sum(parts, axis=0, keepdims=True)
 
     for at in range(max(steps - SLOTS, 0), steps):
         for copy in departures(at):
             copy.wait()
 
 
-def slope(own, steps, dressed, traces):
-    shards, pieces = len(dressed), len(steps[0])
-    rows, vectors = own.shape
-    columns = dressed[0].shape[1]
-    depth = shards * vectors
+def slope(factors, last, early, dressed, traces):
+    pieces, shards = len(last), len(traces)
+    rows, columns = early.shape
+    vectors = dressed.shape[0]
     share = rows // shards
-    block = min(rows // pieces, share, 1024)
+    block = min(rows // pieces, 1024)
     far = pl.BlockSpec(memory_space=pltpu.HBM)
-    early = [own] + [piece for step in steps[:-1] for piece in step]
-    near = [*steps[-1], *dressed, *traces]
     slopes, collision = pl.pallas_call(
         functools.partial(slope_body, pieces),
-        in_specs=[pl.BlockSpec(memory_space=pltpu.SMEM)]
-        + [far] * len(early)
-        + [IN_VMEM] * len(near),
+        in_specs=[far] * len(factors) + [IN_VMEM] * (pieces + 2 + shards),
         out_specs=[far, IN_VMEM],
         scratch_shapes=[
-            pltpu.VMEM((shards - 1, rows, vectors), jnp.bfloat16),
-            pltpu.VMEM((depth, columns), jnp.bfloat16),
+            pltpu.VMEM((shards - 1, share, vectors), jnp.bfloat16),
             pltpu.VMEM((SLOTS, block, columns), jnp.float32),
-            pltpu.SemaphoreType.DMA((rows // block, shards - 1)),
+            pltpu.SemaphoreType.DMA((shards - 1,)),
             pltpu.SemaphoreType.DMA((SLOTS, PARTS)),
         ],
         out_shape=[
             jax.ShapeDtypeStruct((rows, columns), jnp.float32),
             jax.ShapeDtypeStruct((1, share), jnp.float32),
         ],
-        compiler_params=pltpu.CompilerParams(vmem_limit_bytes=28 * MIB),
+        compiler_params=pltpu.CompilerParams(vmem_limit_bytes=20 * MIB),
         cost_estimate=pl.CostEstimate(
-            flops=2 * rows * depth * columns,
-            bytes_accessed=rows * depth * 2 + rows * columns * 4,
+            flops=2 * rows * vectors * columns,
+            bytes_accessed=rows * columns * 4,
             transcendentals=0,
         ),
     )(
-        lax.axis_index("aux").astype(jnp.int32)[None],
-        *[in_hbm(piece) for piece in early],
-        *[in_vmem(piece) for piece in steps[-1]],
-        *[in_vmem(both) for both in dressed],
+        *[in_hbm(piece) for piece in factors],
+        *[in_vmem(piece) for piece in last],
+        in_vmem(early),
+        in_vmem(dressed),
         *traces,
     )
     return slopes, collision.reshape(share)
@@ -390,6 +436,10 @@
         total, pieces = zeros, []
         for i in range(PIECES):
             after = (dressed[-1], traced[-1]) if i == 0 else (total,)
+            if step == aux_size - 1 and i == PIECES - 1:
+                factors = [cholesky_factors] + [one for pair in steps for one in pair]
+                early = slope_early(factors, PIECES, dressed)
+                after += (early,)
             place = in_hbm if step < aux_size - 1 else in_vmem
             piece = gate(shifted(held[i], "aux", 1), place, *after)
             pieces.append(piece)
@@ -404,7 +454,7 @@
 
     trace = jnp.concatenate(traced, axis=0)
     traces = [trace] + [shifted(trace, "aux", shift) for shift in range(1, aux_size)]
-    return slope(cholesky_factors, steps, dressed, traces)
+    return slope(factors, steps[-1], early, dressed[-1], traces)
 
 
 def solution(mesh):

time: 175 us -> 172 us (0.983)
  waiting for transfers between devices: 105 us -> 96.3 us
  local copies, waits for them, and re-layouts: 11.6 us -> 14.8 us
  Pallas kernels: 30.9 us -> 33.9 us
    ppermute x9, waiting for transfers between devices: 71.6 us -> 62.5 us  [shifted(): lax.ppermute(block, axis, [(i, (i + shift) % count) for i in range(count)])]
    pallas_call x1 -> x2, Pallas kernels: 9.66 us -> 13.9 us  [the longest x1 7 us: slope_early(): pl.pallas_call(functools.partial(slope_early_body, pieces), in_specs=[pl....]
    unnamed x21 -> x31, local copies, waits for them, and re-layouts: 11.3 us -> 14.4 us
  transfers between devices with their start and end apart: 29 -> 29, of which waited for: 29 -> 27; matrix products, arithmetic and copies ran while one was open for 1% -> 1% of each run, Pallas kernels for 10% -> 14%
where the time goes in v8:
time: 172 us; the launch traced here: 171 us
  waiting for transfers between devices  96.3 us (56%)
  Pallas kernels  33.9 us (20%)
  starting transfers between devices  24 us (14%)
  local copies, waits for them, and re-layouts  14.8 us (9%)
    ppermute x9, waiting for transfers between devices, shifted(): lax.ppermute(block, axis, [(i, (i + shift) % count) for i in range(count)])  62.5 us
    ppermute x20, waiting for transfers between devices, exchanged(): return lax.ppermute(block, axis, [(i, i ^ bit) for i in range(count)])  33.8 us
    ppermute x20, starting transfers between devices, exchanged(): return lax.ppermute(block, axis, [(i, i ^ bit) for i in range(count)])  14.8 us
    unnamed x31, local copies, waits for them, and re-layouts  14.4 us
    pallas_call x5, Pallas kernels, project(): pl.pallas_call(functools.partial(project_body, first, min(length, 1024)),...  9.57 us
    ppermute x9, starting transfers between devices, shifted(): lax.ppermute(block, axis, [(i, (i + shift) % count) for i in range(count)])  9.18 us
    pallas_call x1, Pallas kernels, slope_early(): pl.pallas_call(functools.partial(slope_early_body, pieces), in_specs=[pl....  7 us
    pallas_call x1, Pallas kernels, slope(): pl.pallas_call(functools.partial(slope_body, pieces), in_specs=[far] * le...  6.91 us
  transfers between devices with their start and end apart: 29, of which 27 were waited for; matrix products, arithmetic and copies ran while one was open for 1% of the time, Pallas kernels for 14%

profile of v8, /device:TPU:0, one launch (start us, length us, event | category | flops | bytes accessed | tf_op | source)
XLA Modules:
  0.0 171.5 jit_solution(7520395553848239558)
XLA Ops:
  0.6 2.4 %shard_map.59 = bf16[4096,128]{1,0:T(8,128)(2,1)} custom-call(bf16[8192,128]{1,0:T(8,128)(2,1)} %refs_0_.5), custom_call_target="tpu_custom_call" | custom-call | tf_op jit(solution)/shard_map/pallas_call | solution.py:88
  3.0 3.1 %collective-permute-start = (bf16[4096,128]{1,0:T(8,128)(2,1)}, bf16[4096,128]{1,0:T(8,128)(2,1)S(1)}, u32[]{:S(2)}, u32[]{:S(2)}) collective-permute-start(bf16[4096,128]{1,0:T(8,128)(2,1)} %shard_map.59), channel_id=1, source_target_pairs={{0,1},{1,2},{2,3},{3,0},{4,5},{5,6},{6,7},{7,4},{8,9},{9,10},{10,1... | collective-permute-start | bytes 3145736 | tf_op jit(solution)/shard_map/ppermute | solution.py:31
  6.1 2.2 %shard_map.66 = bf16[4096,128]{1,0:T(8,128)(2,1)} custom-call(bf16[8192,128]{1,0:T(8,128)(2,1)} %refs_0_.5), custom_call_target="tpu_custom_call" | custom-call | tf_op jit(solution)/shard_map/pallas_call | solution.py:88
  8.3 1.6 collective-permute-start.6
  9.9 3.4 %shard_map.60 = (bf16[8192,512]{1,0:T(8,128)(2,1)S(1)}, f32[256,256]{1,0:T(8,128)S(1)}) custom-call(bf16[8192,512]{1,0:T(8,128)(2,1)} %refs_0_.3, f32[256,256]{1,0:T(8,128)} %refs_1_.1), custom_call_target="tpu_custom_call" | custom-call | tf_op jit(solution)/shard_map/pallas_call | solution.py:68
  13.4 2.8 %shard_map.61 = f32[128,512]{1,0:T(8,128)S(1)} custom-call(bf16[8192,128]{1,0:T(8,128)(2,1)S(1)} %copy-done.2, bf16[8192,512]{1,0:T(8,128)(2,1)S(1)} %get-tuple-element.14.green_ref, f32[128,512]{1,0:T(8,128)S(1)} %broadcast_in_dim.6.acc_ref), custom_call_target="tpu_custom_call" | custom-call | tf_op jit(solution)/shard_map/pallas_call | solution.py:116
  16.2 3.4 %copy-done = bf16[8192,512]{1,0:T(8,128)(2,1)} copy-done((bf16[8192,512]{1,0:T(8,128)(2,1)}, bf16[8192,512]{1,0:T(8,128)(2,1)S(1)}, u32[]{:S(2)}) %copy-start) | copy-done | bytes 8388632
  19.7 1.3 collective-permute-done.1.refs_1_
  21.0 2.5 %collective-permute-start.4 = (f32[64,512]{1,0:T(8,128)S(1)}, f32[64,512]{1,0:T(8,128)S(1)}, u32[]{:S(2)}, u32[]{:S(2)}) collective-permute-start(f32[64,512]{1,0:T(8,128)S(1)} %shard_map.62.refs_0_), channel_id=1, source_target_pairs={{0,24},{4,28},{8,16},{12,20},{16,8},{20,12},{24,0},{28,4},{1,25},{... | collective-permute-start | bytes 393224 | tf_op jit(solution)/shard_map/ppermute | solution.py:36
  24.7 3.1 %collective-permute-done.4.refs_3_ = f32[64,512]{1,0:T(8,128)S(1)} collective-permute-done((f32[64,512]{1,0:T(8,128)S(1)}, f32[64,512]{1,0:T(8,128)S(1)}, u32[]{:S(2)}, u32[]{:S(2)}) %collective-permute-start.4) | collective-permute-done | bytes 131104 | tf_op jit(solution)/shard_map/ppermute | solution.py:36
  27.8 2.5 %collective-permute-done.3.refs_2_ = f32[64,512]{1,0:T(8,128)S(1)} collective-permute-done((f32[64,512]{1,0:T(8,128)S(1)}, f32[64,512]{1,0:T(8,128)S(1)}, u32[]{:S(2)}, u32[]{:S(2)}) %collective-permute-start.3) | collective-permute-done | bytes 131104 | tf_op jit(solution)/shard_map/ppermute | solution.py:36
  31.2 1.0 collective-permute-done.5.other_ref
  32.4 1.0 copy-done.3
  33.4 1.6 collective-permute-start.7
  34.9 3.4 %copy-done.1 = bf16[8192,512]{1,0:T(8,128)(2,1)S(1)} copy-done((bf16[8192,512]{1,0:T(8,128)(2,1)S(1)}, bf16[8192,512]{1,0:T(8,128)(2,1)}, u32[]{:S(2)}) %copy-start.1) | copy-done | bytes 8388632
  38.3 1.2 copy-done.4
  40.5 1.4 shard_map.67.refs_1_.acc_ref
  41.9 13.0 %collective-permute-done.6.refs_0_ = bf16[4096,128]{1,0:T(8,128)(2,1)} collective-permute-done((bf16[4096,128]{1,0:T(8,128)(2,1)}, bf16[4096,128]{1,0:T(8,128)(2,1)}, u32[]{:S(2)}, u32[]{:S(2)}) %collective-permute-start.6) | collective-permute-done | bytes 1048608 | tf_op jit(solution)/shard_map/ppermute | solution.py:31
  54.9 2.8 %shard_map.69 = f32[128,512]{1,0:T(8,128)S(1)} custom-call(bf16[4096,128]{1,0:T(8,128)(2,1)} %shard_map.68.piece_ref.refs_2_, bf16[8192,512]{1,0:T(8,128)(2,1)S(1)} %copy-done.1, f32[128,512]{1,0:T(8,128)S(1)} %shard_map.67.refs_1_.acc_ref), custom_call_target="tpu_custom_call" | custom-call | tf_op jit(solution)/shard_map/pallas_call | solution.py:116
  57.8 1.3 collective-permute-done.8.refs_1_
  59.1 2.7 %collective-permute-start.11 = (f32[64,512]{1,0:T(8,128)S(1)}, f32[64,512]{1,0:T(8,128)S(1)}, u32[]{:S(2)}, u32[]{:S(2)}) collective-permute-start(f32[64,512]{1,0:T(8,128)S(1)} %shard_map.70.refs_0_), channel_id=1, source_target_pairs={{0,24},{4,28},{8,16},{12,20},{16,8},{20,12},{24,0},{28,4},{1,25},{... | collective-permute-start | bytes 393224 | tf_op jit(solution)/shard_map/ppermute | solution.py:36
  62.7 3.1 %collective-permute-done.11.refs_3_ = f32[64,512]{1,0:T(8,128)S(1)} collective-permute-done((f32[64,512]{1,0:T(8,128)S(1)}, f32[64,512]{1,0:T(8,128)S(1)}, u32[]{:S(2)}, u32[]{:S(2)}) %collective-permute-start.11) | collective-permute-done | bytes 131104 | tf_op jit(solution)/shard_map/ppermute | solution.py:36
  65.8 2.7 %collective-permute-done.10.refs_2_ = f32[64,512]{1,0:T(8,128)S(1)} collective-permute-done((f32[64,512]{1,0:T(8,128)S(1)}, f32[64,512]{1,0:T(8,128)S(1)}, u32[]{:S(2)}, u32[]{:S(2)}) %collective-permute-start.10) | collective-permute-done | bytes 131104 | tf_op jit(solution)/shard_map/ppermute | solution.py:36
  69.3 1.2 collective-permute-done.12.other_ref
  70.7 6.6 %collective-permute-done.7.refs_0_ = bf16[4096,128]{1,0:T(8,128)(2,1)S(1)} collective-permute-done((bf16[4096,128]{1,0:T(8,128)(2,1)}, bf16[4096,128]{1,0:T(8,128)(2,1)S(1)}, u32[]{:S(2)}, u32[]{:S(2)}) %collective-permute-start.7) | collective-permute-done | bytes 1048608 | tf_op jit(solution)/shard_map/ppermute | solution.py:31
  77.2 1.0 copy-done.5
  78.3 1.2 copy-done.6
  79.5 1.3 shard_map.74.refs_1_.acc_ref
  80.8 18.9 %collective-permute-done.13.refs_0_ = bf16[4096,128]{1,0:T(8,128)(2,1)S(1)} collective-permute-done((bf16[4096,128]{1,0:T(8,128)(2,1)}, bf16[4096,128]{1,0:T(8,128)(2,1)S(1)}, u32[]{:S(2)}, u32[]{:S(2)}) %collective-permute-start.13) | collective-permute-done | bytes 1048608 | tf_op jit(solution)/shard_map/ppermute | solution.py:31
  99.7 1.0 copy-done.7
  100.7 1.3 copy-done.8
  102.0 1.3 shard_map.76
  103.4 1.3 collective-permute-done.15.refs_1_
  104.8 2.7 %collective-permute-start.18 = (f32[64,512]{1,0:T(8,128)S(1)}, f32[64,512]{1,0:T(8,128)S(1)}, u32[]{:S(2)}, u32[]{:S(2)}) collective-permute-start(f32[64,512]{1,0:T(8,128)S(1)} %shard_map.77.refs_0_), channel_id=1, source_target_pairs={{0,24},{4,28},{8,16},{12,20},{16,8},{20,12},{24,0},{28,4},{1,25},{... | collective-permute-start | bytes 393224 | tf_op jit(solution)/shard_map/ppermute | solution.py:36
  108.4 3.1 %collective-permute-done.18.refs_3_ = f32[64,512]{1,0:T(8,128)S(1)} collective-permute-done((f32[64,512]{1,0:T(8,128)S(1)}, f32[64,512]{1,0:T(8,128)S(1)}, u32[]{:S(2)}, u32[]{:S(2)}) %collective-permute-start.18) | collective-permute-done | bytes 131104 | tf_op jit(solution)/shard_map/ppermute | solution.py:36
  111.4 2.7 %collective-permute-done.17.refs_2_ = f32[64,512]{1,0:T(8,128)S(1)} collective-permute-done((f32[64,512]{1,0:T(8,128)S(1)}, f32[64,512]{1,0:T(8,128)S(1)}, u32[]{:S(2)}, u32[]{:S(2)}) %collective-permute-start.17) | collective-permute-done | bytes 131104 | tf_op jit(solution)/shard_map/ppermute | solution.py:36
  114.9 1.2 collective-permute-done.19.other_ref
  116.3 7.0 %shard_map.81.refs_2_.refs_7_ = f32[8192,512]{1,0:T(8,128)S(1)} custom-call(bf16[8192,128]{1,0:T(8,128)(2,1)} %refs_0_.5, bf16[4096,128]{1,0:T(8,128)(2,1)} %shard_map.65.piece_ref.refs_1_, bf16[4096,128]{1,0:T(8,128)(2,1)} %shard_map.68.piece_ref.refs_2_, bf16[4096,128]{1,0:T(8,128)(2,1)} %shard_map.73.piece_ref.refs_3_, ...), custom_call_target="tpu_custom_call" | custom-call | tf_op jit(solution)/shard_map/pallas_call | solution.py:272
  124.1 19.7 %collective-permute-done.20.refs_0_ = bf16[4096,128]{1,0:T(8,128)(2,1)S(1)} collective-permute-done((bf16[4096,128]{1,0:T(8,128)(2,1)}, bf16[4096,128]{1,0:T(8,128)(2,1)S(1)}, u32[]{:S(2)}, u32[]{:S(2)}) %collective-permute-start.20) | collective-permute-done | bytes 1048608 | tf_op jit(solution)/shard_map/ppermute | solution.py:31
  144.7 1.3 collective-permute-done.21.refs_1_
  146.0 2.5 %collective-permute-start.24 = (f32[64,512]{1,0:T(8,128)S(1)}, f32[64,512]{1,0:T(8,128)S(1)}, u32[]{:S(2)}, u32[]{:S(2)}) collective-permute-start(f32[64,512]{1,0:T(8,128)S(1)} %shard_map.83.refs_0_), channel_id=1, source_target_pairs={{0,24},{4,28},{8,16},{12,20},{16,8},{20,12},{24,0},{28,4},{1,25},{... | collective-permute-start | bytes 393224 | tf_op jit(solution)/shard_map/ppermute | solution.py:36
  149.6 3.2 %collective-permute-done.24.refs_3_ = f32[64,512]{1,0:T(8,128)S(1)} collective-permute-done((f32[64,512]{1,0:T(8,128)S(1)}, f32[64,512]{1,0:T(8,128)S(1)}, u32[]{:S(2)}, u32[]{:S(2)}) %collective-permute-start.24) | collective-permute-done | bytes 131104 | tf_op jit(solution)/shard_map/ppermute | solution.py:36
  152.8 2.5 %collective-permute-done.23.refs_2_ = f32[64,512]{1,0:T(8,128)S(1)} collective-permute-done((f32[64,512]{1,0:T(8,128)S(1)}, f32[64,512]{1,0:T(8,128)S(1)}, u32[]{:S(2)}, u32[]{:S(2)}) %collective-permute-start.23) | collective-permute-done | bytes 131104 | tf_op jit(solution)/shard_map/ppermute | solution.py:36
  156.0 1.2 collective-permute-done.25.other_ref
  157.4 1.8 %collective-permute-start.28 = (f32[4,128]{1,0:T(4,128)S(1)}, f32[4,128]{1,0:T(4,128)S(1)}, u32[]{:S(2)}, u32[]{:S(2)}) collective-permute-start(f32[4,128]{1,0:T(4,128)S(1)} %pad_maximum_fusion.refs_9_), channel_id=1, source_target_pairs={{0,3},{1,0},{2,1},{3,2},{4,7},{5,4},{6,5},{7,6},{8,11},{9,8},{10,9... | collective-permute-start | bytes 6152 | tf_op jit(solution)/shard_map/ppermute | solution.py:31
  159.2 1.0 collective-permute-start.26
  161.0 2.6 %collective-permute-done.27.refs_11_ = f32[4,128]{1,0:T(4,128)S(1)} collective-permute-done((f32[4,128]{1,0:T(4,128)S(1)}, f32[4,128]{1,0:T(4,128)S(1)}, u32[]{:S(2)}, u32[]{:S(2)}) %collective-permute-start.27) | collective-permute-done | bytes 2080 | tf_op jit(solution)/shard_map/ppermute | solution.py:31
  164.6 6.9 %shard_map.86 = (f32[8192,512]{1,0:T(8,128)}, f32[1,2048]{1,0:T(1,128)}) custom-call(bf16[8192,128]{1,0:T(8,128)(2,1)} %refs_0_.5, bf16[4096,128]{1,0:T(8,128)(2,1)} %shard_map.65.piece_ref.refs_1_, bf16[4096,128]{1,0:T(8,128)(2,1)} %shard_map.68.piece_ref.refs_2_, bf16[4096,128]{1,0:T(8,128)(2,1)} %shard_map.73.piece_ref.refs_3_, ...), custom_call_target="tpu_custom_call" | custom-call | flops 1073741824 | bytes 16777216 | tf_op jit(solution)/shard_map/pallas_call | solution.py:379
  (81 shorter events, 12.2 us)
Async XLA Ops:
  0.6 12.7 %copy-start.2 = (bf16[8192,128]{1,0:T(8,128)(2,1)S(1)}, bf16[8192,128]{1,0:T(8,128)(2,1)}, u32[]{:S(2)}) copy-start(bf16[8192,128]{1,0:T(8,128)(2,1)} %refs_0_.5) | copy-start | bytes 6291460
  3.0 29.4 %collective-permute-start = (bf16[4096,128]{1,0:T(8,128)(2,1)}, bf16[4096,128]{1,0:T(8,128)(2,1)S(1)}, u32[]{:S(2)}, u32[]{:S(2)}) collective-permute-start(bf16[4096,128]{1,0:T(8,128)(2,1)} %shard_map.59), channel_id=1, source_target_pairs={{0,1},{1,2},{2,3},{3,0},{4,5},{5,6},{6,7},{7,4},{8,9},{9,10},{10,1... | collective-permute-start | bytes 3145736 | tf_op jit(solution)/shard_map/ppermute | solution.py:31
  8.3 46.6 %collective-permute-start.6 = (bf16[4096,128]{1,0:T(8,128)(2,1)}, bf16[4096,128]{1,0:T(8,128)(2,1)}, u32[]{:S(2)}, u32[]{:S(2)}) collective-permute-start(bf16[4096,128]{1,0:T(8,128)(2,1)} %shard_map.66), channel_id=1, source_target_pairs={{0,1},{1,2},{2,3},{3,0},{4,5},{5,6},{6,7},{7,4},{8,9},{9,10},{10,1... | collective-permute-start | bytes 3145736 | tf_op jit(solution)/shard_map/ppermute | solution.py:31
  9.9 14.7 %copy-start.12 = (f32[512]{0:T(512)S(1)}, f32[512]{0:T(512)}, u32[]{:S(2)}) copy-start(f32[512]{0:T(512)} %param.7) | copy-start | bytes 6148
  13.4 2.8 %copy-start.9 = (f32[128,512]{1,0:T(8,128)}, f32[128,512]{1,0:T(8,128)S(1)}, u32[]{:S(2)}) copy-start(f32[128,512]{1,0:T(8,128)S(1)} %broadcast_in_dim.6.acc_ref) | copy-start | bytes 786436
  16.2 3.4 %copy-start = (bf16[8192,512]{1,0:T(8,128)(2,1)}, bf16[8192,512]{1,0:T(8,128)(2,1)S(1)}, u32[]{:S(2)}) copy-start(bf16[8192,512]{1,0:T(8,128)(2,1)S(1)} %get-tuple-element.14.green_ref) | copy-start | bytes 25165828
  19.6 1.4 collective-permute-start.1
  21.0 6.8 %collective-permute-start.4 = (f32[64,512]{1,0:T(8,128)S(1)}, f32[64,512]{1,0:T(8,128)S(1)}, u32[]{:S(2)}, u32[]{:S(2)}) collective-permute-start(f32[64,512]{1,0:T(8,128)S(1)} %shard_map.62.refs_0_), channel_id=1, source_target_pairs={{0,24},{4,28},{8,16},{12,20},{16,8},{20,12},{24,0},{28,4},{1,25},{... | collective-permute-start | bytes 393224 | tf_op jit(solution)/shard_map/ppermute | solution.py:36
  23.6 6.8 %collective-permute-start.3 = (f32[64,512]{1,0:T(8,128)S(1)}, f32[64,512]{1,0:T(8,128)S(1)}, u32[]{:S(2)}, u32[]{:S(2)}) collective-permute-start(f32[64,512]{1,0:T(8,128)S(1)} %shard_map.62.refs_0_), channel_id=1, source_target_pairs={{0,16},{4,20},{8,24},{12,28},{16,0},{20,4},{24,8},{28,12},{1,17},{... | collective-permute-start | bytes 393224 | tf_op jit(solution)/shard_map/ppermute | solution.py:36
  24.1 6.4 %collective-permute-start.2 = (f32[64,512]{1,0:T(8,128)S(1)}, f32[64,512]{1,0:T(8,128)S(1)}, u32[]{:S(2)}, u32[]{:S(2)}) collective-permute-start(f32[64,512]{1,0:T(8,128)S(1)} %shard_map.62.refs_0_), channel_id=1, source_target_pairs={{0,8},{4,12},{8,0},{12,4},{16,24},{20,28},{24,16},{28,20},{1,9},{5... | collective-permute-start | bytes 393224 | tf_op jit(solution)/shard_map/ppermute | solution.py:36
  30.9 1.3 collective-permute-start.5
  32.4 1.0 copy-start.3
  33.4 43.9 %collective-permute-start.7 = (bf16[4096,128]{1,0:T(8,128)(2,1)}, bf16[4096,128]{1,0:T(8,128)(2,1)S(1)}, u32[]{:S(2)}, u32[]{:S(2)}) collective-permute-start(bf16[4096,128]{1,0:T(8,128)(2,1)} %shard_map.65.piece_ref.refs_1_), channel_id=1, source_target_pairs={{0,1},{1,2},{2,3},{3,0},{4,5},{5,6},{6,7},{7,4},{8,9},{9,10},{10,1... | collective-permute-start | bytes 3145736 | tf_op jit(solution)/shard_map/ppermute | solution.py:31
  34.9 3.4 %copy-start.1 = (bf16[8192,512]{1,0:T(8,128)(2,1)S(1)}, bf16[8192,512]{1,0:T(8,128)(2,1)}, u32[]{:S(2)}) copy-start(bf16[8192,512]{1,0:T(8,128)(2,1)} %copy-done) | copy-start | bytes 25165828
  38.3 1.2 copy-start.4
  39.5 0.9 copy-start.10
  41.9 36.4 %slice-start = ((s8[8388608]{0:T(1024)(128)(4,1)}), s8[4194304]{0:T(1024)(128)(4,1)S(1)}, s32[]{:S(2)}) async-start(s8[8388608]{0:T(1024)(128)(4,1)} %bitcast.9), calls=%async_computation | async-start | bytes 8388608
  41.9 36.4 %copy-start.11 = (f32[128,512]{1,0:T(8,128)S(1)}, f32[128,512]{1,0:T(8,128)}, u32[]{:S(2)}) copy-start(f32[128,512]{1,0:T(8,128)} %copy-done.9) | copy-start | bytes 786436
  54.9 23.4 %slice-start.1 = ((s8[8388608]{0:T(1024)(128)(4,1)}), s8[4194304]{0:T(1024)(128)(4,1)S(1)}, s32[]{:S(2)}) async-start(s8[8388608]{0:T(1024)(128)(4,1)} %bitcast.9), calls=%async_computation.1 | async-start | bytes 8388608
  54.9 44.8 %collective-permute-start.13 = (bf16[4096,128]{1,0:T(8,128)(2,1)}, bf16[4096,128]{1,0:T(8,128)(2,1)S(1)}, u32[]{:S(2)}, u32[]{:S(2)}) collective-permute-start(bf16[4096,128]{1,0:T(8,128)(2,1)} %shard_map.68.piece_ref.refs_2_), channel_id=1, source_target_pairs={{0,1},{1,2},{2,3},{3,0},{4,5},{5,6},{6,7},{7,4},{8,9},{9,10},{10,1... | collective-permute-start | bytes 3145736 | tf_op jit(solution)/shard_map/ppermute | solution.py:31
  57.7 1.4 collective-permute-start.8
  59.1 6.7 %collective-permute-start.11 = (f32[64,512]{1,0:T(8,128)S(1)}, f32[64,512]{1,0:T(8,128)S(1)}, u32[]{:S(2)}, u32[]{:S(2)}) collective-permute-start(f32[64,512]{1,0:T(8,128)S(1)} %shard_map.70.refs_0_), channel_id=1, source_target_pairs={{0,24},{4,28},{8,16},{12,20},{16,8},{20,12},{24,0},{28,4},{1,25},{... | collective-permute-start | bytes 393224 | tf_op jit(solution)/shard_map/ppermute | solution.py:36
  61.9 6.6 %collective-permute-start.10 = (f32[64,512]{1,0:T(8,128)S(1)}, f32[64,512]{1,0:T(8,128)S(1)}, u32[]{:S(2)}, u32[]{:S(2)}) collective-permute-start(f32[64,512]{1,0:T(8,128)S(1)} %shard_map.70.refs_0_), channel_id=1, source_target_pairs={{0,16},{4,20},{8,24},{12,28},{16,0},{20,4},{24,8},{28,12},{1,17},{... | collective-permute-start | bytes 393224 | tf_op jit(solution)/shard_map/ppermute | solution.py:36
  62.4 6.4 %collective-permute-start.9 = (f32[64,512]{1,0:T(8,128)S(1)}, f32[64,512]{1,0:T(8,128)S(1)}, u32[]{:S(2)}, u32[]{:S(2)}) collective-permute-start(f32[64,512]{1,0:T(8,128)S(1)} %shard_map.70.refs_0_), channel_id=1, source_target_pairs={{0,8},{4,12},{8,0},{12,4},{16,24},{20,28},{24,16},{28,20},{1,9},{5... | collective-permute-start | bytes 393224 | tf_op jit(solution)/shard_map/ppermute | solution.py:36
  69.2 1.3 collective-permute-start.12
  77.2 1.0 copy-start.5
  78.2 45.1 %collective-permute-start.14 = (bf16[4096,128]{1,0:T(8,128)(2,1)}, bf16[4096,128]{1,0:T(8,128)(2,1)S(1)}, u32[]{:S(2)}, u32[]{:S(2)}) collective-permute-start(bf16[4096,128]{1,0:T(8,128)(2,1)} %shard_map.73.piece_ref.refs_3_), channel_id=1, source_target_pairs={{0,1},{1,2},{2,3},{3,0},{4,5},{5,6},{6,7},{7,4},{8,9},{9,10},{10,1... | collective-permute-start | bytes 3145736 | tf_op jit(solution)/shard_map/ppermute | solution.py:31
  78.3 1.3 copy-start.6
  99.7 1.0 copy-start.7
  100.7 43.1 %collective-permute-start.20 = (bf16[4096,128]{1,0:T(8,128)(2,1)}, bf16[4096,128]{1,0:T(8,128)(2,1)S(1)}, u32[]{:S(2)}, u32[]{:S(2)}) collective-permute-start(bf16[4096,128]{1,0:T(8,128)(2,1)} %shard_map.75.piece_ref.refs_4_), channel_id=1, source_target_pairs={{0,1},{1,2},{2,3},{3,0},{4,5},{5,6},{6,7},{7,4},{8,9},{9,10},{10,1... | collective-permute-start | bytes 3145736 | tf_op jit(solution)/shard_map/ppermute | solution.py:31
  100.7 1.3 copy-start.8
  103.4 1.4 collective-permute-start.15
  104.8 6.6 %collective-permute-start.18 = (f32[64,512]{1,0:T(8,128)S(1)}, f32[64,512]{1,0:T(8,128)S(1)}, u32[]{:S(2)}, u32[]{:S(2)}) collective-permute-start(f32[64,512]{1,0:T(8,128)S(1)} %shard_map.77.refs_0_), channel_id=1, source_target_pairs={{0,24},{4,28},{8,16},{12,20},{16,8},{20,12},{24,0},{28,4},{1,25},{... | collective-permute-start | bytes 393224 | tf_op jit(solution)/shard_map/ppermute | solution.py:36
  107.5 6.6 %collective-permute-start.17 = (f32[64,512]{1,0:T(8,128)S(1)}, f32[64,512]{1,0:T(8,128)S(1)}, u32[]{:S(2)}, u32[]{:S(2)}) collective-permute-start(f32[64,512]{1,0:T(8,128)S(1)} %shard_map.77.refs_0_), channel_id=1, source_target_pairs={{0,16},{4,20},{8,24},{12,28},{16,0},{20,4},{24,8},{28,12},{1,17},{... | collective-permute-start | bytes 393224 | tf_op jit(solution)/shard_map/ppermute | solution.py:36
  108.0 6.4 %collective-permute-start.16 = (f32[64,512]{1,0:T(8,128)S(1)}, f32[64,512]{1,0:T(8,128)S(1)}, u32[]{:S(2)}, u32[]{:S(2)}) collective-permute-start(f32[64,512]{1,0:T(8,128)S(1)} %shard_map.77.refs_0_), channel_id=1, source_target_pairs={{0,8},{4,12},{8,0},{12,4},{16,24},{20,28},{24,16},{28,20},{1,9},{5... | collective-permute-start | bytes 393224 | tf_op jit(solution)/shard_map/ppermute | solution.py:36
  114.9 1.3 collective-permute-start.19
  144.6 1.4 collective-permute-start.21
  146.0 6.8 %collective-permute-start.24 = (f32[64,512]{1,0:T(8,128)S(1)}, f32[64,512]{1,0:T(8,128)S(1)}, u32[]{:S(2)}, u32[]{:S(2)}) collective-permute-start(f32[64,512]{1,0:T(8,128)S(1)} %shard_map.83.refs_0_), channel_id=1, source_target_pairs={{0,24},{4,28},{8,16},{12,20},{16,8},{20,12},{24,0},{28,4},{1,25},{... | collective-permute-start | bytes 393224 | tf_op jit(solution)/shard_map/ppermute | solution.py:36
  148.6 6.8 %collective-permute-start.23 = (f32[64,512]{1,0:T(8,128)S(1)}, f32[64,512]{1,0:T(8,128)S(1)}, u32[]{:S(2)}, u32[]{:S(2)}) collective-permute-start(f32[64,512]{1,0:T(8,128)S(1)} %shard_map.83.refs_0_), channel_id=1, source_target_pairs={{0,16},{4,20},{8,24},{12,28},{16,0},{20,4},{24,8},{28,12},{1,17},{... | collective-permute-start | bytes 393224 | tf_op jit(solution)/shard_map/ppermute | solution.py:36
  149.1 6.4 %collective-permute-start.22 = (f32[64,512]{1,0:T(8,128)S(1)}, f32[64,512]{1,0:T(8,128)S(1)}, u32[]{:S(2)}, u32[]{:S(2)}) collective-permute-start(f32[64,512]{1,0:T(8,128)S(1)} %shard_map.83.refs_0_), channel_id=1, source_target_pairs={{0,8},{4,12},{8,0},{12,4},{16,24},{20,28},{24,16},{28,20},{1,9},{5... | collective-permute-start | bytes 393224 | tf_op jit(solution)/shard_map/ppermute | solution.py:36
  155.9 1.3 collective-permute-start.25
  157.4 3.6 %collective-permute-start.28 = (f32[4,128]{1,0:T(4,128)S(1)}, f32[4,128]{1,0:T(4,128)S(1)}, u32[]{:S(2)}, u32[]{:S(2)}) collective-permute-start(f32[4,128]{1,0:T(4,128)S(1)} %pad_maximum_fusion.refs_9_), channel_id=1, source_target_pairs={{0,3},{1,0},{2,1},{3,2},{4,7},{5,4},{6,5},{7,6},{8,11},{9,8},{10,9... | collective-permute-start | bytes 6152 | tf_op jit(solution)/shard_map/ppermute | solution.py:31
  159.2 4.5 %collective-permute-start.27 = (f32[4,128]{1,0:T(4,128)S(1)}, f32[4,128]{1,0:T(4,128)S(1)}, u32[]{:S(2)}, u32[]{:S(2)}) collective-permute-start(f32[4,128]{1,0:T(4,128)S(1)} %pad_maximum_fusion.refs_9_), channel_id=1, source_target_pairs={{0,2},{1,3},{2,0},{3,1},{4,6},{5,7},{6,4},{7,5},{8,10},{9,11},{10,... | collective-permute-start | bytes 6152 | tf_op jit(solution)/shard_map/ppermute | solution.py:31
  159.2 5.4 %collective-permute-start.26 = (f32[4,128]{1,0:T(4,128)S(1)}, f32[4,128]{1,0:T(4,128)S(1)}, u32[]{:S(2)}, u32[]{:S(2)}) collective-permute-start(f32[4,128]{1,0:T(4,128)S(1)} %pad_maximum_fusion.refs_9_), channel_id=1, source_target_pairs={{0,1},{1,2},{2,3},{3,0},{4,5},{5,6},{6,7},{7,4},{8,9},{9,10},{10,1... | collective-permute-start | bytes 6152 | tf_op jit(solution)/shard_map/ppermute | solution.py:31

commit v9 on v8

--- a/solution.py
+++ b/solution.py
@@ -34,6 +34,24 @@
 def exchanged(block, axis, bit):
     count = lax.axis_size(axis)
     return lax.ppermute(block, axis, [(i, i ^ bit) for i in range(count)])
+
+
+def gather_traces(trace):
+    rows, count = lax.axis_size("rows"), lax.axis_size("aux")
+    pairs = []
+    for first in range(1, count, 2):
+        shifts = [first, min(first + 1, count - 1)]
+        came = lax.ppermute(
+            trace,
+            ("rows", "aux"),
+            [
+                (row * count + i, row * count + (i + shifts[row % 2]) % count)
+                for row in range(rows)
+                for i in range(count)
+            ],
+        )
+        pairs.append([came] if shifts[0] == shifts[1] else [came, exchanged(came, "rows", 1)])
+    return [trace] + [array for pair in pairs for array in pair]
 
 
 def gate_body(*refs):
@@ -74,26 +92,6 @@
         compiler_params=pltpu.CompilerParams(vmem_limit_bytes=2 * MIB),
         cost_estimate=FREE,
     )(*[in_hbm(array) for array in arrays])
-
-
-def cut_body(first, array_ref, piece_ref, semaphore):
-    move = pltpu.make_async_copy(
-        array_ref.at[pl.ds(first, piece_ref.shape[0]), :], piece_ref, semaphore
-    )
-    move.start()
-    move.wait()
-
-
-def cut(array, first, length):
-    return pl.pallas_call(
-        functools.partial(cut_body, first),
-        out_shape=vmem_shape((length,) + array.shape[1:], array.dtype),
-        in_specs=[pl.BlockSpec(memory_space=pltpu.HBM)],
-        out_specs=IN_VMEM,
-        scratch_shapes=[pltpu.SemaphoreType.DMA],
-        compiler_params=pltpu.CompilerParams(vmem_limit_bytes=2 * MIB),
-        cost_estimate=FREE,
-    )(in_hbm(array))
 
 
 def project_body(first, block, piece_ref, green_ref, acc_ref, total_ref):
@@ -338,10 +336,14 @@
         for copy in departures(at):
             copy.start()
 
+    odd = lax.rem(lax.axis_index("rows"), 2) == 1
     trace = trace_refs[0][...]
     for shift in range(1, shards):
-        other = trace_refs[shift][...]
-        trace = trace + jnp.concatenate([other[shards - shift :], other[: shards - shift]], axis=0)
+        theirs = trace_refs[shift][...]
+        pair = (shift - 1) // 2 * 2 + 1
+        if pair + 1 < shards:
+            theirs = jnp.where(odd == (shift > pair), trace_refs[pair][...], trace_refs[pair + 1][...])
+        trace = trace + jnp.concatenate([theirs[shards - shift :], theirs[: shards - shift]], axis=0)
     row = jnp.concatenate([trace[s : s + 1] for s in range(shards)], axis=1)
     high = row.astype(jnp.bfloat16).astype(jnp.float32)
     middle = (row - high).astype(jnp.bfloat16).astype(jnp.float32)
@@ -429,7 +431,12 @@
         dressed.append(both)
         traced.append(trace)
 
-    held = [cut(cholesky_factors, i * length, length) for i in range(PIECES)]
+    held = [
+        gate(
+            lax.slice_in_dim(cholesky_factors, i * length, (i + 1) * length, axis=0), in_vmem
+        )
+        for i in range(PIECES)
+    ]
     finish(0, project(cholesky_factors, green, 0, zeros))
     steps = []
     for step in range(1, aux_size):
@@ -453,7 +460,7 @@
         finish(step, total)
 
     trace = jnp.concatenate(traced, axis=0)
-    traces = [trace] + [shifted(trace, "aux", shift) for shift in range(1, aux_size)]
+    traces = gather_traces(trace)
     return slope(factors, steps[-1], early, dressed[-1], traces)
 
 

time: 172 us -> 172 us (level)
  Pallas kernels: 33.9 us -> 29.3 us
  local copies, waits for them, and re-layouts: 14.8 us -> 17.9 us
  waiting for transfers between devices: 96.3 us -> 98.4 us
    pallas_call x2 -> x0, Pallas kernels: 4.56 us -> none  [cut(): pl.pallas_call(functools.partial(cut_body, first), out_shape=vmem_shape((...]
    ppermute x9 -> x6, starting transfers between devices: 9.18 us -> 4.74 us  [shifted(): lax.ppermute(block, axis, [(i, (i + shift) % count) for i in range(count)])]
    ppermute x0 -> x2, starting transfers between devices: none -> 3.87 us  [gather_traces(): lax.ppermute(trace, ('rows', 'aux'), [(row * count + i, row * count + (i...]
    slice x0 -> x1, local copies, waits for them, and re-layouts: none -> 3.13 us  [local(): lax.slice_in_dim(cholesky_factors, i * length, (i + 1) * length, axis=0)]
    ppermute x20 -> x21, waiting for transfers between devices: 33.8 us -> 35 us  [exchanged(): return lax.ppermute(block, axis, [(i, i ^ bit) for i in range(count)])]
    ppermute x9 -> x6, waiting for transfers between devices: 62.5 us -> 61.9 us  [shifted(): lax.ppermute(block, axis, [(i, (i + shift) % count) for i in range(count)])]
    ppermute x20 -> x21, starting transfers between devices: 14.8 us -> 14.8 us  [exchanged(): return lax.ppermute(block, axis, [(i, i ^ bit) for i in range(count)])]
  transfers between devices with their start and end apart: 29 -> 29, of which waited for: 27 -> 27; matrix products, arithmetic and copies ran while one was open for 1% -> 1% of each run, Pallas kernels for 14% -> 13%
where the time goes in v9:
time: 172 us
  waiting for transfers between devices  98.4 us (57%)
  Pallas kernels  29.3 us (17%)
  starting transfers between devices  23.4 us (14%)
  local copies, waits for them, and re-layouts  17.9 us (10%)
    ppermute x6, waiting for transfers between devices, shifted(): lax.ppermute(block, axis, [(i, (i + shift) % count) for i in range(count)])  61.9 us
    ppermute x21, waiting for transfers between devices, exchanged(): return lax.ppermute(block, axis, [(i, i ^ bit) for i in range(count)])  35 us
    ppermute x21, starting transfers between devices, exchanged(): return lax.ppermute(block, axis, [(i, i ^ bit) for i in range(count)])  14.8 us
    unnamed x31, local copies, waits for them, and re-layouts  14.4 us
    pallas_call x5, Pallas kernels, project(): pl.pallas_call(functools.partial(project_body, first, min(length, 1024)),...  9.59 us
    pallas_call x1, Pallas kernels, slope_early(): pl.pallas_call(functools.partial(slope_early_body, pieces), in_specs=[pl....  7 us
    pallas_call x1, Pallas kernels, slope(): pl.pallas_call(functools.partial(slope_body, pieces), in_specs=[far] * le...  6.91 us
    ppermute x6, starting transfers between devices, shifted(): lax.ppermute(block, axis, [(i, (i + shift) % count) for i in range(count)])  4.74 us
  transfers between devices with their start and end apart: 29, of which 27 were waited for; matrix products, arithmetic and copies ran while one was open for 1% of the time, Pallas kernels for 13%

profile of v9, /device:TPU:0, one launch (start us, length us, event | category | flops | bytes accessed | tf_op | source)
XLA Modules:
  0.0 171.8 jit_solution(10930570979500678762)
XLA Ops:
  0.6 3.1 %fusion.7 = (bf16[4096,128]{1,0:T(8,128)(2,1)}, bf16[4096,128]{1,0:T(8,128)(2,1)}) fusion(bf16[8192,128]{1,0:T(8,128)(2,1)} %refs_0_.5), kind=kLoop, calls=%fused_computation.15 | loop fusion | bytes 4194304 | tf_op jit(solution)/shard_map/slice | solution.py:436
  3.8 3.0 %collective-permute-start = (bf16[4096,128]{1,0:T(8,128)(2,1)}, bf16[4096,128]{1,0:T(8,128)(2,1)S(1)}, u32[]{:S(2)}, u32[]{:S(2)}) collective-permute-start(bf16[4096,128]{1,0:T(8,128)(2,1)} %shard_map.59), channel_id=1, source_target_pairs={{0,1},{1,2},{2,3},{3,0},{4,5},{5,6},{6,7},{7,4},{8,9},{9,10},{10,1... | collective-permute-start | bytes 3145736 | tf_op jit(solution)/shard_map/ppermute | solution.py:31
  6.8 1.6 collective-permute-start.6
  8.4 3.4 %shard_map.60 = (bf16[8192,512]{1,0:T(8,128)(2,1)S(1)}, f32[256,256]{1,0:T(8,128)S(1)}) custom-call(bf16[8192,512]{1,0:T(8,128)(2,1)} %refs_0_.3, f32[256,256]{1,0:T(8,128)} %refs_1_.1), custom_call_target="tpu_custom_call" | custom-call | tf_op jit(solution)/shard_map/pallas_call | solution.py:86
  11.8 2.8 %shard_map.61 = f32[128,512]{1,0:T(8,128)S(1)} custom-call(bf16[8192,128]{1,0:T(8,128)(2,1)S(1)} %copy-done.2, bf16[8192,512]{1,0:T(8,128)(2,1)S(1)} %get-tuple-element.14.green_ref, f32[128,512]{1,0:T(8,128)S(1)} %broadcast_in_dim.6.acc_ref), custom_call_target="tpu_custom_call" | custom-call | tf_op jit(solution)/shard_map/pallas_call | solution.py:114
  14.7 3.4 %copy-done = bf16[8192,512]{1,0:T(8,128)(2,1)} copy-done((bf16[8192,512]{1,0:T(8,128)(2,1)}, bf16[8192,512]{1,0:T(8,128)(2,1)S(1)}, u32[]{:S(2)}) %copy-start) | copy-done | bytes 8388632
  18.1 1.3 collective-permute-done.1.refs_1_
  19.5 2.5 %collective-permute-start.4 = (f32[64,512]{1,0:T(8,128)S(1)}, f32[64,512]{1,0:T(8,128)S(1)}, u32[]{:S(2)}, u32[]{:S(2)}) collective-permute-start(f32[64,512]{1,0:T(8,128)S(1)} %shard_map.62.refs_0_), channel_id=1, source_target_pairs={{0,24},{4,28},{8,16},{12,20},{16,8},{20,12},{24,0},{28,4},{1,25},{... | collective-permute-start | bytes 393224 | tf_op jit(solution)/shard_map/ppermute | solution.py:36
  23.2 3.1 %collective-permute-done.4.refs_3_ = f32[64,512]{1,0:T(8,128)S(1)} collective-permute-done((f32[64,512]{1,0:T(8,128)S(1)}, f32[64,512]{1,0:T(8,128)S(1)}, u32[]{:S(2)}, u32[]{:S(2)}) %collective-permute-start.4) | collective-permute-done | bytes 131104 | tf_op jit(solution)/shard_map/ppermute | solution.py:36
  26.3 2.5 %collective-permute-done.3.refs_2_ = f32[64,512]{1,0:T(8,128)S(1)} collective-permute-done((f32[64,512]{1,0:T(8,128)S(1)}, f32[64,512]{1,0:T(8,128)S(1)}, u32[]{:S(2)}, u32[]{:S(2)}) %collective-permute-start.3) | collective-permute-done | bytes 131104 | tf_op jit(solution)/shard_map/ppermute | solution.py:36
  29.6 1.0 collective-permute-done.5.other_ref
  30.8 2.2 %collective-permute-done.refs_0_ = bf16[4096,128]{1,0:T(8,128)(2,1)S(1)} collective-permute-done((bf16[4096,128]{1,0:T(8,128)(2,1)}, bf16[4096,128]{1,0:T(8,128)(2,1)S(1)}, u32[]{:S(2)}, u32[]{:S(2)}) %collective-permute-start) | collective-permute-done | bytes 1048608 | tf_op jit(solution)/shard_map/ppermute | solution.py:31
  33.0 1.0 copy-done.3
  34.1 3.4 %copy-done.1 = bf16[8192,512]{1,0:T(8,128)(2,1)S(1)} copy-done((bf16[8192,512]{1,0:T(8,128)(2,1)S(1)}, bf16[8192,512]{1,0:T(8,128)(2,1)}, u32[]{:S(2)}) %copy-start.1) | copy-done | bytes 8388632
  37.4 1.2 copy-done.4
  38.7 0.9 copy-done.10
  39.6 1.4 shard_map.67.refs_1_.acc_ref
  41.0 14.6 %collective-permute-done.6.refs_0_ = bf16[4096,128]{1,0:T(8,128)(2,1)} collective-permute-done((bf16[4096,128]{1,0:T(8,128)(2,1)}, bf16[4096,128]{1,0:T(8,128)(2,1)}, u32[]{:S(2)}, u32[]{:S(2)}) %collective-permute-start.6) | collective-permute-done | bytes 1048608 | tf_op jit(solution)/shard_map/ppermute | solution.py:31
  55.6 2.8 %shard_map.69 = f32[128,512]{1,0:T(8,128)S(1)} custom-call(bf16[4096,128]{1,0:T(8,128)(2,1)} %shard_map.68.piece_ref.refs_2_, bf16[8192,512]{1,0:T(8,128)(2,1)S(1)} %copy-done.1, f32[128,512]{1,0:T(8,128)S(1)} %shard_map.67.refs_1_.acc_ref), custom_call_target="tpu_custom_call" | custom-call | tf_op jit(solution)/shard_map/pallas_call | solution.py:114
  58.5 1.3 collective-permute-done.8.refs_1_
  59.9 2.7 %collective-permute-start.11 = (f32[64,512]{1,0:T(8,128)S(1)}, f32[64,512]{1,0:T(8,128)S(1)}, u32[]{:S(2)}, u32[]{:S(2)}) collective-permute-start(f32[64,512]{1,0:T(8,128)S(1)} %shard_map.70.refs_0_), channel_id=1, source_target_pairs={{0,24},{4,28},{8,16},{12,20},{16,8},{20,12},{24,0},{28,4},{1,25},{... | collective-permute-start | bytes 393224 | tf_op jit(solution)/shard_map/ppermute | solution.py:36
  63.4 3.1 %collective-permute-done.11.refs_3_ = f32[64,512]{1,0:T(8,128)S(1)} collective-permute-done((f32[64,512]{1,0:T(8,128)S(1)}, f32[64,512]{1,0:T(8,128)S(1)}, u32[]{:S(2)}, u32[]{:S(2)}) %collective-permute-start.11) | collective-permute-done | bytes 131104 | tf_op jit(solution)/shard_map/ppermute | solution.py:36
  66.5 2.7 %collective-permute-done.10.refs_2_ = f32[64,512]{1,0:T(8,128)S(1)} collective-permute-done((f32[64,512]{1,0:T(8,128)S(1)}, f32[64,512]{1,0:T(8,128)S(1)}, u32[]{:S(2)}, u32[]{:S(2)}) %collective-permute-start.10) | collective-permute-done | bytes 131104 | tf_op jit(solution)/shard_map/ppermute | solution.py:36
  70.0 1.2 collective-permute-done.12.other_ref
  71.4 6.6 %collective-permute-done.7.refs_0_ = bf16[4096,128]{1,0:T(8,128)(2,1)S(1)} collective-permute-done((bf16[4096,128]{1,0:T(8,128)(2,1)}, bf16[4096,128]{1,0:T(8,128)(2,1)S(1)}, u32[]{:S(2)}, u32[]{:S(2)}) %collective-permute-start.7) | collective-permute-done | bytes 1048608 | tf_op jit(solution)/shard_map/ppermute | solution.py:31
  78.0 1.0 copy-done.5
  79.0 1.2 copy-done.6
  80.2 1.3 shard_map.74.refs_1_.acc_ref
  81.6 18.9 %collective-permute-done.13.refs_0_ = bf16[4096,128]{1,0:T(8,128)(2,1)S(1)} collective-permute-done((bf16[4096,128]{1,0:T(8,128)(2,1)}, bf16[4096,128]{1,0:T(8,128)(2,1)S(1)}, u32[]{:S(2)}, u32[]{:S(2)}) %collective-permute-start.13) | collective-permute-done | bytes 1048608 | tf_op jit(solution)/shard_map/ppermute | solution.py:31
  100.4 1.0 copy-done.7
  101.5 1.3 copy-done.8
  102.7 1.3 shard_map.76
  104.2 1.3 collective-permute-done.15.refs_1_
  105.5 2.7 %collective-permute-start.18 = (f32[64,512]{1,0:T(8,128)S(1)}, f32[64,512]{1,0:T(8,128)S(1)}, u32[]{:S(2)}, u32[]{:S(2)}) collective-permute-start(f32[64,512]{1,0:T(8,128)S(1)} %shard_map.77.refs_0_), channel_id=1, source_target_pairs={{0,24},{4,28},{8,16},{12,20},{16,8},{20,12},{24,0},{28,4},{1,25},{... | collective-permute-start | bytes 393224 | tf_op jit(solution)/shard_map/ppermute | solution.py:36
  109.1 3.1 %collective-permute-done.18.refs_3_ = f32[64,512]{1,0:T(8,128)S(1)} collective-permute-done((f32[64,512]{1,0:T(8,128)S(1)}, f32[64,512]{1,0:T(8,128)S(1)}, u32[]{:S(2)}, u32[]{:S(2)}) %collective-permute-start.18) | collective-permute-done | bytes 131104 | tf_op jit(solution)/shard_map/ppermute | solution.py:36
  112.2 2.7 %collective-permute-done.17.refs_2_ = f32[64,512]{1,0:T(8,128)S(1)} collective-permute-done((f32[64,512]{1,0:T(8,128)S(1)}, f32[64,512]{1,0:T(8,128)S(1)}, u32[]{:S(2)}, u32[]{:S(2)}) %collective-permute-start.17) | collective-permute-done | bytes 131104 | tf_op jit(solution)/shard_map/ppermute | solution.py:36
  115.7 1.2 collective-permute-done.19.other_ref
  117.1 7.0 %shard_map.81.refs_2_.refs_7_ = f32[8192,512]{1,0:T(8,128)S(1)} custom-call(bf16[8192,128]{1,0:T(8,128)(2,1)} %refs_0_.5, bf16[4096,128]{1,0:T(8,128)(2,1)} %shard_map.65.piece_ref.refs_1_, bf16[4096,128]{1,0:T(8,128)(2,1)} %shard_map.68.piece_ref.refs_2_, bf16[4096,128]{1,0:T(8,128)(2,1)} %shard_map.73.piece_ref.refs_3_, ...), custom_call_target="tpu_custom_call" | custom-call | tf_op jit(solution)/shard_map/pallas_call | solution.py:270
  124.8 19.7 %collective-permute-done.20.refs_0_ = bf16[4096,128]{1,0:T(8,128)(2,1)S(1)} collective-permute-done((bf16[4096,128]{1,0:T(8,128)(2,1)}, bf16[4096,128]{1,0:T(8,128)(2,1)S(1)}, u32[]{:S(2)}, u32[]{:S(2)}) %collective-permute-start.20) | collective-permute-done | bytes 1048608 | tf_op jit(solution)/shard_map/ppermute | solution.py:31
  145.4 1.3 collective-permute-done.21.refs_1_
  146.8 2.5 %collective-permute-start.24 = (f32[64,512]{1,0:T(8,128)S(1)}, f32[64,512]{1,0:T(8,128)S(1)}, u32[]{:S(2)}, u32[]{:S(2)}) collective-permute-start(f32[64,512]{1,0:T(8,128)S(1)} %shard_map.83.refs_0_), channel_id=1, source_target_pairs={{0,24},{4,28},{8,16},{12,20},{16,8},{20,12},{24,0},{28,4},{1,25},{... | collective-permute-start | bytes 393224 | tf_op jit(solution)/shard_map/ppermute | solution.py:36
  150.3 3.3 %collective-permute-done.24.refs_3_ = f32[64,512]{1,0:T(8,128)S(1)} collective-permute-done((f32[64,512]{1,0:T(8,128)S(1)}, f32[64,512]{1,0:T(8,128)S(1)}, u32[]{:S(2)}, u32[]{:S(2)}) %collective-permute-start.24) | collective-permute-done | bytes 131104 | tf_op jit(solution)/shard_map/ppermute | solution.py:36
  153.6 2.5 %collective-permute-done.23.refs_2_ = f32[64,512]{1,0:T(8,128)S(1)} collective-permute-done((f32[64,512]{1,0:T(8,128)S(1)}, f32[64,512]{1,0:T(8,128)S(1)}, u32[]{:S(2)}, u32[]{:S(2)}) %collective-permute-start.23) | collective-permute-done | bytes 131104 | tf_op jit(solution)/shard_map/ppermute | solution.py:36
  156.7 1.2 collective-permute-done.25.other_ref
  158.2 3.8 %collective-permute-start.28 = (f32[4,128]{1,0:T(4,128)S(1)}, f32[4,128]{1,0:T(4,128)S(1)}, u32[]{:S(2)}, u32[]{:S(2)}) collective-permute-start(f32[4,128]{1,0:T(4,128)S(1)} %pad_maximum_fusion.refs_9_), channel_id=1, source_target_pairs={{0,3},{1,0},{2,1},{3,2},{4,7},{5,4},{6,5},{7,6},{8,11},{9,8},{10,9... | collective-permute-start | bytes 6152 | tf_op jit(solution)/shard_map/ppermute | solution.py:44
  162.0 1.6 collective-permute-done.26.refs_10_
  163.6 1.2 collective-permute-done.27.refs_11_
  164.7 6.9 %shard_map.86 = (f32[8192,512]{1,0:T(8,128)}, f32[1,2048]{1,0:T(1,128)}) custom-call(bf16[8192,128]{1,0:T(8,128)(2,1)} %refs_0_.5, bf16[4096,128]{1,0:T(8,128)(2,1)} %shard_map.65.piece_ref.refs_1_, bf16[4096,128]{1,0:T(8,128)(2,1)} %shard_map.68.piece_ref.refs_2_, bf16[4096,128]{1,0:T(8,128)(2,1)} %shard_map.73.piece_ref.refs_3_, ...), custom_call_target="tpu_custom_call" | custom-call | flops 1073741824 | bytes 16777216 | tf_op jit(solution)/shard_map/pallas_call | solution.py:381
  (82 shorter events, 9.7 us)
Async XLA Ops:
  0.6 11.2 %copy-start.2 = (bf16[8192,128]{1,0:T(8,128)(2,1)S(1)}, bf16[8192,128]{1,0:T(8,128)(2,1)}, u32[]{:S(2)}) copy-start(bf16[8192,128]{1,0:T(8,128)(2,1)} %refs_0_.5) | copy-start | bytes 6291460
  3.8 29.2 %collective-permute-start = (bf16[4096,128]{1,0:T(8,128)(2,1)}, bf16[4096,128]{1,0:T(8,128)(2,1)S(1)}, u32[]{:S(2)}, u32[]{:S(2)}) collective-permute-start(bf16[4096,128]{1,0:T(8,128)(2,1)} %shard_map.59), channel_id=1, source_target_pairs={{0,1},{1,2},{2,3},{3,0},{4,5},{5,6},{6,7},{7,4},{8,9},{9,10},{10,1... | collective-permute-start | bytes 3145736 | tf_op jit(solution)/shard_map/ppermute | solution.py:31
  6.8 48.8 %collective-permute-start.6 = (bf16[4096,128]{1,0:T(8,128)(2,1)}, bf16[4096,128]{1,0:T(8,128)(2,1)}, u32[]{:S(2)}, u32[]{:S(2)}) collective-permute-start(bf16[4096,128]{1,0:T(8,128)(2,1)} %shard_map.66), channel_id=1, source_target_pairs={{0,1},{1,2},{2,3},{3,0},{4,5},{5,6},{6,7},{7,4},{8,9},{9,10},{10,1... | collective-permute-start | bytes 3145736 | tf_op jit(solution)/shard_map/ppermute | solution.py:31
  8.4 14.7 %copy-start.12 = (f32[512]{0:T(512)S(1)}, f32[512]{0:T(512)}, u32[]{:S(2)}) copy-start(f32[512]{0:T(512)} %param.7) | copy-start | bytes 6148
  11.8 2.8 %copy-start.9 = (f32[128,512]{1,0:T(8,128)}, f32[128,512]{1,0:T(8,128)S(1)}, u32[]{:S(2)}) copy-start(f32[128,512]{1,0:T(8,128)S(1)} %broadcast_in_dim.6.acc_ref) | copy-start | bytes 786436
  14.6 3.4 %copy-start = (bf16[8192,512]{1,0:T(8,128)(2,1)}, bf16[8192,512]{1,0:T(8,128)(2,1)S(1)}, u32[]{:S(2)}) copy-start(bf16[8192,512]{1,0:T(8,128)(2,1)S(1)} %get-tuple-element.14.green_ref) | copy-start | bytes 25165828
  18.1 1.4 collective-permute-start.1
  19.5 6.8 %collective-permute-start.4 = (f32[64,512]{1,0:T(8,128)S(1)}, f32[64,512]{1,0:T(8,128)S(1)}, u32[]{:S(2)}, u32[]{:S(2)}) collective-permute-start(f32[64,512]{1,0:T(8,128)S(1)} %shard_map.62.refs_0_), channel_id=1, source_target_pairs={{0,24},{4,28},{8,16},{12,20},{16,8},{20,12},{24,0},{28,4},{1,25},{... | collective-permute-start | bytes 393224 | tf_op jit(solution)/shard_map/ppermute | solution.py:36
  22.0 6.8 %collective-permute-start.3 = (f32[64,512]{1,0:T(8,128)S(1)}, f32[64,512]{1,0:T(8,128)S(1)}, u32[]{:S(2)}, u32[]{:S(2)}) collective-permute-start(f32[64,512]{1,0:T(8,128)S(1)} %shard_map.62.refs_0_), channel_id=1, source_target_pairs={{0,16},{4,20},{8,24},{12,28},{16,0},{20,4},{24,8},{28,12},{1,17},{... | collective-permute-start | bytes 393224 | tf_op jit(solution)/shard_map/ppermute | solution.py:36
  22.5 6.4 %collective-permute-start.2 = (f32[64,512]{1,0:T(8,128)S(1)}, f32[64,512]{1,0:T(8,128)S(1)}, u32[]{:S(2)}, u32[]{:S(2)}) collective-permute-start(f32[64,512]{1,0:T(8,128)S(1)} %shard_map.62.refs_0_), channel_id=1, source_target_pairs={{0,8},{4,12},{8,0},{12,4},{16,24},{20,28},{24,16},{28,20},{1,9},{5... | collective-permute-start | bytes 393224 | tf_op jit(solution)/shard_map/ppermute | solution.py:36
  29.3 1.3 collective-permute-start.5
  33.0 1.0 copy-start.3
  34.0 44.0 %collective-permute-start.7 = (bf16[4096,128]{1,0:T(8,128)(2,1)}, bf16[4096,128]{1,0:T(8,128)(2,1)S(1)}, u32[]{:S(2)}, u32[]{:S(2)}) collective-permute-start(bf16[4096,128]{1,0:T(8,128)(2,1)} %shard_map.65.piece_ref.refs_1_), channel_id=1, source_target_pairs={{0,1},{1,2},{2,3},{3,0},{4,5},{5,6},{6,7},{7,4},{8,9},{9,10},{10,1... | collective-permute-start | bytes 3145736 | tf_op jit(solution)/shard_map/ppermute | solution.py:31
  34.0 3.4 %copy-start.1 = (bf16[8192,512]{1,0:T(8,128)(2,1)S(1)}, bf16[8192,512]{1,0:T(8,128)(2,1)}, u32[]{:S(2)}) copy-start(bf16[8192,512]{1,0:T(8,128)(2,1)} %copy-done) | copy-start | bytes 25165828
  37.4 1.2 copy-start.4
  38.7 0.9 copy-start.10
  41.0 38.0 %slice-start = ((s8[8388608]{0:T(1024)(128)(4,1)}), s8[4194304]{0:T(1024)(128)(4,1)S(1)}, s32[]{:S(2)}) async-start(s8[8388608]{0:T(1024)(128)(4,1)} %bitcast.9), calls=%async_computation | async-start | bytes 8388608
  41.0 38.0 %copy-start.11 = (f32[128,512]{1,0:T(8,128)S(1)}, f32[128,512]{1,0:T(8,128)}, u32[]{:S(2)}) copy-start(f32[128,512]{1,0:T(8,128)} %copy-done.9) | copy-start | bytes 786436
  55.6 23.4 %slice-start.1 = ((s8[8388608]{0:T(1024)(128)(4,1)}), s8[4194304]{0:T(1024)(128)(4,1)S(1)}, s32[]{:S(2)}) async-start(s8[8388608]{0:T(1024)(128)(4,1)} %bitcast.9), calls=%async_computation.1 | async-start | bytes 8388608
  55.6 44.8 %collective-permute-start.13 = (bf16[4096,128]{1,0:T(8,128)(2,1)}, bf16[4096,128]{1,0:T(8,128)(2,1)S(1)}, u32[]{:S(2)}, u32[]{:S(2)}) collective-permute-start(bf16[4096,128]{1,0:T(8,128)(2,1)} %shard_map.68.piece_ref.refs_2_), channel_id=1, source_target_pairs={{0,1},{1,2},{2,3},{3,0},{4,5},{5,6},{6,7},{7,4},{8,9},{9,10},{10,1... | collective-permute-start | bytes 3145736 | tf_op jit(solution)/shard_map/ppermute | solution.py:31
  58.4 1.4 collective-permute-start.8
  59.9 6.6 %collective-permute-start.11 = (f32[64,512]{1,0:T(8,128)S(1)}, f32[64,512]{1,0:T(8,128)S(1)}, u32[]{:S(2)}, u32[]{:S(2)}) collective-permute-start(f32[64,512]{1,0:T(8,128)S(1)} %shard_map.70.refs_0_), channel_id=1, source_target_pairs={{0,24},{4,28},{8,16},{12,20},{16,8},{20,12},{24,0},{28,4},{1,25},{... | collective-permute-start | bytes 393224 | tf_op jit(solution)/shard_map/ppermute | solution.py:36
  62.6 6.6 %collective-permute-start.10 = (f32[64,512]{1,0:T(8,128)S(1)}, f32[64,512]{1,0:T(8,128)S(1)}, u32[]{:S(2)}, u32[]{:S(2)}) collective-permute-start(f32[64,512]{1,0:T(8,128)S(1)} %shard_map.70.refs_0_), channel_id=1, source_target_pairs={{0,16},{4,20},{8,24},{12,28},{16,0},{20,4},{24,8},{28,12},{1,17},{... | collective-permute-start | bytes 393224 | tf_op jit(solution)/shard_map/ppermute | solution.py:36
  63.1 6.4 %collective-permute-start.9 = (f32[64,512]{1,0:T(8,128)S(1)}, f32[64,512]{1,0:T(8,128)S(1)}, u32[]{:S(2)}, u32[]{:S(2)}) collective-permute-start(f32[64,512]{1,0:T(8,128)S(1)} %shard_map.70.refs_0_), channel_id=1, source_target_pairs={{0,8},{4,12},{8,0},{12,4},{16,24},{20,28},{24,16},{28,20},{1,9},{5... | collective-permute-start | bytes 393224 | tf_op jit(solution)/shard_map/ppermute | solution.py:36
  69.9 1.3 collective-permute-start.12
  78.0 1.0 copy-start.5
  78.9 45.1 %collective-permute-start.14 = (bf16[4096,128]{1,0:T(8,128)(2,1)}, bf16[4096,128]{1,0:T(8,128)(2,1)S(1)}, u32[]{:S(2)}, u32[]{:S(2)}) collective-permute-start(bf16[4096,128]{1,0:T(8,128)(2,1)} %shard_map.73.piece_ref.refs_3_), channel_id=1, source_target_pairs={{0,1},{1,2},{2,3},{3,0},{4,5},{5,6},{6,7},{7,4},{8,9},{9,10},{10,1... | collective-permute-start | bytes 3145736 | tf_op jit(solution)/shard_map/ppermute | solution.py:31
  79.0 1.3 copy-start.6
  100.4 1.0 copy-start.7
  101.4 43.1 %collective-permute-start.20 = (bf16[4096,128]{1,0:T(8,128)(2,1)}, bf16[4096,128]{1,0:T(8,128)(2,1)S(1)}, u32[]{:S(2)}, u32[]{:S(2)}) collective-permute-start(bf16[4096,128]{1,0:T(8,128)(2,1)} %shard_map.75.piece_ref.refs_4_), channel_id=1, source_target_pairs={{0,1},{1,2},{2,3},{3,0},{4,5},{5,6},{6,7},{7,4},{8,9},{9,10},{10,1... | collective-permute-start | bytes 3145736 | tf_op jit(solution)/shard_map/ppermute | solution.py:31
  101.5 1.3 copy-start.8
  104.1 1.4 collective-permute-start.15
  105.5 6.6 %collective-permute-start.18 = (f32[64,512]{1,0:T(8,128)S(1)}, f32[64,512]{1,0:T(8,128)S(1)}, u32[]{:S(2)}, u32[]{:S(2)}) collective-permute-start(f32[64,512]{1,0:T(8,128)S(1)} %shard_map.77.refs_0_), channel_id=1, source_target_pairs={{0,24},{4,28},{8,16},{12,20},{16,8},{20,12},{24,0},{28,4},{1,25},{... | collective-permute-start | bytes 393224 | tf_op jit(solution)/shard_map/ppermute | solution.py:36
  108.2 6.6 %collective-permute-start.17 = (f32[64,512]{1,0:T(8,128)S(1)}, f32[64,512]{1,0:T(8,128)S(1)}, u32[]{:S(2)}, u32[]{:S(2)}) collective-permute-start(f32[64,512]{1,0:T(8,128)S(1)} %shard_map.77.refs_0_), channel_id=1, source_target_pairs={{0,16},{4,20},{8,24},{12,28},{16,0},{20,4},{24,8},{28,12},{1,17},{... | collective-permute-start | bytes 393224 | tf_op jit(solution)/shard_map/ppermute | solution.py:36
  108.7 6.4 %collective-permute-start.16 = (f32[64,512]{1,0:T(8,128)S(1)}, f32[64,512]{1,0:T(8,128)S(1)}, u32[]{:S(2)}, u32[]{:S(2)}) collective-permute-start(f32[64,512]{1,0:T(8,128)S(1)} %shard_map.77.refs_0_), channel_id=1, source_target_pairs={{0,8},{4,12},{8,0},{12,4},{16,24},{20,28},{24,16},{28,20},{1,9},{5... | collective-permute-start | bytes 393224 | tf_op jit(solution)/shard_map/ppermute | solution.py:36
  115.6 1.3 collective-permute-start.19
  145.3 1.4 collective-permute-start.21
  146.8 6.8 %collective-permute-start.24 = (f32[64,512]{1,0:T(8,128)S(1)}, f32[64,512]{1,0:T(8,128)S(1)}, u32[]{:S(2)}, u32[]{:S(2)}) collective-permute-start(f32[64,512]{1,0:T(8,128)S(1)} %shard_map.83.refs_0_), channel_id=1, source_target_pairs={{0,24},{4,28},{8,16},{12,20},{16,8},{20,12},{24,0},{28,4},{1,25},{... | collective-permute-start | bytes 393224 | tf_op jit(solution)/shard_map/ppermute | solution.py:36
  149.3 6.8 %collective-permute-start.23 = (f32[64,512]{1,0:T(8,128)S(1)}, f32[64,512]{1,0:T(8,128)S(1)}, u32[]{:S(2)}, u32[]{:S(2)}) collective-permute-start(f32[64,512]{1,0:T(8,128)S(1)} %shard_map.83.refs_0_), channel_id=1, source_target_pairs={{0,16},{4,20},{8,24},{12,28},{16,0},{20,4},{24,8},{28,12},{1,17},{... | collective-permute-start | bytes 393224 | tf_op jit(solution)/shard_map/ppermute | solution.py:36
  149.8 6.4 %collective-permute-start.22 = (f32[64,512]{1,0:T(8,128)S(1)}, f32[64,512]{1,0:T(8,128)S(1)}, u32[]{:S(2)}, u32[]{:S(2)}) collective-permute-start(f32[64,512]{1,0:T(8,128)S(1)} %shard_map.83.refs_0_), channel_id=1, source_target_pairs={{0,8},{4,12},{8,0},{12,4},{16,24},{20,28},{24,16},{28,20},{1,9},{5... | collective-permute-start | bytes 393224 | tf_op jit(solution)/shard_map/ppermute | solution.py:36
  156.6 1.3 collective-permute-start.25
  158.1 5.4 %collective-permute-start.26 = (f32[4,128]{1,0:T(4,128)S(1)}, f32[4,128]{1,0:T(4,128)S(1)}, u32[]{:S(2)}, u32[]{:S(2)}) collective-permute-start(f32[4,128]{1,0:T(4,128)S(1)} %pad_maximum_fusion.refs_9_), channel_id=1, source_target_pairs={{0,1},{1,2},{2,3},{3,0},{4,6},{5,7},{6,4},{7,5},{8,9},{9,10},{10,1... | collective-permute-start | bytes 6152 | tf_op jit(solution)/shard_map/ppermute | solution.py:44
  158.2 5.4 %collective-permute-start.28 = (f32[4,128]{1,0:T(4,128)S(1)}, f32[4,128]{1,0:T(4,128)S(1)}, u32[]{:S(2)}, u32[]{:S(2)}) collective-permute-start(f32[4,128]{1,0:T(4,128)S(1)} %pad_maximum_fusion.refs_9_), channel_id=1, source_target_pairs={{0,3},{1,0},{2,1},{3,2},{4,7},{5,4},{6,5},{7,6},{8,11},{9,8},{10,9... | collective-permute-start | bytes 6152 | tf_op jit(solution)/shard_map/ppermute | solution.py:44
  163.6 1.2 collective-permute-start.27

commit v10 on v9

--- a/solution.py
+++ b/solution.py
@@ -92,6 +92,26 @@
         compiler_params=pltpu.CompilerParams(vmem_limit_bytes=2 * MIB),
         cost_estimate=FREE,
     )(*[in_hbm(array) for array in arrays])
+
+
+def cut_body(first, array_ref, piece_ref, semaphore):
+    move = pltpu.make_async_copy(
+        array_ref.at[pl.ds(first, piece_ref.shape[0]), :], piece_ref, semaphore
+    )
+    move.start()
+    move.wait()
+
+
+def cut(array, first, length):
+    return pl.pallas_call(
+        functools.partial(cut_body, first),
+        out_shape=vmem_shape((length,) + array.shape[1:], array.dtype),
+        in_specs=[pl.BlockSpec(memory_space=pltpu.HBM)],
+        out_specs=IN_VMEM,
+        scratch_shapes=[pltpu.SemaphoreType.DMA],
+        compiler_params=pltpu.CompilerParams(vmem_limit_bytes=2 * MIB),
+        cost_estimate=FREE,
+    )(in_hbm(array))
 
 
 def project_body(first, block, piece_ref, green_ref, acc_ref, total_ref):
@@ -431,12 +451,7 @@
         dressed.append(both)
         traced.append(trace)
 
-    held = [
-        gate(
-            lax.slice_in_dim(cholesky_factors, i * length, (i + 1) * length, axis=0), in_vmem
-        )
-        for i in range(PIECES)
-    ]
+    held = [cut(cholesky_factors, i * length, length) for i in range(PIECES)]
     finish(0, project(cholesky_factors, green, 0, zeros))
     steps = []
     for step in range(1, aux_size):

time: 172 us -> 171 us (level)
  Pallas kernels: 29.3 us -> 33.9 us
  waiting for transfers between devices: 98.4 us -> 94.7 us
  local copies, waits for them, and re-layouts: 17.9 us -> 14.8 us
    pallas_call x0 -> x2, Pallas kernels: none -> 4.56 us  [cut(): pl.pallas_call(functools.partial(cut_body, first), out_shape=vmem_shape((...]
    ppermute x6, waiting for transfers between devices: 61.9 us -> 58.1 us  [shifted(): lax.ppermute(block, axis, [(i, (i + shift) % count) for i in range(count)])]
    slice x1 -> x0, local copies, waits for them, and re-layouts: 3.13 us -> none  [local(): lax.slice_in_dim(cholesky_factors, i * length, (i + 1) * length, axis=0)]
  transfers between devices with their start and end apart: 29 -> 29, of which waited for: 27 -> 26; matrix products, arithmetic and copies ran while one was open for 1% -> 1% of each run, Pallas kernels for 13% -> 14%
where the time goes in v10:
time: 171 us
  waiting for transfers between devices  94.7 us (55%)
  Pallas kernels  33.9 us (20%)
  starting transfers between devices  25 us (15%)
  local copies, waits for them, and re-layouts  14.8 us (9%)
    ppermute x6, waiting for transfers between devices, shifted(): lax.ppermute(block, axis, [(i, (i + shift) % count) for i in range(count)])  58.1 us
    ppermute x21, waiting for transfers between devices, exchanged(): return lax.ppermute(block, axis, [(i, i ^ bit) for i in range(count)])  35 us
    ppermute x21, starting transfers between devices, exchanged(): return lax.ppermute(block, axis, [(i, i ^ bit) for i in range(count)])  14.8 us
    unnamed x31, local copies, waits for them, and re-layouts  14.4 us
    pallas_call x5, Pallas kernels, project(): pl.pallas_call(functools.partial(project_body, first, min(length, 1024)),...  9.57 us
    pallas_call x1, Pallas kernels, slope_early(): pl.pallas_call(functools.partial(slope_early_body, pieces), in_specs=[pl....  7 us
    pallas_call x1, Pallas kernels, slope(): pl.pallas_call(functools.partial(slope_body, pieces), in_specs=[far] * le...  6.91 us
    ppermute x6, starting transfers between devices, shifted(): lax.ppermute(block, axis, [(i, (i + shift) % count) for i in range(count)])  6.37 us
  transfers between devices with their start and end apart: 29, of which 26 were waited for; matrix products, arithmetic and copies ran while one was open for 1% of the time, Pallas kernels for 14%

profile of v10, /device:TPU:0, one launch (start us, length us, event | category | flops | bytes accessed | tf_op | source)
XLA Modules:
  0.0 170.9 jit_solution(5535669747989806479)
XLA Ops:
  0.6 2.4 %shard_map.59 = bf16[4096,128]{1,0:T(8,128)(2,1)} custom-call(bf16[8192,128]{1,0:T(8,128)(2,1)} %refs_0_.5), custom_call_target="tpu_custom_call" | custom-call | tf_op jit(solution)/shard_map/pallas_call | solution.py:106
  3.0 3.1 %collective-permute-start = (bf16[4096,128]{1,0:T(8,128)(2,1)}, bf16[4096,128]{1,0:T(8,128)(2,1)S(1)}, u32[]{:S(2)}, u32[]{:S(2)}) collective-permute-start(bf16[4096,128]{1,0:T(8,128)(2,1)} %shard_map.59), channel_id=1, source_target_pairs={{0,1},{1,2},{2,3},{3,0},{4,5},{5,6},{6,7},{7,4},{8,9},{9,10},{10,1... | collective-permute-start | bytes 3145736 | tf_op jit(solution)/shard_map/ppermute | solution.py:31
  6.1 2.2 %shard_map.66 = bf16[4096,128]{1,0:T(8,128)(2,1)} custom-call(bf16[8192,128]{1,0:T(8,128)(2,1)} %refs_0_.5), custom_call_target="tpu_custom_call" | custom-call | tf_op jit(solution)/shard_map/pallas_call | solution.py:106
  8.3 1.6 collective-permute-start.6
  9.9 3.4 %shard_map.60 = (bf16[8192,512]{1,0:T(8,128)(2,1)S(1)}, f32[256,256]{1,0:T(8,128)S(1)}) custom-call(bf16[8192,512]{1,0:T(8,128)(2,1)} %refs_0_.3, f32[256,256]{1,0:T(8,128)} %refs_1_.1), custom_call_target="tpu_custom_call" | custom-call | tf_op jit(solution)/shard_map/pallas_call | solution.py:86
  13.4 2.8 %shard_map.61 = f32[128,512]{1,0:T(8,128)S(1)} custom-call(bf16[8192,128]{1,0:T(8,128)(2,1)S(1)} %copy-done.2, bf16[8192,512]{1,0:T(8,128)(2,1)S(1)} %get-tuple-element.14.green_ref, f32[128,512]{1,0:T(8,128)S(1)} %broadcast_in_dim.6.acc_ref), custom_call_target="tpu_custom_call" | custom-call | tf_op jit(solution)/shard_map/pallas_call | solution.py:134
  16.2 3.4 %copy-done = bf16[8192,512]{1,0:T(8,128)(2,1)} copy-done((bf16[8192,512]{1,0:T(8,128)(2,1)}, bf16[8192,512]{1,0:T(8,128)(2,1)S(1)}, u32[]{:S(2)}) %copy-start) | copy-done | bytes 8388632
  19.7 1.3 collective-permute-done.1.refs_1_
  21.0 2.5 %collective-permute-start.4 = (f32[64,512]{1,0:T(8,128)S(1)}, f32[64,512]{1,0:T(8,128)S(1)}, u32[]{:S(2)}, u32[]{:S(2)}) collective-permute-start(f32[64,512]{1,0:T(8,128)S(1)} %shard_map.62.refs_0_), channel_id=1, source_target_pairs={{0,24},{4,28},{8,16},{12,20},{16,8},{20,12},{24,0},{28,4},{1,25},{... | collective-permute-start | bytes 393224 | tf_op jit(solution)/shard_map/ppermute | solution.py:36
  24.7 3.1 %collective-permute-done.4.refs_3_ = f32[64,512]{1,0:T(8,128)S(1)} collective-permute-done((f32[64,512]{1,0:T(8,128)S(1)}, f32[64,512]{1,0:T(8,128)S(1)}, u32[]{:S(2)}, u32[]{:S(2)}) %collective-permute-start.4) | collective-permute-done | bytes 131104 | tf_op jit(solution)/shard_map/ppermute | solution.py:36
  27.8 2.5 %collective-permute-done.3.refs_2_ = f32[64,512]{1,0:T(8,128)S(1)} collective-permute-done((f32[64,512]{1,0:T(8,128)S(1)}, f32[64,512]{1,0:T(8,128)S(1)}, u32[]{:S(2)}, u32[]{:S(2)}) %collective-permute-start.3) | collective-permute-done | bytes 131104 | tf_op jit(solution)/shard_map/ppermute | solution.py:36
  31.2 1.0 collective-permute-done.5.other_ref
  32.4 1.0 copy-done.3
  33.4 1.6 collective-permute-start.7
  34.9 3.4 %copy-done.1 = bf16[8192,512]{1,0:T(8,128)(2,1)S(1)} copy-done((bf16[8192,512]{1,0:T(8,128)(2,1)S(1)}, bf16[8192,512]{1,0:T(8,128)(2,1)}, u32[]{:S(2)}) %copy-start.1) | copy-done | bytes 8388632
  38.3 1.2 copy-done.4
  40.5 1.4 shard_map.67.refs_1_.acc_ref
  41.9 13.0 %collective-permute-done.6.refs_0_ = bf16[4096,128]{1,0:T(8,128)(2,1)} collective-permute-done((bf16[4096,128]{1,0:T(8,128)(2,1)}, bf16[4096,128]{1,0:T(8,128)(2,1)}, u32[]{:S(2)}, u32[]{:S(2)}) %collective-permute-start.6) | collective-permute-done | bytes 1048608 | tf_op jit(solution)/shard_map/ppermute | solution.py:31
  54.9 2.8 %shard_map.69 = f32[128,512]{1,0:T(8,128)S(1)} custom-call(bf16[4096,128]{1,0:T(8,128)(2,1)} %shard_map.68.piece_ref.refs_2_, bf16[8192,512]{1,0:T(8,128)(2,1)S(1)} %copy-done.1, f32[128,512]{1,0:T(8,128)S(1)} %shard_map.67.refs_1_.acc_ref), custom_call_target="tpu_custom_call" | custom-call | tf_op jit(solution)/shard_map/pallas_call | solution.py:134
  57.8 1.3 collective-permute-done.8.refs_1_
  59.1 2.7 %collective-permute-start.11 = (f32[64,512]{1,0:T(8,128)S(1)}, f32[64,512]{1,0:T(8,128)S(1)}, u32[]{:S(2)}, u32[]{:S(2)}) collective-permute-start(f32[64,512]{1,0:T(8,128)S(1)} %shard_map.70.refs_0_), channel_id=1, source_target_pairs={{0,24},{4,28},{8,16},{12,20},{16,8},{20,12},{24,0},{28,4},{1,25},{... | collective-permute-start | bytes 393224 | tf_op jit(solution)/shard_map/ppermute | solution.py:36
  62.7 3.1 %collective-permute-done.11.refs_3_ = f32[64,512]{1,0:T(8,128)S(1)} collective-permute-done((f32[64,512]{1,0:T(8,128)S(1)}, f32[64,512]{1,0:T(8,128)S(1)}, u32[]{:S(2)}, u32[]{:S(2)}) %collective-permute-start.11) | collective-permute-done | bytes 131104 | tf_op jit(solution)/shard_map/ppermute | solution.py:36
  65.8 2.7 %collective-permute-done.10.refs_2_ = f32[64,512]{1,0:T(8,128)S(1)} collective-permute-done((f32[64,512]{1,0:T(8,128)S(1)}, f32[64,512]{1,0:T(8,128)S(1)}, u32[]{:S(2)}, u32[]{:S(2)}) %collective-permute-start.10) | collective-permute-done | bytes 131104 | tf_op jit(solution)/shard_map/ppermute | solution.py:36
  69.3 1.2 collective-permute-done.12.other_ref
  70.7 6.6 %collective-permute-done.7.refs_0_ = bf16[4096,128]{1,0:T(8,128)(2,1)S(1)} collective-permute-done((bf16[4096,128]{1,0:T(8,128)(2,1)}, bf16[4096,128]{1,0:T(8,128)(2,1)S(1)}, u32[]{:S(2)}, u32[]{:S(2)}) %collective-permute-start.7) | collective-permute-done | bytes 1048608 | tf_op jit(solution)/shard_map/ppermute | solution.py:31
  77.2 1.0 copy-done.5
  78.3 1.2 copy-done.6
  79.5 1.3 shard_map.74.refs_1_.acc_ref
  80.8 18.9 %collective-permute-done.13.refs_0_ = bf16[4096,128]{1,0:T(8,128)(2,1)S(1)} collective-permute-done((bf16[4096,128]{1,0:T(8,128)(2,1)}, bf16[4096,128]{1,0:T(8,128)(2,1)S(1)}, u32[]{:S(2)}, u32[]{:S(2)}) %collective-permute-start.13) | collective-permute-done | bytes 1048608 | tf_op jit(solution)/shard_map/ppermute | solution.py:31
  99.7 1.0 copy-done.7
  100.7 1.3 copy-done.8
  102.0 1.3 shard_map.76
  103.4 1.3 collective-permute-done.15.refs_1_
  104.8 2.7 %collective-permute-start.18 = (f32[64,512]{1,0:T(8,128)S(1)}, f32[64,512]{1,0:T(8,128)S(1)}, u32[]{:S(2)}, u32[]{:S(2)}) collective-permute-start(f32[64,512]{1,0:T(8,128)S(1)} %shard_map.77.refs_0_), channel_id=1, source_target_pairs={{0,24},{4,28},{8,16},{12,20},{16,8},{20,12},{24,0},{28,4},{1,25},{... | collective-permute-start | bytes 393224 | tf_op jit(solution)/shard_map/ppermute | solution.py:36
  108.4 3.1 %collective-permute-done.18.refs_3_ = f32[64,512]{1,0:T(8,128)S(1)} collective-permute-done((f32[64,512]{1,0:T(8,128)S(1)}, f32[64,512]{1,0:T(8,128)S(1)}, u32[]{:S(2)}, u32[]{:S(2)}) %collective-permute-start.18) | collective-permute-done | bytes 131104 | tf_op jit(solution)/shard_map/ppermute | solution.py:36
  111.4 2.7 %collective-permute-done.17.refs_2_ = f32[64,512]{1,0:T(8,128)S(1)} collective-permute-done((f32[64,512]{1,0:T(8,128)S(1)}, f32[64,512]{1,0:T(8,128)S(1)}, u32[]{:S(2)}, u32[]{:S(2)}) %collective-permute-start.17) | collective-permute-done | bytes 131104 | tf_op jit(solution)/shard_map/ppermute | solution.py:36
  114.9 1.2 collective-permute-done.19.other_ref
  116.3 7.0 %shard_map.81.refs_2_.refs_7_ = f32[8192,512]{1,0:T(8,128)S(1)} custom-call(bf16[8192,128]{1,0:T(8,128)(2,1)} %refs_0_.5, bf16[4096,128]{1,0:T(8,128)(2,1)} %shard_map.65.piece_ref.refs_1_, bf16[4096,128]{1,0:T(8,128)(2,1)} %shard_map.68.piece_ref.refs_2_, bf16[4096,128]{1,0:T(8,128)(2,1)} %shard_map.73.piece_ref.refs_3_, ...), custom_call_target="tpu_custom_call" | custom-call | tf_op jit(solution)/shard_map/pallas_call | solution.py:290
  124.1 19.7 %collective-permute-done.20.refs_0_ = bf16[4096,128]{1,0:T(8,128)(2,1)S(1)} collective-permute-done((bf16[4096,128]{1,0:T(8,128)(2,1)}, bf16[4096,128]{1,0:T(8,128)(2,1)S(1)}, u32[]{:S(2)}, u32[]{:S(2)}) %collective-permute-start.20) | collective-permute-done | bytes 1048608 | tf_op jit(solution)/shard_map/ppermute | solution.py:31
  144.7 1.3 collective-permute-done.21.refs_1_
  146.0 2.5 %collective-permute-start.24 = (f32[64,512]{1,0:T(8,128)S(1)}, f32[64,512]{1,0:T(8,128)S(1)}, u32[]{:S(2)}, u32[]{:S(2)}) collective-permute-start(f32[64,512]{1,0:T(8,128)S(1)} %shard_map.83.refs_0_), channel_id=1, source_target_pairs={{0,24},{4,28},{8,16},{12,20},{16,8},{20,12},{24,0},{28,4},{1,25},{... | collective-permute-start | bytes 393224 | tf_op jit(solution)/shard_map/ppermute | solution.py:36
  149.6 3.2 %collective-permute-done.24.refs_3_ = f32[64,512]{1,0:T(8,128)S(1)} collective-permute-done((f32[64,512]{1,0:T(8,128)S(1)}, f32[64,512]{1,0:T(8,128)S(1)}, u32[]{:S(2)}, u32[]{:S(2)}) %collective-permute-start.24) | collective-permute-done | bytes 131104 | tf_op jit(solution)/shard_map/ppermute | solution.py:36
  152.8 2.5 %collective-permute-done.23.refs_2_ = f32[64,512]{1,0:T(8,128)S(1)} collective-permute-done((f32[64,512]{1,0:T(8,128)S(1)}, f32[64,512]{1,0:T(8,128)S(1)}, u32[]{:S(2)}, u32[]{:S(2)}) %collective-permute-start.23) | collective-permute-done | bytes 131104 | tf_op jit(solution)/shard_map/ppermute | solution.py:36
  156.0 1.2 collective-permute-done.25.other_ref
  157.5 3.8 %collective-permute-start.28 = (f32[4,128]{1,0:T(4,128)S(1)}, f32[4,128]{1,0:T(4,128)S(1)}, u32[]{:S(2)}, u32[]{:S(2)}) collective-permute-start(f32[4,128]{1,0:T(4,128)S(1)} %pad_maximum_fusion.refs_9_), channel_id=1, source_target_pairs={{0,3},{1,0},{2,1},{3,2},{4,7},{5,4},{6,5},{7,6},{8,11},{9,8},{10,9... | collective-permute-start | bytes 6152 | tf_op jit(solution)/shard_map/ppermute | solution.py:44
  161.3 1.6 collective-permute-done.26.refs_10_
  162.8 1.2 collective-permute-done.27.refs_11_
  164.0 6.9 %shard_map.86 = (f32[8192,512]{1,0:T(8,128)}, f32[1,2048]{1,0:T(1,128)}) custom-call(bf16[8192,128]{1,0:T(8,128)(2,1)} %refs_0_.5, bf16[4096,128]{1,0:T(8,128)(2,1)} %shard_map.65.piece_ref.refs_1_, bf16[4096,128]{1,0:T(8,128)(2,1)} %shard_map.68.piece_ref.refs_2_, bf16[4096,128]{1,0:T(8,128)(2,1)} %shard_map.73.piece_ref.refs_3_, ...), custom_call_target="tpu_custom_call" | custom-call | flops 1073741824 | bytes 16777216 | tf_op jit(solution)/shard_map/pallas_call | solution.py:401
  (81 shorter events, 10.5 us)
Async XLA Ops:
  0.6 12.7 %copy-start.2 = (bf16[8192,128]{1,0:T(8,128)(2,1)S(1)}, bf16[8192,128]{1,0:T(8,128)(2,1)}, u32[]{:S(2)}) copy-start(bf16[8192,128]{1,0:T(8,128)(2,1)} %refs_0_.5) | copy-start | bytes 6291460
  3.0 29.4 %collective-permute-start = (bf16[4096,128]{1,0:T(8,128)(2,1)}, bf16[4096,128]{1,0:T(8,128)(2,1)S(1)}, u32[]{:S(2)}, u32[]{:S(2)}) collective-permute-start(bf16[4096,128]{1,0:T(8,128)(2,1)} %shard_map.59), channel_id=1, source_target_pairs={{0,1},{1,2},{2,3},{3,0},{4,5},{5,6},{6,7},{7,4},{8,9},{9,10},{10,1... | collective-permute-start | bytes 3145736 | tf_op jit(solution)/shard_map/ppermute | solution.py:31
  8.3 46.6 %collective-permute-start.6 = (bf16[4096,128]{1,0:T(8,128)(2,1)}, bf16[4096,128]{1,0:T(8,128)(2,1)}, u32[]{:S(2)}, u32[]{:S(2)}) collective-permute-start(bf16[4096,128]{1,0:T(8,128)(2,1)} %shard_map.66), channel_id=1, source_target_pairs={{0,1},{1,2},{2,3},{3,0},{4,5},{5,6},{6,7},{7,4},{8,9},{9,10},{10,1... | collective-permute-start | bytes 3145736 | tf_op jit(solution)/shard_map/ppermute | solution.py:31
  9.9 14.7 %copy-start.12 = (f32[512]{0:T(512)S(1)}, f32[512]{0:T(512)}, u32[]{:S(2)}) copy-start(f32[512]{0:T(512)} %param.7) | copy-start | bytes 6148
  13.4 2.8 %copy-start.9 = (f32[128,512]{1,0:T(8,128)}, f32[128,512]{1,0:T(8,128)S(1)}, u32[]{:S(2)}) copy-start(f32[128,512]{1,0:T(8,128)S(1)} %broadcast_in_dim.6.acc_ref) | copy-start | bytes 786436
  16.2 3.4 %copy-start = (bf16[8192,512]{1,0:T(8,128)(2,1)}, bf16[8192,512]{1,0:T(8,128)(2,1)S(1)}, u32[]{:S(2)}) copy-start(bf16[8192,512]{1,0:T(8,128)(2,1)S(1)} %get-tuple-element.14.green_ref) | copy-start | bytes 25165828
  19.6 1.4 collective-permute-start.1
  21.0 6.8 %collective-permute-start.4 = (f32[64,512]{1,0:T(8,128)S(1)}, f32[64,512]{1,0:T(8,128)S(1)}, u32[]{:S(2)}, u32[]{:S(2)}) collective-permute-start(f32[64,512]{1,0:T(8,128)S(1)} %shard_map.62.refs_0_), channel_id=1, source_target_pairs={{0,24},{4,28},{8,16},{12,20},{16,8},{20,12},{24,0},{28,4},{1,25},{... | collective-permute-start | bytes 393224 | tf_op jit(solution)/shard_map/ppermute | solution.py:36
  23.6 6.8 %collective-permute-start.3 = (f32[64,512]{1,0:T(8,128)S(1)}, f32[64,512]{1,0:T(8,128)S(1)}, u32[]{:S(2)}, u32[]{:S(2)}) collective-permute-start(f32[64,512]{1,0:T(8,128)S(1)} %shard_map.62.refs_0_), channel_id=1, source_target_pairs={{0,16},{4,20},{8,24},{12,28},{16,0},{20,4},{24,8},{28,12},{1,17},{... | collective-permute-start | bytes 393224 | tf_op jit(solution)/shard_map/ppermute | solution.py:36
  24.1 6.4 %collective-permute-start.2 = (f32[64,512]{1,0:T(8,128)S(1)}, f32[64,512]{1,0:T(8,128)S(1)}, u32[]{:S(2)}, u32[]{:S(2)}) collective-permute-start(f32[64,512]{1,0:T(8,128)S(1)} %shard_map.62.refs_0_), channel_id=1, source_target_pairs={{0,8},{4,12},{8,0},{12,4},{16,24},{20,28},{24,16},{28,20},{1,9},{5... | collective-permute-start | bytes 393224 | tf_op jit(solution)/shard_map/ppermute | solution.py:36
  30.9 1.3 collective-permute-start.5
  32.4 1.0 copy-start.3
  33.4 43.9 %collective-permute-start.7 = (bf16[4096,128]{1,0:T(8,128)(2,1)}, bf16[4096,128]{1,0:T(8,128)(2,1)S(1)}, u32[]{:S(2)}, u32[]{:S(2)}) collective-permute-start(bf16[4096,128]{1,0:T(8,128)(2,1)} %shard_map.65.piece_ref.refs_1_), channel_id=1, source_target_pairs={{0,1},{1,2},{2,3},{3,0},{4,5},{5,6},{6,7},{7,4},{8,9},{9,10},{10,1... | collective-permute-start | bytes 3145736 | tf_op jit(solution)/shard_map/ppermute | solution.py:31
  34.9 3.4 %copy-start.1 = (bf16[8192,512]{1,0:T(8,128)(2,1)S(1)}, bf16[8192,512]{1,0:T(8,128)(2,1)}, u32[]{:S(2)}) copy-start(bf16[8192,512]{1,0:T(8,128)(2,1)} %copy-done) | copy-start | bytes 25165828
  38.3 1.2 copy-start.4
  39.5 0.9 copy-start.10
  41.9 36.4 %slice-start = ((s8[8388608]{0:T(1024)(128)(4,1)}), s8[4194304]{0:T(1024)(128)(4,1)S(1)}, s32[]{:S(2)}) async-start(s8[8388608]{0:T(1024)(128)(4,1)} %bitcast.9), calls=%async_computation | async-start | bytes 8388608
  41.9 36.4 %copy-start.11 = (f32[128,512]{1,0:T(8,128)S(1)}, f32[128,512]{1,0:T(8,128)}, u32[]{:S(2)}) copy-start(f32[128,512]{1,0:T(8,128)} %copy-done.9) | copy-start | bytes 786436
  54.9 23.4 %slice-start.1 = ((s8[8388608]{0:T(1024)(128)(4,1)}), s8[4194304]{0:T(1024)(128)(4,1)S(1)}, s32[]{:S(2)}) async-start(s8[8388608]{0:T(1024)(128)(4,1)} %bitcast.9), calls=%async_computation.1 | async-start | bytes 8388608
  54.9 44.8 %collective-permute-start.13 = (bf16[4096,128]{1,0:T(8,128)(2,1)}, bf16[4096,128]{1,0:T(8,128)(2,1)S(1)}, u32[]{:S(2)}, u32[]{:S(2)}) collective-permute-start(bf16[4096,128]{1,0:T(8,128)(2,1)} %shard_map.68.piece_ref.refs_2_), channel_id=1, source_target_pairs={{0,1},{1,2},{2,3},{3,0},{4,5},{5,6},{6,7},{7,4},{8,9},{9,10},{10,1... | collective-permute-start | bytes 3145736 | tf_op jit(solution)/shard_map/ppermute | solution.py:31
  57.7 1.4 collective-permute-start.8
  59.1 6.7 %collective-permute-start.11 = (f32[64,512]{1,0:T(8,128)S(1)}, f32[64,512]{1,0:T(8,128)S(1)}, u32[]{:S(2)}, u32[]{:S(2)}) collective-permute-start(f32[64,512]{1,0:T(8,128)S(1)} %shard_map.70.refs_0_), channel_id=1, source_target_pairs={{0,24},{4,28},{8,16},{12,20},{16,8},{20,12},{24,0},{28,4},{1,25},{... | collective-permute-start | bytes 393224 | tf_op jit(solution)/shard_map/ppermute | solution.py:36
  61.9 6.6 %collective-permute-start.10 = (f32[64,512]{1,0:T(8,128)S(1)}, f32[64,512]{1,0:T(8,128)S(1)}, u32[]{:S(2)}, u32[]{:S(2)}) collective-permute-start(f32[64,512]{1,0:T(8,128)S(1)} %shard_map.70.refs_0_), channel_id=1, source_target_pairs={{0,16},{4,20},{8,24},{12,28},{16,0},{20,4},{24,8},{28,12},{1,17},{... | collective-permute-start | bytes 393224 | tf_op jit(solution)/shard_map/ppermute | solution.py:36
  62.4 6.4 %collective-permute-start.9 = (f32[64,512]{1,0:T(8,128)S(1)}, f32[64,512]{1,0:T(8,128)S(1)}, u32[]{:S(2)}, u32[]{:S(2)}) collective-permute-start(f32[64,512]{1,0:T(8,128)S(1)} %shard_map.70.refs_0_), channel_id=1, source_target_pairs={{0,8},{4,12},{8,0},{12,4},{16,24},{20,28},{24,16},{28,20},{1,9},{5... | collective-permute-start | bytes 393224 | tf_op jit(solution)/shard_map/ppermute | solution.py:36
  69.2 1.3 collective-permute-start.12
  77.2 1.0 copy-start.5
  78.2 45.1 %collective-permute-start.14 = (bf16[4096,128]{1,0:T(8,128)(2,1)}, bf16[4096,128]{1,0:T(8,128)(2,1)S(1)}, u32[]{:S(2)}, u32[]{:S(2)}) collective-permute-start(bf16[4096,128]{1,0:T(8,128)(2,1)} %shard_map.73.piece_ref.refs_3_), channel_id=1, source_target_pairs={{0,1},{1,2},{2,3},{3,0},{4,5},{5,6},{6,7},{7,4},{8,9},{9,10},{10,1... | collective-permute-start | bytes 3145736 | tf_op jit(solution)/shard_map/ppermute | solution.py:31
  78.3 1.3 copy-start.6
  99.7 1.0 copy-start.7
  100.7 43.1 %collective-permute-start.20 = (bf16[4096,128]{1,0:T(8,128)(2,1)}, bf16[4096,128]{1,0:T(8,128)(2,1)S(1)}, u32[]{:S(2)}, u32[]{:S(2)}) collective-permute-start(bf16[4096,128]{1,0:T(8,128)(2,1)} %shard_map.75.piece_ref.refs_4_), channel_id=1, source_target_pairs={{0,1},{1,2},{2,3},{3,0},{4,5},{5,6},{6,7},{7,4},{8,9},{9,10},{10,1... | collective-permute-start | bytes 3145736 | tf_op jit(solution)/shard_map/ppermute | solution.py:31
  100.7 1.3 copy-start.8
  103.4 1.4 collective-permute-start.15
  104.8 6.6 %collective-permute-start.18 = (f32[64,512]{1,0:T(8,128)S(1)}, f32[64,512]{1,0:T(8,128)S(1)}, u32[]{:S(2)}, u32[]{:S(2)}) collective-permute-start(f32[64,512]{1,0:T(8,128)S(1)} %shard_map.77.refs_0_), channel_id=1, source_target_pairs={{0,24},{4,28},{8,16},{12,20},{16,8},{20,12},{24,0},{28,4},{1,25},{... | collective-permute-start | bytes 393224 | tf_op jit(solution)/shard_map/ppermute | solution.py:36
  107.5 6.6 %collective-permute-start.17 = (f32[64,512]{1,0:T(8,128)S(1)}, f32[64,512]{1,0:T(8,128)S(1)}, u32[]{:S(2)}, u32[]{:S(2)}) collective-permute-start(f32[64,512]{1,0:T(8,128)S(1)} %shard_map.77.refs_0_), channel_id=1, source_target_pairs={{0,16},{4,20},{8,24},{12,28},{16,0},{20,4},{24,8},{28,12},{1,17},{... | collective-permute-start | bytes 393224 | tf_op jit(solution)/shard_map/ppermute | solution.py:36
  108.0 6.4 %collective-permute-start.16 = (f32[64,512]{1,0:T(8,128)S(1)}, f32[64,512]{1,0:T(8,128)S(1)}, u32[]{:S(2)}, u32[]{:S(2)}) collective-permute-start(f32[64,512]{1,0:T(8,128)S(1)} %shard_map.77.refs_0_), channel_id=1, source_target_pairs={{0,8},{4,12},{8,0},{12,4},{16,24},{20,28},{24,16},{28,20},{1,9},{5... | collective-permute-start | bytes 393224 | tf_op jit(solution)/shard_map/ppermute | solution.py:36
  114.9 1.3 collective-permute-start.19
  144.6 1.4 collective-permute-start.21
  146.0 6.8 %collective-permute-start.24 = (f32[64,512]{1,0:T(8,128)S(1)}, f32[64,512]{1,0:T(8,128)S(1)}, u32[]{:S(2)}, u32[]{:S(2)}) collective-permute-start(f32[64,512]{1,0:T(8,128)S(1)} %shard_map.83.refs_0_), channel_id=1, source_target_pairs={{0,24},{4,28},{8,16},{12,20},{16,8},{20,12},{24,0},{28,4},{1,25},{... | collective-permute-start | bytes 393224 | tf_op jit(solution)/shard_map/ppermute | solution.py:36
  148.6 6.8 %collective-permute-start.23 = (f32[64,512]{1,0:T(8,128)S(1)}, f32[64,512]{1,0:T(8,128)S(1)}, u32[]{:S(2)}, u32[]{:S(2)}) collective-permute-start(f32[64,512]{1,0:T(8,128)S(1)} %shard_map.83.refs_0_), channel_id=1, source_target_pairs={{0,16},{4,20},{8,24},{12,28},{16,0},{20,4},{24,8},{28,12},{1,17},{... | collective-permute-start | bytes 393224 | tf_op jit(solution)/shard_map/ppermute | solution.py:36
  149.1 6.4 %collective-permute-start.22 = (f32[64,512]{1,0:T(8,128)S(1)}, f32[64,512]{1,0:T(8,128)S(1)}, u32[]{:S(2)}, u32[]{:S(2)}) collective-permute-start(f32[64,512]{1,0:T(8,128)S(1)} %shard_map.83.refs_0_), channel_id=1, source_target_pairs={{0,8},{4,12},{8,0},{12,4},{16,24},{20,28},{24,16},{28,20},{1,9},{5... | collective-permute-start | bytes 393224 | tf_op jit(solution)/shard_map/ppermute | solution.py:36
  155.9 1.3 collective-permute-start.25
  157.4 5.4 %collective-permute-start.26 = (f32[4,128]{1,0:T(4,128)S(1)}, f32[4,128]{1,0:T(4,128)S(1)}, u32[]{:S(2)}, u32[]{:S(2)}) collective-permute-start(f32[4,128]{1,0:T(4,128)S(1)} %pad_maximum_fusion.refs_9_), channel_id=1, source_target_pairs={{0,1},{1,2},{2,3},{3,0},{4,6},{5,7},{6,4},{7,5},{8,9},{9,10},{10,1... | collective-permute-start | bytes 6152 | tf_op jit(solution)/shard_map/ppermute | solution.py:44
  157.5 5.4 %collective-permute-start.28 = (f32[4,128]{1,0:T(4,128)S(1)}, f32[4,128]{1,0:T(4,128)S(1)}, u32[]{:S(2)}, u32[]{:S(2)}) collective-permute-start(f32[4,128]{1,0:T(4,128)S(1)} %pad_maximum_fusion.refs_9_), channel_id=1, source_target_pairs={{0,3},{1,0},{2,1},{3,2},{4,7},{5,4},{6,5},{7,6},{8,11},{9,8},{10,9... | collective-permute-start | bytes 6152 | tf_op jit(solution)/shard_map/ppermute | solution.py:44
  162.8 1.2 collective-permute-start.27

commit v11 on v10

--- a/solution.py
+++ b/solution.py
@@ -241,7 +241,8 @@
     while bits:
         total = add(*summands)
         partners = [bits[0]] if len(bits) == 1 else [bits[0], bits[1], bits[0] ^ bits[1]]
-        summands = [total] + [exchanged(total, "rows", partner) for partner in partners]
+        came = [exchanged(total, "rows", partner) for partner in partners[::-1]]
+        summands = [total] + came[::-1]
         bits = bits[2:]
     mine = dress(step, summands, weights, green_one)
     return join(mine, exchanged(mine, "rows", 1), trace_weights)

time: 171 us -> 171 us (level)
  no operation moved by 1% of the time
where the time goes in v11:
time: 171 us
  waiting for transfers between devices  94.7 us (55%)
  Pallas kernels  33.9 us (20%)
  starting transfers between devices  25 us (15%)
  local copies, waits for them, and re-layouts  14.8 us (9%)
    ppermute x6, waiting for transfers between devices, shifted(): lax.ppermute(block, axis, [(i, (i + shift) % count) for i in range(count)])  58.1 us
    ppermute x21, waiting for transfers between devices, exchanged(): return lax.ppermute(block, axis, [(i, i ^ bit) for i in range(count)])  35 us
    ppermute x21, starting transfers between devices, exchanged(): return lax.ppermute(block, axis, [(i, i ^ bit) for i in range(count)])  14.8 us
    unnamed x31, local copies, waits for them, and re-layouts  14.4 us
    pallas_call x5, Pallas kernels, project(): pl.pallas_call(functools.partial(project_body, first, min(length, 1024)),...  9.57 us
    pallas_call x1, Pallas kernels, slope_early(): pl.pallas_call(functools.partial(slope_early_body, pieces), in_specs=[pl....  7 us
    pallas_call x1, Pallas kernels, slope(): pl.pallas_call(functools.partial(slope_body, pieces), in_specs=[far] * le...  6.91 us
    ppermute x6, starting transfers between devices, shifted(): lax.ppermute(block, axis, [(i, (i + shift) % count) for i in range(count)])  6.37 us
  transfers between devices with their start and end apart: 29, of which 26 were waited for; matrix products, arithmetic and copies ran while one was open for 1% of the time, Pallas kernels for 14%

profile of v11, /device:TPU:0, one launch (start us, length us, event | category | flops | bytes accessed | tf_op | source)
XLA Modules:
  0.0 170.9 jit_solution(5535669747989806479)
XLA Ops:
  0.6 2.4 %shard_map.59 = bf16[4096,128]{1,0:T(8,128)(2,1)} custom-call(bf16[8192,128]{1,0:T(8,128)(2,1)} %refs_0_.5), custom_call_target="tpu_custom_call" | custom-call | tf_op jit(solution)/shard_map/pallas_call | solution.py:106
  3.0 3.1 %collective-permute-start = (bf16[4096,128]{1,0:T(8,128)(2,1)}, bf16[4096,128]{1,0:T(8,128)(2,1)S(1)}, u32[]{:S(2)}, u32[]{:S(2)}) collective-permute-start(bf16[4096,128]{1,0:T(8,128)(2,1)} %shard_map.59), channel_id=1, source_target_pairs={{0,1},{1,2},{2,3},{3,0},{4,5},{5,6},{6,7},{7,4},{8,9},{9,10},{10,1... | collective-permute-start | bytes 3145736 | tf_op jit(solution)/shard_map/ppermute | solution.py:31
  6.1 2.2 %shard_map.66 = bf16[4096,128]{1,0:T(8,128)(2,1)} custom-call(bf16[8192,128]{1,0:T(8,128)(2,1)} %refs_0_.5), custom_call_target="tpu_custom_call" | custom-call | tf_op jit(solution)/shard_map/pallas_call | solution.py:106
  8.3 1.6 collective-permute-start.6
  9.9 3.4 %shard_map.60 = (bf16[8192,512]{1,0:T(8,128)(2,1)S(1)}, f32[256,256]{1,0:T(8,128)S(1)}) custom-call(bf16[8192,512]{1,0:T(8,128)(2,1)} %refs_0_.3, f32[256,256]{1,0:T(8,128)} %refs_1_.1), custom_call_target="tpu_custom_call" | custom-call | tf_op jit(solution)/shard_map/pallas_call | solution.py:86
  13.4 2.8 %shard_map.61 = f32[128,512]{1,0:T(8,128)S(1)} custom-call(bf16[8192,128]{1,0:T(8,128)(2,1)S(1)} %copy-done.2, bf16[8192,512]{1,0:T(8,128)(2,1)S(1)} %get-tuple-element.14.green_ref, f32[128,512]{1,0:T(8,128)S(1)} %broadcast_in_dim.6.acc_ref), custom_call_target="tpu_custom_call" | custom-call | tf_op jit(solution)/shard_map/pallas_call | solution.py:134
  16.2 3.4 %copy-done = bf16[8192,512]{1,0:T(8,128)(2,1)} copy-done((bf16[8192,512]{1,0:T(8,128)(2,1)}, bf16[8192,512]{1,0:T(8,128)(2,1)S(1)}, u32[]{:S(2)}) %copy-start) | copy-done | bytes 8388632
  19.7 1.3 collective-permute-done.1.refs_1_
  21.0 2.5 %collective-permute-start.4 = (f32[64,512]{1,0:T(8,128)S(1)}, f32[64,512]{1,0:T(8,128)S(1)}, u32[]{:S(2)}, u32[]{:S(2)}) collective-permute-start(f32[64,512]{1,0:T(8,128)S(1)} %shard_map.62.refs_0_), channel_id=1, source_target_pairs={{0,24},{4,28},{8,16},{12,20},{16,8},{20,12},{24,0},{28,4},{1,25},{... | collective-permute-start | bytes 393224 | tf_op jit(solution)/shard_map/ppermute | solution.py:36
  24.7 3.1 %collective-permute-done.4.refs_3_ = f32[64,512]{1,0:T(8,128)S(1)} collective-permute-done((f32[64,512]{1,0:T(8,128)S(1)}, f32[64,512]{1,0:T(8,128)S(1)}, u32[]{:S(2)}, u32[]{:S(2)}) %collective-permute-start.4) | collective-permute-done | bytes 131104 | tf_op jit(solution)/shard_map/ppermute | solution.py:36
  27.8 2.5 %collective-permute-done.3.refs_2_ = f32[64,512]{1,0:T(8,128)S(1)} collective-permute-done((f32[64,512]{1,0:T(8,128)S(1)}, f32[64,512]{1,0:T(8,128)S(1)}, u32[]{:S(2)}, u32[]{:S(2)}) %collective-permute-start.3) | collective-permute-done | bytes 131104 | tf_op jit(solution)/shard_map/ppermute | solution.py:36
  31.2 1.0 collective-permute-done.5.other_ref
  32.4 1.0 copy-done.3
  33.4 1.6 collective-permute-start.7
  34.9 3.4 %copy-done.1 = bf16[8192,512]{1,0:T(8,128)(2,1)S(1)} copy-done((bf16[8192,512]{1,0:T(8,128)(2,1)S(1)}, bf16[8192,512]{1,0:T(8,128)(2,1)}, u32[]{:S(2)}) %copy-start.1) | copy-done | bytes 8388632
  38.3 1.2 copy-done.4
  40.5 1.4 shard_map.67.refs_1_.acc_ref
  41.9 13.0 %collective-permute-done.6.refs_0_ = bf16[4096,128]{1,0:T(8,128)(2,1)} collective-permute-done((bf16[4096,128]{1,0:T(8,128)(2,1)}, bf16[4096,128]{1,0:T(8,128)(2,1)}, u32[]{:S(2)}, u32[]{:S(2)}) %collective-permute-start.6) | collective-permute-done | bytes 1048608 | tf_op jit(solution)/shard_map/ppermute | solution.py:31
  54.9 2.8 %shard_map.69 = f32[128,512]{1,0:T(8,128)S(1)} custom-call(bf16[4096,128]{1,0:T(8,128)(2,1)} %shard_map.68.piece_ref.refs_2_, bf16[8192,512]{1,0:T(8,128)(2,1)S(1)} %copy-done.1, f32[128,512]{1,0:T(8,128)S(1)} %shard_map.67.refs_1_.acc_ref), custom_call_target="tpu_custom_call" | custom-call | tf_op jit(solution)/shard_map/pallas_call | solution.py:134
  57.8 1.3 collective-permute-done.8.refs_1_
  59.1 2.7 %collective-permute-start.11 = (f32[64,512]{1,0:T(8,128)S(1)}, f32[64,512]{1,0:T(8,128)S(1)}, u32[]{:S(2)}, u32[]{:S(2)}) collective-permute-start(f32[64,512]{1,0:T(8,128)S(1)} %shard_map.70.refs_0_), channel_id=1, source_target_pairs={{0,24},{4,28},{8,16},{12,20},{16,8},{20,12},{24,0},{28,4},{1,25},{... | collective-permute-start | bytes 393224 | tf_op jit(solution)/shard_map/ppermute | solution.py:36
  62.7 3.1 %collective-permute-done.11.refs_3_ = f32[64,512]{1,0:T(8,128)S(1)} collective-permute-done((f32[64,512]{1,0:T(8,128)S(1)}, f32[64,512]{1,0:T(8,128)S(1)}, u32[]{:S(2)}, u32[]{:S(2)}) %collective-permute-start.11) | collective-permute-done | bytes 131104 | tf_op jit(solution)/shard_map/ppermute | solution.py:36
  65.8 2.7 %collective-permute-done.10.refs_2_ = f32[64,512]{1,0:T(8,128)S(1)} collective-permute-done((f32[64,512]{1,0:T(8,128)S(1)}, f32[64,512]{1,0:T(8,128)S(1)}, u32[]{:S(2)}, u32[]{:S(2)}) %collective-permute-start.10) | collective-permute-done | bytes 131104 | tf_op jit(solution)/shard_map/ppermute | solution.py:36
  69.3 1.2 collective-permute-done.12.other_ref
  70.7 6.6 %collective-permute-done.7.refs_0_ = bf16[4096,128]{1,0:T(8,128)(2,1)S(1)} collective-permute-done((bf16[4096,128]{1,0:T(8,128)(2,1)}, bf16[4096,128]{1,0:T(8,128)(2,1)S(1)}, u32[]{:S(2)}, u32[]{:S(2)}) %collective-permute-start.7) | collective-permute-done | bytes 1048608 | tf_op jit(solution)/shard_map/ppermute | solution.py:31
  77.2 1.0 copy-done.5
  78.3 1.2 copy-done.6
  79.5 1.3 shard_map.74.refs_1_.acc_ref
  80.8 18.9 %collective-permute-done.13.refs_0_ = bf16[4096,128]{1,0:T(8,128)(2,1)S(1)} collective-permute-done((bf16[4096,128]{1,0:T(8,128)(2,1)}, bf16[4096,128]{1,0:T(8,128)(2,1)S(1)}, u32[]{:S(2)}, u32[]{:S(2)}) %collective-permute-start.13) | collective-permute-done | bytes 1048608 | tf_op jit(solution)/shard_map/ppermute | solution.py:31
  99.7 1.0 copy-done.7
  100.7 1.3 copy-done.8
  102.0 1.3 shard_map.76
  103.4 1.3 collective-permute-done.15.refs_1_
  104.8 2.7 %collective-permute-start.18 = (f32[64,512]{1,0:T(8,128)S(1)}, f32[64,512]{1,0:T(8,128)S(1)}, u32[]{:S(2)}, u32[]{:S(2)}) collective-permute-start(f32[64,512]{1,0:T(8,128)S(1)} %shard_map.77.refs_0_), channel_id=1, source_target_pairs={{0,24},{4,28},{8,16},{12,20},{16,8},{20,12},{24,0},{28,4},{1,25},{... | collective-permute-start | bytes 393224 | tf_op jit(solution)/shard_map/ppermute | solution.py:36
  108.4 3.1 %collective-permute-done.18.refs_3_ = f32[64,512]{1,0:T(8,128)S(1)} collective-permute-done((f32[64,512]{1,0:T(8,128)S(1)}, f32[64,512]{1,0:T(8,128)S(1)}, u32[]{:S(2)}, u32[]{:S(2)}) %collective-permute-start.18) | collective-permute-done | bytes 131104 | tf_op jit(solution)/shard_map/ppermute | solution.py:36
  111.4 2.7 %collective-permute-done.17.refs_2_ = f32[64,512]{1,0:T(8,128)S(1)} collective-permute-done((f32[64,512]{1,0:T(8,128)S(1)}, f32[64,512]{1,0:T(8,128)S(1)}, u32[]{:S(2)}, u32[]{:S(2)}) %collective-permute-start.17) | collective-permute-done | bytes 131104 | tf_op jit(solution)/shard_map/ppermute | solution.py:36
  114.9 1.2 collective-permute-done.19.other_ref
  116.3 7.0 %shard_map.81.refs_2_.refs_7_ = f32[8192,512]{1,0:T(8,128)S(1)} custom-call(bf16[8192,128]{1,0:T(8,128)(2,1)} %refs_0_.5, bf16[4096,128]{1,0:T(8,128)(2,1)} %shard_map.65.piece_ref.refs_1_, bf16[4096,128]{1,0:T(8,128)(2,1)} %shard_map.68.piece_ref.refs_2_, bf16[4096,128]{1,0:T(8,128)(2,1)} %shard_map.73.piece_ref.refs_3_, ...), custom_call_target="tpu_custom_call" | custom-call | tf_op jit(solution)/shard_map/pallas_call | solution.py:291
  124.1 19.7 %collective-permute-done.20.refs_0_ = bf16[4096,128]{1,0:T(8,128)(2,1)S(1)} collective-permute-done((bf16[4096,128]{1,0:T(8,128)(2,1)}, bf16[4096,128]{1,0:T(8,128)(2,1)S(1)}, u32[]{:S(2)}, u32[]{:S(2)}) %collective-permute-start.20) | collective-permute-done | bytes 1048608 | tf_op jit(solution)/shard_map/ppermute | solution.py:31
  144.7 1.3 collective-permute-done.21.refs_1_
  146.0 2.5 %collective-permute-start.24 = (f32[64,512]{1,0:T(8,128)S(1)}, f32[64,512]{1,0:T(8,128)S(1)}, u32[]{:S(2)}, u32[]{:S(2)}) collective-permute-start(f32[64,512]{1,0:T(8,128)S(1)} %shard_map.83.refs_0_), channel_id=1, source_target_pairs={{0,24},{4,28},{8,16},{12,20},{16,8},{20,12},{24,0},{28,4},{1,25},{... | collective-permute-start | bytes 393224 | tf_op jit(solution)/shard_map/ppermute | solution.py:36
  149.6 3.2 %collective-permute-done.24.refs_3_ = f32[64,512]{1,0:T(8,128)S(1)} collective-permute-done((f32[64,512]{1,0:T(8,128)S(1)}, f32[64,512]{1,0:T(8,128)S(1)}, u32[]{:S(2)}, u32[]{:S(2)}) %collective-permute-start.24) | collective-permute-done | bytes 131104 | tf_op jit(solution)/shard_map/ppermute | solution.py:36
  152.8 2.5 %collective-permute-done.23.refs_2_ = f32[64,512]{1,0:T(8,128)S(1)} collective-permute-done((f32[64,512]{1,0:T(8,128)S(1)}, f32[64,512]{1,0:T(8,128)S(1)}, u32[]{:S(2)}, u32[]{:S(2)}) %collective-permute-start.23) | collective-permute-done | bytes 131104 | tf_op jit(solution)/shard_map/ppermute | solution.py:36
  156.0 1.2 collective-permute-done.25.other_ref
  157.5 3.8 %collective-permute-start.28 = (f32[4,128]{1,0:T(4,128)S(1)}, f32[4,128]{1,0:T(4,128)S(1)}, u32[]{:S(2)}, u32[]{:S(2)}) collective-permute-start(f32[4,128]{1,0:T(4,128)S(1)} %pad_maximum_fusion.refs_9_), channel_id=1, source_target_pairs={{0,3},{1,0},{2,1},{3,2},{4,7},{5,4},{6,5},{7,6},{8,11},{9,8},{10,9... | collective-permute-start | bytes 6152 | tf_op jit(solution)/shard_map/ppermute | solution.py:44
  161.3 1.6 collective-permute-done.26.refs_10_
  162.8 1.2 collective-permute-done.27.refs_11_
  164.0 6.9 %shard_map.86 = (f32[8192,512]{1,0:T(8,128)}, f32[1,2048]{1,0:T(1,128)}) custom-call(bf16[8192,128]{1,0:T(8,128)(2,1)} %refs_0_.5, bf16[4096,128]{1,0:T(8,128)(2,1)} %shard_map.65.piece_ref.refs_1_, bf16[4096,128]{1,0:T(8,128)(2,1)} %shard_map.68.piece_ref.refs_2_, bf16[4096,128]{1,0:T(8,128)(2,1)} %shard_map.73.piece_ref.refs_3_, ...), custom_call_target="tpu_custom_call" | custom-call | flops 1073741824 | bytes 16777216 | tf_op jit(solution)/shard_map/pallas_call | solution.py:402
  (81 shorter events, 10.5 us)
Async XLA Ops:
  0.6 12.7 %copy-start.2 = (bf16[8192,128]{1,0:T(8,128)(2,1)S(1)}, bf16[8192,128]{1,0:T(8,128)(2,1)}, u32[]{:S(2)}) copy-start(bf16[8192,128]{1,0:T(8,128)(2,1)} %refs_0_.5) | copy-start | bytes 6291460
  3.0 29.4 %collective-permute-start = (bf16[4096,128]{1,0:T(8,128)(2,1)}, bf16[4096,128]{1,0:T(8,128)(2,1)S(1)}, u32[]{:S(2)}, u32[]{:S(2)}) collective-permute-start(bf16[4096,128]{1,0:T(8,128)(2,1)} %shard_map.59), channel_id=1, source_target_pairs={{0,1},{1,2},{2,3},{3,0},{4,5},{5,6},{6,7},{7,4},{8,9},{9,10},{10,1... | collective-permute-start | bytes 3145736 | tf_op jit(solution)/shard_map/ppermute | solution.py:31
  8.3 46.6 %collective-permute-start.6 = (bf16[4096,128]{1,0:T(8,128)(2,1)}, bf16[4096,128]{1,0:T(8,128)(2,1)}, u32[]{:S(2)}, u32[]{:S(2)}) collective-permute-start(bf16[4096,128]{1,0:T(8,128)(2,1)} %shard_map.66), channel_id=1, source_target_pairs={{0,1},{1,2},{2,3},{3,0},{4,5},{5,6},{6,7},{7,4},{8,9},{9,10},{10,1... | collective-permute-start | bytes 3145736 | tf_op jit(solution)/shard_map/ppermute | solution.py:31
  9.9 14.7 %copy-start.12 = (f32[512]{0:T(512)S(1)}, f32[512]{0:T(512)}, u32[]{:S(2)}) copy-start(f32[512]{0:T(512)} %param.7) | copy-start | bytes 6148
  13.4 2.8 %copy-start.9 = (f32[128,512]{1,0:T(8,128)}, f32[128,512]{1,0:T(8,128)S(1)}, u32[]{:S(2)}) copy-start(f32[128,512]{1,0:T(8,128)S(1)} %broadcast_in_dim.6.acc_ref) | copy-start | bytes 786436
  16.2 3.4 %copy-start = (bf16[8192,512]{1,0:T(8,128)(2,1)}, bf16[8192,512]{1,0:T(8,128)(2,1)S(1)}, u32[]{:S(2)}) copy-start(bf16[8192,512]{1,0:T(8,128)(2,1)S(1)} %get-tuple-element.14.green_ref) | copy-start | bytes 25165828
  19.6 1.4 collective-permute-start.1
  21.0 6.8 %collective-permute-start.4 = (f32[64,512]{1,0:T(8,128)S(1)}, f32[64,512]{1,0:T(8,128)S(1)}, u32[]{:S(2)}, u32[]{:S(2)}) collective-permute-start(f32[64,512]{1,0:T(8,128)S(1)} %shard_map.62.refs_0_), channel_id=1, source_target_pairs={{0,24},{4,28},{8,16},{12,20},{16,8},{20,12},{24,0},{28,4},{1,25},{... | collective-permute-start | bytes 393224 | tf_op jit(solution)/shard_map/ppermute | solution.py:36
  23.6 6.8 %collective-permute-start.3 = (f32[64,512]{1,0:T(8,128)S(1)}, f32[64,512]{1,0:T(8,128)S(1)}, u32[]{:S(2)}, u32[]{:S(2)}) collective-permute-start(f32[64,512]{1,0:T(8,128)S(1)} %shard_map.62.refs_0_), channel_id=1, source_target_pairs={{0,16},{4,20},{8,24},{12,28},{16,0},{20,4},{24,8},{28,12},{1,17},{... | collective-permute-start | bytes 393224 | tf_op jit(solution)/shard_map/ppermute | solution.py:36
  24.1 6.4 %collective-permute-start.2 = (f32[64,512]{1,0:T(8,128)S(1)}, f32[64,512]{1,0:T(8,128)S(1)}, u32[]{:S(2)}, u32[]{:S(2)}) collective-permute-start(f32[64,512]{1,0:T(8,128)S(1)} %shard_map.62.refs_0_), channel_id=1, source_target_pairs={{0,8},{4,12},{8,0},{12,4},{16,24},{20,28},{24,16},{28,20},{1,9},{5... | collective-permute-start | bytes 393224 | tf_op jit(solution)/shard_map/ppermute | solution.py:36
  30.9 1.3 collective-permute-start.5
  32.4 1.0 copy-start.3
  33.4 43.9 %collective-permute-start.7 = (bf16[4096,128]{1,0:T(8,128)(2,1)}, bf16[4096,128]{1,0:T(8,128)(2,1)S(1)}, u32[]{:S(2)}, u32[]{:S(2)}) collective-permute-start(bf16[4096,128]{1,0:T(8,128)(2,1)} %shard_map.65.piece_ref.refs_1_), channel_id=1, source_target_pairs={{0,1},{1,2},{2,3},{3,0},{4,5},{5,6},{6,7},{7,4},{8,9},{9,10},{10,1... | collective-permute-start | bytes 3145736 | tf_op jit(solution)/shard_map/ppermute | solution.py:31
  34.9 3.4 %copy-start.1 = (bf16[8192,512]{1,0:T(8,128)(2,1)S(1)}, bf16[8192,512]{1,0:T(8,128)(2,1)}, u32[]{:S(2)}) copy-start(bf16[8192,512]{1,0:T(8,128)(2,1)} %copy-done) | copy-start | bytes 25165828
  38.3 1.2 copy-start.4
  39.5 0.9 copy-start.10
  41.9 36.4 %slice-start = ((s8[8388608]{0:T(1024)(128)(4,1)}), s8[4194304]{0:T(1024)(128)(4,1)S(1)}, s32[]{:S(2)}) async-start(s8[8388608]{0:T(1024)(128)(4,1)} %bitcast.9), calls=%async_computation | async-start | bytes 8388608
  41.9 36.4 %copy-start.11 = (f32[128,512]{1,0:T(8,128)S(1)}, f32[128,512]{1,0:T(8,128)}, u32[]{:S(2)}) copy-start(f32[128,512]{1,0:T(8,128)} %copy-done.9) | copy-start | bytes 786436
  54.9 23.4 %slice-start.1 = ((s8[8388608]{0:T(1024)(128)(4,1)}), s8[4194304]{0:T(1024)(128)(4,1)S(1)}, s32[]{:S(2)}) async-start(s8[8388608]{0:T(1024)(128)(4,1)} %bitcast.9), calls=%async_computation.1 | async-start | bytes 8388608
  54.9 44.8 %collective-permute-start.13 = (bf16[4096,128]{1,0:T(8,128)(2,1)}, bf16[4096,128]{1,0:T(8,128)(2,1)S(1)}, u32[]{:S(2)}, u32[]{:S(2)}) collective-permute-start(bf16[4096,128]{1,0:T(8,128)(2,1)} %shard_map.68.piece_ref.refs_2_), channel_id=1, source_target_pairs={{0,1},{1,2},{2,3},{3,0},{4,5},{5,6},{6,7},{7,4},{8,9},{9,10},{10,1... | collective-permute-start | bytes 3145736 | tf_op jit(solution)/shard_map/ppermute | solution.py:31
  57.7 1.4 collective-permute-start.8
  59.1 6.7 %collective-permute-start.11 = (f32[64,512]{1,0:T(8,128)S(1)}, f32[64,512]{1,0:T(8,128)S(1)}, u32[]{:S(2)}, u32[]{:S(2)}) collective-permute-start(f32[64,512]{1,0:T(8,128)S(1)} %shard_map.70.refs_0_), channel_id=1, source_target_pairs={{0,24},{4,28},{8,16},{12,20},{16,8},{20,12},{24,0},{28,4},{1,25},{... | collective-permute-start | bytes 393224 | tf_op jit(solution)/shard_map/ppermute | solution.py:36
  61.9 6.6 %collective-permute-start.10 = (f32[64,512]{1,0:T(8,128)S(1)}, f32[64,512]{1,0:T(8,128)S(1)}, u32[]{:S(2)}, u32[]{:S(2)}) collective-permute-start(f32[64,512]{1,0:T(8,128)S(1)} %shard_map.70.refs_0_), channel_id=1, source_target_pairs={{0,16},{4,20},{8,24},{12,28},{16,0},{20,4},{24,8},{28,12},{1,17},{... | collective-permute-start | bytes 393224 | tf_op jit(solution)/shard_map/ppermute | solution.py:36
  62.4 6.4 %collective-permute-start.9 = (f32[64,512]{1,0:T(8,128)S(1)}, f32[64,512]{1,0:T(8,128)S(1)}, u32[]{:S(2)}, u32[]{:S(2)}) collective-permute-start(f32[64,512]{1,0:T(8,128)S(1)} %shard_map.70.refs_0_), channel_id=1, source_target_pairs={{0,8},{4,12},{8,0},{12,4},{16,24},{20,28},{24,16},{28,20},{1,9},{5... | collective-permute-start | bytes 393224 | tf_op jit(solution)/shard_map/ppermute | solution.py:36
  69.2 1.3 collective-permute-start.12
  77.2 1.0 copy-start.5
  78.2 45.1 %collective-permute-start.14 = (bf16[4096,128]{1,0:T(8,128)(2,1)}, bf16[4096,128]{1,0:T(8,128)(2,1)S(1)}, u32[]{:S(2)}, u32[]{:S(2)}) collective-permute-start(bf16[4096,128]{1,0:T(8,128)(2,1)} %shard_map.73.piece_ref.refs_3_), channel_id=1, source_target_pairs={{0,1},{1,2},{2,3},{3,0},{4,5},{5,6},{6,7},{7,4},{8,9},{9,10},{10,1... | collective-permute-start | bytes 3145736 | tf_op jit(solution)/shard_map/ppermute | solution.py:31
  78.3 1.3 copy-start.6
  99.7 1.0 copy-start.7
  100.7 43.1 %collective-permute-start.20 = (bf16[4096,128]{1,0:T(8,128)(2,1)}, bf16[4096,128]{1,0:T(8,128)(2,1)S(1)}, u32[]{:S(2)}, u32[]{:S(2)}) collective-permute-start(bf16[4096,128]{1,0:T(8,128)(2,1)} %shard_map.75.piece_ref.refs_4_), channel_id=1, source_target_pairs={{0,1},{1,2},{2,3},{3,0},{4,5},{5,6},{6,7},{7,4},{8,9},{9,10},{10,1... | collective-permute-start | bytes 3145736 | tf_op jit(solution)/shard_map/ppermute | solution.py:31
  100.7 1.3 copy-start.8
  103.4 1.4 collective-permute-start.15
  104.8 6.6 %collective-permute-start.18 = (f32[64,512]{1,0:T(8,128)S(1)}, f32[64,512]{1,0:T(8,128)S(1)}, u32[]{:S(2)}, u32[]{:S(2)}) collective-permute-start(f32[64,512]{1,0:T(8,128)S(1)} %shard_map.77.refs_0_), channel_id=1, source_target_pairs={{0,24},{4,28},{8,16},{12,20},{16,8},{20,12},{24,0},{28,4},{1,25},{... | collective-permute-start | bytes 393224 | tf_op jit(solution)/shard_map/ppermute | solution.py:36
  107.5 6.6 %collective-permute-start.17 = (f32[64,512]{1,0:T(8,128)S(1)}, f32[64,512]{1,0:T(8,128)S(1)}, u32[]{:S(2)}, u32[]{:S(2)}) collective-permute-start(f32[64,512]{1,0:T(8,128)S(1)} %shard_map.77.refs_0_), channel_id=1, source_target_pairs={{0,16},{4,20},{8,24},{12,28},{16,0},{20,4},{24,8},{28,12},{1,17},{... | collective-permute-start | bytes 393224 | tf_op jit(solution)/shard_map/ppermute | solution.py:36
  108.0 6.4 %collective-permute-start.16 = (f32[64,512]{1,0:T(8,128)S(1)}, f32[64,512]{1,0:T(8,128)S(1)}, u32[]{:S(2)}, u32[]{:S(2)}) collective-permute-start(f32[64,512]{1,0:T(8,128)S(1)} %shard_map.77.refs_0_), channel_id=1, source_target_pairs={{0,8},{4,12},{8,0},{12,4},{16,24},{20,28},{24,16},{28,20},{1,9},{5... | collective-permute-start | bytes 393224 | tf_op jit(solution)/shard_map/ppermute | solution.py:36
  114.9 1.3 collective-permute-start.19
  144.6 1.4 collective-permute-start.21
  146.0 6.8 %collective-permute-start.24 = (f32[64,512]{1,0:T(8,128)S(1)}, f32[64,512]{1,0:T(8,128)S(1)}, u32[]{:S(2)}, u32[]{:S(2)}) collective-permute-start(f32[64,512]{1,0:T(8,128)S(1)} %shard_map.83.refs_0_), channel_id=1, source_target_pairs={{0,24},{4,28},{8,16},{12,20},{16,8},{20,12},{24,0},{28,4},{1,25},{... | collective-permute-start | bytes 393224 | tf_op jit(solution)/shard_map/ppermute | solution.py:36
  148.6 6.8 %collective-permute-start.23 = (f32[64,512]{1,0:T(8,128)S(1)}, f32[64,512]{1,0:T(8,128)S(1)}, u32[]{:S(2)}, u32[]{:S(2)}) collective-permute-start(f32[64,512]{1,0:T(8,128)S(1)} %shard_map.83.refs_0_), channel_id=1, source_target_pairs={{0,16},{4,20},{8,24},{12,28},{16,0},{20,4},{24,8},{28,12},{1,17},{... | collective-permute-start | bytes 393224 | tf_op jit(solution)/shard_map/ppermute | solution.py:36
  149.1 6.4 %collective-permute-start.22 = (f32[64,512]{1,0:T(8,128)S(1)}, f32[64,512]{1,0:T(8,128)S(1)}, u32[]{:S(2)}, u32[]{:S(2)}) collective-permute-start(f32[64,512]{1,0:T(8,128)S(1)} %shard_map.83.refs_0_), channel_id=1, source_target_pairs={{0,8},{4,12},{8,0},{12,4},{16,24},{20,28},{24,16},{28,20},{1,9},{5... | collective-permute-start | bytes 393224 | tf_op jit(solution)/shard_map/ppermute | solution.py:36
  155.9 1.3 collective-permute-start.25
  157.4 5.4 %collective-permute-start.26 = (f32[4,128]{1,0:T(4,128)S(1)}, f32[4,128]{1,0:T(4,128)S(1)}, u32[]{:S(2)}, u32[]{:S(2)}) collective-permute-start(f32[4,128]{1,0:T(4,128)S(1)} %pad_maximum_fusion.refs_9_), channel_id=1, source_target_pairs={{0,1},{1,2},{2,3},{3,0},{4,6},{5,7},{6,4},{7,5},{8,9},{9,10},{10,1... | collective-permute-start | bytes 6152 | tf_op jit(solution)/shard_map/ppermute | solution.py:44
  157.5 5.4 %collective-permute-start.28 = (f32[4,128]{1,0:T(4,128)S(1)}, f32[4,128]{1,0:T(4,128)S(1)}, u32[]{:S(2)}, u32[]{:S(2)}) collective-permute-start(f32[4,128]{1,0:T(4,128)S(1)} %pad_maximum_fusion.refs_9_), channel_id=1, source_target_pairs={{0,3},{1,0},{2,1},{3,2},{4,7},{5,4},{6,5},{7,6},{8,11},{9,8},{10,9... | collective-permute-start | bytes 6152 | tf_op jit(solution)/shard_map/ppermute | solution.py:44
  162.8 1.2 collective-permute-start.27
